TPU v7x, 32 devices: a whole 2x2x4 slice. The times are simulated.
32 devices in a mesh: dp: 8 (over z, x), tensor: 4 (over y, core).
Axes of the slice: x: 2, y: 2, z: 4, core: 2. Of those that a mesh axis runs over, the one named last changes fastest.
Arguments:
- inputs: bfloat16 [16384, 1024], P(('dp', 'tensor')), may hold values from -12 to 12
- cotangent: bfloat16 [16384, 1024], P(('dp', 'tensor')), may hold values from -12 to 12
- routes: int32 [16384, 1], P('dp'), may hold values from 0 to 3
- prefixes: int32 [16], P('dp'), may hold values from 102 to 512
- gain_one: float32 [1024], replicated, may hold values from 0.5 to 1.5
- shift_one: float32 [1024], replicated, may hold values from -1.25 to 1.25
- qkv_weight: bfloat16 [1024, 3, 1024], P(None, None, 'tensor'), may hold values from -0.1875 to 0.1875
- out_weight: bfloat16 [1024, 1024], P('tensor'), may hold values from -1.5 to 1.5
- gain_two: float32 [1024], replicated, may hold values from 0.5 to 1.5
- shift_two: float32 [1024], replicated, may hold values from -1.25 to 1.25
- up_weight: bfloat16 [1024, 4096], P(None, 'tensor'), may hold values from -0.1875 to 0.1875
- down_weight: bfloat16 [4096, 1024], P('tensor'), may hold values from -0.1875 to 0.1875
- expert_up: bfloat16 [4, 1024, 4096], P(None, None, 'tensor'), may hold values from -0.1875 to 0.1875
- expert_down: bfloat16 [4, 4096, 1024], P(None, 'tensor'), may hold values from -0.5 to 0.5
- router_weight: bfloat16 [1024, 4], replicated, may hold values from -0.125 to 0.125
- mix_weight: bfloat16 [1024, 2], replicated, may hold values from -0.125 to 0.125
Outputs:
- layer_output: bfloat16 [16384, 1024], P(('dp', 'tensor'))
- input_grad: float32 [16384, 1024], P(('dp', 'tensor'))
- gain_one_grad: float32 [1024], P(('dp', 'tensor'))
- shift_one_grad: float32 [1024], P(('dp', 'tensor'))
- qkv_weight_grad: float32 [1024, 3, 1024], P('dp', None, 'tensor')
- out_weight_grad: float32 [1024, 1024], P('tensor', 'dp')
- gain_two_grad: float32 [1024], P(('dp', 'tensor'))
- shift_two_grad: float32 [1024], P(('dp', 'tensor'))
- up_weight_grad: float32 [1024, 4096], P('dp', 'tensor')
- down_weight_grad: float32 [4096, 1024], P('tensor', 'dp')
- expert_up_grad: float32 [4, 1024, 4096], P(None, 'dp', 'tensor')
- expert_down_grad: float32 [4, 4096, 1024], P(None, 'tensor', 'dp')
- router_weight_grad: float32 [1024, 4], P(('dp', 'tensor'))
- mix_weight_grad: float32 [1024, 2], P(('dp', 'tensor'))
All inputs are finite; a program needn't handle non-finite values.
Results may differ from a plain program's by a relative error of at most 0.03.
Values may be sent and summed in bfloat16 or wider, within the bound.
No kernel may reach another device: no remote copies, remote signals or barrier semaphores. Data moves between devices by JAX's collectives and lax.ppermute only.
A program may use at most 320 MiB of HBM per device.

v0:
```python
from functools import partial

import jax
import jax.numpy as jnp
from jax import lax
from jax.sharding import PartitionSpec as P

HD = 64
TILE = 128
TGROUP = 4


epsilon = 1e-05
exact_mode = lax.Precision.HIGHEST
masked_score = -1e30


def layer_norm(values, norm_gain, norm_shift):
    average = jnp.mean(values, axis=-1, keepdims=True)
    centered = values - average
    variance = jnp.mean(centered * centered, axis=-1, keepdims=True)
    return centered * lax.rsqrt(variance + epsilon) * norm_gain + norm_shift


def gelu_exact(values):
    return jax.nn.gelu(values, approximate=False)


def product(left_side, right_side, pattern):
    return jnp.einsum(pattern, left_side, right_side, preferred_element_type=jnp.float32)


def visible_mask(first_row, row_count, length, prefix_len):
    query_pos = first_row + jnp.arange(row_count)[:, None]
    key_pos = jnp.arange(length)[None, :]
    return (key_pos <= query_pos) | (key_pos < prefix_len)


def mixing_terms(normed, router_matrix, mix_matrix, chosen):
    route_prob = jax.nn.softmax(jnp.dot(normed, router_matrix, precision=exact_mode), axis=-1)
    gate_prob = jnp.sum(route_prob * chosen, axis=-1)
    mixing = jax.nn.softmax(jnp.dot(normed, mix_matrix, precision=exact_mode), axis=-1)
    return (mixing[:, 0], mixing[:, 1] * gate_prob)


def expert_slots(route_ids, expert_count, tile_rows):
    onehot = (route_ids[:, None] == jnp.arange(expert_count)[None, :]).astype(jnp.int32)
    counts = jnp.sum(onehot, axis=0)
    padded = (counts + tile_rows - 1) // tile_rows * tile_rows
    expert_ends = jnp.cumsum(padded)
    expert_starts = expert_ends - padded
    position = jnp.cumsum(onehot, axis=0) - onehot
    slot_index = jnp.sum(onehot * (expert_starts[None, :] + position), axis=1)
    return (slot_index, expert_starts, expert_ends)


def attend_forward(seq_pair, head_count, score_scale):
    qkv_seq, prefix_len = seq_pair
    length = qkv_seq.shape[0]
    block_rows = min(512, length)
    queries = qkv_seq[:, 0].reshape(length, head_count, -1)
    key_rows = qkv_seq[:, 1].reshape(length, head_count, -1)
    value_rows = qkv_seq[:, 2].reshape(length, head_count, -1)
    context_parts = []
    lse_parts = []
    for first_row in range(0, length, block_rows):
        scores = (
            product(queries[first_row : first_row + block_rows], key_rows, "qhd,khd->hqk")
            * score_scale
        )
        visible = visible_mask(first_row, block_rows, length, prefix_len)
        scores = jnp.where(visible[None], scores, masked_score)
        row_max = jnp.max(scores, axis=-1, keepdims=True)
        weights = jnp.exp(scores - row_max)
        weight_sum = jnp.sum(weights, axis=-1, keepdims=True)
        probability = (weights / weight_sum).astype(jnp.bfloat16)
        context = product(probability, value_rows, "hqk,khd->qhd")
        context_parts.append(context.reshape(block_rows, -1).astype(jnp.bfloat16))
        lse_parts.append((row_max + jnp.log(weight_sum))[:, :, 0])
    return (jnp.concatenate(context_parts, 0), jnp.concatenate(lse_parts, 1))


def attend_backward(seq_items, head_count, score_scale):
    qkv_seq, lse_seq, grad_seq, prefix_len = seq_items
    length = qkv_seq.shape[0]
    block_rows = min(512, length)
    queries = qkv_seq[:, 0].reshape(length, head_count, -1)
    key_rows = qkv_seq[:, 1].reshape(length, head_count, -1)
    value_rows = qkv_seq[:, 2].reshape(length, head_count, -1)
    key_grad = jnp.zeros(key_rows.shape, jnp.float32)
    value_grad = jnp.zeros(value_rows.shape, jnp.float32)
    query_grads = []
    for first_row in range(0, length, block_rows):
        query_block = queries[first_row : first_row + block_rows]
        scores = product(query_block, key_rows, "qhd,khd->hqk") * score_scale
        visible = visible_mask(first_row, block_rows, length, prefix_len)
        scores = jnp.where(visible[None], scores, masked_score)
        probability = jnp.exp(scores - lse_seq[:, first_row : first_row + block_rows, None])
        grad_block = grad_seq[first_row : first_row + block_rows].reshape(
            block_rows, head_count, -1
        )
        value_grad = value_grad + product(
            probability.astype(jnp.bfloat16), grad_block, "hqk,qhd->khd"
        )
        prob_grad = product(grad_block, value_rows, "qhd,khd->hqk")
        row_inner = jnp.sum(probability * prob_grad, axis=-1, keepdims=True)
        score_grad = (probability * (prob_grad - row_inner)).astype(jnp.bfloat16)
        query_grads.append(product(score_grad, key_rows, "hqk,khd->qhd") * score_scale)
        key_grad = key_grad + product(score_grad, query_block, "hqk,qhd->khd") * score_scale
    query_grad = jnp.concatenate(query_grads, 0)
    stacked = jnp.stack([query_grad, key_grad, value_grad], axis=1)
    return stacked.reshape(length, 3, -1).astype(jnp.bfloat16)


def with_margin(buffer, margin_rows):
    return jnp.concatenate([buffer, jnp.zeros((margin_rows, buffer.shape[1]), buffer.dtype)], 0)


def expert_weight_grads(
    rows_buffer, pre_grad_buffer, hidden_buffer, cot_buffer, expert_starts, expert_ends, window_rows
):
    rows_wide = with_margin(rows_buffer, window_rows)
    pre_wide = with_margin(pre_grad_buffer, window_rows)
    hidden_wide = with_margin(hidden_buffer, window_rows)
    cot_wide = with_margin(cot_buffer, window_rows)
    model_width = rows_buffer.shape[1]
    hidden_width = hidden_buffer.shape[1]
    up_list = []
    down_list = []
    for expert_index in range(expert_starts.shape[0]):
        block_first = expert_starts[expert_index]
        block_end = expert_ends[expert_index]
        block_count = (block_end - block_first + window_rows - 1) // window_rows

        def add_block(block_index, totals, block_first=block_first, block_end=block_end):
            begin = block_first + block_index * window_rows
            inside = (begin + jnp.arange(window_rows) < block_end)[:, None]
            row_block = lax.dynamic_slice_in_dim(rows_wide, begin, window_rows, 0)
            hidden_block = lax.dynamic_slice_in_dim(hidden_wide, begin, window_rows, 0)
            pre_block = jnp.where(
                inside,
                lax.dynamic_slice_in_dim(pre_wide, begin, window_rows, 0),
                jnp.zeros((), jnp.bfloat16),
            )
            cot_block = jnp.where(
                inside,
                lax.dynamic_slice_in_dim(cot_wide, begin, window_rows, 0),
                jnp.zeros((), jnp.bfloat16),
            )
            return (
                totals[0] + product(row_block, pre_block, "nd,nf->df"),
                totals[1] + product(hidden_block, cot_block, "nf,nd->fd"),
            )

        start_totals = (
            jnp.zeros((model_width, hidden_width), jnp.float32),
            jnp.zeros((hidden_width, model_width), jnp.float32),
        )
        up_total, down_total = lax.fori_loop(0, block_count, add_block, start_totals)
        up_list.append(up_total)
        down_list.append(down_total)
    return (jnp.stack(up_list, 0), jnp.stack(down_list, 0))


def shards(
    inputs,
    cotangent,
    routes,
    prefixes,
    gain_one,
    shift_one,
    qkv_weight,
    out_weight,
    gain_two,
    shift_two,
    up_weight,
    down_weight,
    expert_up,
    expert_down,
    router_weight,
    mix_weight,
):
    own_rows, model_width = inputs.shape
    heads_local = qkv_weight.shape[2]
    head_count = heads_local // HD
    seq_count = prefixes.shape[0]
    total_rows = routes.shape[0]
    seq_len = total_rows // seq_count
    expert_count = expert_up.shape[0]
    score_scale = HD ** (-0.5)
    own_start = lax.axis_index("tensor") * own_rows
    route_ids = routes[:, 0]
    own_routes = lax.dynamic_slice_in_dim(route_ids, own_start, own_rows)
    picked = (own_routes[:, None] == jnp.arange(expert_count)[None, :]).astype(jnp.float32)
    router_wide = router_weight.astype(jnp.float32)
    mixer_wide = mix_weight.astype(jnp.float32)
    inputs_wide = inputs.astype(jnp.float32)
    normed_one_wide, norm_one_back = jax.vjp(layer_norm, inputs_wide, gain_one, shift_one)
    normed_one = normed_one_wide.astype(jnp.bfloat16)
    gathered_one = lax.all_gather(normed_one, "tensor", axis=0, tiled=True)
    qkv_matrix = qkv_weight.reshape(model_width, 3 * heads_local)
    qkv_flat = product(gathered_one, qkv_matrix, "nd,dc->nc").astype(jnp.bfloat16)
    qkv_seq = qkv_flat.reshape(seq_count, seq_len, 3, heads_local)
    contexts, lse_all = lax.map(
        partial(attend_forward, head_count=head_count, score_scale=score_scale), (qkv_seq, prefixes)
    )
    context_flat = contexts.reshape(total_rows, heads_local)
    attention = lax.psum_scatter(
        product(
            lax.slice_in_dim(context_flat, 0, own_rows * lax.axis_size("tensor"), axis=0),
            out_weight,
            "nh,hd->nd",
        ).astype(jnp.bfloat16),
        "tensor",
        scatter_dimension=0,
        tiled=True,
    ).astype(jnp.float32)
    middle = inputs_wide + attention
    normed_two_wide, norm_two_back = jax.vjp(layer_norm, middle, gain_two, shift_two)
    normed_two = normed_two_wide.astype(jnp.bfloat16)

    def own_mixing(normed, router_matrix, mix_matrix):
        return mixing_terms(normed, router_matrix, mix_matrix, picked)

    (dense_coef, expert_coef), mixing_back = jax.vjp(
        own_mixing, normed_two.astype(jnp.float32), router_wide, mixer_wide
    )
    gathered_two = lax.all_gather(normed_two, "tensor", axis=0, tiled=True)
    dense_pre = product(gathered_two, up_weight, "nd,df->nf")
    dense_hidden = gelu_exact(dense_pre).astype(jnp.bfloat16)
    dense_part = product(dense_hidden, down_weight, "nf,fd->nd")
    slot_index, expert_starts, expert_ends = expert_slots(route_ids, expert_count, TILE)
    buffer_rows = total_rows + expert_count * TILE
    tile_first = jnp.arange(buffer_rows // TILE) * TILE
    tile_owner = jnp.minimum(
        jnp.sum((expert_ends[None, :] <= tile_first[:, None]).astype(jnp.int32), 1),
        expert_count - 1,
    )
    step_count = buffer_rows // (TILE * TGROUP)
    owner_steps = tile_owner.reshape(step_count, TGROUP)
    routed_rows = (
        jnp.zeros((buffer_rows, model_width), jnp.bfloat16).at[slot_index].set(gathered_two)
    )
    routed_steps = routed_rows.reshape(step_count, TGROUP, TILE, model_width)

    def expert_forward(running, scan_item):
        tile_rows, owners = scan_item
        pre_act = product(tile_rows, expert_up[owners], "tnd,tdf->tnf")
        hidden = gelu_exact(pre_act).astype(jnp.bfloat16)
        branch = product(hidden, expert_down[owners], "tnf,tfd->tnd")
        return (running, (pre_act, hidden, branch))

    _, (expert_pre, expert_hidden, expert_result) = lax.scan(
        expert_forward, jnp.zeros((), jnp.float32), (routed_steps, owner_steps)
    )
    expert_part = expert_result.reshape(buffer_rows, model_width)[slot_index]
    dense_own, expert_own = (
        lax.psum_scatter(
            dense_part.astype(jnp.bfloat16), "tensor", scatter_dimension=0, tiled=True
        ).astype(jnp.float32),
        lax.psum_scatter(
            expert_part.astype(jnp.bfloat16), "tensor", scatter_dimension=0, tiled=True
        ).astype(jnp.float32),
    )
    layer_output = (
        middle + dense_coef[:, None] * dense_own + expert_coef[:, None] * expert_own
    ).astype(jnp.bfloat16)
    upstream = cotangent.astype(jnp.float32)
    dense_low = (upstream * dense_coef[:, None]).astype(jnp.bfloat16)
    expert_low = (upstream * expert_coef[:, None]).astype(jnp.bfloat16)
    coef_grads = (jnp.sum(upstream * dense_own, axis=1), jnp.sum(upstream * expert_own, axis=1))
    dense_cot, expert_cot = (
        lax.all_gather(dense_low, "tensor", axis=0, tiled=True),
        lax.all_gather(expert_low, "tensor", axis=0, tiled=True),
    )
    normed_from_mix, router_grad, mixer_grad = mixing_back((coef_grads[0], coef_grads[1]))
    dense_hidden_grad = product(dense_cot, down_weight, "nd,fd->nf")
    _, dense_gelu_back = jax.vjp(gelu_exact, dense_pre)
    dense_pre_grad = dense_gelu_back(dense_hidden_grad)[0].astype(jnp.bfloat16)
    down_grad = product(dense_hidden, dense_cot, "nf,nd->fd")
    up_grad = product(gathered_two, dense_pre_grad, "nd,nf->df")
    cot_buffer = jnp.zeros((buffer_rows, model_width), jnp.bfloat16).at[slot_index].set(expert_cot)
    cot_steps = cot_buffer.reshape(step_count, TGROUP, TILE, model_width)

    def expert_backward(running, scan_item):
        tile_cot, pre_act, owners = scan_item
        hidden_grad = product(tile_cot, expert_down[owners], "tnd,tfd->tnf")
        _, gelu_back = jax.vjp(gelu_exact, pre_act)
        pre_grad = gelu_back(hidden_grad)[0].astype(jnp.bfloat16)
        row_grad = product(pre_grad, expert_up[owners], "tnf,tdf->tnd")
        return (running, (pre_grad, row_grad))

    _, (expert_pre_grad, row_grads) = lax.scan(
        expert_backward, jnp.zeros((), jnp.float32), (cot_steps, expert_pre, owner_steps)
    )
    hidden_width = expert_hidden.shape[-1]
    expert_up_total, expert_down_total = expert_weight_grads(
        routed_rows,
        expert_pre_grad.reshape(buffer_rows, hidden_width),
        expert_hidden.reshape(buffer_rows, hidden_width),
        cot_buffer,
        expert_starts,
        expert_ends,
        TILE * TGROUP,
    )
    expert_input_grad = row_grads.reshape(buffer_rows, model_width)[slot_index]
    dense_term = product(
        lax.slice_in_dim(dense_pre_grad, 0, own_rows * lax.axis_size("tensor"), axis=0),
        up_weight,
        "nf,df->nd",
    )
    normed_two_grad = (
        lax.psum_scatter(
            (dense_term + expert_input_grad).astype(jnp.bfloat16),
            "tensor",
            scatter_dimension=0,
            tiled=True,
        ).astype(jnp.float32)
        + normed_from_mix
    )
    middle_from_norm, gain_two_grad, shift_two_grad = norm_two_back(normed_two_grad)
    middle_grad = upstream + middle_from_norm
    middle_cot = lax.all_gather(middle_grad.astype(jnp.bfloat16), "tensor", axis=0, tiled=True)
    out_grad = product(context_flat, middle_cot, "nh,nd->hd")
    context_grad = product(middle_cot, out_weight, "nd,hd->nh").astype(jnp.bfloat16)
    qkv_grad = lax.map(
        partial(attend_backward, head_count=head_count, score_scale=score_scale),
        (qkv_seq, lse_all, context_grad.reshape(seq_count, seq_len, heads_local), prefixes),
    )
    qkv_grad_flat = qkv_grad.reshape(total_rows, 3 * heads_local)
    qkv_weight_grad = product(gathered_one, qkv_grad_flat, "nd,nc->dc").reshape(
        model_width, 3, heads_local
    )
    normed_one_grad = lax.psum_scatter(
        product(qkv_grad_flat, qkv_matrix, "nc,dc->nd").astype(jnp.bfloat16),
        "tensor",
        scatter_dimension=0,
        tiled=True,
    ).astype(jnp.float32)
    input_from_norm, gain_one_grad, shift_one_grad = norm_one_back(normed_one_grad)
    input_grad = middle_grad + input_from_norm
    qkv_out, attn_out_grad, up_out, down_out, expert_up_out, expert_down_out = (
        lax.psum_scatter(
            qkv_weight_grad.astype(jnp.bfloat16), "dp", scatter_dimension=0, tiled=True
        ).astype(jnp.float32),
        lax.psum_scatter(
            out_grad.astype(jnp.bfloat16), "dp", scatter_dimension=1, tiled=True
        ).astype(jnp.float32),
        lax.psum_scatter(
            up_grad.astype(jnp.bfloat16), "dp", scatter_dimension=0, tiled=True
        ).astype(jnp.float32),
        lax.psum_scatter(
            down_grad.astype(jnp.bfloat16), "dp", scatter_dimension=1, tiled=True
        ).astype(jnp.float32),
        lax.psum_scatter(
            expert_up_total.astype(jnp.bfloat16), "dp", scatter_dimension=1, tiled=True
        ).astype(jnp.float32),
        lax.psum_scatter(
            expert_down_total.astype(jnp.bfloat16), "dp", scatter_dimension=2, tiled=True
        ).astype(jnp.float32),
    )
    gain_one_out, shift_one_out, gain_two_out, shift_two_out, router_out, mixer_out = (
        lax.psum_scatter(gain_one_grad, ("dp", "tensor"), scatter_dimension=0, tiled=True),
        lax.psum_scatter(shift_one_grad, ("dp", "tensor"), scatter_dimension=0, tiled=True),
        lax.psum_scatter(gain_two_grad, ("dp", "tensor"), scatter_dimension=0, tiled=True),
        lax.psum_scatter(shift_two_grad, ("dp", "tensor"), scatter_dimension=0, tiled=True),
        lax.psum_scatter(router_grad, ("dp", "tensor"), scatter_dimension=0, tiled=True),
        lax.psum_scatter(mixer_grad, ("dp", "tensor"), scatter_dimension=0, tiled=True),
    )
    return (
        layer_output,
        input_grad,
        gain_one_out,
        shift_one_out,
        qkv_out,
        attn_out_grad,
        gain_two_out,
        shift_two_out,
        up_out,
        down_out,
        expert_up_out,
        expert_down_out,
        router_out,
        mixer_out,
    )


def solution(mesh):
    in_specs = (
        P(("dp", "tensor"), None),
        P(("dp", "tensor"), None),
        P("dp", None),
        P("dp"),
        P(),
        P(),
        P(None, None, "tensor"),
        P("tensor", None),
        P(),
        P(),
        P(None, "tensor"),
        P("tensor", None),
        P(None, None, "tensor"),
        P(None, "tensor", None),
        P(),
        P(),
    )
    out_specs = (
        P(("dp", "tensor"), None),
        P(("dp", "tensor"), None),
        P(("dp", "tensor")),
        P(("dp", "tensor")),
        P("dp", None, "tensor"),
        P("tensor", "dp"),
        P(("dp", "tensor")),
        P(("dp", "tensor")),
        P("dp", "tensor"),
        P("tensor", "dp"),
        P(None, "dp", "tensor"),
        P(None, "tensor", "dp"),
        P(("dp", "tensor"), None),
        P(("dp", "tensor"), None),
    )
    return jax.shard_map(shards, mesh=mesh, in_specs=in_specs, out_specs=out_specs, check_vma=False)
```

profile of v0, /device:TPU:0, one launch (start us, length us, event | category | flops | bytes accessed | tf_op | source)
XLA Modules:
  0.0 2009.0 jit_solution(16404738495456824774)
XLA Ops:
  17.0 34.7 %all-gather.6.cloned.1.call-done = bf16[2048,1024]{1,0:T(8,128)(2,1)} async-done(((bf16[512,1024]{1,0:T(8,128)(2,1)}), bf16[2048,1024]{1,0:T(8,128)(2,1)}) %all-gather.6.cloned.1.call-update) | async-done | bytes 4194320 | tf_op jit(solution)/shard_map/all_gather | solution.py:200
  51.6 7.8 convolution_convert_fusion.3
  59.4 9.4 reshape.729
  68.8 7.2 copy.52
  76.0 38.3 %while.96 = (s32[]{:T(128)}, bf16[2,1024,256]{2,1,0:T(8,128)(2,1)}, f32[2,4,1024]{2,1,0:T(4,128)S(1)}, bf16[2,1024,3,256]{1,3,2,0:T(8,128)(2,1)}, s32[2]{0:T(128)S(1)}, /*index=5*/s32[]{:T(128)}) while((s32[]{:T(128)}, bf16[2,1024,256]{2,1,0:T(8,128)(2,1)}, f32[2,4,1024]{2,1,0:T(4,128)S(1)}, bf16[2,1024,3,256]{1,3,2,0:T(8,128)(2,1)}, ...), condition=%wide.region_7.8_spmd, body=%wide.region_2.7_spmd.sunk | while | flops 1127482880 | bytes 67279448 | solution.py:204
  119.0 44.6 %reduce-scatter.24.cloned.1.call-done = bf16[512,1024]{1,0:T(8,128)(2,1)} async-done(((bf16[2048,1024]{1,0:T(8,128)(2,1)}), bf16[512,1024]{1,0:T(8,128)(2,1)}) %reduce-scatter.24.cloned.1.call-update) | async-done | bytes 1048592 | tf_op jit(solution)/shard_map/reduce_scatter | solution.py:208
  181.9 22.5 %all-gather.8.cloned.1.call-done = bf16[2048,1024]{1,0:T(8,128)(2,1)} async-done(((bf16[512,1024]{1,0:T(8,128)(2,1)}), bf16[2048,1024]{1,0:T(8,128)(2,1)}) %all-gather.8.cloned.1.call-update) | async-done | bytes 4194320 | tf_op jit(solution)/shard_map/all_gather | solution.py:228
  204.4 11.4 fusion.245
  215.8 25.2 %all-gather.10.cloned.1.call-done = bf16[2048,1024]{1,0:T(8,128)(2,1)} async-done(((bf16[512,1024]{1,0:T(8,128)(2,1)}), bf16[2048,1024]{1,0:T(8,128)(2,1)}) %all-gather.10.cloned.1.call-update) | async-done | bytes 4194320 | tf_op jit(solution)/shard_map/all_gather | solution.py:273
  241.0 26.3 %add_convert_fusion.1 = (bf16[2048,1024]{1,0:T(8,128)(2,1)}, f32[2048,1024]{1,0:T(8,128)}) fusion(f32[2048,1024]{1,0:T(8,128)} %fusion.245, bf16[2048,1024]{1,0:T(8,128)(2,1)} %all-gather.10.cloned.1.call-done, bf16[1024,1024]{1,0:T(8,128)(2,1)S(1)} %copy-done), kind=kOutput, calls=%fused_computation.251 | convolution fusion | flops 4445962240 | bytes 27262976 | tf_op jit(solution)/shard_map/nd,fd->nf/dot_general | solution.py:30
  267.3 8.1 multiply_convert_fusion.2
  283.7 13.7 scatter_custom_fusion
  305.7 271.1 %while.97 = (s32[]{:T(128)}, f32[5,4,128,1024]{3,2,1,0:T(8,128)}, bf16[5,4,128,1024]{3,2,1,0:T(8,128)(2,1)}, bf16[5,4,128,1024]{3,2,1,0:T(8,128)(2,1)}, bf16[5,4...) while((s32[]{:T(128)}, f32[5,4,128,1024]{3,2,1,0:T(8,128)}, ...), condition=%wide.region_25.26_spmd, body=%wide.region_24.25_spmd.sunk | while | flops 2260993024 | bytes 99358928 | solution.py:253
  306.2 12.5 fusion.391
  345.8 9.1 bitcast_dynamic-update-slice_fusion.12
  360.4 12.3 fusion.391
  399.9 9.1 bitcast_dynamic-update-slice_fusion.12
  414.5 12.3 fusion.391
  454.0 9.1 bitcast_dynamic-update-slice_fusion.12
  468.6 12.3 fusion.391
  508.1 9.1 bitcast_dynamic-update-slice_fusion.12
  522.8 12.3 fusion.391
  562.3 9.1 bitcast_dynamic-update-slice_fusion.12
  576.9 14.1 gather_fusion.8
  592.8 42.9 %reduce-scatter.28.cloned.1.call-done = bf16[512,1024]{1,0:T(8,128)(2,1)} async-done(((bf16[2048,1024]{1,0:T(8,128)(2,1)}), bf16[512,1024]{1,0:T(8,128)(2,1)}) %reduce-scatter.28.cloned.1.call-update) | async-done | bytes 1048592 | tf_op jit(solution)/shard_map/reduce_scatter | solution.py:261
  641.0 34.6 %all-gather.12.cloned.1.call-done = bf16[2048,1024]{1,0:T(8,128)(2,1)} async-done(((bf16[512,1024]{1,0:T(8,128)(2,1)}), bf16[2048,1024]{1,0:T(8,128)(2,1)}) %all-gather.12.cloned.1.call-update) | async-done | bytes 4194320 | tf_op jit(solution)/shard_map/all_gather | solution.py:274
  675.6 13.7 scatter_custom_fusion.1
  697.5 247.9 %while.98 = (s32[]{:T(128)}, bf16[5,4,128,1024]{3,2,1,0:T(8,128)(2,1)}, f32[5,4,128,1024]{3,2,1,0:T(8,128)}, f32[5,4,128,1024]{3,2,1,0:T(8,128)}, bf16[5,4,128,1...) while((s32[]{:T(128)}, ...), condition=%wide.region_29.30_spmd, body=%wide.region_28.29_spmd.sunk | while | flops 2218787840 | bytes 92280528 | solution.py:293
  697.7 12.3 fusion.396
  720.1 10.6 bitcast_dynamic-update-slice_fusion.13
  747.3 12.3 fusion.396
  769.6 10.5 bitcast_dynamic-update-slice_fusion.13
  796.8 12.3 fusion.396
  819.1 10.6 bitcast_dynamic-update-slice_fusion.13
  846.3 12.3 fusion.396
  868.6 10.6 bitcast_dynamic-update-slice_fusion.13
  895.9 12.3 fusion.396
  918.2 10.6 bitcast_dynamic-update-slice_fusion.13
  945.4 15.7 gather_fusion.9
  961.1 11.8 add_convert_fusion
  976.0 41.7 %reduce-scatter.30.cloned.1.call-done = bf16[512,1024]{1,0:T(8,128)(2,1)} async-done(((bf16[2048,1024]{1,0:T(8,128)(2,1)}), bf16[512,1024]{1,0:T(8,128)(2,1)}) %reduce-scatter.30.cloned.1.call-update) | async-done | bytes 1048592 | tf_op jit(solution)/shard_map/reduce_scatter | solution.py:313
  1027.6 8.0 convolution_convert_fusion.5
  1038.5 9.4 convolution_convert_fusion.6
  1084.7 14.2 while.100
  1104.0 27.9 %while.101 = (s32[]{:T(128)}, f32[1024,1024]{1,0:T(8,128)}, f32[1024,1024]{1,0:T(8,128)}, s32[]{:T(128)}, s32[]{:T(128)}, /*index=5*/bf16[3072,1024]{1,0:T(8,128...) while((s32[]{:T(128)}, f32[1024,1024]{1,0:T(8,128)}, ...), condition=%wide.region_59.60_spmd, body=%wide.region_58.59_spmd.sunk | while | flops 2150630400 | bytes 20975304 | solution.py:159
  1136.9 13.8 while.102
  1155.8 14.5 while.103
  1192.9 14.9 copy.64
  1207.7 12.2 copy.83
  1237.7 104.2 %while.99 = (s32[]{:T(128)}, bf16[2,1024,3,256]{1,3,2,0:T(8,128)(2,1)}, bf16[2,1024,3,256]{1,3,2,0:T(8,128)(2,1)}, s32[2]{0:T(128)S(1)}, f32[2,4,1024]{2,1,0:T(4...) while((s32[]{:T(128)}, bf16[2,1024,3,256]{1,3,2,0:T(8,128)(2,1)}, ...), condition=%wide.region_40.41_spmd, body=%wide.region_37.40_spmd.sunk | while | flops 2756965888 | bytes 214588176 | solution.py:326
  1247.1 7.4 multiply_reduce_fusion.9
  1259.3 8.1 multiply_reduce_fusion.8
  1270.6 8.3 multiply_convert_fusion.4
  1299.0 7.4 multiply_reduce_fusion.9
  1311.2 8.1 multiply_reduce_fusion.8
  1322.5 8.3 multiply_convert_fusion.4
  1354.6 7.0 convolution_convert_fusion.1
  1366.8 105.1 %reduce-scatter.46.cloned.1.call-done = f32[32,4]{1,0:T(8,128)} async-done(((f32[1024,4]{1,0:T(8,128)}), f32[32,4]{1,0:T(8,128)}) %reduce-scatter.46.cloned.1.call-update) | async-done | bytes 528
  1473.3 59.7 %reduce-scatter.40.cloned.1.call-done = bf16[128,256]{1,0:T(8,128)(2,1)} async-done(((bf16[1024,256]{1,0:T(8,128)(2,1)}), bf16[128,256]{1,0:T(8,128)(2,1)}) %reduce-scatter.40.cloned.1.call-update) | async-done | bytes 65552
  1534.6 150.4 %reduce-scatter.44.cloned.1.call-done = bf16[128,4096]{1,0:T(8,128)(2,1)} async-done(((bf16[1024,4096]{1,0:T(8,128)(2,1)}), bf16[128,4096]{1,0:T(8,128)(2,1)}) %reduce-scatter.44.cloned.1.call-update) | async-done | bytes 1048592
  1689.4 147.6 %reduce-scatter.38.cloned.1.call-done = bf16[4,128,1024]{2,1,0:T(8,128)(2,1)} async-done(((bf16[4,1024,1024]{2,1,0:T(8,128)(2,1)}), bf16[4,128,1024]{2,1,0:T(8,128)(2,1)}) %reduce-scatter.38.cloned.1.call-update) | async-done | bytes 1048592 | tf_op jit(solution)/shard_map/reduce_scatter | solution.py:355
  1839.7 65.4 %reduce-scatter.34.cloned.1.call-done = bf16[128,3,256]{2,0,1:T(8,128)(2,1)} async-done(((bf16[1024,3,256]{2,0,1:T(8,128)(2,1)}), bf16[128,3,256]{2,0,1:T(8,128)(2,1)}) %reduce-scatter.34.cloned.1.call-update) | async-done | bytes 196624 | tf_op jit(solution)/shard_map/reduce_scatter | solution.py:343
  1906.8 44.2 %reduce-scatter.32.cloned.1.call-done = bf16[512,1024]{1,0:T(8,128)(2,1)} async-done(((bf16[2048,1024]{1,0:T(8,128)(2,1)}), bf16[512,1024]{1,0:T(8,128)(2,1)}) %reduce-scatter.32.cloned.1.call-update) | async-done | bytes 1048592 | tf_op jit(solution)/shard_map/reduce_scatter | solution.py:334
  1955.5 39.6 %all-reduce.10 = (f32[1024]{0:T(1024)S(1)}, f32[1024]{0:T(1024)S(1)}, f32[1024]{0:T(1024)S(1)}, f32[1024]{0:T(1024)S(1)}) all-reduce(f32[1024]{0:T(1024)S(1)} %get-tuple-element.441, f32[1024]{0:T(1024)S(1)} %get-tuple-element.444, f32[1024]{0:T(1024)S(1)} %copy-done.75, ...), channel_id=7, replica_groups=mesh['dp'=8,'tensor'=4] {'dp','tensor'}, use_global_device_ids=true, to_apply=%region_45.46.clone | all-reduce | flops 4096 | bytes 32768
  (522 shorter events, 664.3 us)
Async XLA Ops:
  7.2 233.8 %copy-start = (bf16[1024,1024]{1,0:T(8,128)(2,1)S(1)}, bf16[1024,1024]{1,0:T(8,128)(2,1)}, u32[]{:S(2)}) copy-start(bf16[1024,1024]{1,0:T(8,128)(2,1)} %param.43) | copy-start | bytes 6291460
  7.2 44.4 %all-gather.6.cloned.1.call-start = ((), (), s32[]{:S(2)}) async-start(), calls=%async_computation.13 | async-start | bytes 5242880 | tf_op jit(solution)/shard_map/all_gather | solution.py:200
  14.3 149.3 %reduce-scatter.24.cloned.1.call-start = ((), (), s32[]{:S(2)}) async-start(), calls=%async_computation.14 | async-start | bytes 5242880 | tf_op jit(solution)/shard_map/reduce_scatter | solution.py:208
  118.9 44.7 %copy-start.5 = (bf16[512,1024]{1,0:T(8,128)(2,1)S(1)}, bf16[512,1024]{1,0:T(8,128)(2,1)}, u32[]{:S(2)}) copy-start(bf16[512,1024]{1,0:T(8,128)(2,1)} %param.32) | copy-start | bytes 3145732
  118.9 49.2 %copy-start.46 = (f32[1024]{0:T(1024)S(1)}, f32[1024]{0:T(1024)}, u32[]{:S(2)}) copy-start(f32[1024]{0:T(1024)} %param.40) | copy-start | bytes 12292
  118.9 49.2 %copy-start.83 = (f32[1024]{0:T(1024)S(1)}, f32[1024]{0:T(1024)}, u32[]{:S(2)}) copy-start(f32[1024]{0:T(1024)} %param.41) | copy-start | bytes 12292
  118.9 50.9 %copy-start.73 = (bf16[1024,2]{0,1:T(2,128)(2,1)S(1)}, bf16[1024,2]{0,1:T(2,128)(2,1)}, u32[]{:S(2)}) copy-start(bf16[1024,2]{0,1:T(2,128)(2,1)} %param.47) | copy-start | bytes 12292
  118.9 85.4 %all-gather.8.cloned.1.call-start = ((), (), s32[]{:S(2)}) async-start(), calls=%async_computation.15 | async-start | bytes 5242880 | tf_op jit(solution)/shard_map/all_gather | solution.py:228
  169.7 71.2 %all-gather.10.cloned.1.call-start = ((), (), s32[]{:S(2)}) async-start(), calls=%async_computation.18 | async-start | bytes 5242880 | tf_op jit(solution)/shard_map/all_gather | solution.py:273
  175.7 417.1 %reduce-scatter.26.cloned.1.call-start = ((), (), s32[]{:S(2)}) async-start(), calls=%async_computation.16 | async-start | bytes 5242880 | tf_op jit(solution)/shard_map/reduce_scatter | solution.py:258
  176.1 39.7 %copy-start.80 = (s32[4,1]{0,1:T(1,128)}, s32[4,1]{0,1:T(1,128)S(1)}, u32[]{:S(2)}) copy-start(s32[4,1]{0,1:T(1,128)S(1)} %reduce-window.10) | copy-start | bytes 52
  178.0 37.8 %copy-start.77 = (s32[4]{0:T(128)}, s32[4]{0:T(128)S(1)}, u32[]{:S(2)}) copy-start(s32[4]{0:T(128)S(1)} %multiply_subtract_fusion) | copy-start | bytes 52
  178.2 105.4 %copy-start.50 = (s32[2048,1]{0,1:T(1,128)}, s32[2048,1]{0,1:T(1,128)S(1)}, u32[]{:S(2)}) copy-start(s32[2048,1]{0,1:T(1,128)S(1)} %compare_select_fusion.2) | copy-start | bytes 24580
  283.6 352.0 %reduce-scatter.28.cloned.1.call-start = ((), (), s32[]{:S(2)}) async-start(), calls=%async_computation.17 | async-start | bytes 5242880 | tf_op jit(solution)/shard_map/reduce_scatter | solution.py:261
  305.7 271.2 %copy-start.31 = (s32[2048]{0:T(1024)S(1)}, s32[2048]{0:T(1024)}, u32[]{:S(2)}) copy-start(s32[2048]{0:T(1024)} %broadcast_clamp_fusion) | copy-start | bytes 24580
  591.0 44.6 %copy-start.14 = (bf16[512,1024]{1,0:T(8,128)(2,1)S(1)}, bf16[512,1024]{1,0:T(8,128)(2,1)}, u32[]{:S(2)}) copy-start(bf16[512,1024]{1,0:T(8,128)(2,1)} %param.33) | copy-start | bytes 3145732
  591.0 47.4 %copy-start.79 = (f32[512,1]{0,1:T(1,128)S(1)}, f32[512,1]{0,1:T(1,128)}, u32[]{:S(2)}) copy-start(f32[512,1]{0,1:T(1,128)} %get-tuple-element.637) | copy-start | bytes 6148
  591.0 48.1 %copy-start.62 = (f32[512,2]{0,1:T(2,128)S(1)}, f32[512,2]{0,1:T(2,128)}, u32[]{:S(2)}) copy-start(f32[512,2]{0,1:T(2,128)} %copy-done.61) | copy-start | bytes 12292
  591.1 84.5 %all-gather.12.cloned.1.call-start = ((), (), s32[]{:S(2)}) async-start(), calls=%async_computation.19 | async-start | bytes 5242880 | tf_op jit(solution)/shard_map/all_gather | solution.py:274
  592.3 97.0 %copy-start.59 = (s32[512,1]{0,1:T(1,128)}, s32[512,1]{0,1:T(1,128)S(1)}, u32[]{:S(2)}) copy-start(s32[512,1]{0,1:T(1,128)S(1)} %constant_dynamic-slice_fusion.4) | copy-start | bytes 6148
  592.7 96.6 %copy-start.26 = (f32[512,4]{0,1:T(4,128)}, f32[512,4]{0,1:T(4,128)S(1)}, u32[]{:S(2)}) copy-start(f32[512,4]{0,1:T(4,128)S(1)} %get-tuple-element.652) | copy-start | bytes 24580
  592.7 96.6 %copy-start.40 = (f32[512]{0:T(512)}, f32[512]{0:T(512)S(1)}, u32[]{:S(2)}) copy-start(f32[512]{0:T(512)S(1)} %get-tuple-element.651) | copy-start | bytes 6148
  592.7 96.6 %copy-start.42 = (f32[512]{0:T(512)}, f32[512]{0:T(512)S(1)}, u32[]{:S(2)}) copy-start(f32[512]{0:T(512)S(1)} %fusion.218) | copy-start | bytes 6148
  638.5 50.8 %copy-start.57 = (f32[512]{0:T(512)}, f32[512]{0:T(512)S(1)}, u32[]{:S(2)}) copy-start(f32[512]{0:T(512)S(1)} %mul.406) | copy-start | bytes 6148
  639.7 49.6 %copy-start.63 = (f32[512,1]{0,1:T(1,128)}, f32[512,1]{0,1:T(1,128)S(1)}, u32[]{:S(2)}) copy-start(f32[512,1]{0,1:T(1,128)S(1)} %get-tuple-element.640) | copy-start | bytes 6148
  640.9 376.8 %reduce-scatter.30.cloned.1.call-start = ((), (), s32[]{:S(2)}) async-start(), calls=%async_computation.20 | async-start | bytes 5242880 | tf_op jit(solution)/shard_map/reduce_scatter | solution.py:313
  697.5 247.9 %copy-start.32 = (s32[2048]{0:T(1024)S(1)}, s32[2048]{0:T(1024)}, u32[]{:S(2)}) copy-start(s32[2048]{0:T(1024)} %broadcast_clamp_fusion) | copy-start | bytes 24580
  972.9 44.8 %copy-start.6 = (bf16[512,1024]{1,0:T(8,128)(2,1)S(1)}, bf16[512,1024]{1,0:T(8,128)(2,1)}, u32[]{:S(2)}) copy-start(bf16[512,1024]{1,0:T(8,128)(2,1)} %param.32) | copy-start | bytes 3145732
  972.9 44.8 %copy-start.13 = (bf16[512,1024]{1,0:T(8,128)(2,1)S(1)}, bf16[512,1024]{1,0:T(8,128)(2,1)}, u32[]{:S(2)}) copy-start(bf16[512,1024]{1,0:T(8,128)(2,1)} %reduce-scatter.24.cloned.1.call-done) | copy-start | bytes 3145732
  972.9 44.8 %copy-start.27 = (f32[512,4]{0,1:T(4,128)S(1)}, f32[512,4]{0,1:T(4,128)}, u32[]{:S(2)}) copy-start(f32[512,4]{0,1:T(4,128)} %copy-done.26) | copy-start | bytes 24580
  972.9 44.8 %copy-start.41 = (f32[512]{0:T(512)S(1)}, f32[512]{0:T(512)}, u32[]{:S(2)}) copy-start(f32[512]{0:T(512)} %copy-done.40) | copy-start | bytes 6148
  973.0 44.8 %copy-start.43 = (f32[512]{0:T(512)S(1)}, f32[512]{0:T(512)}, u32[]{:S(2)}) copy-start(f32[512]{0:T(512)} %copy-done.42) | copy-start | bytes 6148
  973.0 44.8 %copy-start.45 = (f32[512]{0:T(512)S(1)}, f32[512]{0:T(512)}, u32[]{:S(2)}) copy-start(f32[512]{0:T(512)} %copy-done.44) | copy-start | bytes 6148
  973.0 44.8 %copy-start.47 = (f32[1024]{0:T(1024)S(1)}, f32[1024]{0:T(1024)}, u32[]{:S(2)}) copy-start(f32[1024]{0:T(1024)} %param.40) | copy-start | bytes 12292
  973.0 44.8 %copy-start.52 = (bf16[1024,4]{0,1:T(4,128)(2,1)S(1)}, bf16[1024,4]{0,1:T(4,128)(2,1)}, u32[]{:S(2)}) copy-start(bf16[1024,4]{0,1:T(4,128)(2,1)} %param.46) | copy-start | bytes 24580
  973.0 44.8 %copy-start.56 = (f32[512]{0:T(512)S(1)}, f32[512]{0:T(512)}, u32[]{:S(2)}) copy-start(f32[512]{0:T(512)} %copy-done.55) | copy-start | bytes 6148
  973.0 44.8 %copy-start.58 = (f32[512]{0:T(512)S(1)}, f32[512]{0:T(512)}, u32[]{:S(2)}) copy-start(f32[512]{0:T(512)} %copy-done.57) | copy-start | bytes 6148
  973.0 44.8 %copy-start.60 = (s32[512,1]{0,1:T(1,128)S(1)}, s32[512,1]{0,1:T(1,128)}, u32[]{:S(2)}) copy-start(s32[512,1]{0,1:T(1,128)} %copy-done.59) | copy-start | bytes 6148
  973.1 206.6 %all-gather.14.cloned.1.call-start = ((), (), s32[]{:S(2)}) async-start(), calls=%async_computation.21 | async-start | bytes 5242880 | tf_op jit(solution)/shard_map/all_gather | solution.py:323
  976.0 46.4 %copy-start.72 = (f32[512]{0:T(512)S(1)}, f32[512]{0:T(512)}, u32[]{:S(2)}) copy-start(f32[512]{0:T(512)} %copy-done.71) | copy-start | bytes 6148
  976.0 46.4 %copy-start.18 = (bf16[512,1024]{1,0:T(8,128)(2,1)S(1)}, bf16[512,1024]{1,0:T(8,128)(2,1)}, u32[]{:S(2)}) copy-start(bf16[512,1024]{1,0:T(8,128)(2,1)} %reduce-scatter.26.cloned.1.call-done) | copy-start | bytes 3145732
  976.0 46.4 %copy-start.64 = (f32[512,1]{0,1:T(1,128)S(1)}, f32[512,1]{0,1:T(1,128)}, u32[]{:S(2)}) copy-start(f32[512,1]{0,1:T(1,128)} %copy-done.63) | copy-start | bytes 6148
  976.0 46.4 %copy-start.68 = (f32[512,1]{0,1:T(1,128)S(1)}, f32[512,1]{0,1:T(1,128)}, u32[]{:S(2)}) copy-start(f32[512,1]{0,1:T(1,128)} %copy-done.67) | copy-start | bytes 6148
  1027.6 334.1 %reduce-scatter.42.cloned.1.call-start = ((), (), s32[]{:S(2)}) async-start(), calls=%async_computation.27 | async-start | bytes 2359296
  1038.3 325.4 %reduce-scatter.36.cloned.1.call-start = ((), (), s32[]{:S(2)}) async-start(), calls=%async_computation.24 | async-start | bytes 2359296 | tf_op jit(solution)/shard_map/reduce_scatter | solution.py:349
  1047.9 12.6 slice-start.2
  1047.9 317.6 %reduce-scatter.48.cloned.1.call-start = ((), (), s32[]{:S(2)}) async-start(), calls=%async_computation.30 | async-start | bytes 540672
  1065.8 406.1 %reduce-scatter.46.cloned.1.call-start = ((), (), s32[]{:S(2)}) async-start(), calls=%async_computation.29 | async-start | bytes 540672
  1067.9 465.1 %reduce-scatter.40.cloned.1.call-start = ((), (), s32[]{:S(2)}) async-start(), calls=%async_computation.26 | async-start | bytes 589824
  1186.0 499.0 %reduce-scatter.44.cloned.1.call-start = ((), (), s32[]{:S(2)}) async-start(), calls=%async_computation.28 | async-start | bytes 9437184
  1219.9 617.0 %reduce-scatter.38.cloned.1.call-start = ((), (), s32[]{:S(2)}) async-start(), calls=%async_computation.25 | async-start | bytes 9437184 | tf_op jit(solution)/shard_map/reduce_scatter | solution.py:355
  1232.2 672.9 %reduce-scatter.34.cloned.1.call-start = ((), (), s32[]{:S(2)}) async-start(), calls=%async_computation.23 | async-start | bytes 1769472 | tf_op jit(solution)/shard_map/reduce_scatter | solution.py:343
  1259.3 11.3 copy-start.2
  1311.2 11.3 copy-start.2
  1354.6 596.4 %reduce-scatter.32.cloned.1.call-start = ((), (), s32[]{:S(2)}) async-start(), calls=%async_computation.22 | async-start | bytes 5242880 | tf_op jit(solution)/shard_map/reduce_scatter | solution.py:334
  1686.9 264.1 %copy-start.7 = (bf16[512,1024]{1,0:T(8,128)(2,1)S(1)}, bf16[512,1024]{1,0:T(8,128)(2,1)}, u32[]{:S(2)}) copy-start(bf16[512,1024]{1,0:T(8,128)(2,1)} %param.32) | copy-start | bytes 3145732
  1686.9 264.1 %copy-start.36 = (f32[512]{0:T(512)S(1)}, f32[512]{0:T(512)}, u32[]{:S(2)}) copy-start(f32[512]{0:T(512)} %copy-done.35) | copy-start | bytes 6148
  1686.9 264.1 %copy-start.37 = (f32[1024]{0:T(1024)S(1)}, f32[1024]{0:T(1024)}, u32[]{:S(2)}) copy-start(f32[1024]{0:T(1024)} %param.36) | copy-start | bytes 12292
  1687.9 265.0 %copy-start.70 = (f32[512]{0:T(512)S(1)}, f32[512]{0:T(512)}, u32[]{:S(2)}) copy-start(f32[512]{0:T(512)} %copy-done.69) | copy-start | bytes 6148
  1687.9 265.0 %copy-start.54 = (f32[512]{0:T(512)S(1)}, f32[512]{0:T(512)}, u32[]{:S(2)}) copy-start(f32[512]{0:T(512)} %copy-done.53) | copy-start | bytes 6148
  1689.4 266.2 %copy-start.75 = (f32[1024]{0:T(1024)S(1)}, f32[1024]{0:T(1024)}, u32[]{:S(2)}) copy-start(f32[1024]{0:T(1024)} %get-tuple-element.439) | copy-start | bytes 12292
  1689.4 266.2 %copy-start.76 = (f32[1024]{0:T(1024)S(1)}, f32[1024]{0:T(1024)}, u32[]{:S(2)}) copy-start(f32[1024]{0:T(1024)} %get-tuple-element.443) | copy-start | bytes 12292
  1689.4 308.1 %copy-start.66 = (f32[512]{0:T(512)S(1)}, f32[512]{0:T(512)}, u32[]{:S(2)}) copy-start(f32[512]{0:T(512)} %copy-done.65) | copy-start | bytes 6148
  1953.0 49.0 %copy-start.1 = (bf16[1024,1024]{1,0:T(8,128)(2,1)S(1)}, bf16[1024,1024]{1,0:T(8,128)(2,1)}, u32[]{:S(2)}) copy-start(bf16[1024,1024]{1,0:T(8,128)(2,1)} %param.43) | copy-start | bytes 6291460
  (50 other events, 180.8 us)
Sparse Core Ops, SparseCore 0:
  14.4 37.1 all-gather.5
  119.0 44.4 reduce-scatter.23
  169.9 34.4 all-gather.7
  206.4 34.4 all-gather.9
  283.7 44.5 reduce-scatter.25
  591.2 44.3 reduce-scatter.27
  641.1 34.4 all-gather.11
  973.2 44.5 reduce-scatter.29
  1027.7 34.4 all-gather.13
  1066.2 67.7 reduce-scatter.41
  1138.1 66.5 reduce-scatter.35
  1206.8 133.0 reduce-scatter.47
  1342.2 129.6 reduce-scatter.45
  1475.1 57.8 reduce-scatter.39
  1536.9 148.0 reduce-scatter.43
  1688.5 148.3 reduce-scatter.37
  1840.6 64.4 reduce-scatter.33
  1907.5 43.4 reduce-scatter.31
where the time goes:
time: 2020 us; the launch traced here: 2010 us
  waiting for transfers between devices  819 us (41%)
  local copies, waits for them, and re-layouts  539 us (27%)
  matrix products  433 us (21%)
  other arithmetic  150 us (7%)
  blocking collectives  39.6 us (2%)
  between operations  20.7 us (1%)
    dot_general x70, matrix products, product(): jnp.einsum(pattern, left_side, right_side, preferred_element_type=jnp.flo...  420 us
    unnamed x23, waiting for transfers between devices  316 us
    reduce_scatter x1, waiting for transfers between devices, shards(): lax.psum_scatter(expert_up_total.astype(jnp.bfloat16), 'dp', scatter_dime...  148 us
    gather x15, local copies, waits for them, and re-layouts, expert_forward(): branch = product(hidden, expert_down[owners], 'tnf,tfd->tnd')  112 us
    gather x15, local copies, waits for them, and re-layouts, expert_backward(): row_grad = product(pre_grad, expert_up[owners], 'tnf,tdf->tnd')  111 us
    reduce_scatter x1, waiting for transfers between devices, shards(): lax.psum_scatter(qkv_weight_grad.astype(jnp.bfloat16), 'dp', scatter_dime...  65.4 us
    unnamed x188, local copies, waits for them, and re-layouts  56.1 us
    gather x10, local copies, waits for them, and re-layouts, expert_backward(): hidden_grad = product(tile_cot, expert_down[owners], 'tnd,tfd->tnf')  50 us
  transfers between devices with their start and end apart: 18, of which 13 were waited for; matrix products, arithmetic and copies ran while one was open for 33% of the time, Pallas kernels for 0%

commit v1 on v0

v1 whole, which is shorter than its diff:
```python
from functools import partial
import jax, jax.numpy as jnp
from jax import lax
from jax.experimental import pallas as pl
from jax.experimental.pallas import tpu as pltpu
from jax.sharding import PartitionSpec as P

BF = jnp.bfloat16
F32 = jnp.float32
TILE_DENSE = 512
TILE_EXPERT = 256
PIECE = 16
VMEM = 60 * 1024 * 1024
ANY = pl.BlockSpec(memory_space=pl.ANY)
SMEM = pl.BlockSpec(memory_space=pltpu.SMEM)


def dot(a, b, ca, cb):
    return lax.dot_general(a, b, (((ca,), (cb,)), ((), ())), preferred_element_type=F32)


def bit_reverse(value, bits):
    out = jnp.int32(0)
    for k in range(bits):
        out = out | (((value >> k) & 1) << (bits - 1 - k))
    return out


def lane_softmax(logits, first, last):
    lane = lax.broadcasted_iota(jnp.int32, logits.shape, 1)
    inside = (lane >= first) & (lane < last)
    masked = jnp.where(inside, logits, -1e30)
    top = jnp.max(masked, axis=1, keepdims=True)
    e = jnp.where(inside, jnp.exp(masked - top), 0.0)
    return e / jnp.sum(e, axis=1, keepdims=True)


def pick_lane(v, index):
    lane = lax.broadcasted_iota(jnp.int32, v.shape, 1)
    return jnp.sum(jnp.where(lane == index, v, 0.0), axis=1, keepdims=True)


def gelu_parts(pre):
    phi = 0.5 * (1.0 + lax.erf(pre * 0.7071067811865476))
    pdf = jnp.exp(pre * pre * -0.5) * 0.3989422804014327
    return pre * phi, phi + pre * pdf


def ffn_kernel(cfg, *refs):
    (experts, chunks, rows, d, f, bits, TM) = cfg
    n = chunks * rows
    halves = 1 << (bits - 1)
    blk = d >> bits
    it = iter(refs)
    take = lambda k: [next(it) for _ in range(k)]
    me_ref, blk_ref, bnd_ref = take(3)
    x_hbm, dy_hbm = take(chunks), take(chunks)
    rm_ref, up_hbm, dn_hbm = take(3)
    if experts:
        out_in, rg_in, dots_in = take(3)
        groups = chunks // experts[1]
        out_refs, rg_refs = take(experts[1]), take(experts[1])
        dots_ref, = take(1)
        keep_refs, send_refs = take(experts[0]), take(experts[0])
    else:
        out_ref, rg_ref, dots_ref = take(3)
        keep_refs, send_refs = take(1), take(1)
    X, DY, UP, DN, UA, DA, ST, xsem, wsem, gsem = take(10)
    if experts:
        XG, DG, VAL, OA, RA, DOT, TR, TL, TH, osem = take(10)
    else:
        OB, RB, osem = take(3)
    me = me_ref[0]
    lanes = bnd_ref.shape[1] - 1
    copies = []
    for q in range(chunks):
        sl = pl.ds(q * rows, rows)
        copies.append(pltpu.make_async_copy(x_hbm[q], X.at[sl], xsem.at[q]))
        copies.append(pltpu.make_async_copy(dy_hbm[q], DY.at[sl], xsem.at[chunks + q]))

    def weights(e, slot):
        u = up_hbm.at[e] if experts else up_hbm
        w = dn_hbm.at[e] if experts else dn_hbm
        return (pltpu.make_async_copy(u, UP.at[slot], wsem.at[slot, 0]),
                pltpu.make_async_copy(w, DN.at[slot], wsem.at[slot, 1]))

    for c in weights(0, 0):
        c.start()
    for c in copies:
        c.start()

    def flush_copies(g):
        return (pltpu.make_async_copy(ST.at[:, pl.ds(0, halves)], keep_refs[g], gsem.at[0]),
                pltpu.make_async_copy(ST.at[:, pl.ds(halves, halves)], send_refs[g], gsem.at[1]))

    def stage():
        def body(c, _):
            slot = bit_reverse(c ^ me, bits)
            r = pl.ds(pl.multiple_of(c * blk, blk), blk)
            ST[0, slot] = UA[r, :].astype(BF)
            ST[1, slot] = DA[r, :].astype(BF)
            return 0
        lax.fori_loop(0, 1 << bits, body, 0)

    def tile(xt, dyt, coef_of, up_w, dn_w, first):
        logits = dot(xt, rm_ref[...], 1, 0)
        mixing = lane_softmax(logits, lanes, lanes + 2)
        coef = coef_of(logits, mixing)
        pre = dot(xt, up_w[...], 1, 0)
        g = dot(dyt, dn_w[...], 1, 1)
        hid, dg = gelu_parts(pre)
        hid = hid.astype(BF)
        dots = jnp.sum(hid.astype(F32) * g, axis=1, keepdims=True)
        pg = (g * dg * coef).astype(BF)
        cot = (dyt.astype(F32) * coef).astype(BF)
        ua = dot(xt, pg, 0, 0)
        da = dot(cot, hid, 0, 0)

        @pl.when(first)
        def _():
            UA[...] = ua
            DA[...] = da

        @pl.when(jnp.logical_not(first))
        def _():
            UA[...] += ua
            DA[...] += da
        out = dot(hid, dn_w[...], 1, 0) * coef
        rg = dot(pg, up_w[...], 1, 1)
        return dots, out, rg

    if not experts:
        for c in weights(0, 0):
            c.wait()

        def dense_tile(i, _):
            slot = i % 2
            sl = pl.ds(pl.multiple_of(i * TM, TM), TM)
            for q in range(chunks):
                @pl.when(i * TM == q * rows)
                def _(q=q):
                    copies[2 * q].wait()
                    copies[2 * q + 1].wait()
            outs = (pltpu.make_async_copy(OB.at[slot], out_ref.at[sl], osem.at[0, slot]),
                    pltpu.make_async_copy(RB.at[slot], rg_ref.at[sl], osem.at[1, slot]))
            dots, out, rg = tile(X[sl, :], DY[sl, :], lambda l, m: pick_lane(m, lanes), UP.at[0], DN.at[0], i == 0)
            dots_ref[:, sl] = jnp.broadcast_to(dots, (TM, 128)).T[0:8, :]

            @pl.when(i >= 2)
            def _():
                for c in outs:
                    c.wait()
            OB[slot] = out.astype(BF)
            RB[slot] = rg.astype(BF)
            for c in outs:
                c.start()
            return 0
        lax.fori_loop(0, n // TM, dense_tile, 0)
        stage()
        for c in flush_copies(0):
            c.start()
        for slot in range(min(2, n // TM)):
            sl = pl.ds(0, TM)
            pltpu.make_async_copy(OB.at[slot], out_ref.at[sl], osem.at[0, slot]).wait()
            pltpu.make_async_copy(RB.at[slot], rg_ref.at[sl], osem.at[1, slot]).wait()
        for c in flush_copies(0):
            c.wait()
        return

    count = experts[0]
    OA[...] = jnp.zeros_like(OA)
    RA[...] = jnp.zeros_like(RA)
    DOT[...] = jnp.zeros_like(DOT)
    dense = (pltpu.make_async_copy(out_in, X, xsem.at[0]), pltpu.make_async_copy(rg_in, DY, xsem.at[1]))
    for c in copies:
        c.wait()
    iota16 = lax.broadcasted_iota(jnp.int32, (PIECE, 128), 0)

    def one_expert(e, _):
        slot = e % 2
        for c in weights(e, slot):
            c.wait()

        @pl.when(e + 1 < count)
        def _():
            for c in weights(e + 1, 1 - slot):
                c.start()
        total = jnp.int32(0)
        for q in range(chunks):
            lo, hi = bnd_ref[blk_ref[q], e], bnd_ref[blk_ref[q], e + 1]
            p0 = lo // PIECE
            p1 = jnp.where(hi > lo, (hi + PIECE - 1) // PIECE, p0)

            def add(p, _, lo=lo, hi=hi, p0=p0, total=total, q=q):
                k = total + p - p0
                TR[k] = q * rows + p * PIECE
                TL[k] = lo - p * PIECE
                TH[k] = hi - p * PIECE
                return 0
            lax.fori_loop(p0, p1, add, 0)
            total = total + p1 - p0
        tiles = (total * PIECE + TM - 1) // TM

        def pad(k, _):
            TR[k] = 0
            TL[k] = 0
            TH[k] = 0
            return 0
        lax.fori_loop(total, tiles * (TM // PIECE), pad, 0)

        def expert_tile(i, _):
            base = i * (TM // PIECE)
            for p in range(TM // PIECE):
                r = pl.ds(pl.multiple_of(TR[base + p], PIECE), PIECE)
                XG[pl.ds(p * PIECE, PIECE), :] = X[r, :]
                DG[pl.ds(p * PIECE, PIECE), :] = DY[r, :]
                ok = (iota16 >= TL[base + p]) & (iota16 < TH[base + p])
                VAL[pl.ds(p * PIECE, PIECE), :] = jnp.where(ok, 1.0, 0.0)
            valid = VAL[:, 0:1]

            def coef_of(logits, mixing):
                return pick_lane(mixing, lanes + 1) * pick_lane(lane_softmax(logits, 0, lanes), e) * valid
            dots, out, rg = tile(XG[...], DG[...], coef_of, UP.at[slot], DN.at[slot], i == 0)
            dots = jnp.broadcast_to(dots * valid, (TM, 128))
            for p in range(TM // PIECE):
                r = pl.ds(pl.multiple_of(TR[base + p], PIECE), PIECE)
                s = slice(p * PIECE, (p + 1) * PIECE)
                OA[r, :] += out[s]
                RA[r, :] += rg[s]
                DOT[r, :] += dots[s]
            return 0

        @pl.when(tiles == 0)
        def _():
            UA[...] = jnp.zeros_like(UA)
            DA[...] = jnp.zeros_like(DA)
        lax.fori_loop(0, tiles, expert_tile, 0)

        @pl.when(e == count - 1)
        def _():
            for c in dense:
                c.start()

        @pl.when(e > 0)
        def _():
            for c in flush_copies(0):
                c.wait()
        stage()
        for g in range(count):
            @pl.when(e == g)
            def _(g=g):
                for c in flush_copies(g):
                    c.start()
        return 0
    lax.fori_loop(0, count, one_expert, 0)
    per = groups * rows
    for c in dense:
        c.wait()

    def finish(i, _):
        sl = pl.ds(pl.multiple_of(i * TM, TM), TM)
        X[sl, :] = (OA[sl, :] + X[sl, :].astype(F32)).astype(BF)
        DY[sl, :] = (RA[sl, :] + DY[sl, :].astype(F32)).astype(BF)
        return 0
    lax.fori_loop(0, n // TM, finish, 0)
    outs = []
    for k in range(experts[1]):
        sl = pl.ds(k * per, per)
        outs.append(pltpu.make_async_copy(X.at[sl], out_refs[k], osem.at[0, k]))
        outs.append(pltpu.make_async_copy(DY.at[sl], rg_refs[k], osem.at[1, k]))
    for c in outs:
        c.start()
    dots_t = jnp.concatenate([DOT[pl.ds(i * TM, TM), :].T[0:8, :] for i in range(n // TM)], axis=1)
    row = lax.broadcasted_iota(jnp.int32, (8, n), 0)
    dots_ref[...] = jnp.where(row == 0, dots_in[...], dots_t)
    for c in outs:
        c.wait()
    for c in flush_copies(0):
        c.wait()


def ffn_dense(me, blocks, bounds, xs, dys, rm, up, down, bits):
    chunks = len(xs)
    rows, d = xs[0].shape
    f = up.shape[1]
    n = chunks * rows
    halves = 1 << (bits - 1)
    blk = d >> bits
    tm = min(TILE_DENSE, rows)
    grad = jax.ShapeDtypeStruct((2, halves, blk, f), BF)
    flat = jax.ShapeDtypeStruct((n, d), BF)
    flops = 12 * n * d * f
    return pl.pallas_call(
        partial(ffn_kernel, (None, chunks, rows, d, f, bits, tm)),
        name="ffn_dense",
        out_shape=(flat, flat, jax.ShapeDtypeStruct((8, n), F32), grad, grad),
        in_specs=[SMEM, SMEM, SMEM] + [ANY] * (2 * chunks) + [pl.BlockSpec(memory_space=pltpu.VMEM)] + [ANY] * 2,
        out_specs=(ANY, ANY, pl.BlockSpec(memory_space=pltpu.VMEM), ANY, ANY),
        scratch_shapes=[
            pltpu.VMEM((n, d), BF), pltpu.VMEM((n, d), BF),
            pltpu.VMEM((1, d, f), BF), pltpu.VMEM((1, f, d), BF),
            pltpu.VMEM((d, f), F32), pltpu.VMEM((d, f), F32),
            pltpu.VMEM((2, 2 * halves, blk, f), BF),
            pltpu.SemaphoreType.DMA((2 * chunks,)), pltpu.SemaphoreType.DMA((1, 2)), pltpu.SemaphoreType.DMA((2,)),
            pltpu.VMEM((2, tm, d), BF), pltpu.VMEM((2, tm, d), BF), pltpu.SemaphoreType.DMA((2, 2)),
        ],
        cost_estimate=pl.CostEstimate(flops=flops, bytes_accessed=8 * n * d + 8 * d * f, transcendentals=n * f),
        compiler_params=pltpu.CompilerParams(vmem_limit_bytes=VMEM),
    )(me, blocks, bounds, *xs, *dys, rm, up, down)


def ffn_experts(me, blocks, bounds, xs, dys, rm, up, down, out_d, rg_d, dots_d, members, bits):
    chunks = len(xs)
    rows, d = xs[0].shape
    count, _, f = up.shape
    n = chunks * rows
    halves = 1 << (bits - 1)
    blk = d >> bits
    groups = chunks // members
    tm = TILE_EXPERT
    grad = jax.ShapeDtypeStruct((2, halves, blk, f), BF)
    part = jax.ShapeDtypeStruct((groups * rows, d), BF)
    table = n // PIECE + count * chunks + 2 * tm // PIECE
    vm = pl.BlockSpec(memory_space=pltpu.VMEM)
    return pl.pallas_call(
        partial(ffn_kernel, ((count, members), chunks, rows, d, f, bits, tm)),
        name="ffn_experts",
        out_shape=(part,) * (2 * members) + (jax.ShapeDtypeStruct((8, n), F32),) + (grad,) * (2 * count),
        in_specs=[SMEM, SMEM, SMEM] + [ANY] * (2 * chunks) + [vm] + [ANY] * 4 + [vm],
        out_specs=(ANY,) * (2 * members) + (vm,) + (ANY,) * (2 * count),
        scratch_shapes=[
            pltpu.VMEM((n, d), BF), pltpu.VMEM((n, d), BF),
            pltpu.VMEM((2, d, f), BF), pltpu.VMEM((2, f, d), BF),
            pltpu.VMEM((d, f), F32), pltpu.VMEM((d, f), F32),
            pltpu.VMEM((2, 2 * halves, blk, f), BF),
            pltpu.SemaphoreType.DMA((2 * chunks,)), pltpu.SemaphoreType.DMA((2, 2)), pltpu.SemaphoreType.DMA((2,)),
            pltpu.VMEM((tm, d), BF), pltpu.VMEM((tm, d), BF), pltpu.VMEM((tm, 128), F32),
            pltpu.VMEM((n, d), F32), pltpu.VMEM((n, d), F32), pltpu.VMEM((n, 128), F32),
            pltpu.SMEM((table,), jnp.int32), pltpu.SMEM((table,), jnp.int32), pltpu.SMEM((table,), jnp.int32),
            pltpu.SemaphoreType.DMA((2, members)),
        ],
        cost_estimate=pl.CostEstimate(flops=12 * n * d * f, bytes_accessed=16 * n * d + 8 * count * d * f, transcendentals=n * f),
        compiler_params=pltpu.CompilerParams(vmem_limit_bytes=VMEM),
    )(me, blocks, bounds, *xs, *dys, rm, up, down, out_d, rg_d, dots_d)


HD = 64
LANES = 128


def head_part(v, h):
    lane = lax.broadcasted_iota(jnp.int32, v.shape, 1)
    return jnp.where((lane // HD) == h, v, jnp.zeros((), v.dtype))


def masked_scores(st, key_first, query_first, prefix):
    key_pos = key_first + lax.broadcasted_iota(jnp.int32, st.shape, 0)
    query_pos = query_first + lax.broadcasted_iota(jnp.int32, st.shape, 1)
    seen = key_pos <= query_pos
    if prefix is not None:
        seen = seen | (key_pos < prefix)
    return jnp.where(seen, st, -1e30)


def score_block(k2, qm, half, length, prefix):
    mid = length // 2
    if half == 0:
        return masked_scores(dot(k2[0:mid], qm, 1, 1), 0, 0, prefix)
    low = dot(k2[0:mid], qm, 1, 1)
    high = masked_scores(dot(k2[mid:length], qm, 1, 1), mid, mid, None)
    return jnp.concatenate([low, high], 0)


def attn_forward_kernel(length, prefix_ref, n1_ref, w_ref, q_ref, k_ref, v_ref, ctx_ref, lse_ref):
    mid = length // 2
    prefix = prefix_ref[0]
    n1 = n1_ref[...]
    q_ref[...] = dot(n1, w_ref[0], 1, 0).astype(BF)
    k_ref[...] = dot(n1, w_ref[1], 1, 0).astype(BF)
    v_ref[...] = dot(n1, w_ref[2], 1, 0).astype(BF)
    vt = v_ref[...].T
    k2 = k_ref[...]
    for half in range(2):
        rows = pl.ds(half * mid, mid)
        q2 = q_ref[rows, :] * jnp.asarray(HD ** -0.5, BF)
        keys = mid * (half + 1)
        parts = []
        for h in range(2):
            st = score_block(k2, head_part(q2, h), half, length, prefix)
            top = jnp.max(st, axis=0, keepdims=True)
            p = jnp.exp(st - top)
            total = jnp.sum(p, axis=0, keepdims=True)
            c = dot(vt[h * HD:(h + 1) * HD, 0:keys], p.astype(BF), 1, 0)
            parts.append(c / total)
            lse_ref[0, h:h + 1, rows] = top + jnp.log(total)
        ctx_ref[rows, :] = jnp.concatenate(parts, 0).T.astype(BF)


def attn_forward(prefix, n1, w):
    length, d = n1.shape
    heads = w.shape[2]
    pairs = heads // LANES
    col = pl.BlockSpec((length, LANES), lambda p, *_: (0, p))
    out = jax.ShapeDtypeStruct((length, heads), BF)
    return pl.pallas_call(
        partial(attn_forward_kernel, length),
        name="attn_forward",
        grid_spec=pltpu.PrefetchScalarGridSpec(
            num_scalar_prefetch=1, grid=(pairs,),
            in_specs=[pl.BlockSpec((length, d), lambda p, *_: (0, 0)), pl.BlockSpec((3, d, LANES), lambda p, *_: (0, 0, p))],
            out_specs=[col] * 4 + [pl.BlockSpec((1, 8, length), lambda p, *_: (p, 0, 0))]),
        out_shape=[out] * 4 + [jax.ShapeDtypeStruct((pairs, 8, length), F32)],
        cost_estimate=pl.CostEstimate(flops=6 * length * d * heads + 12 * length * length * heads, bytes_accessed=4 * length * d + 10 * length * heads, transcendentals=length * length * heads // HD),
        compiler_params=pltpu.CompilerParams(vmem_limit_bytes=VMEM),
    )(prefix, n1, w)


def attn_backward_kernel(length, bits, members, based, prefix_ref, me_ref, j_ref, *refs):
    it = iter(refs)
    take = lambda k: [next(it) for _ in range(k)]
    mcs = take(members)
    n1_ref, wo_ref, w_ref, q_ref, k_ref, v_ref, ctx_ref, lse_ref = take(8)
    bases = take(members) if based else []
    ng_refs = take(members)
    grad_ref, NG, MC, DC, DK, DV, DQ, sem = it
    rows_each = length // members
    where = [pl.ds(pl.multiple_of(lax.rem(j_ref[0] + k, members) * rows_each, rows_each), rows_each) for k in range(members)]
    mid = length // 2
    prefix = prefix_ref[0]
    me = me_ref[0]
    pair = pl.program_id(0)
    copies = [pltpu.make_async_copy(mcs[k], MC.at[where[k]], sem.at[k]) for k in range(members)]

    @pl.when(pair == 0)
    def _():
        for c in copies:
            c.start()
        for c in copies:
            c.wait()
    mc = MC[...]
    DC[...] = dot(mc, wo_ref[...], 1, 1).astype(BF)
    k2, v2 = k_ref[...], v_ref[...]
    kt = k2.T
    scale = jnp.asarray(HD ** -0.5, BF)
    for half in range(2):
        rows = pl.ds(half * mid, mid)
        q2 = q_ref[rows, :] * scale
        dc2 = DC[rows, :]
        keys = mid * (half + 1)
        dv = jnp.zeros((keys, LANES), F32)
        dk = jnp.zeros((keys, LANES), F32)
        dq = []
        for h in range(2):
            qm, dcm = head_part(q2, h), head_part(dc2, h)
            st = score_block(k2, qm, half, length, prefix)
            p = jnp.exp(st - lse_ref[0, h:h + 1, rows])
            dv = dv + dot(p.astype(BF), dcm, 1, 0)
            dp = dot(v2[0:keys], dcm, 1, 1)
            ds = (p * (dp - jnp.sum(p * dp, axis=0, keepdims=True))).astype(BF)
            dk = dk + dot(ds, qm, 1, 0)
            dq.append(dot(kt[h * HD:(h + 1) * HD, 0:keys], ds, 1, 0))
        DQ[rows, :] = (jnp.concatenate(dq, 0) * HD ** -0.5).T.astype(BF)
        if half == 0:
            DK[0:mid, :] = dk
            DV[0:mid, :] = dv
        else:
            DK[0:mid, :] += dk[0:mid]
            DV[0:mid, :] += dv[0:mid]
            DK[mid:length, :] = dk[mid:length]
            DV[mid:length, :] = dv[mid:length]
    dq, dk, dv = DQ[...], DK[...].astype(BF), DV[...].astype(BF)
    ng = dot(dq, w_ref[0], 1, 1) + dot(dk, w_ref[1], 1, 1) + dot(dv, w_ref[2], 1, 1)

    @pl.when(pair == 0)
    def _():
        NG[...] = ng

    @pl.when(pair > 0)
    def _():
        NG[...] += ng
    n1 = n1_ref[...]
    grads = [dot(n1, x, 0, 0) for x in (dq, dk, dv)] + [dot(mc, ctx_ref[...], 0, 0)]
    blk = n1.shape[1] >> bits
    for c in range(1 << bits):
        slot = bit_reverse(jnp.int32(c) ^ me, bits)
        for i in range(4):
            grad_ref[slot, i] = grads[i][c * blk:(c + 1) * blk].astype(BF)

    @pl.when(pair == pl.num_programs(0) - 1)
    def _():
        for k in range(members):
            done = NG[where[k], :]
            if based:
                done = done + bases[k][...].astype(F32)
            ng_refs[k][...] = done.astype(BF)


def attn_backward(prefix, me, j, mcs, n1, wo, w, saved, base, bits):
    q, k, v, ctx, lse = saved
    length, d = n1.shape
    heads = w.shape[2]
    pairs = heads // LANES
    blk = d >> bits
    members = len(mcs)
    col = pl.BlockSpec((length, LANES), lambda p, *_: (0, p))
    full = pl.BlockSpec((length, d), lambda p, *_: (0, 0))
    part = pl.BlockSpec((length // members, d), lambda p, *_: (0, 0))
    extra = [] if base is None else list(base)
    res = pl.pallas_call(
        partial(attn_backward_kernel, length, bits, members, base is not None),
        name="attn_backward",
        grid_spec=pltpu.PrefetchScalarGridSpec(
            num_scalar_prefetch=3, grid=(pairs,),
            in_specs=[ANY] * members + [full, pl.BlockSpec((LANES, d), lambda p, *_: (p, 0)), pl.BlockSpec((3, d, LANES), lambda p, *_: (0, 0, p)),
                      col, col, col, col, pl.BlockSpec((1, 8, length), lambda p, *_: (p, 0, 0))] + [part] * len(extra),
            out_specs=[part] * members + [pl.BlockSpec((1 << bits, 4, blk, LANES), lambda p, *_: (0, 0, 0, p))],
            scratch_shapes=[pltpu.VMEM((length, d), F32), pltpu.VMEM((length, d), BF), pltpu.VMEM((length, LANES), BF),
                            pltpu.VMEM((length, LANES), F32), pltpu.VMEM((length, LANES), F32), pltpu.VMEM((length, LANES), BF),
                            pltpu.SemaphoreType.DMA((members,))]),
        out_shape=[jax.ShapeDtypeStruct((length // members, d), BF)] * members + [jax.ShapeDtypeStruct((1 << bits, 4, blk, heads), BF)],
        cost_estimate=pl.CostEstimate(flops=16 * length * d * heads + 30 * length * length * heads, bytes_accessed=8 * length * d + 20 * length * heads, transcendentals=length * length * heads // HD),
        compiler_params=pltpu.CompilerParams(vmem_limit_bytes=VMEM),
    )(prefix, me, j, *mcs, n1, wo, w, q, k, v, ctx, lse, *extra)
    return res[:members], res[members]


EPS = 1e-5


def normalise(v):
    centered = v - jnp.mean(v, axis=1, keepdims=True)
    r = lax.rsqrt(jnp.mean(centered * centered, axis=1, keepdims=True) + EPS)
    return centered * r, r


def norm_backward(xhat, r, grad, gain):
    scaled = grad * gain
    return r * (scaled - jnp.mean(scaled, axis=1, keepdims=True) - xhat * jnp.mean(scaled * xhat, axis=1, keepdims=True))


def order_rows(pos, rows_to_slots):
    n = pos.shape[1] if rows_to_slots else pos.shape[0]
    slot = lax.broadcasted_iota(jnp.int32, (n, n), 0 if rows_to_slots else 1)
    return jnp.where(slot == pos, 1.0, 0.0).astype(BF)


def first_norm_kernel(members, j_ref, *refs):
    xs, gain, shift, out = refs[:members], refs[members], refs[members + 1], refs[members + 2]
    for k in range(members):
        @pl.when(pl.program_id(0) == k)
        def _(k=k):
            xhat, _ = normalise(xs[k][...].astype(F32))
            out[...] = (xhat * gain[...] + shift[...]).astype(BF)


def first_norm(j, xs, gain, shift):
    members = len(xs)
    rows, d = xs[0].shape
    fixed = lambda shape: pl.BlockSpec(shape, lambda p, *_: (0, 0))
    return pl.pallas_call(
        partial(first_norm_kernel, members),
        name="first_norm",
        grid_spec=pltpu.PrefetchScalarGridSpec(
            num_scalar_prefetch=1, grid=(members,),
            in_specs=[fixed((rows, d))] * members + [fixed((1, d))] * 2,
            out_specs=pl.BlockSpec((rows, d), lambda p, j_ref: (lax.rem(j_ref[0] + p, members), 0))),
        out_shape=jax.ShapeDtypeStruct((members * rows, d), BF),
        cost_estimate=pl.CostEstimate(flops=10 * members * rows * d, bytes_accessed=4 * members * rows * d, transcendentals=0),
        compiler_params=pltpu.CompilerParams(vmem_limit_bytes=VMEM),
    )(j, *xs, gain, shift)


def project_others_kernel(parts, j_ref, *refs):
    out = refs[-1]
    total = dot(refs[0][...], refs[parts][...], 1, 0)
    for i in range(1, parts):
        total = total + dot(refs[i][...], refs[parts + i][...], 1, 0)
    out[0] = total.astype(BF)


def project_others(j, contexts, weights, members):
    parts = len(contexts)
    length, heads = contexts[0].shape
    d = weights[0].shape[1]
    rows = length // members
    return pl.pallas_call(
        partial(project_others_kernel, parts),
        name="project_others",
        grid_spec=pltpu.PrefetchScalarGridSpec(
            num_scalar_prefetch=1, grid=(members - 1,),
            in_specs=[pl.BlockSpec((rows, heads), lambda p, j_ref: (lax.rem(j_ref[0] + p + 1, members), 0))] * parts + [pl.BlockSpec((heads, d), lambda p, *_: (0, 0))] * parts,
            out_specs=pl.BlockSpec((1, rows, d), lambda p, *_: (p, 0, 0))),
        out_shape=jax.ShapeDtypeStruct((members - 1, rows, d), BF),
        cost_estimate=pl.CostEstimate(flops=2 * parts * length * heads * d, bytes_accessed=2 * length * d, transcendentals=0),
        compiler_params=pltpu.CompilerParams(vmem_limit_bytes=VMEM),
    )(j, *contexts, *weights)


def second_norm_kernel(parts, others, j_ref, *refs):
    it = iter(refs)
    ctx = [next(it) for _ in range(parts)]
    wo = [next(it) for _ in range(parts)]
    came = [next(it) for _ in range(others)]
    x, gain, shift, pos, middle, n2 = it
    total = dot(ctx[0][...], wo[0][...], 1, 0)
    for i in range(1, parts):
        total = total + dot(ctx[i][...], wo[i][...], 1, 0)
    for c in came:
        total = total + c[...].astype(F32)
    mid = x[...].astype(F32) + total
    middle[...] = mid
    xhat, _ = normalise(mid)
    normed = (xhat * gain[...] + shift[...]).astype(BF)
    n2[...] = dot(order_rows(pos[...], True), normed, 1, 0).astype(BF)


def second_norm(j, contexts, weights, came, x, gain, shift, pos, members):
    parts, others = len(contexts), len(came)
    rows, d = x.shape
    heads = contexts[0].shape[1]
    fixed = lambda shape: pl.BlockSpec(shape, lambda p, *_: (0, 0))
    return pl.pallas_call(
        partial(second_norm_kernel, parts, others),
        name="second_norm",
        grid_spec=pltpu.PrefetchScalarGridSpec(
            num_scalar_prefetch=1, grid=(1,),
            in_specs=[pl.BlockSpec((rows, heads), lambda p, j_ref: (j_ref[0], 0))] * parts + [fixed((heads, d))] * parts
            + [fixed((rows, d))] * (others + 1) + [fixed((1, d))] * 2 + [fixed((1, rows))],
            out_specs=[fixed((rows, d))] * 2),
        out_shape=[jax.ShapeDtypeStruct((rows, d), F32), jax.ShapeDtypeStruct((rows, d), BF)],
        cost_estimate=pl.CostEstimate(flops=2 * rows * d * (rows + parts * heads), bytes_accessed=12 * rows * d, transcendentals=0),
        compiler_params=pltpu.CompilerParams(vmem_limit_bytes=VMEM),
    )(j, *contexts, *weights, *came, x, gain, shift, pos)


def hi_lo(v):
    hi = v.astype(BF)
    return hi, (v - hi.astype(F32)).astype(BF)


def middle_backward_kernel(lead, single, bnd_ref, t_ref, *refs):
    it = iter(refs)
    stacked = [next(it) for _ in range(lead)]
    flat = [next(it) for _ in range(single)]
    dots, n2, rm, middle, dy, gain, pos, mg_ref, mc_ref, sums_ref = it
    t = t_ref[0]
    total = stacked[0][0].astype(F32)
    for s in stacked[1:]:
        total = total + s[0].astype(F32)
    for s in flat:
        total = total + s[...].astype(F32)
    n2v, rmv = n2[...], rm[...]
    rows = n2v.shape[0]
    experts = bnd_ref.shape[1] - 1
    logits = dot(n2v, rmv, 1, 0)
    route_prob = lane_softmax(logits, 0, experts)
    mixing = lane_softmax(logits, experts, experts + 2)
    row = lax.broadcasted_iota(jnp.int32, (rows, 1), 0)
    route = jnp.zeros((rows, 1), jnp.int32)
    for e in range(1, experts):
        route = route + (row >= bnd_ref[t, e]).astype(jnp.int32)
    gate = pick_lane(route_prob, route)
    m0, m1 = pick_lane(mixing, experts), pick_lane(mixing, experts + 1)
    dense_dot, expert_dot = dots[:, 0:1], dots[:, 1:2]
    d0, d1 = dense_dot, expert_dot * gate
    inner = m0 * d0 + m1 * d1
    lane = lax.broadcasted_iota(jnp.int32, logits.shape, 1)
    grad = expert_dot * (m1 * gate) * (jnp.where(lane == route, 1.0, 0.0) - route_prob)
    grad = jnp.where(lane < experts, grad, 0.0)
    grad = jnp.where(lane == experts, m0 * (d0 - inner), grad)
    grad = jnp.where(lane == experts + 1, m1 * (d1 - inner), grad)
    hi, lo = hi_lo(grad)
    total = total + dot(hi, rmv, 1, 1) + dot(lo, rmv, 1, 1)
    sums_ref[0:8, :] = (dot(hi.T, n2v, 1, 0) + dot(lo.T, n2v, 1, 0))[0:8]
    g = dot(order_rows(pos[...], False), total.astype(BF), 1, 0)
    xhat, r = normalise(middle[...])
    sums_ref[8:16, :] = jnp.zeros((8, g.shape[1]), F32)
    sums_ref[8:9, :] = jnp.sum(g * xhat, axis=0, keepdims=True)
    sums_ref[9:10, :] = jnp.sum(g, axis=0, keepdims=True)
    mg = dy[...].astype(F32) + norm_backward(xhat, r, g, gain[...])
    mg_ref[...] = mg
    mc_ref[...] = mg.astype(BF)


def middle_backward(bounds, t, stacked, flat, dots, n2, rm, middle, dy, gain, pos):
    rows, d = n2.shape
    fixed = lambda shape: pl.BlockSpec(shape, lambda p, *_: (0, 0))
    big = fixed((rows, d))
    return pl.pallas_call(
        partial(middle_backward_kernel, len(stacked), len(flat)),
        name="middle_backward",
        grid_spec=pltpu.PrefetchScalarGridSpec(
            num_scalar_prefetch=2, grid=(1,),
            in_specs=[pl.BlockSpec((1, rows, d), lambda p, *_: (0, 0, 0))] * len(stacked) + [big] * len(flat)
            + [fixed((rows, 8)), big, fixed((d, 128)), big, big, fixed((1, d)), fixed((rows, 1))],
            out_specs=[big, big, fixed((16, d))]),
        out_shape=[jax.ShapeDtypeStruct((rows, d), F32), jax.ShapeDtypeStruct((rows, d), BF), jax.ShapeDtypeStruct((16, d), F32)],
        cost_estimate=pl.CostEstimate(flops=2 * rows * d * rows, bytes_accessed=20 * rows * d, transcendentals=0),
        compiler_params=pltpu.CompilerParams(vmem_limit_bytes=VMEM),
    )(bounds, t, *stacked, *flat, dots, n2, rm, middle, dy, gain, pos)


def layer_out_kernel(lead, *refs):
    stacked, flat = refs[:lead], refs[lead:-3]
    middle, pos, out = refs[-3:]
    total = stacked[0][0].astype(F32)
    for s in stacked[1:]:
        total = total + s[0].astype(F32)
    for s in flat:
        total = total + s[...].astype(F32)
    hi, lo = hi_lo(total)
    move = order_rows(pos[...], False)
    out[...] = (middle[...] + dot(move, hi, 1, 0) + dot(move, lo, 1, 0)).astype(BF)


def layer_out(stacked, flat, middle, pos):
    rows, d = middle.shape
    fixed = lambda shape: pl.BlockSpec(shape, lambda p: (0, 0))
    big = fixed((rows, d))
    return pl.pallas_call(
        partial(layer_out_kernel, len(stacked)),
        name="layer_out",
        grid=(1,),
        in_specs=[pl.BlockSpec((1, rows, d), lambda p: (0, 0, 0))] * len(stacked) + [big] * len(flat) + [big, fixed((rows, 1))],
        out_specs=big,
        out_shape=jax.ShapeDtypeStruct((rows, d), BF),
        cost_estimate=pl.CostEstimate(flops=4 * rows * d * rows, bytes_accessed=14 * rows * d, transcendentals=0),
        compiler_params=pltpu.CompilerParams(vmem_limit_bytes=VMEM),
    )(*stacked, *flat, middle, pos)


def input_backward_kernel(count, *refs):
    parts = refs[:count]
    x, mg, gain, out, sums = refs[count:]
    g = parts[0][...].astype(F32)
    for p in parts[1:]:
        g = g + p[...].astype(F32)
    xhat, r = normalise(x[...].astype(F32))
    sums[...] = jnp.zeros_like(sums)
    sums[0:1, :] = jnp.sum(g * xhat, axis=0, keepdims=True)
    sums[1:2, :] = jnp.sum(g, axis=0, keepdims=True)
    out[...] = mg[...] + norm_backward(xhat, r, g, gain[...])


def input_backward(parts, x, mg, gain):
    rows, d = x.shape
    fixed = lambda shape: pl.BlockSpec(shape, lambda p: (0, 0))
    big = fixed((rows, d))
    return pl.pallas_call(
        partial(input_backward_kernel, len(parts)),
        name="input_backward",
        grid=(1,),
        in_specs=[big] * (len(parts) + 2) + [fixed((1, d))],
        out_specs=[big, fixed((8, d))],
        out_shape=[jax.ShapeDtypeStruct((rows, d), F32), jax.ShapeDtypeStruct((8, d), F32)],
        cost_estimate=pl.CostEstimate(flops=20 * rows * d, bytes_accessed=14 * rows * d, transcendentals=0),
        compiler_params=pltpu.CompilerParams(vmem_limit_bytes=VMEM),
    )(*parts, x, mg, gain)


def wide(v):
    return v.astype(F32)


def halve(keep, send, axis, slots):
    stage = 0
    while True:
        bit = slots[stage]
        n = lax.axis_size("dp")
        came = lax.ppermute(send, "dp", [(i, i ^ (1 << bit)) for i in range(n)])
        stage += 1
        if stage == len(slots):
            return lax.squeeze(wide(keep) + wide(came), (axis,))
        half = keep.shape[axis] // 2
        cut = lambda v, a: wide(lax.slice_in_dim(v, a * half, (a + 1) * half, axis=axis))
        keep, send = [(cut(keep, a) + cut(came, a)).astype(BF) for a in range(2)]


def sum_everywhere(v):
    for axis in ("tensor", "dp"):
        n = lax.axis_size(axis)
        bit = 1
        while bit < n:
            v = v + lax.ppermute(v, axis, [(i, i ^ bit) for i in range(n)])
            bit *= 2
    return v


def shards(inputs, cotangent, routes, prefixes, gain_one, shift_one, qkv_weight, out_weight, gain_two, shift_two,
           up_weight, down_weight, expert_up, expert_down, router_weight, mix_weight):
    rows, d = inputs.shape
    tensor = lax.axis_size("tensor")
    dp = lax.axis_size("dp")
    bits = dp.bit_length() - 1
    seqs = prefixes.shape[0]
    members = tensor // seqs
    experts = expert_up.shape[0]
    t = lax.axis_index("tensor")
    s, j = t // members, t % members
    me = lax.axis_index("dp").astype(jnp.int32).reshape(1)
    j1 = j.astype(jnp.int32).reshape(1)
    t1 = t.astype(jnp.int32).reshape(1)
    place = lambda a, b: (a % seqs) * members + b % members
    everyone = [(a, b) for a in range(seqs) for b in range(members)]

    def from_member(v, k):
        return lax.ppermute(v, "tensor", [(place(a, b), place(a, b - k)) for a, b in everyone])

    def to_member(v, k):
        return from_member(v, -k)

    def from_sequence(v, k):
        return lax.ppermute(v, "tensor", [(place(a, b), place(a - k, b)) for a, b in everyone])

    def to_sequence(v, k):
        return from_sequence(v, -k)

    route_blocks = routes.reshape(tensor, rows)
    counts = jnp.stack([jnp.sum((route_blocks == e).astype(jnp.int32), axis=1) for e in range(experts)], axis=1)
    bounds = jnp.concatenate([jnp.zeros((tensor, 1), jnp.int32)] + [jnp.sum(counts[:, :e + 1], axis=1, keepdims=True) for e in range(experts)], axis=1)
    own_route = lax.dynamic_slice_in_dim(routes, t * rows, rows, 0)
    key_col = own_route * rows + jnp.arange(rows, dtype=jnp.int32)[:, None]
    key_row = key_col.reshape(1, rows)
    pos_row = jnp.sum((key_col < key_row).astype(jnp.int32), axis=0, keepdims=True)
    pos_col = jnp.sum((key_row < key_col).astype(jnp.int32), axis=1, keepdims=True)
    blocks = jnp.stack([((s + ds) % seqs) * members + (j + dj) % members for dj in range(members) for ds in range(seqs)]).astype(jnp.int32)

    w_own = jnp.transpose(qkv_weight, (1, 0, 2))
    w_all = [w_own] + [from_sequence(w_own, ds) for ds in range(1, seqs)]
    wo_all = [out_weight] + [from_sequence(out_weight, ds) for ds in range(1, seqs)]
    xs = [inputs] + [from_member(inputs, k) for k in range(1, members)]
    gain_one, shift_one, gain_two, shift_two = [v.reshape(1, d) for v in (gain_one, shift_one, gain_two, shift_two)]
    prefix = lax.dynamic_slice_in_dim(prefixes, s, 1)
    n1 = first_norm(j1, xs, gain_one, shift_one)
    saved = [attn_forward(prefix, n1, w) for w in w_all]
    contexts = [v[3] for v in saved]
    sent = project_others(j1, contexts, wo_all, members)
    came = [to_member(sent[k - 1], k) for k in range(1, members)]
    middle, n2 = second_norm(j1, contexts, wo_all, came, inputs, gain_two, shift_two, pos_row, members)

    def gather(v):
        mine = [v] + [from_sequence(v, ds) for ds in range(1, seqs)]
        out = list(mine)
        for k in range(1, members):
            out += [from_member(m, k) for m in mine]
        return out

    dys = dot(order_rows(pos_row, True), cotangent, 1, 0).astype(BF)
    dy_all = gather(dys)
    n2_all = gather(n2)
    rm = jnp.concatenate([router_weight, mix_weight, jnp.zeros((d, 128 - experts - 2), BF)], axis=1)
    out_d, rg_d, dots_d, keep_d, send_d = ffn_dense(me, blocks, bounds, n2_all, dy_all, rm, up_weight, down_weight, bits)
    res = ffn_experts(me, blocks, bounds, n2_all, dy_all, rm, expert_up, expert_down, out_d, rg_d, dots_d, members, bits)
    outs, rgs, dots = res[:members], res[members:2 * members], res[2 * members]
    keep_e, send_e = res[2 * members + 1:2 * members + 1 + experts], res[2 * members + 1 + experts:]

    def scatter(parts):
        stacked = [parts[0]] + [to_member(parts[k], k) for k in range(1, members)]
        flat = []
        for ds in range(1, seqs):
            term = wide(stacked[0][ds])
            for v in stacked[1:]:
                term = term + wide(v[ds])
            flat.append(to_sequence(term.astype(BF), ds))
        return stacked, flat

    per = seqs * rows
    dot_parts = [dots[:, k * per:(k + 1) * per] for k in range(members)]
    for k in range(1, members):
        dot_parts[0] = dot_parts[0] + to_member(dot_parts[k], k)
    own_dots = dot_parts[0][:, 0:rows]
    for ds in range(1, seqs):
        own_dots = own_dots + to_sequence(dot_parts[0][:, ds * rows:(ds + 1) * rows], ds)
    stacked, flat = scatter([v.reshape(seqs, rows, d) for v in rgs])
    mg, mc, sums_two = middle_backward(bounds, t1, stacked, flat, own_dots.T, n2, rm, middle, cotangent, gain_two, pos_col)
    mcs = [mc] + [from_member(mc, k) for k in range(1, members)]
    ngs = None
    grads = [None] * seqs
    for ds in list(range(1, seqs)) + [0]:
        ngs, grads[ds] = attn_backward(prefix, me, j1, mcs, n1, wo_all[ds], w_all[ds], saved[ds], ngs, bits)
    ng_parts = [ngs[0]] + [to_member(ngs[k], k) for k in range(1, members)]
    input_grad, sums_one = input_backward(ng_parts, inputs, mg, gain_one)
    stacked_o, flat_o = scatter([v.reshape(seqs, rows, d) for v in outs])
    layer_output = layer_out(stacked_o, flat_o, middle, pos_col)

    slots = tuple(range(bits))
    totals = [halve(k, v, 1, slots) for k, v in zip([keep_d] + list(keep_e), [send_d] + list(send_e))]
    half = 1 << (bits - 1)
    attn_total = wide(grads[0])
    for ds in range(1, seqs):
        attn_total = attn_total + wide(to_sequence(grads[ds], ds))
    attn_total = attn_total.astype(BF)
    attn_grad = halve(attn_total[:half], attn_total[half:], 0, slots)
    up_out, down_out = totals[0][0], totals[0][1].T
    expert_up_out = jnp.stack([v[0] for v in totals[1:]])
    expert_down_out = jnp.stack([v[1].T for v in totals[1:]])
    qkv_out = jnp.transpose(attn_grad[0:3], (1, 0, 2))
    out_out = attn_grad[3].T
    lanes = d // (dp * tensor)
    first = (lax.axis_index("dp") * tensor + t) * lanes
    two = lax.dynamic_slice_in_dim(sum_everywhere(sums_two), first, lanes, 1)
    one = lax.dynamic_slice_in_dim(sum_everywhere(sums_one), first, lanes, 1)
    return (layer_output, input_grad, one[0], one[1], qkv_out, out_out, two[8], two[9], up_out, down_out,
            expert_up_out, expert_down_out, two[0:experts].T, two[experts:experts + 2].T)


def solution(mesh):
    both = ("dp", "tensor")
    in_specs = (P(both, None), P(both, None), P("dp", None), P("dp"), P(), P(), P(None, None, "tensor"), P("tensor", None), P(), P(),
                P(None, "tensor"), P("tensor", None), P(None, None, "tensor"), P(None, "tensor", None), P(), P())
    out_specs = (P(both, None), P(both, None), P(both), P(both), P("dp", None, "tensor"), P("tensor", "dp"), P(both), P(both),
                 P("dp", "tensor"), P("tensor", "dp"), P(None, "dp", "tensor"), P(None, "tensor", "dp"), P(both, None), P(both, None))
    return jax.shard_map(shards, mesh=mesh, in_specs=in_specs, out_specs=out_specs, check_vma=False)
```

time: 2020 us -> 708 us (0.35)
  local copies, waits for them, and re-layouts: 539 us -> 20.9 us
  waiting for transfers between devices: 819 us -> 325 us
  matrix products: 433 us -> 1.65 us
  Pallas kernels: 0 us -> 235 us
  other arithmetic: 150 us -> 55.5 us
  starting transfers between devices: 1.49 us -> 59.6 us
  blocking collectives: 39.6 us -> 0 us
    dot_general x74 -> x1, matrix products: 429 us -> 1.65 us  [dot(): lax.dot_general(a, b, (((ca,), (cb,)), ((), ())), preferred_element_type=...]
    reduce_scatter x8 -> x0, waiting for transfers between devices: 386 us -> none  [the longest x1 148 us: shards(): lax.psum_scatter(expert_up_total.astype(jnp.bfloat16), 'dp', scatter_dime...]
    gather x52 -> x0, local copies, waits for them, and re-layouts: 353 us -> none  [the longest x15 112 us: expert_forward(): branch = product(hidden, expert_down[owners], 'tnf,tfd->tnd')]
    ppermute x0 -> x47, waiting for transfers between devices: none -> 325 us  [the longest x18 214 us: halve(): came = lax.ppermute(send, 'dp', [(i, i ^ 1 << bit) for i in range(n)])]
    unnamed x23 -> x0, waiting for transfers between devices: 316 us -> none
    pallas_call x0 -> x12, Pallas kernels: none -> 235 us  [the longest x1 79.3 us: ffn_experts(): pl.pallas_call(partial(ffn_kernel, ((count, members), chunks, rows, d, f,...]
    all_gather x5 -> x0, waiting for transfers between devices: 117 us -> none  [the longest x1 34.7 us: shards(): gathered_one = lax.all_gather(normed_one, 'tensor', axis=0, tiled=True)]
    ppermute x0 -> x47, starting transfers between devices: none -> 59.6 us  [the longest x18 38.9 us: halve(): came = lax.ppermute(send, 'dp', [(i, i ^ 1 << bit) for i in range(n)])]
  transfers between devices with their start and end apart: 18 -> 47, of which waited for: 13 -> 23; matrix products, arithmetic and copies ran while one was open for 33% -> 10% of each run, Pallas kernels for 0% -> 27%
where the time goes in v1:
time: 708 us; the launch traced here: 699 us
  waiting for transfers between devices  325 us (46%)
  Pallas kernels  235 us (33%)
  starting transfers between devices  59.6 us (8%)
  other arithmetic  55.5 us (8%)
  local copies, waits for them, and re-layouts  20.9 us (3%)
    ppermute x18, waiting for transfers between devices, halve(): came = lax.ppermute(send, 'dp', [(i, i ^ 1 << bit) for i in range(n)])  214 us
    pallas_call x1, Pallas kernels, ffn_experts(): pl.pallas_call(partial(ffn_kernel, ((count, members), chunks, rows, d, f,...  79.3 us
    ppermute x8, waiting for transfers between devices, from_sequence(): lax.ppermute(v, 'tensor', [(place(a, b), place(a - k, b)) for a, b in eve...  70.7 us
    pallas_call x2, Pallas kernels, attn_backward(): pl.pallas_call(partial(attn_backward_kernel, length, bits, members, base...  54.9 us
    pallas_call x1, Pallas kernels, ffn_dense(): pl.pallas_call(partial(ffn_kernel, (None, chunks, rows, d, f, bits, tm)),...  41.8 us
    ppermute x18, starting transfers between devices, halve(): came = lax.ppermute(send, 'dp', [(i, i ^ 1 << bit) for i in range(n)])  38.9 us
    ppermute x10, waiting for transfers between devices, sum_everywhere(): v = v + lax.ppermute(v, axis, [(i, i ^ bit) for i in range(n)])  37 us
    convert_element_type x12, other arithmetic, halve(): keep, send = [(cut(keep, a) + cut(came, a)).astype(BF) for a in range(2)]  32 us
  transfers between devices with their start and end apart: 47, of which 23 were waited for; matrix products, arithmetic and copies ran while one was open for 10% of the time, Pallas kernels for 27%

profile of v1, /device:TPU:0, one launch (start us, length us, event | category | flops | bytes accessed | tf_op | source)
XLA Modules:
  0.0 699.1 jit_solution(7734394059199264020)
XLA Ops:
  0.6 3.0 collective-permute-start.1
  7.5 4.1 first_norm.1.n1_ref.refs_2_
  11.6 13.0 %attn_forward.2 = (bf16[1024,256]{1,0:T(8,128)(2,1)}, bf16[1024,256]{1,0:T(8,128)(2,1)}, bf16[1024,256]{1,0:T(8,128)(2,1)}, bf16[1024,256]{1,0:T(8,128)(2,1)}, f32[2,8,1024]{2,1,0:T(8,128)}) custom-call(s32[1]{0:T(128)} %dynamic_slice.12.prefix_ref, bf16[1024,1024]{1,0:T(8,128)(2,1)} %first_norm.1.n1_ref.refs_2_, bf16[3,1024,256]{2,1,0:T(8,128)(2,1)} %bitcast.113), custom_call_target="tpu_custom_call" | custom-call | flops 4831838208 | bytes 6815744 | tf_op jit(solution)/shard_map/attn_forward/pallas_call | solution.py:405
  24.6 14.6 %collective-permute-done.1.w_ref.refs_4_ = bf16[3,1024,256]{2,1,0:T(8,128)(2,1)} collective-permute-done((bf16[3,1024,256]{2,1,0:T(8,128)(2,1)}, bf16[3,1024,256]{2,1,0:T(8,128)(2,1)}, u32[]{:S(2)}, u32[]{:S(2)}) %collective-permute-start.1) | collective-permute-done | bytes 1572896 | tf_op jit(solution)/shard_map/ppermute | solution.py:813
  39.2 13.3 %attn_forward.3 = (bf16[1024,256]{1,0:T(8,128)(2,1)}, bf16[1024,256]{1,0:T(8,128)(2,1)}, bf16[1024,256]{1,0:T(8,128)(2,1)}, bf16[1024,256]{1,0:T(8,128)(2,1)}, f32[2,8,1024]{2,1,0:T(8,128)}) custom-call(s32[1]{0:T(128)} %dynamic_slice.12.prefix_ref, bf16[1024,1024]{1,0:T(8,128)(2,1)} %first_norm.1.n1_ref.refs_2_, ...), custom_call_target="tpu_custom_call" | custom-call | flops 4831838208 | bytes 6815744 | tf_op jit(solution)/shard_map/attn_forward/pallas_call | solution.py:405
  53.4 3.0 project_others.1
  56.8 1.7 convolution_convert_fusion.refs_7_
  58.4 2.1 collective-permute-start.7
  61.5 4.9 second_norm.1
  67.2 17.5 %collective-permute-done.7.refs_8_ = bf16[512,1024]{1,0:T(8,128)(2,1)S(1)} collective-permute-done((bf16[512,1024]{1,0:T(8,128)(2,1)}, bf16[512,1024]{1,0:T(8,128)(2,1)S(1)}, u32[]{:S(2)}, u32[]{:S(2)}) %collective-permute-start.7) | collective-permute-done | bytes 1048608 | tf_op jit(solution)/shard_map/ppermute | solution.py:813
  85.2 21.9 %collective-permute-done.4.refs_4_ = bf16[512,1024]{1,0:T(8,128)(2,1)} collective-permute-done((bf16[512,1024]{1,0:T(8,128)(2,1)}, bf16[512,1024]{1,0:T(8,128)(2,1)}, u32[]{:S(2)}, u32[]{:S(2)}) %collective-permute-start.4) | collective-permute-done | bytes 1048608 | tf_op jit(solution)/shard_map/ppermute | solution.py:813
  110.9 41.8 %ffn_dense.1 = (bf16[2048,1024]{1,0:T(8,128)(2,1)}, bf16[2048,1024]{1,0:T(8,128)(2,1)}, f32[8,2048]{1,0:T(8,128)}, bf16[2,4,128,1024]{3,2,1,0:T(8,128)(2,1)}, bf16[2,4,128,1024]{3,2,1,0:T(8,128)(2,1)}) custom-call(s32[1]{0:T(128)} %bitcast.refs_0_.me_ref, s32[4]{0:T(128)} %pad_add_fusion.refs_1_, s32[4,5]{1,0:T(4,128)} %concatenate.8.refs_2_.bnd_ref, ...), custom_call_target="tpu_custom_call" | custom-call | flops 25769803776 | bytes 25165824 | tf_op jit(solution)/shard_map/ffn_dense/pallas_call | solution.py:293
  152.6 1.8 collective-permute-start.32
  154.4 79.3 %ffn_experts.1 = (bf16[1024,1024]{1,0:T(8,128)(2,1)}, bf16[1024,1024]{1,0:T(8,128)(2,1)}, bf16[1024,1024]{1,0:T(8,128)(2,1)}, bf16[1024,1024]{1,0:T(8,128)(2,1)}...) custom-call(s32[1]{0:T(128)} %bitcast.refs_0_.me_ref, ...), custom_call_target="tpu_custom_call" | custom-call | flops 25769803776 | bytes 67108864 | tf_op jit(solution)/shard_map/ffn_experts/pallas_call | solution.py:325
  234.1 2.0 collective-permute-start.38
  237.4 1.8 collective-permute-done.14
  240.3 1.6 collective-permute-start.15
  241.9 6.8 collective-permute-done.15
  248.8 2.0 collective-permute-start.44
  252.4 1.6 fusion
  254.0 4.1 add_convert_fusion.10
  258.1 24.8 %collective-permute-done.35 = bf16[2,4,128,1024]{3,2,1,0:T(8,128)(2,1)} collective-permute-done((bf16[2,4,128,1024]{3,2,1,0:T(8,128)(2,1)}, bf16[2,4,128,1024]{3,2,1,0:T(8,128)(2,1)}, u32[]{:S(2)}, u32[]{:S(2)}) %collective-permute-start.35) | collective-permute-done | bytes 2097184 | tf_op jit(solution)/shard_map/ppermute | solution.py:770
  284.4 4.0 add_convert_fusion.8
  288.4 39.4 %collective-permute-done.38 = bf16[2,4,128,1024]{3,2,1,0:T(8,128)(2,1)} collective-permute-done((bf16[2,4,128,1024]{3,2,1,0:T(8,128)(2,1)}, bf16[2,4,128,1024]{3,2,1,0:T(8,128)(2,1)}, u32[]{:S(2)}, u32[]{:S(2)}) %collective-permute-start.38) | collective-permute-done | bytes 2097184 | tf_op jit(solution)/shard_map/ppermute | solution.py:770
  329.3 4.0 add_convert_fusion.6
  333.3 39.4 %collective-permute-done.41 = bf16[2,4,128,1024]{3,2,1,0:T(8,128)(2,1)} collective-permute-done((bf16[2,4,128,1024]{3,2,1,0:T(8,128)(2,1)}, bf16[2,4,128,1024]{3,2,1,0:T(8,128)(2,1)}, u32[]{:S(2)}, u32[]{:S(2)}) %collective-permute-start.41) | collective-permute-done | bytes 2097184 | tf_op jit(solution)/shard_map/ppermute | solution.py:770
  374.3 3.7 add_convert_fusion.4
  378.0 39.0 %collective-permute-done.44 = bf16[2,4,128,1024]{3,2,1,0:T(8,128)(2,1)} collective-permute-done((bf16[2,4,128,1024]{3,2,1,0:T(8,128)(2,1)}, bf16[2,4,128,1024]{3,2,1,0:T(8,128)(2,1)}, u32[]{:S(2)}, u32[]{:S(2)}) %collective-permute-start.44) | collective-permute-done | bytes 2097184 | tf_op jit(solution)/shard_map/ppermute | solution.py:770
  417.0 1.6 collective-permute-start.39
  418.6 4.0 add_convert_fusion.2
  424.4 1.6 collective-permute-start.11
  426.0 10.6 %middle_backward.1 = (f32[512,1024]{1,0:T(8,128)}, bf16[512,1024]{1,0:T(8,128)(2,1)}, f32[16,1024]{1,0:T(8,128)}) custom-call(s32[4,5]{1,0:T(4,128)} %concatenate.8.refs_2_.bnd_ref, s32[1]{0:T(128)} %bitcast.22.t_ref, bf16[2,512,1024]{2,1,0:T(8,128)(2,1)} %bitcast.96, bf16[2,512,1024]{2,1,0:T(8,128)(2,1)} %collective-permute-done.12.refs_1_, ...), custom_call_target="tpu_custom_call" | custom-call | flops 536870912 | bytes 10485760 | tf_op jit(solution)/shard_map/middle_backward/pallas_call | solution.py:689
  436.7 1.7 collective-permute-start.45
  438.3 2.4 add_convert_fusion.19
  440.8 2.0 add_convert_fusion.17
  445.2 2.1 add_convert_fusion.15
  447.3 2.9 collective-permute-done.28
  450.2 26.9 %collective-permute-done.42 = bf16[2,2,128,1024]{3,2,1,0:T(8,128)(2,1)} collective-permute-done((bf16[2,2,128,1024]{3,2,1,0:T(8,128)(2,1)}, bf16[2,2,128,1024]{3,2,1,0:T(8,128)(2,1)}, u32[]{:S(2)}, u32[]{:S(2)}) %collective-permute-start.42) | collective-permute-done | bytes 1048608 | tf_op jit(solution)/shard_map/ppermute | solution.py:770
  478.6 2.8 collective-permute-done.29
  481.9 23.6 %collective-permute-done.45 = bf16[2,2,128,1024]{3,2,1,0:T(8,128)(2,1)S(1)} collective-permute-done((bf16[2,2,128,1024]{3,2,1,0:T(8,128)(2,1)}, bf16[2,2,128,1024]{3,2,1,0:T(8,128)(2,1)S(1)}, u32[]{:S(2)}, u32[]{:S(2)}) %collective-permute-start.45) | collective-permute-done | bytes 1048608 | tf_op jit(solution)/shard_map/ppermute | solution.py:770
  506.7 3.1 collective-permute-done.30
  509.8 3.4 collective-permute-start.40
  513.3 4.9 layer_out.1
  518.2 22.0 %collective-permute-done.31 = f32[16,1024]{1,0:T(8,128)S(1)} collective-permute-done((f32[16,1024]{1,0:T(8,128)S(1)}, f32[16,1024]{1,0:T(8,128)S(1)}, u32[]{:S(2)}, u32[]{:S(2)}) %collective-permute-start.31) | collective-permute-done | bytes 65568 | tf_op jit(solution)/shard_map/ppermute | solution.py:784
  542.0 2.9 collective-permute-start.46
  544.9 2.6 convert_add_fusion.6
  547.5 26.8 %attn_backward.2 = (bf16[512,1024]{1,0:T(8,128)(2,1)}, bf16[512,1024]{1,0:T(8,128)(2,1)}, bf16[8,4,128,256]{3,2,1,0:T(8,128)(2,1)}) custom-call(s32[1]{0:T(128)} %dynamic_slice.12.prefix_ref, s32[1]{0:T(128)} %bitcast.refs_0_.me_ref, s32[1]{0:T(128)} %bitcast.9.j_ref, bf16[512,1024]{1,0:T(8,128)(2,1)} %get-tuple-element.67.refs_0_, ...), custom_call_target="tpu_custom_call" | custom-call | flops 12348030976 | bytes 13631488 | tf_op jit(solution)/shard_map/attn_backward/pallas_call | solution.py:509
  574.3 1.6 collective-permute-start.23
  579.5 2.4 convert_add_fusion.4
  581.9 28.1 %attn_backward.3 = (bf16[512,1024]{1,0:T(8,128)(2,1)}, bf16[512,1024]{1,0:T(8,128)(2,1)}, bf16[8,4,128,256]{3,2,1,0:T(8,128)(2,1)}) custom-call(s32[1]{0:T(128)} %dynamic_slice.12.prefix_ref, s32[1]{0:T(128)} %bitcast.refs_0_.me_ref, s32[1]{0:T(128)} %bitcast.9.j_ref, bf16[512,1024]{1,0:T(8,128)(2,1)} %get-tuple-element.67.refs_0_, ...), custom_call_target="tpu_custom_call" | custom-call | flops 12348030976 | bytes 13631488 | tf_op jit(solution)/shard_map/attn_backward/pallas_call | solution.py:509
  610.1 9.8 %collective-permute-done.23 = bf16[8,4,128,256]{3,2,1,0:T(8,128)(2,1)} collective-permute-done((bf16[8,4,128,256]{3,2,1,0:T(8,128)(2,1)}, bf16[8,4,128,256]{3,2,1,0:T(8,128)(2,1)}, u32[]{:S(2)}, u32[]{:S(2)}) %collective-permute-start.23) | collective-permute-done | bytes 2097184 | tf_op jit(solution)/shard_map/ppermute | solution.py:813
  620.0 3.0 add_convert_fusion
  625.8 2.4 convert_add_fusion.3
  629.5 5.6 input_backward.1
  638.1 8.2 %collective-permute-done.24 = bf16[4,4,128,256]{3,2,1,0:T(8,128)(2,1)} collective-permute-done((bf16[4,4,128,256]{3,2,1,0:T(8,128)(2,1)}, bf16[4,4,128,256]{3,2,1,0:T(8,128)(2,1)}, u32[]{:S(2)}, u32[]{:S(2)}) %collective-permute-start.24) | collective-permute-done | bytes 1048608 | tf_op jit(solution)/shard_map/ppermute | solution.py:770
  646.3 2.3 add_convert_fusion.22
  648.6 17.3 %collective-permute-start.25 = (bf16[2,4,128,256]{3,2,1,0:T(8,128)(2,1)}, bf16[2,4,128,256]{3,2,1,0:T(8,128)(2,1)}, u32[]{:S(2)}, u32[]{:S(2)}) collective-permute-start(bf16[2,4,128,256]{3,2,1,0:T(8,128)(2,1)} %get-tuple-element.158), channel_id=1, source_target_pairs={{0,8},{4,12},{8,0},{12,4},{16,24},{20,28},{24,16},{28,20},{1,9},{5... | collective-permute-start | bytes 1572872 | tf_op jit(solution)/shard_map/ppermute | solution.py:770
  666.0 1.7 collective-permute-start.20
  668.0 2.0 collective-permute-done.20
  671.5 2.0 copy.68
  673.5 1.8 copy.69
  675.3 3.3 collective-permute-done.21
  678.6 2.9 collective-permute-start.22
  684.0 12.3 %collective-permute-done.26 = bf16[1,4,128,256]{3,2,1,0:T(8,128)(2,1)S(1)} collective-permute-done((bf16[1,4,128,256]{3,2,1,0:T(8,128)(2,1)S(1)}, bf16[1,4,128,256]{3,2,1,0:T(8,128)(2,1)S(1)}, u32[]{:S(2)}, u32[]{:S(2)}) %collective-permute-start.26) | collective-permute-done | bytes 262176 | tf_op jit(solution)/shard_map/ppermute | solution.py:770
  (187 shorter events, 46.7 us)
Async XLA Ops:
  0.6 38.6 %collective-permute-start.1 = (bf16[3,1024,256]{2,1,0:T(8,128)(2,1)}, bf16[3,1024,256]{2,1,0:T(8,128)(2,1)}, u32[]{:S(2)}, u32[]{:S(2)}) collective-permute-start(bf16[3,1024,256]{2,1,0:T(8,128)(2,1)} %bitcast.112), channel_id=1, source_target_pairs={{0,2},{1,3},{2,0},{3,1},{4,6},{5,7},{6,4},{7,5},{8,10},{9,11},{10,... | collective-permute-start | bytes 4718600 | tf_op jit(solution)/shard_map/ppermute | solution.py:813
  3.7 2.9 collective-permute-start
  3.7 48.8 %collective-permute-start.2 = (bf16[256,1024]{1,0:T(8,128)(2,1)}, bf16[256,1024]{1,0:T(8,128)(2,1)S(1)}, u32[]{:S(2)}, u32[]{:S(2)}) collective-permute-start(bf16[256,1024]{1,0:T(8,128)(2,1)} %refs_3_.1), channel_id=1, source_target_pairs={{0,2},{1,3},{2,0},{3,1},{4,6},{5,7},{6,4},{7,5},{8,10},{9,11},{10,... | collective-permute-start | bytes 1572872 | tf_op jit(solution)/shard_map/ppermute | solution.py:813
  52.5 4.3 copy-start.22
  56.4 4.1 collective-permute-start.3
  58.4 26.3 %collective-permute-start.7 = (bf16[512,1024]{1,0:T(8,128)(2,1)}, bf16[512,1024]{1,0:T(8,128)(2,1)S(1)}, u32[]{:S(2)}, u32[]{:S(2)}) collective-permute-start(bf16[512,1024]{1,0:T(8,128)(2,1)} %convolution_convert_fusion.refs_7_), channel_id=1, source_target_pairs={{0,2},{1,3},{2,0},{3,1},{4,6},{5,7},{6,4},{7,5},{8,10},{9,11},{10,... | collective-permute-start | bytes 3145736 | tf_op jit(solution)/shard_map/ppermute | solution.py:813
  61.5 46.7 %copy-start.29 = (bf16[1024,4]{0,1:T(4,128)(2,1)S(1)}, bf16[1024,4]{0,1:T(4,128)(2,1)}, u32[]{:S(2)}) copy-start(bf16[1024,4]{0,1:T(4,128)(2,1)} %param.30) | copy-start | bytes 24580
  61.5 46.9 %copy-start.30 = (bf16[1024,2]{0,1:T(2,128)(2,1)S(1)}, bf16[1024,2]{0,1:T(2,128)(2,1)}, u32[]{:S(2)}) copy-start(bf16[1024,2]{0,1:T(2,128)(2,1)} %param.31) | copy-start | bytes 12292
  66.4 40.7 %collective-permute-start.4 = (bf16[512,1024]{1,0:T(8,128)(2,1)}, bf16[512,1024]{1,0:T(8,128)(2,1)}, u32[]{:S(2)}, u32[]{:S(2)}) collective-permute-start(bf16[512,1024]{1,0:T(8,128)(2,1)} %get-tuple-element.57.refs_3_.refs_4_), channel_id=1, source_target_pairs={{0,2},{1,3},{2,0},{3,1},{4,6},{5,7},{6,4},{7,5},{8,10},{9,11},{10,... | collective-permute-start | bytes 3145736 | tf_op jit(solution)/shard_map/ppermute | solution.py:813
  67.2 43.6 %collective-permute-start.8 = (bf16[512,1024]{1,0:T(8,128)(2,1)}, bf16[512,1024]{1,0:T(8,128)(2,1)}, u32[]{:S(2)}, u32[]{:S(2)}) collective-permute-start(bf16[512,1024]{1,0:T(8,128)(2,1)} %convolution_convert_fusion.refs_7_), channel_id=1, source_target_pairs={{0,1},{1,0},{2,3},{3,2},{4,5},{5,4},{6,7},{7,6},{8,9},{9,8},{10,11... | collective-permute-start | bytes 3145736 | tf_op jit(solution)/shard_map/ppermute | solution.py:807
  84.7 26.2 %copy-start.31 = (bf16[512,1024]{1,0:T(8,128)(2,1)}, bf16[512,1024]{1,0:T(8,128)(2,1)S(1)}, u32[]{:S(2)}) copy-start(bf16[512,1024]{1,0:T(8,128)(2,1)S(1)} %collective-permute-done.7.refs_8_) | copy-start | bytes 3145732
  84.7 26.1 %collective-permute-start.9 = (bf16[512,1024]{1,0:T(8,128)(2,1)S(1)}, bf16[512,1024]{1,0:T(8,128)(2,1)}, u32[]{:S(2)}, u32[]{:S(2)}) collective-permute-start(bf16[512,1024]{1,0:T(8,128)(2,1)S(1)} %collective-permute-done.7.refs_8_), channel_id=1, source_target_pairs={{0,1},{1,0},{2,3},{3,2},{4,5},{5,4},{6,7},{7,6},{8,9},{9,8},{10,11... | collective-permute-start | bytes 3145736 | tf_op jit(solution)/shard_map/ppermute | solution.py:807
  84.7 26.1 %collective-permute-start.5 = (bf16[512,1024]{1,0:T(8,128)(2,1)}, bf16[512,1024]{1,0:T(8,128)(2,1)}, u32[]{:S(2)}, u32[]{:S(2)}) collective-permute-start(bf16[512,1024]{1,0:T(8,128)(2,1)} %get-tuple-element.57.refs_3_.refs_4_), channel_id=1, source_target_pairs={{0,1},{1,0},{2,3},{3,2},{4,5},{5,4},{6,7},{7,6},{8,9},{9,8},{10,11... | collective-permute-start | bytes 3145736 | tf_op jit(solution)/shard_map/ppermute | solution.py:807
  107.1 3.8 collective-permute-start.6
  152.6 96.1 %collective-permute-start.32 = (bf16[2,4,128,1024]{3,2,1,0:T(8,128)(2,1)}, bf16[2,4,128,1024]{3,2,1,0:T(8,128)(2,1)}, u32[]{:S(2)}, u32[]{:S(2)}) collective-permute-start(bf16[2,4,128,1024]{3,2,1,0:T(8,128)(2,1)} %get-tuple-element.87), channel_id=1, source_target_pairs={{0,4},{4,0},{8,12},{12,8},{16,20},{20,16},{24,28},{28,24},{1,5},{5... | collective-permute-start | bytes 6291464 | tf_op jit(solution)/shard_map/ppermute | solution.py:770
  233.8 17.9 %collective-permute-start.12 = (bf16[2,512,1024]{2,1,0:T(8,128)(2,1)}, bf16[2,512,1024]{2,1,0:T(8,128)(2,1)}, u32[]{:S(2)}, u32[]{:S(2)}) collective-permute-start(bf16[2,512,1024]{2,1,0:T(8,128)(2,1)} %bitcast.111), channel_id=1, source_target_pairs={{0,1},{1,0},{2,3},{3,2},{4,5},{5,4},{6,7},{7,6},{8,9},{9,8},{10,11... | collective-permute-start | bytes 6291464 | tf_op jit(solution)/shard_map/ppermute | solution.py:807
  234.1 48.8 %collective-permute-start.35 = (bf16[2,4,128,1024]{3,2,1,0:T(8,128)(2,1)}, bf16[2,4,128,1024]{3,2,1,0:T(8,128)(2,1)}, u32[]{:S(2)}, u32[]{:S(2)}) collective-permute-start(bf16[2,4,128,1024]{3,2,1,0:T(8,128)(2,1)} %get-tuple-element.89), channel_id=1, source_target_pairs={{0,4},{4,0},{8,12},{12,8},{16,20},{20,16},{24,28},{28,24},{1,5},{5... | collective-permute-start | bytes 6291464 | tf_op jit(solution)/shard_map/ppermute | solution.py:770
  234.1 93.7 %collective-permute-start.38 = (bf16[2,4,128,1024]{3,2,1,0:T(8,128)(2,1)}, bf16[2,4,128,1024]{3,2,1,0:T(8,128)(2,1)}, u32[]{:S(2)}, u32[]{:S(2)}) collective-permute-start(bf16[2,4,128,1024]{3,2,1,0:T(8,128)(2,1)} %get-tuple-element.91), channel_id=1, source_target_pairs={{0,4},{4,0},{8,12},{12,8},{16,20},{20,16},{24,28},{28,24},{1,5},{5... | collective-permute-start | bytes 6291464 | tf_op jit(solution)/shard_map/ppermute | solution.py:770
  236.9 15.5 %copy-start.2 = (bf16[1024,1024]{1,0:T(8,128)(2,1)S(1)}, bf16[1024,1024]{1,0:T(8,128)(2,1)}, u32[]{:S(2)}) copy-start(bf16[1024,1024]{1,0:T(8,128)(2,1)} %get-tuple-element.64) | copy-start | bytes 6291460
  237.1 2.1 collective-permute-start.14
  240.3 8.4 %collective-permute-start.15 = (f32[8,512]{0,1:T(8,128)S(1)}, f32[8,512]{0,1:T(8,128)S(1)}, u32[]{:S(2)}, u32[]{:S(2)}) collective-permute-start(f32[8,512]{0,1:T(8,128)S(1)} %slice.339), channel_id=1, source_target_pairs={{0,2},{1,3},{2,0},{3,1},{4,6},{5,7},{6,4},{7,5},{8,10},{9,11},{10,... | collective-permute-start | bytes 49160 | tf_op jit(solution)/shard_map/ppermute | solution.py:813
  248.7 124.0 %collective-permute-start.41 = (bf16[2,4,128,1024]{3,2,1,0:T(8,128)(2,1)}, bf16[2,4,128,1024]{3,2,1,0:T(8,128)(2,1)}, u32[]{:S(2)}, u32[]{:S(2)}) collective-permute-start(bf16[2,4,128,1024]{3,2,1,0:T(8,128)(2,1)} %get-tuple-element.93), channel_id=1, source_target_pairs={{0,4},{4,0},{8,12},{12,8},{16,20},{20,16},{24,28},{28,24},{1,5},{5... | collective-permute-start | bytes 6291464 | tf_op jit(solution)/shard_map/ppermute | solution.py:770
  248.8 168.2 %collective-permute-start.44 = (bf16[2,4,128,1024]{3,2,1,0:T(8,128)(2,1)}, bf16[2,4,128,1024]{3,2,1,0:T(8,128)(2,1)}, u32[]{:S(2)}, u32[]{:S(2)}) collective-permute-start(bf16[2,4,128,1024]{3,2,1,0:T(8,128)(2,1)} %get-tuple-element.95), channel_id=1, source_target_pairs={{0,4},{4,0},{8,12},{12,8},{16,20},{20,16},{24,28},{28,24},{1,5},{5... | collective-permute-start | bytes 6291464 | tf_op jit(solution)/shard_map/ppermute | solution.py:770
  251.6 171.0 %collective-permute-start.10 = (bf16[2,512,1024]{2,1,0:T(8,128)(2,1)}, bf16[2,512,1024]{2,1,0:T(8,128)(2,1)S(1)}, u32[]{:S(2)}, u32[]{:S(2)}) collective-permute-start(bf16[2,512,1024]{2,1,0:T(8,128)(2,1)} %bitcast.110), channel_id=1, source_target_pairs={{0,1},{1,0},{2,3},{3,2},{4,5},{5,4},{6,7},{7,6},{8,9},{9,8},{10,11... | collective-permute-start | bytes 6291464 | tf_op jit(solution)/shard_map/ppermute | solution.py:807
  254.0 30.4 %copy-start.12 = (bf16[2,4,128,1024]{3,2,1,0:T(8,128)(2,1)S(1)}, bf16[2,4,128,1024]{3,2,1,0:T(8,128)(2,1)}, u32[]{:S(2)}) copy-start(bf16[2,4,128,1024]{3,2,1,0:T(8,128)(2,1)} %get-tuple-element.88) | copy-start | bytes 6291460
  282.9 153.8 %collective-permute-start.33 = (bf16[2,2,128,1024]{3,2,1,0:T(8,128)(2,1)}, bf16[2,2,128,1024]{3,2,1,0:T(8,128)(2,1)}, u32[]{:S(2)}, u32[]{:S(2)}) collective-permute-start(bf16[2,2,128,1024]{3,2,1,0:T(8,128)(2,1)} %get-tuple-element.156), channel_id=1, source_target_pairs={{0,8},{4,12},{8,0},{12,4},{16,24},{20,28},{24,16},{28,20},{1,9},{5... | collective-permute-start | bytes 3145736 | tf_op jit(solution)/shard_map/ppermute | solution.py:770
  284.4 44.9 %copy-start.11 = (bf16[2,4,128,1024]{3,2,1,0:T(8,128)(2,1)S(1)}, bf16[2,4,128,1024]{3,2,1,0:T(8,128)(2,1)}, u32[]{:S(2)}) copy-start(bf16[2,4,128,1024]{3,2,1,0:T(8,128)(2,1)} %get-tuple-element.90) | copy-start | bytes 6291460
  327.8 96.6 %collective-permute-start.13 = (bf16[512,1024]{1,0:T(8,128)(2,1)S(1)}, bf16[512,1024]{1,0:T(8,128)(2,1)S(1)}, u32[]{:S(2)}, u32[]{:S(2)}) collective-permute-start(bf16[512,1024]{1,0:T(8,128)(2,1)S(1)} %fusion), channel_id=1, source_target_pairs={{0,2},{1,3},{2,0},{3,1},{4,6},{5,7},{6,4},{7,5},{8,10},{9,11},{10,... | collective-permute-start | bytes 3145736 | tf_op jit(solution)/shard_map/ppermute | solution.py:813
  329.3 45.0 %copy-start.10 = (bf16[2,4,128,1024]{3,2,1,0:T(8,128)(2,1)S(1)}, bf16[2,4,128,1024]{3,2,1,0:T(8,128)(2,1)}, u32[]{:S(2)}) copy-start(bf16[2,4,128,1024]{3,2,1,0:T(8,128)(2,1)} %get-tuple-element.92) | copy-start | bytes 6291460
  372.7 68.0 %collective-permute-start.36 = (bf16[2,2,128,1024]{3,2,1,0:T(8,128)(2,1)}, bf16[2,2,128,1024]{3,2,1,0:T(8,128)(2,1)}, u32[]{:S(2)}, u32[]{:S(2)}) collective-permute-start(bf16[2,2,128,1024]{3,2,1,0:T(8,128)(2,1)} %get-tuple-element.148), channel_id=1, source_target_pairs={{0,8},{4,12},{8,0},{12,4},{16,24},{20,28},{24,16},{28,20},{1,9},{5... | collective-permute-start | bytes 3145736 | tf_op jit(solution)/shard_map/ppermute | solution.py:770
  374.3 44.3 %copy-start.9 = (bf16[2,4,128,1024]{3,2,1,0:T(8,128)(2,1)S(1)}, bf16[2,4,128,1024]{3,2,1,0:T(8,128)(2,1)}, u32[]{:S(2)}) copy-start(bf16[2,4,128,1024]{3,2,1,0:T(8,128)(2,1)} %get-tuple-element.94) | copy-start | bytes 6291460
  417.0 27.2 %collective-permute-start.39 = (bf16[2,2,128,1024]{3,2,1,0:T(8,128)(2,1)}, bf16[2,2,128,1024]{3,2,1,0:T(8,128)(2,1)}, u32[]{:S(2)}, u32[]{:S(2)}) collective-permute-start(bf16[2,2,128,1024]{3,2,1,0:T(8,128)(2,1)} %get-tuple-element.150), channel_id=1, source_target_pairs={{0,8},{4,12},{8,0},{12,4},{16,24},{20,28},{24,16},{28,20},{1,9},{5... | collective-permute-start | bytes 3145736 | tf_op jit(solution)/shard_map/ppermute | solution.py:770
  418.6 4.5 copy-start
  422.6 54.5 %collective-permute-start.42 = (bf16[2,2,128,1024]{3,2,1,0:T(8,128)(2,1)}, bf16[2,2,128,1024]{3,2,1,0:T(8,128)(2,1)}, u32[]{:S(2)}, u32[]{:S(2)}) collective-permute-start(bf16[2,2,128,1024]{3,2,1,0:T(8,128)(2,1)} %get-tuple-element.152), channel_id=1, source_target_pairs={{0,8},{4,12},{8,0},{12,4},{16,24},{20,28},{24,16},{28,20},{1,9},{5... | collective-permute-start | bytes 3145736 | tf_op jit(solution)/shard_map/ppermute | solution.py:770
  424.4 88.8 %collective-permute-start.11 = (bf16[512,1024]{1,0:T(8,128)(2,1)}, bf16[512,1024]{1,0:T(8,128)(2,1)}, u32[]{:S(2)}, u32[]{:S(2)}) collective-permute-start(bf16[512,1024]{1,0:T(8,128)(2,1)} %fusion.1), channel_id=1, source_target_pairs={{0,2},{1,3},{2,0},{3,1},{4,6},{5,7},{6,4},{7,5},{8,10},{9,11},{10,... | collective-permute-start | bytes 3145736 | tf_op jit(solution)/shard_map/ppermute | solution.py:813
  426.0 14.7 %copy-start.6 = (bf16[2,2,128,1024]{3,2,1,0:T(8,128)(2,1)S(1)}, bf16[2,2,128,1024]{3,2,1,0:T(8,128)(2,1)}, u32[]{:S(2)}) copy-start(bf16[2,2,128,1024]{3,2,1,0:T(8,128)(2,1)} %get-tuple-element.147) | copy-start | bytes 3145732
  436.7 7.5 %copy-start.25 = (f32[16,1024]{1,0:T(8,128)S(1)}, f32[16,1024]{1,0:T(8,128)}, u32[]{:S(2)}) copy-start(f32[16,1024]{1,0:T(8,128)} %get-tuple-element.85) | copy-start | bytes 196612
  436.7 8.6 %copy-start.5 = (bf16[2,2,128,1024]{3,2,1,0:T(8,128)(2,1)S(1)}, bf16[2,2,128,1024]{3,2,1,0:T(8,128)(2,1)}, u32[]{:S(2)}) copy-start(bf16[2,2,128,1024]{3,2,1,0:T(8,128)(2,1)} %get-tuple-element.149) | copy-start | bytes 3145732
  436.7 68.8 %collective-permute-start.45 = (bf16[2,2,128,1024]{3,2,1,0:T(8,128)(2,1)}, bf16[2,2,128,1024]{3,2,1,0:T(8,128)(2,1)S(1)}, u32[]{:S(2)}, u32[]{:S(2)}) collective-permute-start(bf16[2,2,128,1024]{3,2,1,0:T(8,128)(2,1)} %get-tuple-element.154), channel_id=1, source_target_pairs={{0,8},{4,12},{8,0},{12,4},{16,24},{20,28},{24,16},{28,20},{1,9},{5... | collective-permute-start | bytes 3145736 | tf_op jit(solution)/shard_map/ppermute | solution.py:770
  440.8 2.0 collective-permute-start.27
  442.8 62.7 %copy-start.3 = (bf16[2,2,128,1024]{3,2,1,0:T(8,128)(2,1)S(1)}, bf16[2,2,128,1024]{3,2,1,0:T(8,128)(2,1)}, u32[]{:S(2)}) copy-start(bf16[2,2,128,1024]{3,2,1,0:T(8,128)(2,1)} %get-tuple-element.153) | copy-start | bytes 3145732
  442.8 99.2 %collective-permute-start.34 = (bf16[2,1,128,1024]{3,2,1,0:T(8,128)(2,1)}, bf16[2,1,128,1024]{3,2,1,0:T(8,128)(2,1)}, u32[]{:S(2)}, u32[]{:S(2)}) collective-permute-start(bf16[2,1,128,1024]{3,2,1,0:T(8,128)(2,1)} %add_convert_fusion.19), channel_id=1, source_target_pairs={{0,16},{4,20},{8,24},{12,28},{16,0},{20,4},{24,8},{28,12},{1,17},{... | collective-permute-start | bytes 1572872 | tf_op jit(solution)/shard_map/ppermute | solution.py:770
  444.2 5.9 collective-permute-start.28
  450.2 97.3 %collective-permute-start.16 = (bf16[512,1024]{1,0:T(8,128)(2,1)}, bf16[512,1024]{1,0:T(8,128)(2,1)}, u32[]{:S(2)}, u32[]{:S(2)}) collective-permute-start(bf16[512,1024]{1,0:T(8,128)(2,1)} %get-tuple-element.67.refs_0_), channel_id=1, source_target_pairs={{0,1},{1,0},{2,3},{3,2},{4,5},{5,4},{6,7},{7,6},{8,9},{9,8},{10,11... | collective-permute-start | bytes 3145736 | tf_op jit(solution)/shard_map/ppermute | solution.py:807
  477.1 4.3 collective-permute-start.29
  481.4 94.5 %collective-permute-start.37 = (bf16[2,1,128,1024]{3,2,1,0:T(8,128)(2,1)}, bf16[2,1,128,1024]{3,2,1,0:T(8,128)(2,1)}, u32[]{:S(2)}, u32[]{:S(2)}) collective-permute-start(bf16[2,1,128,1024]{3,2,1,0:T(8,128)(2,1)} %add_convert_fusion.17), channel_id=1, source_target_pairs={{0,16},{4,20},{8,24},{12,28},{16,0},{20,4},{24,8},{28,12},{1,17},{... | collective-permute-start | bytes 1572872 | tf_op jit(solution)/shard_map/ppermute | solution.py:770
  505.5 4.3 collective-permute-start.30
  509.8 69.7 %collective-permute-start.40 = (bf16[2,1,128,1024]{3,2,1,0:T(8,128)(2,1)}, bf16[2,1,128,1024]{3,2,1,0:T(8,128)(2,1)}, u32[]{:S(2)}, u32[]{:S(2)}) collective-permute-start(bf16[2,1,128,1024]{3,2,1,0:T(8,128)(2,1)} %add_convert_fusion.15), channel_id=1, source_target_pairs={{0,16},{4,20},{8,24},{12,28},{16,0},{20,4},{24,8},{28,12},{1,17},{... | collective-permute-start | bytes 1572872 | tf_op jit(solution)/shard_map/ppermute | solution.py:770
  513.3 27.0 %collective-permute-start.31 = (f32[16,1024]{1,0:T(8,128)S(1)}, f32[16,1024]{1,0:T(8,128)S(1)}, u32[]{:S(2)}, u32[]{:S(2)}) collective-permute-start(f32[16,1024]{1,0:T(8,128)S(1)} %add.226), channel_id=1, source_target_pairs={{0,16},{4,20},{8,24},{12,28},{16,0},{20,4},{24,8},{28,12},{1,17},{... | collective-permute-start | bytes 196616 | tf_op jit(solution)/shard_map/ppermute | solution.py:784
  540.2 85.6 %collective-permute-start.43 = (bf16[2,1,128,1024]{3,2,1,0:T(8,128)(2,1)S(1)}, bf16[2,1,128,1024]{3,2,1,0:T(8,128)(2,1)}, u32[]{:S(2)}, u32[]{:S(2)}) collective-permute-start(bf16[2,1,128,1024]{3,2,1,0:T(8,128)(2,1)S(1)} %add_convert_fusion.13), channel_id=1, source_target_pairs={{0,16},{4,20},{8,24},{12,28},{16,0},{20,4},{24,8},{28,12},{1,17},{... | collective-permute-start | bytes 1572872 | tf_op jit(solution)/shard_map/ppermute | solution.py:770
  542.0 86.2 %collective-permute-start.46 = (bf16[2,1,128,1024]{3,2,1,0:T(8,128)(2,1)}, bf16[2,1,128,1024]{3,2,1,0:T(8,128)(2,1)}, u32[]{:S(2)}, u32[]{:S(2)}) collective-permute-start(bf16[2,1,128,1024]{3,2,1,0:T(8,128)(2,1)} %add_convert_fusion.11), channel_id=1, source_target_pairs={{0,16},{4,20},{8,24},{12,28},{16,0},{20,4},{24,8},{28,12},{1,17},{... | collective-permute-start | bytes 1572872 | tf_op jit(solution)/shard_map/ppermute | solution.py:770
  574.3 45.6 %collective-permute-start.23 = (bf16[8,4,128,256]{3,2,1,0:T(8,128)(2,1)}, bf16[8,4,128,256]{3,2,1,0:T(8,128)(2,1)}, u32[]{:S(2)}, u32[]{:S(2)}) collective-permute-start(bf16[8,4,128,256]{3,2,1,0:T(8,128)(2,1)} %get-tuple-element.84), channel_id=1, source_target_pairs={{0,2},{1,3},{2,0},{3,1},{4,6},{5,7},{6,4},{7,5},{8,10},{9,11},{10,... | collective-permute-start | bytes 6291464 | tf_op jit(solution)/shard_map/ppermute | solution.py:813
  610.0 19.5 %collective-permute-start.17 = (bf16[512,1024]{1,0:T(8,128)(2,1)}, bf16[512,1024]{1,0:T(8,128)(2,1)}, u32[]{:S(2)}, u32[]{:S(2)}) collective-permute-start(bf16[512,1024]{1,0:T(8,128)(2,1)} %get-tuple-element.79), channel_id=1, source_target_pairs={{0,1},{1,0},{2,3},{3,2},{4,5},{5,4},{6,7},{7,6},{8,9},{9,8},{10,11... | collective-permute-start | bytes 3145736 | tf_op jit(solution)/shard_map/ppermute | solution.py:807
  624.1 4.1 copy-start.19
  624.1 22.2 %collective-permute-start.24 = (bf16[4,4,128,256]{3,2,1,0:T(8,128)(2,1)}, bf16[4,4,128,256]{3,2,1,0:T(8,128)(2,1)}, u32[]{:S(2)}, u32[]{:S(2)}) collective-permute-start(bf16[4,4,128,256]{3,2,1,0:T(8,128)(2,1)} %slice.341), channel_id=1, source_target_pairs={{0,4},{4,0},{8,12},{12,8},{16,20},{20,16},{24,28},{28,24},{1,5},{5... | collective-permute-start | bytes 3145736 | tf_op jit(solution)/shard_map/ppermute | solution.py:770
  635.2 1.4 collective-permute-start.18
  636.6 31.2 %copy-start.15 = (f32[1,1024,128]{1,2,0:T(8,128)S(1)}, f32[1,1024,128]{1,2,0:T(8,128)}, u32[]{:S(2)}) copy-start(f32[1,1024,128]{1,2,0:T(8,128)} %get-tuple-element.159) | copy-start | bytes 1572868
  636.6 31.2 %copy-start.17 = (f32[1,1024,128]{1,2,0:T(8,128)S(1)}, f32[1,1024,128]{1,2,0:T(8,128)}, u32[]{:S(2)}) copy-start(f32[1,1024,128]{1,2,0:T(8,128)} %get-tuple-element.161) | copy-start | bytes 1572868
  636.6 29.4 %collective-permute-start.19 = (f32[8,1024]{1,0:T(8,128)S(1)}, f32[8,1024]{1,0:T(8,128)S(1)}, u32[]{:S(2)}, u32[]{:S(2)}) collective-permute-start(f32[8,1024]{1,0:T(8,128)S(1)} %add.210), channel_id=1, source_target_pairs={{0,2},{1,3},{2,0},{3,1},{4,6},{5,7},{6,4},{7,5},{8,10},{9,11},{10,... | collective-permute-start | bytes 98312 | tf_op jit(solution)/shard_map/ppermute | solution.py:784
  648.6 32.9 %collective-permute-start.25 = (bf16[2,4,128,256]{3,2,1,0:T(8,128)(2,1)}, bf16[2,4,128,256]{3,2,1,0:T(8,128)(2,1)}, u32[]{:S(2)}, u32[]{:S(2)}) collective-permute-start(bf16[2,4,128,256]{3,2,1,0:T(8,128)(2,1)} %get-tuple-element.158), channel_id=1, source_target_pairs={{0,8},{4,12},{8,0},{12,4},{16,24},{20,28},{24,16},{28,20},{1,9},{5... | collective-permute-start | bytes 1572872 | tf_op jit(solution)/shard_map/ppermute | solution.py:770
  666.0 4.0 collective-permute-start.20
  670.0 8.6 %collective-permute-start.21 = (f32[8,1024]{1,0:T(8,128)S(1)}, f32[8,1024]{1,0:T(8,128)S(1)}, u32[]{:S(2)}, u32[]{:S(2)}) collective-permute-start(f32[8,1024]{1,0:T(8,128)S(1)} %add.212), channel_id=1, source_target_pairs={{0,8},{4,12},{8,0},{12,4},{16,24},{20,28},{24,16},{28,20},{1,9},{5... | collective-permute-start | bytes 98312 | tf_op jit(solution)/shard_map/ppermute | solution.py:784
  678.6 4.8 collective-permute-start.22
  682.6 13.8 %collective-permute-start.26 = (bf16[1,4,128,256]{3,2,1,0:T(8,128)(2,1)S(1)}, bf16[1,4,128,256]{3,2,1,0:T(8,128)(2,1)S(1)}, u32[]{:S(2)}, u32[]{:S(2)}) collective-permute-start(bf16[1,4,128,256]{3,2,1,0:T(8,128)(2,1)S(1)} %add_convert_fusion.23), channel_id=1, source_target_pairs={{0,16},{4,20},{8,24},{12,28},{16,0},{20,4},{24,8},{28,12},{1,17},{... | collective-permute-start | bytes 786440 | tf_op jit(solution)/shard_map/ppermute | solution.py:770
  (15 other events, 32.2 us)

commit v2 on v1

v2 whole, which is shorter than its diff:
```python
from functools import partial
import jax, jax.numpy as jnp
from jax import lax
from jax.experimental import pallas as pl
from jax.experimental.pallas import tpu as pltpu
from jax.sharding import PartitionSpec as P

BF = jnp.bfloat16
F32 = jnp.float32
TILE_DENSE = 512
TILE_EXPERT = 256
PIECE = 16
SMALL = pl.CostEstimate(flops=0, bytes_accessed=0, transcendentals=0)
VMEM = 60 * 1024 * 1024
ANY = pl.BlockSpec(memory_space=pl.ANY)
SMEM = pl.BlockSpec(memory_space=pltpu.SMEM)


def dot(a, b, ca, cb):
    return lax.dot_general(a, b, (((ca,), (cb,)), ((), ())), preferred_element_type=F32)


def slot_of(value, order):
    out = jnp.int32(0)
    for k, bit in enumerate(order):
        out = out | (((value >> bit) & 1) << (len(order) - 1 - k))
    return out


def skip(kernel, scalars, deps):
    return lambda *refs: kernel(*refs[:scalars], *refs[scalars + deps:])


def lane_softmax(logits, first, last):
    lane = lax.broadcasted_iota(jnp.int32, logits.shape, 1)
    inside = (lane >= first) & (lane < last)
    masked = jnp.where(inside, logits, -1e30)
    top = jnp.max(masked, axis=1, keepdims=True)
    e = jnp.where(inside, jnp.exp(masked - top), 0.0)
    return e / jnp.sum(e, axis=1, keepdims=True)


def pick_lane(v, index):
    lane = lax.broadcasted_iota(jnp.int32, v.shape, 1)
    return jnp.sum(jnp.where(lane == index, v, 0.0), axis=1, keepdims=True)


def gelu_parts(pre):
    phi = 0.5 * (1.0 + lax.erf(pre * 0.7071067811865476))
    pdf = jnp.exp(pre * pre * -0.5) * 0.3989422804014327
    return pre * phi, phi + pre * pdf


def ffn_tile(lanes, rm, xt, dyt, coef_of, up_w, dn_w, UA, DA, ready):
    logits = dot(xt, rm[...], 1, 0)
    mixing = lane_softmax(logits, lanes, lanes + 2)
    coef = coef_of(logits, mixing)
    pre = dot(xt, up_w[...], 1, 0)
    g = dot(dyt, dn_w[...], 1, 1)
    hid, dg = gelu_parts(pre)
    hid = hid.astype(BF)
    dots = jnp.sum(hid.astype(F32) * g, axis=1, keepdims=True)
    pg = (g * dg * coef).astype(BF)
    cot = (dyt.astype(F32) * coef).astype(BF)
    out = dot(hid, dn_w[...], 1, 0) * coef
    rg = dot(pg, up_w[...], 1, 1)
    ready()
    UA[...] += dot(xt, pg, 0, 0)
    DA[...] += dot(cot, hid, 0, 0)
    return dots, out, rg


def stage_grads(ST, UA, DA, me, up_order, dn_order):
    bits = len(up_order)
    blk = UA.shape[0] >> bits

    def body(c, _):
        r = pl.ds(pl.multiple_of(c * blk, blk), blk)
        ST[slot_of(c ^ me, up_order), 0] = UA[r, :].astype(BF)
        ST[slot_of(c ^ me, dn_order), 1] = DA[r, :].astype(BF)
        return 0
    lax.fori_loop(0, 1 << bits, body, 0)


def column(v, n):
    return jnp.broadcast_to(v, (v.shape[0], n))


def dense_kernel(cfg, me_ref, *refs):
    chunks, rows, tm, lanes, orders, first, deps = cfg
    it = iter(refs[deps:])
    take = lambda k: [next(it) for _ in range(k)]
    x_hbm, dy_hbm = take(chunks), take(chunks)
    rm, up_hbm, dn_hbm = take(3)
    base_o, base_r, sums_in = ([], [], []) if first else (take(chunks), take(chunks), take(2))
    out_refs, rg_refs = take(chunks), take(chunks)
    dots_ref, = take(1)
    ends = take(2) if first else take(4)
    X, DY, UP, DN, UA, DA, OB, RB, xsem, wsem, gsem, osem = take(12)
    ST, BO, BR, bsem = (None,) * 4 if first else take(4)
    per = rows // tm
    weights = [pltpu.make_async_copy(up_hbm, UP, wsem.at[0]), pltpu.make_async_copy(dn_hbm, DN, wsem.at[1])]
    loads, bases = [], []
    for q in range(chunks):
        sl = pl.ds(q * rows, rows)
        loads.append([pltpu.make_async_copy(x_hbm[q], X.at[sl], xsem.at[q]), pltpu.make_async_copy(dy_hbm[q], DY.at[sl], xsem.at[chunks + q])])
        if not first:
            bases.append([pltpu.make_async_copy(base_o[q], BO.at[sl], bsem.at[q]), pltpu.make_async_copy(base_r[q], BR.at[sl], bsem.at[chunks + q])])
    sums = [] if first else [pltpu.make_async_copy(sums_in[0], UA, gsem.at[0]), pltpu.make_async_copy(sums_in[1], DA, gsem.at[1])]
    for c in loads[0] + weights + sums + [c for q in loads[1:] for c in q] + [c for q in bases for c in q]:
        c.start()
    if first:
        UA[...] = jnp.zeros_like(UA)
        DA[...] = jnp.zeros_like(DA)
    for c in weights:
        c.wait()

    def outs(q, part, slot):
        sl = pl.ds(part * tm, tm)
        return [pltpu.make_async_copy(OB.at[slot], out_refs[q].at[sl], osem.at[0, slot]),
                pltpu.make_async_copy(RB.at[slot], rg_refs[q].at[sl], osem.at[1, slot])]

    def one(i, _):
        slot = i % 2
        sl = pl.ds(pl.multiple_of(i * tm, tm), tm)
        for q in range(chunks):
            @pl.when(i == q * per)
            def _(q=q):
                for c in loads[q]:
                    c.wait()

        def ready():
            if not first:
                @pl.when(i == 0)
                def _():
                    for c in sums:
                        c.wait()
        dots, out, rg = ffn_tile(lanes, rm, X[sl, :], DY[sl, :], lambda l, m: pick_lane(m, lanes), UP, DN, UA, DA, ready)
        dots_ref[:, sl] = column(dots, 128).T[0:8, :]
        if not first:
            for q in range(chunks):
                @pl.when(i == q * per)
                def _(q=q):
                    for c in bases[q]:
                        c.wait()
            out = out + BO[sl, :].astype(F32)
            rg = rg + BR[sl, :].astype(F32)

        @pl.when(i >= 2)
        def _():
            for c in outs(0, 0, slot):
                c.wait()
        OB[slot] = out.astype(BF)
        RB[slot] = rg.astype(BF)
        for q in range(chunks):
            for part in range(per):
                @pl.when(i == q * per + part)
                def _(q=q, part=part):
                    for c in outs(q, part, slot):
                        c.start()
        return 0
    lax.fori_loop(0, chunks * per, one, 0)
    row = lax.broadcasted_iota(jnp.int32, dots_ref.shape, 0)
    dots_ref[...] = jnp.where(row == 0, dots_ref[...], 0.0)
    if first:
        last = [pltpu.make_async_copy(UA, ends[0], gsem.at[0]), pltpu.make_async_copy(DA, ends[1], gsem.at[1])]
    else:
        stage_grads(ST, UA, DA, me_ref[0], *orders)
        half = ST.shape[0] // 2
        last = [pltpu.make_async_copy(ST.at[pl.ds(h * half, half), pl.ds(m, 1)], ends[2 * m + h], bsem.at[2 * m + h]) for m in range(2) for h in range(2)]
    for c in last:
        c.start()
    for slot in range(min(2, chunks * per)):
        for c in outs(0, 0, slot):
            c.wait()
    for c in last:
        c.wait()


def ffn_dense(me, xs, dys, rm, up, down, lanes, orders, base=None, sums=None, deps=()):
    chunks = len(xs)
    rows, d = xs[0].shape
    f = up.shape[1]
    n = chunks * rows
    tm = min(TILE_DENSE, rows)
    first = base is None
    bits = len(orders[0])
    half = 1 << (bits - 1)
    vm = pl.BlockSpec(memory_space=pltpu.VMEM)
    part = jax.ShapeDtypeStruct((rows, d), BF)
    total = jax.ShapeDtypeStruct((d, f), F32)
    grad = jax.ShapeDtypeStruct((half, 1, d >> bits, f), BF)
    ends = [total] * 2 if first else [grad] * 4
    more = [] if first else list(base[0]) + list(base[1]) + list(sums)
    scratch = [pltpu.VMEM((n, d), BF), pltpu.VMEM((n, d), BF), pltpu.VMEM((d, f), BF), pltpu.VMEM((f, d), BF), pltpu.VMEM((d, f), F32), pltpu.VMEM((d, f), F32),
               pltpu.VMEM((2, tm, d), BF), pltpu.VMEM((2, tm, d), BF),
               pltpu.SemaphoreType.DMA((2 * chunks,)), pltpu.SemaphoreType.DMA((2,)), pltpu.SemaphoreType.DMA((2,)), pltpu.SemaphoreType.DMA((2, 2))]
    if not first:
        scratch += [pltpu.VMEM((2 * half, 2, d >> bits, f), BF), pltpu.VMEM((n, d), BF), pltpu.VMEM((n, d), BF), pltpu.SemaphoreType.DMA((max(4, 2 * chunks),))]
    res = pl.pallas_call(
        partial(dense_kernel, (chunks, rows, tm, lanes, orders, first, len(deps))),
        name="ffn_dense",
        out_shape=[part] * (2 * chunks) + [jax.ShapeDtypeStruct((8, n), F32)] + ends,
        in_specs=[SMEM] + [ANY] * (len(deps) + 2 * chunks) + [vm] + [ANY] * (2 + len(more)),
        out_specs=[ANY] * (2 * chunks) + [vm] + [ANY] * len(ends),
        scratch_shapes=scratch,
        cost_estimate=SMALL,
        compiler_params=pltpu.CompilerParams(vmem_limit_bytes=VMEM),
    )(me, *deps, *xs, *dys, rm, up, down, *more)
    return res[:chunks], res[chunks:2 * chunks], res[2 * chunks], res[2 * chunks + 1:]


def expert_kernel(cfg, me_ref, blk_ref, bnd_ref, *refs):
    first, count, chunks, rows, d, tm, lanes, order, has, deps = cfg
    n = chunks * rows
    it = iter(refs[deps:])
    take = lambda k: [next(it) for _ in range(k)]
    x_hbm, dy_hbm = take(chunks), take(chunks)
    rm, up_hbm, dn_hbm = take(3)
    based = [q for q in range(chunks) if has[q]]
    base_o, base_r = take(len(based)), take(len(based))
    out_refs, rg_refs = take(chunks), take(chunks)
    dots_ref, = take(1)
    keep_refs, send_refs = take(count), take(count)
    X, DY, UP, DN, UA, DA, ST, XG, DG, VAL, OA, RA, DOT, TR, TL, TH, xsem, wsem, gsem, osem = it
    half = ST.shape[0] // 2
    pieces = tm // PIECE
    rows_of = [pl.ds(q * rows, rows) for q in range(chunks)]
    copies = []
    for q in range(chunks):
        copies.append(pltpu.make_async_copy(x_hbm[q], X.at[rows_of[q]], xsem.at[q]))
        copies.append(pltpu.make_async_copy(dy_hbm[q], DY.at[rows_of[q]], xsem.at[chunks + q]))
    earlier = []
    for k, q in enumerate(based):
        earlier.append(pltpu.make_async_copy(base_o[k], X.at[rows_of[q]], xsem.at[q]))
        earlier.append(pltpu.make_async_copy(base_r[k], DY.at[rows_of[q]], xsem.at[chunks + q]))

    def weights(e, slot):
        return [pltpu.make_async_copy(up_hbm.at[first + e], UP.at[slot], wsem.at[slot, 0]),
                pltpu.make_async_copy(dn_hbm.at[first + e], DN.at[slot], wsem.at[slot, 1])]

    def flush(g):
        return [pltpu.make_async_copy(ST.at[pl.ds(0, half)], keep_refs[g], gsem.at[0]),
                pltpu.make_async_copy(ST.at[pl.ds(half, half)], send_refs[g], gsem.at[1])]

    for c in copies + weights(0, 0):
        c.start()
    OA[...] = jnp.zeros_like(OA)
    RA[...] = jnp.zeros_like(RA)
    DOT[...] = jnp.zeros_like(DOT)
    iota16 = lax.broadcasted_iota(jnp.int32, (PIECE, 128), 0)

    def one_expert(e, _):
        slot = e % 2
        total = jnp.int32(0)
        for q in range(chunks):
            lo, hi = bnd_ref[blk_ref[q], first + e], bnd_ref[blk_ref[q], first + e + 1]
            p0 = lo // PIECE
            p1 = jnp.where(hi > lo, (hi + PIECE - 1) // PIECE, p0)

            def add(p, _, lo=lo, hi=hi, p0=p0, total=total, q=q):
                k = total + p - p0
                TR[k] = q * rows + p * PIECE
                TL[k] = lo - p * PIECE
                TH[k] = hi - p * PIECE
                return 0
            lax.fori_loop(p0, p1, add, 0)
            total = total + p1 - p0
        tiles = (total + pieces - 1) // pieces

        def pad(k, _):
            TR[k] = 0
            TL[k] = 0
            TH[k] = 0
            return 0
        lax.fori_loop(total, tiles * pieces, pad, 0)
        UA[...] = jnp.zeros_like(UA)
        DA[...] = jnp.zeros_like(DA)

        @pl.when(e == 0)
        def _():
            for c in copies:
                c.wait()
        for c in weights(e, slot):
            c.wait()

        @pl.when(e + 1 < count)
        def _():
            for c in weights(e + 1, 1 - slot):
                c.start()

        def one_tile(i, _):
            base = i * pieces
            for p in range(pieces):
                r = pl.ds(pl.multiple_of(TR[base + p], PIECE), PIECE)
                XG[pl.ds(p * PIECE, PIECE), :] = X[r, :]
                DG[pl.ds(p * PIECE, PIECE), :] = DY[r, :]
                ok = (iota16 >= TL[base + p]) & (iota16 < TH[base + p])
                VAL[pl.ds(p * PIECE, PIECE), :] = jnp.where(ok, 1.0, 0.0)
            valid = VAL[:, 0:1]

            def coef_of(logits, mixing):
                return pick_lane(mixing, lanes + 1) * pick_lane(lane_softmax(logits, 0, lanes), first + e) * valid
            dots, out, rg = ffn_tile(lanes, rm, XG[...], DG[...], coef_of, UP.at[slot], DN.at[slot], UA, DA, lambda: None)
            dots = column(dots * valid, 128)
            for p in range(pieces):
                r = pl.ds(pl.multiple_of(TR[base + p], PIECE), PIECE)
                s = slice(p * PIECE, (p + 1) * PIECE)
                OA[r, :] += out[s]
                RA[r, :] += rg[s]
                DOT[r, :] += dots[s]
            return 0
        lax.fori_loop(0, tiles, one_tile, 0)

        @pl.when(e == count - 1)
        def _():
            for c in earlier:
                c.start()

        @pl.when(e > 0)
        def _():
            for c in flush(0):
                c.wait()
        stage_grads(ST, UA, DA, me_ref[0], order, order)
        for g in range(count):
            @pl.when(e == g)
            def _(g=g):
                for c in flush(g):
                    c.start()
        return 0
    lax.fori_loop(0, count, one_expert, 0)
    for c in earlier:
        c.wait()
    last = []
    for q in range(chunks):
        r = rows_of[q]
        o, g = OA[r, :], RA[r, :]
        if has[q]:
            o, g = o + X[r, :].astype(F32), g + DY[r, :].astype(F32)
        X[r, :] = o.astype(BF)
        DY[r, :] = g.astype(BF)
        last += [pltpu.make_async_copy(X.at[r], out_refs[q], osem.at[0, q]), pltpu.make_async_copy(DY.at[r], rg_refs[q], osem.at[1, q])]
        for c in last[-2:]:
            c.start()
    step = min(256, rows)
    row = lax.broadcasted_iota(jnp.int32, (8, step), 0)
    for i in range(n // step):
        sl = pl.ds(i * step, step)
        dots_ref[:, sl] = jnp.where(row == 1, DOT[sl, :].T[0:8, :], 0.0)
    for c in last + flush(0):
        c.wait()


def ffn_experts(me, blocks, bounds, xs, dys, rm, up, down, first, count, base, order, deps=()):
    chunks = len(xs)
    rows, d = xs[0].shape
    lanes, _, f = up.shape
    n = chunks * rows
    tm = TILE_EXPERT
    bits = len(order)
    half = 1 << (bits - 1)
    grad = jax.ShapeDtypeStruct((half, 2, d >> bits, f), BF)
    part = jax.ShapeDtypeStruct((rows, d), BF)
    table = n // PIECE + chunks * lanes + 2 * tm // PIECE
    vm = pl.BlockSpec(memory_space=pltpu.VMEM)
    has = tuple(b is not None for b in base[0])
    more = [b for k in range(2) for b in base[k] if b is not None]
    res = pl.pallas_call(
        partial(expert_kernel, (first, count, chunks, rows, d, tm, lanes, order, has, len(deps))),
        name="ffn_experts",
        out_shape=[part] * (2 * chunks) + [jax.ShapeDtypeStruct((8, n), F32)] + [grad] * (2 * count),
        in_specs=[SMEM] * 3 + [ANY] * (len(deps) + 2 * chunks) + [vm] + [ANY] * (2 + len(more)),
        out_specs=[ANY] * (2 * chunks) + [vm] + [ANY] * (2 * count),
        scratch_shapes=[
            pltpu.VMEM((n, d), BF), pltpu.VMEM((n, d), BF), pltpu.VMEM((2, d, f), BF), pltpu.VMEM((2, f, d), BF),
            pltpu.VMEM((d, f), F32), pltpu.VMEM((d, f), F32), pltpu.VMEM((2 * half, 2, d >> bits, f), BF),
            pltpu.VMEM((tm, d), BF), pltpu.VMEM((tm, d), BF), pltpu.VMEM((tm, 128), F32),
            pltpu.VMEM((n, d), F32), pltpu.VMEM((n, d), F32), pltpu.VMEM((n, 128), F32),
            pltpu.SMEM((table,), jnp.int32), pltpu.SMEM((table,), jnp.int32), pltpu.SMEM((table,), jnp.int32),
            pltpu.SemaphoreType.DMA((2 * chunks,)), pltpu.SemaphoreType.DMA((2, 2)), pltpu.SemaphoreType.DMA((2,)), pltpu.SemaphoreType.DMA((2, chunks)),
        ],
        cost_estimate=SMALL,
        compiler_params=pltpu.CompilerParams(vmem_limit_bytes=VMEM),
    )(me, blocks, bounds, *deps, *xs, *dys, rm, up, down, *more)
    at = 2 * chunks + 1
    return res[:chunks], res[chunks:2 * chunks], res[2 * chunks], res[at:at + count], res[at + count:]


def split_add_kernel(deps, *refs):
    ka, kb, ca, cb, keep, send = refs[deps:]
    keep[...] = (ka[...].astype(F32) + ca[...].astype(F32)).astype(BF)
    send[...] = (kb[...].astype(F32) + cb[...].astype(F32)).astype(BF)


def split_add(kept, came, deps=()):
    h, m, blk, f = kept.shape
    near = pl.BlockSpec((1, 1, blk, f), lambda i, k: (i, k, 0, 0))
    far = pl.BlockSpec((1, 1, blk, f), lambda i, k: (i + h // 2, k, 0, 0))
    out = jax.ShapeDtypeStruct((h // 2, m, blk, f), BF)
    return pl.pallas_call(
        partial(split_add_kernel, len(deps)),
        name="split_add",
        grid=(h // 2, m),
        in_specs=[ANY] * len(deps) + [near, far, near, far],
        out_specs=[near, near],
        out_shape=[out, out],
        cost_estimate=SMALL,
        compiler_params=pltpu.CompilerParams(vmem_limit_bytes=VMEM),
    )(*deps, kept, kept, came, came)


def last_add_kernel(deps, turns, *refs):
    kept, came = refs[deps:deps + 2]
    outs = refs[-len(turns):]
    for k, turned in enumerate(turns):
        total = kept[0, k].astype(F32) + came[0, k].astype(F32)
        outs[k][...] = (total.T if turned else total).reshape(outs[k].shape)


def last_add(kept, came, turns, place=None, stacks=None, deps=()):
    _, m, blk, f = kept.shape
    shapes = [(f, blk) if turned else (blk, f) for turned in turns]
    aliases = {}
    if place is None:
        out_shape = [jax.ShapeDtypeStruct(s, F32) for s in shapes]
        out_specs = [pl.BlockSpec(s, lambda i: (0, 0)) for s in shapes]
    else:
        count, at = place
        out_shape = [jax.ShapeDtypeStruct((count,) + s, F32) for s in shapes]
        out_specs = [pl.BlockSpec((1,) + s, lambda i: (at, 0, 0)) for s in shapes]
        if stacks is not None:
            aliases = {k: k for k in range(m)}
            deps = tuple(stacks) + tuple(deps)
    full = pl.BlockSpec((1, m, blk, f), lambda i: (0, 0, 0, 0))
    return pl.pallas_call(
        partial(last_add_kernel, len(deps), turns),
        name="last_add",
        grid=(1,),
        in_specs=[ANY] * len(deps) + [full, full],
        out_specs=out_specs,
        out_shape=out_shape,
        input_output_aliases=aliases,
        cost_estimate=SMALL,
        compiler_params=pltpu.CompilerParams(vmem_limit_bytes=VMEM),
    )(*deps, kept, came)


def hold(v, deps):
    return pl.pallas_call(
        lambda *refs: None,
        name="hold",
        in_specs=[ANY] * (1 + len(deps)),
        out_specs=ANY,
        out_shape=jax.ShapeDtypeStruct(v.shape, v.dtype),
        input_output_aliases={0: 0},
        cost_estimate=SMALL,
    )(v, *deps)


HD = 64
LANES = 128


def head_part(v, h):
    lane = lax.broadcasted_iota(jnp.int32, v.shape, 1)
    return jnp.where((lane // HD) == h, v, jnp.zeros((), v.dtype))


def masked_scores(st, key_first, query_first, prefix):
    key_pos = key_first + lax.broadcasted_iota(jnp.int32, st.shape, 0)
    query_pos = query_first + lax.broadcasted_iota(jnp.int32, st.shape, 1)
    seen = key_pos <= query_pos
    if prefix is not None:
        seen = seen | (key_pos < prefix)
    return jnp.where(seen, st, -1e30)


def score_block(k2, qm, half, length, prefix):
    mid = length // 2
    if half == 0:
        return masked_scores(dot(k2[0:mid], qm, 1, 1), 0, 0, prefix)
    low = dot(k2[0:mid], qm, 1, 1)
    high = masked_scores(dot(k2[mid:length], qm, 1, 1), mid, mid, None)
    return jnp.concatenate([low, high], 0)


def attn_forward_kernel(length, pieces, aliased, prefix_ref, at_ref, *refs):
    n1_ref = refs[0]
    w_refs = [(r, i) for r, n in zip(refs[1:], pieces) for i in range(n)]
    q_ref, k_ref, v_ref, ctx_ref, lse_ref = refs[1 + len(pieces) + aliased:]
    mid = length // 2
    prefix = prefix_ref[0]
    n1 = n1_ref[...]
    for out, (w, i) in zip((q_ref, k_ref, v_ref), w_refs):
        out[...] = dot(n1, w[i], 1, 0).astype(BF)
    vt = v_ref[...].T
    k2 = k_ref[...]
    for half in range(2):
        rows = pl.ds(half * mid, mid)
        q2 = q_ref[rows, :] * jnp.asarray(HD ** -0.5, BF)
        keys = mid * (half + 1)
        parts = []
        for h in range(2):
            st = score_block(k2, head_part(q2, h), half, length, prefix)
            top = jnp.max(st, axis=0, keepdims=True)
            p = jnp.exp(st - top)
            total = jnp.sum(p, axis=0, keepdims=True)
            c = dot(vt[h * HD:(h + 1) * HD, 0:keys], p.astype(BF), 1, 0)
            parts.append(c / total)
            lse_ref[0, h:h + 1, rows] = top + jnp.log(total)
        ctx_ref[rows, :] = jnp.concatenate(parts, 0).T.astype(BF)


def attn_forward(prefix, at, n1, ws, heads, earlier=(), deps=()):
    length, d = n1.shape
    pairs = ws[0].shape[2] // LANES
    col = pl.BlockSpec((length, LANES), lambda p, _, at_ref: (0, at_ref[p]))
    out = jax.ShapeDtypeStruct((length, heads), BF)
    done = len(earlier)
    skipped = len(deps)
    return pl.pallas_call(
        skip(partial(attn_forward_kernel, length, tuple(w.shape[0] for w in ws), done), 2, skipped),
        name="attn_forward",
        grid_spec=pltpu.PrefetchScalarGridSpec(
            num_scalar_prefetch=2, grid=(pairs,),
            in_specs=[ANY] * skipped + [pl.BlockSpec((length, d), lambda p, *_: (0, 0))]
            + [pl.BlockSpec((w.shape[0], d, LANES), lambda p, *_: (0, 0, p)) for w in ws] + [ANY] * done,
            out_specs=[col] * 4 + [pl.BlockSpec((1, 8, length), lambda p, _, at_ref: (at_ref[p], 0, 0))]),
        out_shape=[out] * 4 + [jax.ShapeDtypeStruct((heads // LANES, 8, length), F32)],
        input_output_aliases={3 + skipped + len(ws) + k: k for k in range(done)},
        cost_estimate=SMALL,
        compiler_params=pltpu.CompilerParams(vmem_limit_bytes=VMEM),
    )(prefix, at, *deps, n1, *ws, *earlier)


def attn_backward_kernel(length, bits, members, based, prefix_ref, me_ref, j_ref, *refs):
    it = iter(refs)
    take = lambda k: [next(it) for _ in range(k)]
    mcs = take(members)
    n1_ref, wo_ref, w_ref, q_ref, k_ref, v_ref, ctx_ref, lse_ref = take(8)
    bases = take(members) if based else []
    ng_refs = take(members)
    grad_ref, NG, MC, DC, DK, DV, DQ, sem = it
    rows_each = length // members
    where = [pl.ds(pl.multiple_of(lax.rem(j_ref[0] + k, members) * rows_each, rows_each), rows_each) for k in range(members)]
    mid = length // 2
    prefix = prefix_ref[0]
    me = me_ref[0]
    pair = pl.program_id(0)
    copies = [pltpu.make_async_copy(mcs[k], MC.at[where[k]], sem.at[k]) for k in range(members)]

    @pl.when(pair == 0)
    def _():
        for c in copies:
            c.start()
        for c in copies:
            c.wait()
    mc = MC[...]
    DC[...] = dot(mc, wo_ref[...], 1, 1).astype(BF)
    k2, v2 = k_ref[...], v_ref[...]
    kt = k2.T
    scale = jnp.asarray(HD ** -0.5, BF)
    for half in range(2):
        rows = pl.ds(half * mid, mid)
        q2 = q_ref[rows, :] * scale
        dc2 = DC[rows, :]
        keys = mid * (half + 1)
        dv = jnp.zeros((keys, LANES), F32)
        dk = jnp.zeros((keys, LANES), F32)
        dq = []
        for h in range(2):
            qm, dcm = head_part(q2, h), head_part(dc2, h)
            st = score_block(k2, qm, half, length, prefix)
            p = jnp.exp(st - lse_ref[0, h:h + 1, rows])
            dv = dv + dot(p.astype(BF), dcm, 1, 0)
            dp = dot(v2[0:keys], dcm, 1, 1)
            ds = (p * (dp - jnp.sum(p * dp, axis=0, keepdims=True))).astype(BF)
            dk = dk + dot(ds, qm, 1, 0)
            dq.append(dot(kt[h * HD:(h + 1) * HD, 0:keys], ds, 1, 0))
        DQ[rows, :] = (jnp.concatenate(dq, 0) * HD ** -0.5).T.astype(BF)
        if half == 0:
            DK[0:mid, :] = dk
            DV[0:mid, :] = dv
        else:
            DK[0:mid, :] += dk[0:mid]
            DV[0:mid, :] += dv[0:mid]
            DK[mid:length, :] = dk[mid:length]
            DV[mid:length, :] = dv[mid:length]
    dq, dk, dv = DQ[...], DK[...].astype(BF), DV[...].astype(BF)
    ng = dot(dq, w_ref[0], 1, 1) + dot(dk, w_ref[1], 1, 1) + dot(dv, w_ref[2], 1, 1)

    @pl.when(pair == 0)
    def _():
        NG[...] = ng

    @pl.when(pair > 0)
    def _():
        NG[...] += ng
    n1 = n1_ref[...]
    grads = [dot(n1, x, 0, 0) for x in (dq, dk, dv)] + [dot(mc, ctx_ref[...], 0, 0)]
    blk = n1.shape[1] >> bits
    for c in range(1 << bits):
        slot = slot_of(jnp.int32(c) ^ me, range(bits))
        for i in range(4):
            grad_ref[slot, i] = grads[i][c * blk:(c + 1) * blk].astype(BF)

    @pl.when(pair == pl.num_programs(0) - 1)
    def _():
        for k in range(members):
            done = NG[where[k], :]
            if based:
                done = done + bases[k][...].astype(F32)
            ng_refs[k][...] = done.astype(BF)


def attn_backward(prefix, me, j, mcs, n1, wo, w, saved, base, bits, deps=()):
    q, k, v, ctx, lse = saved
    length, d = n1.shape
    heads = w.shape[2]
    pairs = heads // LANES
    blk = d >> bits
    members = len(mcs)
    col = pl.BlockSpec((length, LANES), lambda p, *_: (0, p))
    full = pl.BlockSpec((length, d), lambda p, *_: (0, 0))
    part = pl.BlockSpec((length // members, d), lambda p, *_: (0, 0))
    extra = [] if base is None else list(base)
    res = pl.pallas_call(
        skip(partial(attn_backward_kernel, length, bits, members, base is not None), 3, len(deps)),
        name="attn_backward",
        grid_spec=pltpu.PrefetchScalarGridSpec(
            num_scalar_prefetch=3, grid=(pairs,),
            in_specs=[ANY] * (len(deps) + members) + [full, pl.BlockSpec((LANES, d), lambda p, *_: (p, 0)), pl.BlockSpec((3, d, LANES), lambda p, *_: (0, 0, p)),
                      col, col, col, col, pl.BlockSpec((1, 8, length), lambda p, *_: (p, 0, 0))] + [part] * len(extra),
            out_specs=[part] * members + [pl.BlockSpec((1 << bits, 4, blk, LANES), lambda p, *_: (0, 0, 0, p))],
            scratch_shapes=[pltpu.VMEM((length, d), F32), pltpu.VMEM((length, d), BF), pltpu.VMEM((length, LANES), BF),
                            pltpu.VMEM((length, LANES), F32), pltpu.VMEM((length, LANES), F32), pltpu.VMEM((length, LANES), BF),
                            pltpu.SemaphoreType.DMA((members,))]),
        out_shape=[jax.ShapeDtypeStruct((length // members, d), BF)] * members + [jax.ShapeDtypeStruct((1 << bits, 4, blk, heads), BF)],
        cost_estimate=SMALL,
        compiler_params=pltpu.CompilerParams(vmem_limit_bytes=VMEM),
    )(prefix, me, j, *deps, *mcs, n1, wo, w, q, k, v, ctx, lse, *extra)
    return res[:members], res[members]


EPS = 1e-5


def normalise(v):
    centered = v - jnp.mean(v, axis=1, keepdims=True)
    r = lax.rsqrt(jnp.mean(centered * centered, axis=1, keepdims=True) + EPS)
    return centered * r, r


def norm_backward(xhat, r, grad, gain):
    scaled = grad * gain
    return r * (scaled - jnp.mean(scaled, axis=1, keepdims=True) - xhat * jnp.mean(scaled * xhat, axis=1, keepdims=True))


def order_rows(pos, rows_to_slots):
    n = pos.shape[1] if rows_to_slots else pos.shape[0]
    slot = lax.broadcasted_iota(jnp.int32, (n, n), 0 if rows_to_slots else 1)
    return jnp.where(slot == pos, 1.0, 0.0).astype(BF)


def first_norm_kernel(members, j_ref, *refs):
    xs, (gain, shift, dy, pos, out, sorted_dy) = refs[:members], refs[members:]
    for k in range(members):
        @pl.when(pl.program_id(0) == k)
        def _(k=k):
            xhat, _ = normalise(xs[k][...].astype(F32))
            out[...] = (xhat * gain[...] + shift[...]).astype(BF)
            if k == 0:
                sorted_dy[...] = dot(order_rows(pos[...], True), dy[...], 1, 0).astype(BF)


def first_norm(j, xs, gain, shift, dy, pos):
    members = len(xs)
    rows, d = xs[0].shape
    fixed = lambda shape: pl.BlockSpec(shape, lambda p, *_: (0, 0))
    return pl.pallas_call(
        partial(first_norm_kernel, members),
        name="first_norm",
        grid_spec=pltpu.PrefetchScalarGridSpec(
            num_scalar_prefetch=1, grid=(members,),
            in_specs=[fixed((rows, d))] * members + [fixed((1, d))] * 2 + [fixed((rows, d)), fixed((1, rows))],
            out_specs=[pl.BlockSpec((rows, d), lambda p, j_ref: (lax.rem(j_ref[0] + p, members), 0)), fixed((rows, d))]),
        out_shape=[jax.ShapeDtypeStruct((members * rows, d), BF), jax.ShapeDtypeStruct((rows, d), BF)],
        cost_estimate=SMALL,
        compiler_params=pltpu.CompilerParams(vmem_limit_bytes=VMEM),
    )(j, *xs, gain, shift, dy, pos)


def project_kernel(parts, *refs):
    total = dot(refs[0][...], refs[parts][...], 1, 0)
    for i in range(1, parts):
        total = total + dot(refs[i][...], refs[parts + i][...], 1, 0)
    refs[-1][0] = total.astype(BF)


def project(contexts, weights, members):
    parts = len(contexts)
    length, heads = contexts[0].shape
    d = weights[0].shape[1]
    rows = length // members
    return pl.pallas_call(
        partial(project_kernel, parts),
        name="project",
        grid=(members,),
        in_specs=[pl.BlockSpec((rows, heads), lambda p: (p, 0))] * parts + [pl.BlockSpec((heads, d), lambda p: (0, 0))] * parts,
        out_specs=pl.BlockSpec((1, rows, d), lambda p: (p, 0, 0)),
        out_shape=jax.ShapeDtypeStruct((members, rows, d), BF),
        cost_estimate=SMALL,
        compiler_params=pltpu.CompilerParams(vmem_limit_bytes=VMEM),
    )(*contexts, *weights)


def second_norm_kernel(came, x, gain, shift, pos, middle, n2):
    mid = x[...].astype(F32)
    for k in range(came.shape[0]):
        mid = mid + came[k].astype(F32)
    middle[...] = mid
    xhat, _ = normalise(mid)
    normed = (xhat * gain[...] + shift[...]).astype(BF)
    n2[...] = dot(order_rows(pos[...], True), normed, 1, 0).astype(BF)


def second_norm(came, x, gain, shift, pos):
    rows, d = x.shape
    fixed = lambda shape: pl.BlockSpec(shape, lambda p: (0,) * len(shape))
    return pl.pallas_call(
        second_norm_kernel,
        name="second_norm",
        grid=(1,),
        in_specs=[fixed(came.shape), fixed((rows, d)), fixed((1, d)), fixed((1, d)), fixed((1, rows))],
        out_specs=[fixed((rows, d))] * 2,
        out_shape=[jax.ShapeDtypeStruct((rows, d), F32), jax.ShapeDtypeStruct((rows, d), BF)],
        cost_estimate=SMALL,
        compiler_params=pltpu.CompilerParams(vmem_limit_bytes=VMEM),
    )(came, x, gain, shift, pos)


def add_small(a, b, deps):
    def kernel(*refs):
        refs[-1][...] = refs[-3][...] + refs[-2][...]
    full = pl.BlockSpec(memory_space=pltpu.VMEM)
    return pl.pallas_call(kernel, name="add_small", in_specs=[ANY] * len(deps) + [full, full], out_specs=full,
                          out_shape=jax.ShapeDtypeStruct(a.shape, a.dtype), cost_estimate=SMALL)(*deps, a, b)


def hi_lo(v):
    hi = v.astype(BF)
    return hi, (v - hi.astype(F32)).astype(BF)


def middle_backward_kernel(single, bnd_ref, t_ref, *refs):
    it = iter(refs)
    parts = [next(it) for _ in range(single)]
    dots, n2, rm, middle, dy, gain, pos, mg_ref, mc_ref, sums_ref = it
    t = t_ref[0]
    total = parts[0][...].astype(F32)
    for p in parts[1:]:
        total = total + p[...].astype(F32)
    n2v, rmv = n2[...], rm[...]
    rows = n2v.shape[0]
    experts = bnd_ref.shape[1] - 1
    logits = dot(n2v, rmv, 1, 0)
    route_prob = lane_softmax(logits, 0, experts)
    mixing = lane_softmax(logits, experts, experts + 2)
    row = lax.broadcasted_iota(jnp.int32, (rows, 1), 0)
    route = jnp.zeros((rows, 1), jnp.int32)
    for e in range(1, experts):
        route = route + (row >= bnd_ref[t, e]).astype(jnp.int32)
    gate = pick_lane(route_prob, route)
    m0, m1 = pick_lane(mixing, experts), pick_lane(mixing, experts + 1)
    dense_dot, expert_dot = dots[:, 0:1], dots[:, 1:2]
    d0, d1 = dense_dot, expert_dot * gate
    inner = m0 * d0 + m1 * d1
    lane = lax.broadcasted_iota(jnp.int32, logits.shape, 1)
    grad = expert_dot * (m1 * gate) * (jnp.where(lane == route, 1.0, 0.0) - route_prob)
    grad = jnp.where(lane < experts, grad, 0.0)
    grad = jnp.where(lane == experts, m0 * (d0 - inner), grad)
    grad = jnp.where(lane == experts + 1, m1 * (d1 - inner), grad)
    hi, lo = hi_lo(grad)
    total = total + dot(hi, rmv, 1, 1) + dot(lo, rmv, 1, 1)
    sums_ref[0:8, :] = (dot(hi.T, n2v, 1, 0) + dot(lo.T, n2v, 1, 0))[0:8]
    g = dot(order_rows(pos[...], False), total.astype(BF), 1, 0)
    xhat, r = normalise(middle[...])
    sums_ref[8:16, :] = jnp.zeros((8, g.shape[1]), F32)
    sums_ref[8:9, :] = jnp.sum(g * xhat, axis=0, keepdims=True)
    sums_ref[9:10, :] = jnp.sum(g, axis=0, keepdims=True)
    mg = dy[...].astype(F32) + norm_backward(xhat, r, g, gain[...])
    mg_ref[...] = mg
    mc_ref[...] = mg.astype(BF)


def middle_backward(bounds, t, parts, dots, n2, rm, middle, dy, gain, pos, deps=()):
    rows, d = n2.shape
    fixed = lambda shape: pl.BlockSpec(shape, lambda p, *_: (0, 0))
    big = fixed((rows, d))
    return pl.pallas_call(
        skip(partial(middle_backward_kernel, len(parts)), 2, len(deps)),
        name="middle_backward",
        grid_spec=pltpu.PrefetchScalarGridSpec(
            num_scalar_prefetch=2, grid=(1,),
            in_specs=[ANY] * len(deps) + [big] * len(parts)
            + [fixed((rows, 8)), big, fixed((d, 128)), big, big, fixed((1, d)), fixed((rows, 1))],
            out_specs=[big, big, fixed((16, d))]),
        out_shape=[jax.ShapeDtypeStruct((rows, d), F32), jax.ShapeDtypeStruct((rows, d), BF), jax.ShapeDtypeStruct((16, d), F32)],
        cost_estimate=SMALL,
        compiler_params=pltpu.CompilerParams(vmem_limit_bytes=VMEM),
    )(bounds, t, *deps, *parts, dots, n2, rm, middle, dy, gain, pos)


def layer_out_kernel(*refs):
    parts, (middle, pos, out) = refs[:-3], refs[-3:]
    total = parts[0][...].astype(F32)
    for p in parts[1:]:
        total = total + p[...].astype(F32)
    hi, lo = hi_lo(total)
    move = order_rows(pos[...], False)
    out[...] = (middle[...] + dot(move, hi, 1, 0) + dot(move, lo, 1, 0)).astype(BF)


def layer_out(parts, middle, pos, deps=()):
    rows, d = middle.shape
    big = pl.BlockSpec((rows, d), lambda p: (0, 0))
    return pl.pallas_call(
        skip(layer_out_kernel, 0, len(deps)),
        name="layer_out",
        grid=(1,),
        in_specs=[ANY] * len(deps) + [big] * (len(parts) + 1) + [pl.BlockSpec((rows, 1), lambda p: (0, 0))],
        out_specs=big,
        out_shape=jax.ShapeDtypeStruct((rows, d), BF),
        cost_estimate=SMALL,
        compiler_params=pltpu.CompilerParams(vmem_limit_bytes=VMEM),
    )(*deps, *parts, middle, pos)


def add_parts_kernel(*refs):
    total = refs[0][...].astype(F32)
    for p in refs[1:-1]:
        total = total + p[...].astype(F32)
    refs[-1][...] = total.astype(BF)


def add_parts(parts, deps=()):
    rows, d = parts[0].shape
    tile = pl.BlockSpec((rows // 2, d), lambda p: (p, 0))
    return pl.pallas_call(
        skip(add_parts_kernel, 0, len(deps)),
        name="add_parts",
        grid=(2,),
        in_specs=[ANY] * len(deps) + [tile] * len(parts),
        out_specs=tile,
        out_shape=jax.ShapeDtypeStruct((rows, d), BF),
        cost_estimate=SMALL,
        compiler_params=pltpu.CompilerParams(vmem_limit_bytes=VMEM),
    )(*deps, *parts)


def input_backward_kernel(count, *refs):
    parts = refs[:count]
    x, mg, gain, out, sums = refs[count:]
    g = parts[0][...].astype(F32)
    for p in parts[1:]:
        g = g + p[...].astype(F32)
    xhat, r = normalise(x[...].astype(F32))
    sums[...] = jnp.zeros_like(sums)
    sums[0:1, :] = jnp.sum(g * xhat, axis=0, keepdims=True)
    sums[1:2, :] = jnp.sum(g, axis=0, keepdims=True)
    out[...] = mg[...] + norm_backward(xhat, r, g, gain[...])


def input_backward(parts, x, mg, gain, deps=()):
    rows, d = x.shape
    fixed = lambda shape: pl.BlockSpec(shape, lambda p: (0, 0))
    big = fixed((rows, d))
    return pl.pallas_call(
        skip(partial(input_backward_kernel, len(parts)), 0, len(deps)),
        name="input_backward",
        grid=(1,),
        in_specs=[ANY] * len(deps) + [big] * (len(parts) + 2) + [fixed((1, d))],
        out_specs=[big, fixed((8, d))],
        out_shape=[jax.ShapeDtypeStruct((rows, d), F32), jax.ShapeDtypeStruct((8, d), F32)],
        cost_estimate=SMALL,
        compiler_params=pltpu.CompilerParams(vmem_limit_bytes=VMEM),
    )(*deps, *parts, x, mg, gain)


class Everywhere:
    def __init__(self, v):
        self.v = v
        self.hops = [(axis, 1 << b) for axis in ("tensor", "dp") for b in range(lax.axis_size(axis).bit_length() - 1)]
        self.launch()

    def launch(self):
        if self.hops:
            axis, bit = self.hops.pop(0)
            self.came = lax.ppermute(self.v, axis, [(i, i ^ bit) for i in range(lax.axis_size(axis))])
        else:
            self.came = None

    def add(self, mark):
        if self.came is None:
            return mark
        self.v = add_small(self.v, self.came, mark)
        self.launch()
        return (self.v,)


def over_dp(v, bit):
    return lax.ppermute(v, "dp", [(i, i ^ (1 << bit)) for i in range(lax.axis_size("dp"))])


def shards(inputs, cotangent, routes, prefixes, gain_one, shift_one, qkv_weight, out_weight, gain_two, shift_two,
           up_weight, down_weight, expert_up, expert_down, router_weight, mix_weight):
    rows, d = inputs.shape
    tensor = lax.axis_size("tensor")
    dp = lax.axis_size("dp")
    bits = dp.bit_length() - 1
    seqs = prefixes.shape[0]
    members = tensor // seqs
    experts = expert_up.shape[0]
    heads = qkv_weight.shape[2]
    pairs = heads // LANES
    t = lax.axis_index("tensor")
    s, j = t // members, t % members
    me = lax.axis_index("dp").astype(jnp.int32)
    me1, j1, t1 = me.reshape(1), j.astype(jnp.int32).reshape(1), t.astype(jnp.int32).reshape(1)
    place = lambda a, b: (a % seqs) * members + b % members
    everyone = [(a, b) for a in range(seqs) for b in range(members)]

    def from_member(v, k):
        return lax.ppermute(v, "tensor", [(place(a, b), place(a, b - k)) for a, b in everyone])

    def from_sequence(v, k):
        return lax.ppermute(v, "tensor", [(place(a, b), place(a - k, b)) for a, b in everyone])

    def to_member(v, k):
        return from_member(v, -k)

    def to_sequence(v, k):
        return from_sequence(v, -k)

    route_blocks = routes.reshape(tensor, rows)
    bounds = jnp.stack([jnp.sum((route_blocks < e).astype(jnp.int32), axis=1) for e in range(experts + 1)], axis=1)
    key_col = lax.dynamic_slice_in_dim(routes, t * rows, rows, 0) * rows + jnp.arange(rows, dtype=jnp.int32)[:, None]
    key_row = key_col.reshape(1, rows)
    pos_row = jnp.sum((key_col < key_row).astype(jnp.int32), axis=0, keepdims=True)
    pos_col = jnp.sum((key_row < key_col).astype(jnp.int32), axis=1, keepdims=True)
    chunk = [(dj, ds) for dj in range(members) for ds in range(seqs)]
    blocks = jnp.stack([((s + ds) % seqs) * members + (j + dj) % members for dj, ds in chunk]).astype(jnp.int32)
    near = [q for q, (dj, ds) in enumerate(chunk) if ds == 0]
    far = [q for q, (dj, ds) in enumerate(chunk) if ds > 0]

    xs = [inputs] + [from_member(inputs, k) for k in range(1, members)]
    flip = me & 1
    relay = pairs % 2 == 0 and dp > 1
    w_own = jnp.transpose(qkv_weight, (1, 0, 2))
    fetched = []
    for ds in range(1, seqs):
        if relay:
            half = lax.dynamic_slice_in_dim(qkv_weight, flip * (heads // 2), heads // 2, 2)
            fetched.append([from_sequence(jnp.transpose(half[:, a:b], (1, 0, 2)), ds) for a, b in ((0, 2), (2, 3))])
        else:
            fetched.append([from_sequence(w_own, ds)])
    wo_all = [out_weight] + [from_sequence(out_weight, ds) for ds in range(1, seqs)]
    gain_one, shift_one, gain_two, shift_two = [v.reshape(1, d) for v in (gain_one, shift_one, gain_two, shift_two)]
    prefix = lax.dynamic_slice_in_dim(prefixes, s, 1)
    n1, dys = first_norm(j1, xs, gain_one, shift_one, cotangent, pos_row)
    columns = jnp.arange(pairs, dtype=jnp.int32)
    pieces = [[] for _ in fetched]
    fence = (n1,)
    if relay:
        for k, got in enumerate(fetched):
            held = hold(got[0], (n1,))
            pieces[k] = [[held], [over_dp(held, 0)]]
            fence += (held,)
    saved = [attn_forward(prefix, columns, n1, [w_own], heads, deps=fence[1:])]
    if relay:
        for k, got in enumerate(fetched):
            held = hold(got[1], (saved[0][4],))
            pieces[k][0].append(held)
            pieces[k][1].append(over_dp(held, 0))
    else:
        pieces = [[got] for got in fetched]
    w_all = [w_own]
    for halves in pieces:
        part = ()
        for k, ws in enumerate(halves):
            at = (columns + (flip ^ k) * (pairs // 2))[:pairs // 2] if relay else columns
            part = attn_forward(prefix, at, n1, ws, heads, part, deps=() if part else (saved[-1][4],))
        saved.append(part)
        whole = [jnp.concatenate(ws, axis=0) for ws in halves]
        if relay:
            whole = [jnp.where(flip == 0, jnp.concatenate(whole, axis=2), jnp.concatenate(whole[::-1], axis=2))]
        w_all.append(whole[0])
    contexts = [v[3] for v in saved]

    def spread(mine):
        out = list(mine)
        for k in range(1, members):
            out += [from_member(m, k) for m in mine]
        return out

    dy_mine = [dys] + [from_sequence(dys, ds) for ds in range(1, seqs)]
    dy_near = [dys] + [from_member(dys, k) for k in range(1, members)]
    sent = project(contexts, wo_all, members)
    came = lax.all_to_all(sent, "tensor", 0, 0, axis_index_groups=[[place(a, b) for b in range(members)] for a in range(seqs)], tiled=True)
    middle, n2 = second_norm(came, inputs, gain_two, shift_two, pos_row)
    n2_mine = [n2] + [from_sequence(n2, ds) for ds in range(1, seqs)]
    n2_near = [n2] + [from_member(n2, k) for k in range(1, members)]

    rm = jnp.concatenate([router_weight, mix_weight, jnp.zeros((d, LANES - experts - 2), BF)], axis=1)
    straight = tuple(range(bits))
    turned = straight[1:] + straight[:1]
    orders = (straight, turned)
    pick = lambda v, which: [v[q] for q in which]
    out_a, rg_a, dots_a, sums = ffn_dense(me1, n2_near, dy_near, rm, up_weight, down_weight, experts, orders, deps=tuple(dy_mine[1:]))
    n2_all, dy_all = [], []
    n2_far, dy_far = [[hold(v, (out_a[0],)) for v in mine[1:]] for mine in (n2_mine, dy_mine)]
    for k in range(members):
        n2_all += [n2_near[k]] + [from_member(v, k) if k else v for v in n2_far]
        dy_all += [dy_near[k]] + [from_member(v, k) if k else v for v in dy_far]
    base = [[None] * tensor, [None] * tensor]
    for k, q in enumerate(near):
        base[0][q], base[1][q] = out_a[k], rg_a[k]
    cut = 1 if experts > 1 else experts
    out_e, rg_e, dots_e, keep_e, send_e = ffn_experts(me1, blocks, bounds, n2_all, dy_all, rm, expert_up, expert_down, 0, cut, base, straight)
    keep_e, send_e, dots = list(keep_e), list(send_e), dots_e
    if cut < experts:
        out_e, rg_e, dots_e, more_k, more_s = ffn_experts(me1, blocks, bounds, n2_all, dy_all, rm, expert_up, expert_down, cut, experts - cut, (out_e, rg_e), straight)
        keep_e, send_e, dots = keep_e + list(more_k), send_e + list(more_s), dots + dots_e
    out_e, rg_e = list(out_e), list(rg_e)
    out_b, rg_b, dots_b, ends = ffn_dense(me1, pick(n2_all, far), pick(dy_all, far), rm, up_weight, down_weight, experts, orders,
                                          (pick(out_e, far), pick(rg_e, far)), sums)
    for k, q in enumerate(far):
        out_e[q], rg_e[q] = out_b[k], rg_b[k]

    index = {c: q for q, c in enumerate(chunk)}
    cols = lambda v, k, n=1: v[:, k * rows:(k + n) * rows]
    dot_part = []
    for q, (dj, ds) in enumerate(chunk):
        dense_part = cols(dots_a, near.index(q)) if ds == 0 else cols(dots_b, far.index(q))
        dot_part.append(cols(dots, q) + dense_part)
    held = jnp.concatenate(dot_part[:seqs], axis=1)
    for k in range(1, members):
        held = held + to_member(jnp.concatenate(dot_part[k * seqs:(k + 1) * seqs], axis=1), k)
    own_dots = cols(held, 0)
    for ds in range(1, seqs):
        own_dots = own_dots + to_sequence(cols(held, ds), ds)

    def to_owner(parts):
        mine = [[parts[index[0, ds]]] + [to_member(parts[index[k, ds]], k) for k in range(1, members)] for ds in range(seqs)]
        return mine[0], mine[1:]

    def onward(terms, deps):
        sums = [add_parts(v, deps) for v in terms]
        return [to_sequence(v, ds + 1) for ds, v in enumerate(sums)], sums

    class Halving:
        def __init__(self, keep, send, order):
            self.keep, self.send, self.order, self.at = keep, send, order, 0

        def launch(self, deps=()):
            if deps:
                self.send = hold(self.send, deps)
            self.came = over_dp(self.send, self.order[self.at])
            self.at += 1

        def add(self, mark):
            self.keep, self.send = split_add(self.keep, self.came, mark)
            self.launch()
            return (self.send,)

        def rest(self, mark):
            while self.at < bits:
                mark = self.add(mark)
            return mark

    sums_e = [Halving(keep_e[e], send_e[e], straight) for e in range(experts)]
    down_sum, up_sum = Halving(ends[2], ends[3], turned), Halving(ends[0], ends[1], straight)
    rg_near, rg_far = to_owner(rg_e)
    for e in range(min(experts, 3)):
        sums_e[e].launch()
    down_sum.launch()
    came_far, terms = onward(rg_far, ())
    mark = tuple(terms[:1])
    for e in range(min(experts, 2)):
        mark = sums_e[e].add(mark)
    mg, mc, sums_two = middle_backward(bounds, t1, rg_near + came_far, own_dots.T, n2, rm, middle, cotangent, gain_two, pos_col, mark)
    mcs = [mc] + [from_member(mc, k) for k in range(1, members)]
    mark = down_sum.add((mc,))
    ngs = None
    grads = [None] * seqs
    for ds in list(range(1, seqs)) + [0]:
        ngs, grads[ds] = attn_backward(prefix, me1, j1, mcs, n1, wo_all[ds], w_all[ds], saved[ds], ngs, bits, mark)
        mark = (grads[ds],)
        if ds == 1 or seqs == 1:
            for e in range(3, experts):
                sums_e[e].launch(mark)
            mark = sums_e[0].add(mark)
            if experts > 2:
                mark = sums_e[2].add(mark)
    moved = [to_sequence(grads[ds], ds) for ds in range(1, seqs)]
    ng_parts = [ngs[0]] + [to_member(ngs[k], k) for k in range(1, members)]
    up_sum.launch(mark)
    if experts > 1:
        mark = sums_e[1].add(mark)
    input_grad, sums_one = input_backward(ng_parts, inputs, mg, gain_one, mark)
    mark = (sums_one,)
    sums = Everywhere(jnp.concatenate([sums_two, sums_one], axis=0))
    stacks = None

    def finish(e, mark):
        mark = sums_e[e].rest(mark)
        done = last_add(sums_e[e].keep, sums_e[e].came, (False, True), (experts, e), stacks, mark)
        return done, (done[1],)

    stacks, mark = finish(0, mark)
    if experts > 2:
        mark = sums_e[2].add(mark)
    mark = down_sum.add(mark)
    mark = sums.add(mark)
    for e in range(3, experts):
        mark = sums_e[e].add(mark)
    keep = grads[0]
    for v in moved[:-1]:
        keep = (keep.astype(F32) + v.astype(F32)).astype(BF)
    if moved:
        keep, send = split_add(keep, moved[-1], mark)
        mark = (send,)
    else:
        keep, send = keep[:dp // 2], keep[dp // 2:]
    attn_sum = Halving(keep, send, straight)
    attn_sum.launch()
    out_near, out_far = to_owner([hold(v, mark) for v in out_e])
    out_came, terms = onward(out_far, mark)
    mark = tuple(terms[:1]) or mark
    if experts > 1:
        stacks, mark = finish(1, mark)
    mark = sums.add(mark)
    mark = up_sum.add(mark)
    mark = down_sum.rest(mark)
    down_out, = last_add(down_sum.keep, down_sum.came, (True,), deps=mark)
    mark = (down_out,)
    for e in range(3, experts):
        mark = sums_e[e].add(mark)
    mark = sums.add(mark)
    if experts > 2:
        stacks, mark = finish(2, mark)
    layer_output = layer_out(out_near + out_came, middle, pos_col, mark)
    mark = (layer_output,)
    mark = attn_sum.add(mark)
    mark = sums.add(mark)
    mark = up_sum.add(mark)
    for e in range(3, experts):
        stacks, mark = finish(e, mark)
    expert_up_out, expert_down_out = stacks
    mark = attn_sum.add(mark)
    while sums.came is not None:
        mark = sums.add(mark)
    mark = up_sum.rest(mark)
    up_out, = last_add(up_sum.keep, up_sum.came, (False,), deps=mark)
    mark = attn_sum.rest((up_out,))
    *qkv_parts, out_out = last_add(attn_sum.keep, attn_sum.came, (False, False, False, True), deps=mark)
    lanes = d // (dp * tensor)
    begin = (me * tensor + t) * lanes
    small = lax.dynamic_slice_in_dim(sums.v, begin, lanes, 1)
    return (layer_output, input_grad, small[16], small[17], jnp.stack(qkv_parts, axis=1), out_out, small[8], small[9], up_out, down_out,
            expert_up_out, expert_down_out, small[0:experts].T, small[experts:experts + 2].T)


def solution(mesh):
    both = ("dp", "tensor")
    in_specs = (P(both, None), P(both, None), P("dp", None), P("dp"), P(), P(), P(None, None, "tensor"), P("tensor", None), P(), P(),
                P(None, "tensor"), P("tensor", None), P(None, None, "tensor"), P(None, "tensor", None), P(), P())
    out_specs = (P(both, None), P(both, None), P(both), P(both), P("dp", None, "tensor"), P("tensor", "dp"), P(both), P(both),
                 P("dp", "tensor"), P("tensor", "dp"), P(None, "dp", "tensor"), P(None, "tensor", "dp"), P(both, None), P(both, None))
    return jax.shard_map(shards, mesh=mesh, in_specs=in_specs, out_specs=out_specs, check_vma=False)
```

time: 708 us -> 596 us (0.84)
  waiting for transfers between devices: 325 us -> 155 us
  Pallas kernels: 235 us -> 333 us
  other arithmetic: 55.5 us -> 11.1 us
  starting transfers between devices: 59.6 us -> 46.9 us
  local copies, waits for them, and re-layouts: 20.9 us -> 30.8 us
  blocking collectives: 0 us -> 8.71 us
    ppermute x28, waiting for transfers between devices: 251 us -> 120 us  [the longest x23 78.4 us: over_dp(): lax.ppermute(v, 'dp', [(i, i ^ 1 << bit) for i in range(lax.axis_size('dp...]
    pallas_call x11 -> x53, Pallas kernels: 231 us -> 328 us  [the longest x2 80.2 us: ffn_experts(): pl.pallas_call(partial(expert_kernel, (first, count, chunks, rows, d, tm,...]
    ppermute x8 -> x9, waiting for transfers between devices: 70.7 us -> 29.5 us  [from_sequence(): lax.ppermute(v, 'tensor', [(place(a, b), place(a - k, b)) for a, b in eve...]
    convert_element_type x16 -> x1, other arithmetic: 38.2 us -> 0.11 us  [shards(): (route_blocks < e).astype(jnp.int32)]
    unnamed x69 -> x102, local copies, waits for them, and re-layouts: 7.87 us -> 20.4 us
    ppermute x28, starting transfers between devices: 46.3 us -> 34.4 us  [the longest x23 28.3 us: over_dp(): lax.ppermute(v, 'dp', [(i, i ^ 1 << bit) for i in range(lax.axis_size('dp...]
    add x18 -> x6, other arithmetic: 12.6 us -> 2.83 us  [the longest x1 1.1 us: shards(): held + to_member(jnp.concatenate(dot_part[k * seqs:(k + 1) * seqs], axis=...]
    all_to_all x0 -> x1, blocking collectives: none -> 8.71 us  [shards(): lax.all_to_all(sent, 'tensor', 0, 0, axis_index_groups=[[place(a, b) for...]
  transfers between devices with their start and end apart: 47 -> 49, of which waited for: 23 -> 14; matrix products, arithmetic and copies ran while one was open for 10% -> 4% of each run, Pallas kernels for 27% -> 50%
where the time goes in v2:
time: 596 us; the launch traced here: 588 us
  Pallas kernels  333 us (56%)
  waiting for transfers between devices  155 us (26%)
  starting transfers between devices  46.9 us (8%)
  local copies, waits for them, and re-layouts  30.8 us (5%)
  other arithmetic  11.1 us (2%)
  blocking collectives  8.71 us (1%)
    pallas_call x2, Pallas kernels, ffn_experts(): pl.pallas_call(partial(expert_kernel, (first, count, chunks, rows, d, tm,...  80.2 us
    ppermute x23, waiting for transfers between devices, over_dp(): lax.ppermute(v, 'dp', [(i, i ^ 1 << bit) for i in range(lax.axis_size('dp...  78.4 us
    pallas_call x2, Pallas kernels, attn_backward(): pl.pallas_call(skip(partial(attn_backward_kernel, length, bits, members,...  54.9 us
    pallas_call x15, Pallas kernels, split_add(): pl.pallas_call(partial(split_add_kernel, len(deps)), name='split_add', gr...  53.8 us
    pallas_call x2, Pallas kernels, ffn_dense(): pl.pallas_call(partial(dense_kernel, (chunks, rows, tm, lanes, orders, fi...  49.9 us
    ppermute x5, waiting for transfers between devices, launch(): lax.ppermute(self.v, axis, [(i, i ^ bit) for i in range(lax.axis_size(axi...  42 us
    pallas_call x3, Pallas kernels, attn_forward(): pl.pallas_call(skip(partial(attn_forward_kernel, length, tuple((w.shape[0...  31.7 us
    ppermute x9, waiting for transfers between devices, from_sequence(): lax.ppermute(v, 'tensor', [(place(a, b), place(a - k, b)) for a, b in eve...  29.5 us
  transfers between devices with their start and end apart: 49, of which 14 were waited for; matrix products, arithmetic and copies ran while one was open for 4% of the time, Pallas kernels for 50%

profile of v2, /device:TPU:0, one launch (start us, length us, event | category | flops | bytes accessed | tf_op | source)
XLA Modules:
  0.0 587.6 jit_solution(7894783624504803364)
XLA Ops:
  2.2 2.6 collective-permute-start
  8.4 5.1 first_norm.1
  13.6 4.0 collective-permute-done.refs_0_
  18.4 1.9 collective-permute-start.2
  23.0 14.3 %attn_forward.3 = (bf16[1024,256]{1,0:T(8,128)(2,1)}, bf16[1024,256]{1,0:T(8,128)(2,1)}, bf16[1024,256]{1,0:T(8,128)(2,1)}, bf16[1024,256]{1,0:T(8,128)(2,1)}, f32[2,8,1024]{2,1,0:T(8,128)}) custom-call(s32[1]{0:T(128)} %dynamic_slice.12.refs_0_, s32[2]{0:T(128)} %iota.11.refs_1_, bf16[2,1024,128]{2,1,0:T(8,128)(2,1)} %hold.10.refs_2_.refs_4_, ...), custom_call_target="tpu_custom_call" | custom-call | tf_op jit(solution)/shard_map/attn_forward/pallas_call | solution.py:521
  39.7 8.7 %attn_forward.4 = (bf16[1024,256]{1,0:T(8,128)(2,1)}, bf16[1024,256]{1,0:T(8,128)(2,1)}, bf16[1024,256]{1,0:T(8,128)(2,1)}, bf16[1024,256]{1,0:T(8,128)(2,1)}, f32[2,8,1024]{2,1,0:T(8,128)}) custom-call(s32[1]{0:T(128)} %dynamic_slice.12.refs_0_, s32[1]{0:T(128)} %bitcast.64, f32[2,8,1024]{2,1,0:T(8,128)} %get-tuple-element.130.refs_1_.refs_2_.refs_13_, ...), custom_call_target="tpu_custom_call" | custom-call | tf_op jit(solution)/shard_map/attn_forward/pallas_call | solution.py:521
  49.0 8.7 %attn_forward.5 = (bf16[1024,256]{1,0:T(8,128)(2,1)}, bf16[1024,256]{1,0:T(8,128)(2,1)}, bf16[1024,256]{1,0:T(8,128)(2,1)}, bf16[1024,256]{1,0:T(8,128)(2,1)}, f32[2,8,1024]{2,1,0:T(8,128)}) custom-call(s32[1]{0:T(128)} %dynamic_slice.12.refs_0_, s32[1]{0:T(128)} %bitcast.63, ...), custom_call_target="tpu_custom_call", output_to_operand_aliasing={{0}: (5, {}), {1}: (6, {}), {2}: (7, {}), {3}: (8, {}), {4}... | custom-call | tf_op jit(solution)/shard_map/attn_forward/pallas_call | solution.py:521
  58.6 3.8 project.1
  62.3 8.7 %all_to_all.5.came = bf16[2,512,1024]{2,1,0:T(8,128)(2,1)} all-to-all(bf16[2,512,1024]{2,1,0:T(8,128)(2,1)} %project.1), channel_id=1, replica_groups={{0,1},{2,3},{4,5},{6,7},{8,9},{10,11},{12,13},{14,15},{16,17},{18,19},{..., dimensions={0} | all-to-all | bytes 4194304 | tf_op jit(solution)/shard_map/all_to_all | solution.py:1009
  71.1 4.4 second_norm.1
  75.6 2.0 collective-permute-start.6
  78.7 1.8 maximum_maximum_fusion.refs_5_.refs_8_.refs_4_
  81.6 23.6 %ffn_dense.2 = (bf16[512,1024]{1,0:T(8,128)(2,1)}, bf16[512,1024]{1,0:T(8,128)(2,1)}, bf16[512,1024]{1,0:T(8,128)(2,1)}, bf16[512,1024]{1,0:T(8,128)(2,1)}, f32[...) custom-call(s32[1]{0:T(128)} %bitcast.me_ref.refs_1_, bf16[512,1024]{1,0:T(8,128)(2,1)} %copy-done, ...), custom_call_target="tpu_custom_call" | custom-call | tf_op jit(solution)/shard_map/ffn_dense/pallas_call | solution.py:200
  110.7 26.0 %ffn_experts.2 = (bf16[512,1024]{1,0:T(8,128)(2,1)}, bf16[512,1024]{1,0:T(8,128)(2,1)}, bf16[512,1024]{1,0:T(8,128)(2,1)}, bf16[512,1024]{1,0:T(8,128)(2,1)}, bf...) custom-call(s32[1]{0:T(128)} %bitcast.me_ref.refs_1_, ...), custom_call_target="tpu_custom_call" | custom-call | tf_op jit(solution)/shard_map/ffn_experts/pallas_call | solution.py:368
  138.3 54.2 %ffn_experts.3 = (bf16[512,1024]{1,0:T(8,128)(2,1)}, bf16[512,1024]{1,0:T(8,128)(2,1)}, bf16[512,1024]{1,0:T(8,128)(2,1)}, bf16[512,1024]{1,0:T(8,128)(2,1)}, bf...) custom-call(s32[1]{0:T(128)} %bitcast.me_ref.refs_1_, ...), custom_call_target="tpu_custom_call" | custom-call | tf_op jit(solution)/shard_map/ffn_experts/pallas_call | solution.py:368
  193.1 26.3 %ffn_dense.3 = (bf16[512,1024]{1,0:T(8,128)(2,1)}, bf16[512,1024]{1,0:T(8,128)(2,1)}, bf16[512,1024]{1,0:T(8,128)(2,1)}, bf16[512,1024]{1,0:T(8,128)(2,1)}, f32[...) custom-call(s32[1]{0:T(128)} %bitcast.me_ref.refs_1_, ...), custom_call_target="tpu_custom_call" | custom-call | tf_op jit(solution)/shard_map/ffn_dense/pallas_call | solution.py:200
  219.9 3.1 collective-permute-done.12.refs_1_
  224.0 2.6 add_parts.2.refs_0_
  227.3 1.8 collective-permute-done.17
  230.2 2.0 collective-permute-start.18
  232.2 25.4 %collective-permute-done.18 = f32[8,512]{0,1:T(8,128)S(1)} collective-permute-done((f32[8,512]{0,1:T(8,128)S(1)}, f32[8,512]{0,1:T(8,128)S(1)}, u32[]{:S(2)}, u32[]{:S(2)}) %collective-permute-start.18) | collective-permute-done | bytes 16416 | tf_op jit(solution)/shard_map/ppermute | solution.py:937
  262.3 4.2 split_add.15
  266.5 4.2 split_add.16
  270.8 10.6 %middle_backward.1 = (f32[512,1024]{1,0:T(8,128)}, bf16[512,1024]{1,0:T(8,128)(2,1)}, f32[16,1024]{1,0:T(8,128)}) custom-call(s32[4,5]{1,0:T(4,128)} %stack.50.bnd_ref.refs_0_, s32[1]{0:T(128)} %bitcast.7.refs_1_, bf16[2,2,128,1024]{3,2,1,0:T(8,128)(2,1)} %get-tuple-element.164.refs_2_, bf16[512,1024]{1,0:T(8,128)(2,1)} %get-tuple-element.165.refs_3_, ...), custom_call_target="tpu_custom_call" | custom-call | tf_op jit(solution)/shard_map/middle_backward/pallas_call | solution.py:800
  285.5 2.4 split_add.17
  288.9 27.0 %attn_backward.2 = (bf16[512,1024]{1,0:T(8,128)(2,1)}, bf16[512,1024]{1,0:T(8,128)(2,1)}, bf16[8,4,128,256]{3,2,1,0:T(8,128)(2,1)}) custom-call(s32[1]{0:T(128)} %dynamic_slice.12.refs_0_, s32[1]{0:T(128)} %bitcast.me_ref.refs_1_, s32[1]{0:T(128)} %bitcast.1.j_ref.refs_2_, bf16[2,1,128,1024]{3,2,1,0:T(8,128)(2,1)} %get-tuple-element.175.refs_3_, ...), custom_call_target="tpu_custom_call" | custom-call | tf_op jit(solution)/shard_map/attn_backward/pallas_call | solution.py:627
  319.8 2.4 split_add.18
  322.2 4.2 split_add.19
  326.3 27.9 %attn_backward.3 = (bf16[512,1024]{1,0:T(8,128)(2,1)}, bf16[512,1024]{1,0:T(8,128)(2,1)}, bf16[8,4,128,256]{3,2,1,0:T(8,128)(2,1)}) custom-call(s32[1]{0:T(128)} %dynamic_slice.12.refs_0_, s32[1]{0:T(128)} %bitcast.me_ref.refs_1_, s32[1]{0:T(128)} %bitcast.1.j_ref.refs_2_, bf16[2,2,128,1024]{3,2,1,0:T(8,128)(2,1)} %get-tuple-element.185.refs_3_, ...), custom_call_target="tpu_custom_call" | custom-call | tf_op jit(solution)/shard_map/attn_backward/pallas_call | solution.py:627
  354.7 2.6 collective-permute-start.25
  357.3 2.6 collective-permute-start.27
  359.9 2.7 split_add.20
  362.6 5.6 input_backward.1
  369.0 20.8 %collective-permute-done.25.refs_2_ = bf16[1,2,128,1024]{3,2,1,0:T(8,128)(2,1)} collective-permute-done((bf16[1,2,128,1024]{3,2,1,0:T(8,128)(2,1)}, bf16[1,2,128,1024]{3,2,1,0:T(8,128)(2,1)}, u32[]{:S(2)}, u32[]{:S(2)}) %collective-permute-start.25) | collective-permute-done | bytes 524320 | tf_op jit(solution)/shard_map/ppermute | solution.py:912
  389.7 2.4 last_add.7
  392.1 10.6 %collective-permute-done.26.refs_3_.refs_4_ = bf16[2,2,128,1024]{3,2,1,0:T(8,128)(2,1)} collective-permute-done((bf16[2,2,128,1024]{3,2,1,0:T(8,128)(2,1)}, bf16[2,2,128,1024]{3,2,1,0:T(8,128)(2,1)}, u32[]{:S(2)}, u32[]{:S(2)}) %collective-permute-start.26) | collective-permute-done | bytes 1048608 | tf_op jit(solution)/shard_map/ppermute | solution.py:912
  402.7 2.4 split_add.21
  405.9 2.0 split_add.22
  410.1 4.2 split_add.23
  414.3 9.7 %split_add.24 = (bf16[4,4,128,256]{3,2,1,0:T(8,128)(2,1)}, bf16[4,4,128,256]{3,2,1,0:T(8,128)(2,1)}) custom-call(bf16[2,2,128,1024]{3,2,1,0:T(8,128)(2,1)} %get-tuple-element.208.refs_0_, bf16[8,4,128,256]{3,2,1,0:T(8,128)(2,1)} %get-tuple-element.191.refs_0_.refs_1_.refs_2_, bf16[8,4,128,256]{3,2,1,0:T(8,128)(2,1)} %get-tuple-element.191.refs_0_.refs_1_.refs_2_, ...), custom_call_target="tpu_custom_call" | custom-call | tf_op jit(solution)/shard_map/split_add/pallas_call | solution.py:400
  424.7 2.8 collective-permute-start.36
  428.5 2.4 add_parts.3.refs_2_
  432.5 18.3 %collective-permute-done.32.refs_4_ = bf16[1,2,128,1024]{3,2,1,0:T(8,128)(2,1)} collective-permute-done((bf16[1,2,128,1024]{3,2,1,0:T(8,128)(2,1)}, bf16[1,2,128,1024]{3,2,1,0:T(8,128)(2,1)}, u32[]{:S(2)}, u32[]{:S(2)}) %collective-permute-start.32) | collective-permute-done | bytes 524320 | tf_op jit(solution)/shard_map/ppermute | solution.py:912
  453.9 4.9 collective-permute-done.33.refs_2_
  460.3 21.2 %collective-permute-done.35.refs_2_ = bf16[1,1,128,1024]{3,2,1,0:T(8,128)(2,1)S(1)} collective-permute-done((bf16[1,1,128,1024]{3,2,1,0:T(8,128)(2,1)S(1)}, bf16[1,1,128,1024]{3,2,1,0:T(8,128)(2,1)S(1)}, u32[]{:S(2)}, u32[]{:S(2)}) %collective-permute-start.35) | collective-permute-done | bytes 262176 | tf_op jit(solution)/shard_map/ppermute | solution.py:912
  481.5 2.5 last_add.8
  487.1 2.4 split_add.25
  490.4 2.1 collective-permute-start.43
  492.4 2.0 last_add.9.refs_0_
  494.5 2.4 split_add.26
  498.5 7.5 %collective-permute-done.38.refs_4_ = bf16[1,2,128,1024]{3,2,1,0:T(8,128)(2,1)} collective-permute-done((bf16[1,2,128,1024]{3,2,1,0:T(8,128)(2,1)}, bf16[1,2,128,1024]{3,2,1,0:T(8,128)(2,1)}, u32[]{:S(2)}, u32[]{:S(2)}) %collective-permute-start.38) | collective-permute-done | bytes 524320 | tf_op jit(solution)/shard_map/ppermute | solution.py:912
  505.9 2.4 last_add.10
  508.3 4.9 layer_out.1.refs_0_
  514.2 5.4 split_add.27
  519.6 2.8 collective-permute-start.45
  522.5 22.5 %collective-permute-done.42.refs_2_ = f32[24,1024]{1,0:T(8,128)S(1)} collective-permute-done((f32[24,1024]{1,0:T(8,128)S(1)}, f32[24,1024]{1,0:T(8,128)S(1)}, u32[]{:S(2)}, u32[]{:S(2)}) %collective-permute-start.42) | collective-permute-done | bytes 98336 | tf_op jit(solution)/shard_map/ppermute | solution.py:899
  548.0 2.0 split_add.28
  550.1 2.9 collective-permute-start.46
  553.8 2.4 last_add.11
  557.0 3.2 split_add.29
  560.2 13.7 %collective-permute-done.46.refs_2_ = f32[24,1024]{1,0:T(8,128)S(1)} collective-permute-done((f32[24,1024]{1,0:T(8,128)S(1)}, f32[24,1024]{1,0:T(8,128)S(1)}, u32[]{:S(2)}, u32[]{:S(2)}) %collective-permute-start.46) | collective-permute-done | bytes 98336 | tf_op jit(solution)/shard_map/ppermute | solution.py:899
  578.2 1.9 last_add.12.refs_0_
  583.4 1.9 last_add.13
  585.3 1.8 pad_maximum_fusion
  (237 shorter events, 70.2 us)
Async XLA Ops:
  0.6 6.8 %collective-permute-start.1 = (bf16[512,1024]{1,0:T(8,128)(2,1)}, bf16[512,1024]{1,0:T(8,128)(2,1)S(1)}, u32[]{:S(2)}, u32[]{:S(2)}) collective-permute-start(bf16[512,1024]{1,0:T(8,128)(2,1)} %refs_3_.1), channel_id=1, source_target_pairs={{0,1},{1,0},{2,3},{3,2},{4,5},{5,4},{6,7},{7,6},{8,9},{9,8},{10,11... | collective-permute-start | bytes 3145736 | tf_op jit(solution)/shard_map/ppermute | solution.py:934
  2.2 15.4 %collective-permute-start = (bf16[2,1024,128]{2,1,0:T(8,128)(2,1)S(1)}, bf16[2,1024,128]{2,1,0:T(8,128)(2,1)S(1)}, u32[]{:S(2)}, u32[]{:S(2)}) collective-permute-start(bf16[2,1024,128]{2,1,0:T(8,128)(2,1)S(1)} %dynamic-slice_bitcast_fusion), channel_id=1, source_target_pairs={{0,2},{1,3},{2,0},{3,1},{4,6},{5,7},{6,4},{7,5},{8,10},{9,11},{10,... | collective-permute-start | bytes 1572872 | tf_op jit(solution)/shard_map/ppermute | solution.py:937
  5.8 31.5 %collective-permute-start.3 = (bf16[1,1024,128]{2,1,0:T(8,128)(2,1)S(1)}, bf16[1,1024,128]{2,1,0:T(8,128)(2,1)S(1)}, u32[]{:S(2)}, u32[]{:S(2)}) collective-permute-start(bf16[1,1024,128]{2,1,0:T(8,128)(2,1)S(1)} %dynamic-slice_bitcast_fusion.1), channel_id=1, source_target_pairs={{0,2},{1,3},{2,0},{3,1},{4,6},{5,7},{6,4},{7,5},{8,10},{9,11},{10,... | collective-permute-start | bytes 786440 | tf_op jit(solution)/shard_map/ppermute | solution.py:937
  13.6 8.3 %copy-start.48 = (s32[2]{0:T(128)S(1)}, s32[2]{0:T(128)}, u32[]{:S(2)}) copy-start(s32[2]{0:T(128)} %param.19) | copy-start | bytes 28
  18.4 29.9 %collective-permute-start.2 = (bf16[2,1024,128]{2,1,0:T(8,128)(2,1)}, bf16[2,1024,128]{2,1,0:T(8,128)(2,1)}, u32[]{:S(2)}, u32[]{:S(2)}) collective-permute-start(bf16[2,1024,128]{2,1,0:T(8,128)(2,1)} %hold.10.refs_2_.refs_4_), channel_id=1, source_target_pairs={{0,4},{4,0},{8,12},{12,8},{16,20},{20,16},{24,28},{28,24},{1,5},{5... | collective-permute-start | bytes 1572872 | tf_op jit(solution)/shard_map/ppermute | solution.py:912
  20.3 37.4 %collective-permute-start.5 = (bf16[256,1024]{1,0:T(8,128)(2,1)S(1)}, bf16[256,1024]{1,0:T(8,128)(2,1)S(1)}, u32[]{:S(2)}, u32[]{:S(2)}) collective-permute-start(bf16[256,1024]{1,0:T(8,128)(2,1)S(1)} %copy-done.17), channel_id=1, source_target_pairs={{0,2},{1,3},{2,0},{3,1},{4,6},{5,7},{6,4},{7,5},{8,10},{9,11},{10,... | collective-permute-start | bytes 1572872 | tf_op jit(solution)/shard_map/ppermute | solution.py:937
  23.0 16.6 %copy-start.3 = (bf16[512,1024]{1,0:T(8,128)(2,1)S(1)}, bf16[512,1024]{1,0:T(8,128)(2,1)}, u32[]{:S(2)}) copy-start(bf16[512,1024]{1,0:T(8,128)(2,1)} %get-tuple-element.138.refs_3_.refs_4_) | copy-start | bytes 3145732
  38.0 10.3 %collective-permute-start.4 = (bf16[1,1024,128]{2,1,0:T(8,128)(2,1)}, bf16[1,1024,128]{2,1,0:T(8,128)(2,1)S(1)}, u32[]{:S(2)}, u32[]{:S(2)}) collective-permute-start(bf16[1,1024,128]{2,1,0:T(8,128)(2,1)} %hold.11.refs_5_), channel_id=1, source_target_pairs={{0,4},{4,0},{8,12},{12,8},{16,20},{20,16},{24,28},{28,24},{1,5},{5... | collective-permute-start | bytes 786440 | tf_op jit(solution)/shard_map/ppermute | solution.py:912
  39.6 41.0 %collective-permute-start.9 = (bf16[512,1024]{1,0:T(8,128)(2,1)S(1)}, bf16[512,1024]{1,0:T(8,128)(2,1)}, u32[]{:S(2)}, u32[]{:S(2)}) collective-permute-start(bf16[512,1024]{1,0:T(8,128)(2,1)S(1)} %copy-done.3), channel_id=1, source_target_pairs={{0,1},{1,0},{2,3},{3,2},{4,5},{5,4},{6,7},{7,6},{8,9},{9,8},{10,11... | collective-permute-start | bytes 3145736 | tf_op jit(solution)/shard_map/ppermute | solution.py:934
  39.6 41.0 %collective-permute-start.7 = (bf16[512,1024]{1,0:T(8,128)(2,1)S(1)}, bf16[512,1024]{1,0:T(8,128)(2,1)S(1)}, u32[]{:S(2)}, u32[]{:S(2)}) collective-permute-start(bf16[512,1024]{1,0:T(8,128)(2,1)S(1)} %copy-done.3), channel_id=1, source_target_pairs={{0,2},{1,3},{2,0},{3,1},{4,6},{5,7},{6,4},{7,5},{8,10},{9,11},{10,... | collective-permute-start | bytes 3145736 | tf_op jit(solution)/shard_map/ppermute | solution.py:937
  75.4 5.1 collective-permute-start.8
  75.6 29.8 %collective-permute-start.6 = (bf16[512,1024]{1,0:T(8,128)(2,1)}, bf16[512,1024]{1,0:T(8,128)(2,1)S(1)}, u32[]{:S(2)}, u32[]{:S(2)}) collective-permute-start(bf16[512,1024]{1,0:T(8,128)(2,1)} %get-tuple-element.137.refs_1_.refs_0_.refs_7_), channel_id=1, source_target_pairs={{0,2},{1,3},{2,0},{3,1},{4,6},{5,7},{6,4},{7,5},{8,10},{9,11},{10,... | collective-permute-start | bytes 3145736 | tf_op jit(solution)/shard_map/ppermute | solution.py:937
  105.3 4.1 collective-permute-start.11
  106.4 3.3 collective-permute-start.10
  136.7 124.0 %collective-permute-start.13 = (bf16[4,2,128,1024]{3,2,1,0:T(8,128)(2,1)}, bf16[4,2,128,1024]{3,2,1,0:T(8,128)(2,1)S(1)}, u32[]{:S(2)}, u32[]{:S(2)}) collective-permute-start(bf16[4,2,128,1024]{3,2,1,0:T(8,128)(2,1)} %get-tuple-element.160), channel_id=1, source_target_pairs={{0,4},{4,0},{8,12},{12,8},{16,20},{20,16},{24,28},{28,24},{1,5},{5... | collective-permute-start | bytes 6291464 | tf_op jit(solution)/shard_map/ppermute | solution.py:912
  192.5 74.0 %collective-permute-start.14 = (bf16[4,2,128,1024]{3,2,1,0:T(8,128)(2,1)}, bf16[4,2,128,1024]{3,2,1,0:T(8,128)(2,1)}, u32[]{:S(2)}, u32[]{:S(2)}) collective-permute-start(bf16[4,2,128,1024]{3,2,1,0:T(8,128)(2,1)} %get-tuple-element.163), channel_id=1, source_target_pairs={{0,4},{4,0},{8,12},{12,8},{16,20},{20,16},{24,28},{28,24},{1,5},{5... | collective-permute-start | bytes 6291464 | tf_op jit(solution)/shard_map/ppermute | solution.py:912
  219.3 7.4 %copy-start.40 = (f32[8,2048]{1,0:T(8,128)S(1)}, f32[8,2048]{1,0:T(8,128)}, u32[]{:S(2)}) copy-start(f32[8,2048]{1,0:T(8,128)} %get-tuple-element.167) | copy-start | bytes 196612
  219.4 7.4 %copy-start.43 = (f32[8,1024]{1,0:T(8,128)S(1)}, f32[8,1024]{1,0:T(8,128)}, u32[]{:S(2)}) copy-start(f32[8,1024]{1,0:T(8,128)} %get-tuple-element.169) | copy-start | bytes 98308
  219.4 7.4 %copy-start.44 = (f32[8,1024]{1,0:T(8,128)S(1)}, f32[8,1024]{1,0:T(8,128)}, u32[]{:S(2)}) copy-start(f32[8,1024]{1,0:T(8,128)} %get-tuple-element.170) | copy-start | bytes 98308
  219.4 3.7 collective-permute-start.12
  219.5 51.3 %collective-permute-start.15 = (bf16[512,1024]{1,0:T(8,128)(2,1)}, bf16[512,1024]{1,0:T(8,128)(2,1)}, u32[]{:S(2)}, u32[]{:S(2)}) collective-permute-start(bf16[512,1024]{1,0:T(8,128)(2,1)} %get-tuple-element.166), channel_id=1, source_target_pairs={{0,1},{1,0},{2,3},{3,2},{4,5},{5,4},{6,7},{7,6},{8,9},{9,8},{10,11... | collective-permute-start | bytes 3145736 | tf_op jit(solution)/shard_map/ppermute | solution.py:934
  226.6 44.2 %collective-permute-start.16 = (bf16[512,1024]{1,0:T(8,128)(2,1)}, bf16[512,1024]{1,0:T(8,128)(2,1)}, u32[]{:S(2)}, u32[]{:S(2)}) collective-permute-start(bf16[512,1024]{1,0:T(8,128)(2,1)} %add_parts.2.refs_0_), channel_id=1, source_target_pairs={{0,2},{1,3},{2,0},{3,1},{4,6},{5,7},{6,4},{7,5},{8,10},{9,11},{10,... | collective-permute-start | bytes 3145736 | tf_op jit(solution)/shard_map/ppermute | solution.py:937
  227.0 2.1 collective-permute-start.17
  230.2 27.4 %collective-permute-start.18 = (f32[8,512]{0,1:T(8,128)S(1)}, f32[8,512]{0,1:T(8,128)S(1)}, u32[]{:S(2)}, u32[]{:S(2)}) collective-permute-start(f32[8,512]{0,1:T(8,128)S(1)} %slice.85), channel_id=1, source_target_pairs={{0,2},{1,3},{2,0},{3,1},{4,6},{5,7},{6,4},{7,5},{8,10},{9,11},{10,... | collective-permute-start | bytes 49160 | tf_op jit(solution)/shard_map/ppermute | solution.py:937
  257.7 64.5 %collective-permute-start.22 = (bf16[4,2,128,1024]{3,2,1,0:T(8,128)(2,1)}, bf16[4,2,128,1024]{3,2,1,0:T(8,128)(2,1)}, u32[]{:S(2)}, u32[]{:S(2)}) collective-permute-start(bf16[4,2,128,1024]{3,2,1,0:T(8,128)(2,1)} %get-tuple-element.184), channel_id=1, source_target_pairs={{0,4},{4,0},{8,12},{12,8},{16,20},{20,16},{24,28},{28,24},{1,5},{5... | collective-permute-start | bytes 6291464 | tf_op jit(solution)/shard_map/ppermute | solution.py:912
  260.8 24.8 %collective-permute-start.19 = (bf16[4,1,128,1024]{3,2,1,0:T(8,128)(2,1)}, bf16[4,1,128,1024]{3,2,1,0:T(8,128)(2,1)}, u32[]{:S(2)}, u32[]{:S(2)}) collective-permute-start(bf16[4,1,128,1024]{3,2,1,0:T(8,128)(2,1)} %get-tuple-element.174), channel_id=1, source_target_pairs={{0,8},{4,12},{8,0},{12,4},{16,24},{20,28},{24,16},{28,20},{1,9},{5... | collective-permute-start | bytes 3145736 | tf_op jit(solution)/shard_map/ppermute | solution.py:912
  270.8 13.0 %copy-start.24 = (bf16[1,1024,128]{2,1,0:T(8,128)(2,1)S(1)}, bf16[1,1024,128]{2,1,0:T(8,128)(2,1)}, u32[]{:S(2)}) copy-start(bf16[1,1024,128]{2,1,0:T(8,128)(2,1)} %copy-done.23) | copy-start | bytes 786436
  270.8 13.1 %copy-start.8 = (bf16[2,1024,128]{2,1,0:T(8,128)(2,1)S(1)}, bf16[2,1024,128]{2,1,0:T(8,128)(2,1)}, u32[]{:S(2)}) copy-start(bf16[2,1024,128]{2,1,0:T(8,128)(2,1)} %hold.10.refs_2_.refs_4_) | copy-start | bytes 1572868
  270.8 13.1 %copy-start.15 = (bf16[1,1024,128]{2,1,0:T(8,128)(2,1)S(1)}, bf16[1,1024,128]{2,1,0:T(8,128)(2,1)}, u32[]{:S(2)}) copy-start(bf16[1,1024,128]{2,1,0:T(8,128)(2,1)} %hold.11.refs_5_) | copy-start | bytes 786436
  281.4 6.5 %collective-permute-start.20 = (bf16[512,1024]{1,0:T(8,128)(2,1)}, bf16[512,1024]{1,0:T(8,128)(2,1)S(1)}, u32[]{:S(2)}, u32[]{:S(2)}) collective-permute-start(bf16[512,1024]{1,0:T(8,128)(2,1)} %get-tuple-element.172.refs_0_.refs_4_), channel_id=1, source_target_pairs={{0,1},{1,0},{2,3},{3,2},{4,5},{5,4},{6,7},{7,6},{8,9},{9,8},{10,11... | collective-permute-start | bytes 3145736 | tf_op jit(solution)/shard_map/ppermute | solution.py:934
  281.4 38.4 %collective-permute-start.21 = (bf16[2,2,128,1024]{3,2,1,0:T(8,128)(2,1)}, bf16[2,2,128,1024]{3,2,1,0:T(8,128)(2,1)}, u32[]{:S(2)}, u32[]{:S(2)}) collective-permute-start(bf16[2,2,128,1024]{3,2,1,0:T(8,128)(2,1)} %get-tuple-element.161.refs_0_), channel_id=1, source_target_pairs={{0,8},{4,12},{8,0},{12,4},{16,24},{20,28},{24,16},{28,20},{1,9},{5... | collective-permute-start | bytes 3145736 | tf_op jit(solution)/shard_map/ppermute | solution.py:912
  315.9 94.2 %collective-permute-start.29 = (bf16[4,2,128,1024]{3,2,1,0:T(8,128)(2,1)}, bf16[4,2,128,1024]{3,2,1,0:T(8,128)(2,1)}, u32[]{:S(2)}, u32[]{:S(2)}) collective-permute-start(bf16[4,2,128,1024]{3,2,1,0:T(8,128)(2,1)} %hold.14), channel_id=1, source_target_pairs={{0,4},{4,0},{8,12},{12,8},{16,20},{20,16},{24,28},{28,24},{1,5},{5... | collective-permute-start | bytes 6291464 | tf_op jit(solution)/shard_map/ppermute | solution.py:912
  317.5 96.8 %collective-permute-start.30 = (bf16[8,4,128,256]{3,2,1,0:T(8,128)(2,1)S(1)}, bf16[8,4,128,256]{3,2,1,0:T(8,128)(2,1)}, u32[]{:S(2)}, u32[]{:S(2)}) collective-permute-start(bf16[8,4,128,256]{3,2,1,0:T(8,128)(2,1)S(1)} %copy-done.6), channel_id=1, source_target_pairs={{0,2},{1,3},{2,0},{3,1},{4,6},{5,7},{6,4},{7,5},{8,10},{9,11},{10,... | collective-permute-start | bytes 6291464 | tf_op jit(solution)/shard_map/ppermute | solution.py:937
  318.0 36.6 %collective-permute-start.23 = (bf16[2,2,128,1024]{3,2,1,0:T(8,128)(2,1)}, bf16[2,2,128,1024]{3,2,1,0:T(8,128)(2,1)S(1)}, u32[]{:S(2)}, u32[]{:S(2)}) collective-permute-start(bf16[2,2,128,1024]{3,2,1,0:T(8,128)(2,1)} %get-tuple-element.164.refs_2_), channel_id=1, source_target_pairs={{0,8},{4,12},{8,0},{12,4},{16,24},{20,28},{24,16},{28,20},{1,9},{5... | collective-permute-start | bytes 3145736 | tf_op jit(solution)/shard_map/ppermute | solution.py:912
  326.3 33.5 %copy-start.42 = (f32[16,1024]{1,0:T(8,128)S(1)}, f32[16,1024]{1,0:T(8,128)}, u32[]{:S(2)}) copy-start(f32[16,1024]{1,0:T(8,128)} %get-tuple-element.205) | copy-start | bytes 196612
  354.2 3.1 collective-permute-start.24
  354.3 48.4 %collective-permute-start.26 = (bf16[2,2,128,1024]{3,2,1,0:T(8,128)(2,1)}, bf16[2,2,128,1024]{3,2,1,0:T(8,128)(2,1)}, u32[]{:S(2)}, u32[]{:S(2)}) collective-permute-start(bf16[2,2,128,1024]{3,2,1,0:T(8,128)(2,1)} %get-tuple-element.185.refs_3_), channel_id=1, source_target_pairs={{0,8},{4,12},{8,0},{12,4},{16,24},{20,28},{24,16},{28,20},{1,9},{5... | collective-permute-start | bytes 3145736 | tf_op jit(solution)/shard_map/ppermute | solution.py:912
  354.7 35.1 %collective-permute-start.25 = (bf16[1,2,128,1024]{3,2,1,0:T(8,128)(2,1)}, bf16[1,2,128,1024]{3,2,1,0:T(8,128)(2,1)}, u32[]{:S(2)}, u32[]{:S(2)}) collective-permute-start(bf16[1,2,128,1024]{3,2,1,0:T(8,128)(2,1)} %get-tuple-element.182.refs_0_), channel_id=1, source_target_pairs={{0,16},{4,20},{8,24},{12,28},{16,0},{20,4},{24,8},{28,12},{1,17},{... | collective-permute-start | bytes 1572872 | tf_op jit(solution)/shard_map/ppermute | solution.py:912
  357.3 47.8 %collective-permute-start.27 = (bf16[2,1,128,1024]{3,2,1,0:T(8,128)(2,1)}, bf16[2,1,128,1024]{3,2,1,0:T(8,128)(2,1)S(1)}, u32[]{:S(2)}, u32[]{:S(2)}) collective-permute-start(bf16[2,1,128,1024]{3,2,1,0:T(8,128)(2,1)} %get-tuple-element.175.refs_3_), channel_id=1, source_target_pairs={{0,16},{4,20},{8,24},{12,28},{16,0},{20,4},{24,8},{28,12},{1,17},{... | collective-permute-start | bytes 1572872 | tf_op jit(solution)/shard_map/ppermute | solution.py:912
  369.0 36.1 %copy-start.30 = (f32[24,1024]{1,0:T(8,128)}, f32[24,1024]{1,0:T(8,128)S(1)}, u32[]{:S(2)}) copy-start(f32[24,1024]{1,0:T(8,128)S(1)} %constant_dynamic-update-slice_fusion.2.refs_1_) | copy-start | bytes 294916
  389.7 18.2 %collective-permute-start.28 = (f32[24,1024]{1,0:T(8,128)S(1)}, f32[24,1024]{1,0:T(8,128)S(1)}, u32[]{:S(2)}, u32[]{:S(2)}) collective-permute-start(f32[24,1024]{1,0:T(8,128)S(1)} %constant_dynamic-update-slice_fusion.2.refs_1_), channel_id=1, source_target_pairs={{0,1},{1,0},{2,3},{3,2},{4,5},{5,4},{6,7},{7,6},{8,9},{9,8},{10,11... | collective-permute-start | bytes 294920 | tf_op jit(solution)/shard_map/ppermute | solution.py:899
  424.1 3.4 collective-permute-start.31
  424.1 28.2 %collective-permute-start.34 = (bf16[4,1,128,1024]{3,2,1,0:T(8,128)(2,1)}, bf16[4,1,128,1024]{3,2,1,0:T(8,128)(2,1)}, u32[]{:S(2)}, u32[]{:S(2)}) collective-permute-start(bf16[4,1,128,1024]{3,2,1,0:T(8,128)(2,1)} %hold.17), channel_id=1, source_target_pairs={{0,4},{4,0},{8,12},{12,8},{16,20},{20,16},{24,28},{28,24},{1,5},{5... | collective-permute-start | bytes 3145736 | tf_op jit(solution)/shard_map/ppermute | solution.py:912
  424.7 26.1 %collective-permute-start.32 = (bf16[1,2,128,1024]{3,2,1,0:T(8,128)(2,1)}, bf16[1,2,128,1024]{3,2,1,0:T(8,128)(2,1)}, u32[]{:S(2)}, u32[]{:S(2)}) collective-permute-start(bf16[1,2,128,1024]{3,2,1,0:T(8,128)(2,1)} %get-tuple-element.193.refs_0_), channel_id=1, source_target_pairs={{0,16},{4,20},{8,24},{12,28},{16,0},{20,4},{24,8},{28,12},{1,17},{... | collective-permute-start | bytes 1572872 | tf_op jit(solution)/shard_map/ppermute | solution.py:912
  424.7 60.9 %collective-permute-start.36 = (bf16[2,2,128,1024]{3,2,1,0:T(8,128)(2,1)}, bf16[2,2,128,1024]{3,2,1,0:T(8,128)(2,1)S(1)}, u32[]{:S(2)}, u32[]{:S(2)}) collective-permute-start(bf16[2,2,128,1024]{3,2,1,0:T(8,128)(2,1)} %get-tuple-element.208.refs_0_), channel_id=1, source_target_pairs={{0,8},{4,12},{8,0},{12,4},{16,24},{20,28},{24,16},{28,20},{1,9},{5... | collective-permute-start | bytes 3145736 | tf_op jit(solution)/shard_map/ppermute | solution.py:912
  427.5 80.9 %collective-permute-start.39 = (bf16[512,1024]{1,0:T(8,128)(2,1)}, bf16[512,1024]{1,0:T(8,128)(2,1)}, u32[]{:S(2)}, u32[]{:S(2)}) collective-permute-start(bf16[512,1024]{1,0:T(8,128)(2,1)} %hold.19), channel_id=1, source_target_pairs={{0,1},{1,0},{2,3},{3,2},{4,5},{5,4},{6,7},{7,6},{8,9},{9,8},{10,11... | collective-permute-start | bytes 3145736 | tf_op jit(solution)/shard_map/ppermute | solution.py:934
  427.5 23.3 %copy-start.1 = (bf16[4,4,128,256]{3,2,1,0:T(8,128)(2,1)S(1)}, bf16[4,4,128,256]{3,2,1,0:T(8,128)(2,1)}, u32[]{:S(2)}) copy-start(bf16[4,4,128,256]{3,2,1,0:T(8,128)(2,1)} %get-tuple-element.209.refs_1_.refs_0_) | copy-start | bytes 3145732
  427.5 24.8 %copy-start.26 = (f32[24,1024]{1,0:T(8,128)S(1)}, f32[24,1024]{1,0:T(8,128)}, u32[]{:S(2)}) copy-start(f32[24,1024]{1,0:T(8,128)} %add_small.5.refs_0_.refs_1_) | copy-start | bytes 294916
  427.5 31.3 %copy-start.31 = (bf16[1,1,128,1024]{3,2,1,0:T(8,128)(2,1)S(1)}, bf16[1,1,128,1024]{3,2,1,0:T(8,128)(2,1)}, u32[]{:S(2)}) copy-start(bf16[1,1,128,1024]{3,2,1,0:T(8,128)(2,1)} %get-tuple-element.204.refs_0_) | copy-start | bytes 786436
  430.9 77.4 %collective-permute-start.40 = (bf16[512,1024]{1,0:T(8,128)(2,1)}, bf16[512,1024]{1,0:T(8,128)(2,1)}, u32[]{:S(2)}, u32[]{:S(2)}) collective-permute-start(bf16[512,1024]{1,0:T(8,128)(2,1)} %add_parts.3.refs_2_), channel_id=1, source_target_pairs={{0,2},{1,3},{2,0},{3,1},{4,6},{5,7},{6,4},{7,5},{8,10},{9,11},{10,... | collective-permute-start | bytes 3145736 | tf_op jit(solution)/shard_map/ppermute | solution.py:937
  450.8 62.5 %collective-permute-start.41 = (bf16[4,4,128,256]{3,2,1,0:T(8,128)(2,1)S(1)}, bf16[4,4,128,256]{3,2,1,0:T(8,128)(2,1)S(1)}, u32[]{:S(2)}, u32[]{:S(2)}) collective-permute-start(bf16[4,4,128,256]{3,2,1,0:T(8,128)(2,1)S(1)} %copy-done.1), channel_id=1, source_target_pairs={{0,4},{4,0},{8,12},{12,8},{16,20},{20,16},{24,28},{28,24},{1,5},{5... | collective-permute-start | bytes 3145736 | tf_op jit(solution)/shard_map/ppermute | solution.py:912
  452.3 6.5 %collective-permute-start.33 = (f32[24,1024]{1,0:T(8,128)S(1)}, f32[24,1024]{1,0:T(8,128)S(1)}, u32[]{:S(2)}, u32[]{:S(2)}) collective-permute-start(f32[24,1024]{1,0:T(8,128)S(1)} %copy-done.26), channel_id=1, source_target_pairs={{0,2},{1,3},{2,0},{3,1},{4,6},{5,7},{6,4},{7,5},{8,10},{9,11},{10,... | collective-permute-start | bytes 294920 | tf_op jit(solution)/shard_map/ppermute | solution.py:899
  458.8 25.2 %copy-start.35 = (f32[24,1024]{1,0:T(8,128)}, f32[24,1024]{1,0:T(8,128)S(1)}, u32[]{:S(2)}) copy-start(f32[24,1024]{1,0:T(8,128)S(1)} %collective-permute-done.33.refs_2_) | copy-start | bytes 294916
  458.8 22.7 %collective-permute-start.35 = (bf16[1,1,128,1024]{3,2,1,0:T(8,128)(2,1)S(1)}, bf16[1,1,128,1024]{3,2,1,0:T(8,128)(2,1)S(1)}, u32[]{:S(2)}, u32[]{:S(2)}) collective-permute-start(bf16[1,1,128,1024]{3,2,1,0:T(8,128)(2,1)S(1)} %copy-done.31), channel_id=1, source_target_pairs={{0,4},{4,0},{8,12},{12,8},{16,20},{20,16},{24,28},{28,24},{1,5},{5... | collective-permute-start | bytes 786440 | tf_op jit(solution)/shard_map/ppermute | solution.py:912
  481.5 24.5 %collective-permute-start.38 = (bf16[1,2,128,1024]{3,2,1,0:T(8,128)(2,1)}, bf16[1,2,128,1024]{3,2,1,0:T(8,128)(2,1)}, u32[]{:S(2)}, u32[]{:S(2)}) collective-permute-start(bf16[1,2,128,1024]{3,2,1,0:T(8,128)(2,1)} %get-tuple-element.202.refs_0_), channel_id=1, source_target_pairs={{0,16},{4,20},{8,24},{12,28},{16,0},{20,4},{24,8},{28,12},{1,17},{... | collective-permute-start | bytes 1572872 | tf_op jit(solution)/shard_map/ppermute | solution.py:912
  485.6 4.8 collective-permute-start.37
  490.4 56.8 %collective-permute-start.43 = (bf16[2,1,128,1024]{3,2,1,0:T(8,128)(2,1)}, bf16[2,1,128,1024]{3,2,1,0:T(8,128)(2,1)S(1)}, u32[]{:S(2)}, u32[]{:S(2)}) collective-permute-start(bf16[2,1,128,1024]{3,2,1,0:T(8,128)(2,1)} %get-tuple-element.217.refs_0_), channel_id=1, source_target_pairs={{0,8},{4,12},{8,0},{12,4},{16,24},{20,28},{24,16},{28,20},{1,9},{5... | collective-permute-start | bytes 1572872 | tf_op jit(solution)/shard_map/ppermute | solution.py:912
  505.9 47.1 %collective-permute-start.44 = (bf16[1,2,128,1024]{3,2,1,0:T(8,128)(2,1)}, bf16[1,2,128,1024]{3,2,1,0:T(8,128)(2,1)S(1)}, u32[]{:S(2)}, u32[]{:S(2)}) collective-permute-start(bf16[1,2,128,1024]{3,2,1,0:T(8,128)(2,1)} %get-tuple-element.220.refs_0_), channel_id=1, source_target_pairs={{0,16},{4,20},{8,24},{12,28},{16,0},{20,4},{24,8},{28,12},{1,17},{... | collective-permute-start | bytes 1572872 | tf_op jit(solution)/shard_map/ppermute | solution.py:912
  514.2 8.2 %copy-start.28 = (f32[24,1024]{1,0:T(8,128)S(1)}, f32[24,1024]{1,0:T(8,128)}, u32[]{:S(2)}) copy-start(f32[24,1024]{1,0:T(8,128)} %add_small.7.refs_2_.refs_1_) | copy-start | bytes 294916
  519.6 36.5 %collective-permute-start.45 = (bf16[2,4,128,256]{3,2,1,0:T(8,128)(2,1)}, bf16[2,4,128,256]{3,2,1,0:T(8,128)(2,1)S(1)}, u32[]{:S(2)}, u32[]{:S(2)}) collective-permute-start(bf16[2,4,128,256]{3,2,1,0:T(8,128)(2,1)} %get-tuple-element.228.refs_0_), channel_id=1, source_target_pairs={{0,8},{4,12},{8,0},{12,4},{16,24},{20,28},{24,16},{28,20},{1,9},{5... | collective-permute-start | bytes 1572872 | tf_op jit(solution)/shard_map/ppermute | solution.py:912
  522.4 22.6 %collective-permute-start.42 = (f32[24,1024]{1,0:T(8,128)S(1)}, f32[24,1024]{1,0:T(8,128)S(1)}, u32[]{:S(2)}, u32[]{:S(2)}) collective-permute-start(f32[24,1024]{1,0:T(8,128)S(1)} %copy-done.28), channel_id=1, source_target_pairs={{0,8},{4,12},{8,0},{12,4},{16,24},{20,28},{24,16},{28,20},{1,9},{5... | collective-permute-start | bytes 294920 | tf_op jit(solution)/shard_map/ppermute | solution.py:899
  550.0 27.4 %collective-permute-start.47 = (bf16[1,1,128,1024]{3,2,1,0:T(8,128)(2,1)}, bf16[1,1,128,1024]{3,2,1,0:T(8,128)(2,1)S(1)}, u32[]{:S(2)}, u32[]{:S(2)}) collective-permute-start(bf16[1,1,128,1024]{3,2,1,0:T(8,128)(2,1)} %get-tuple-element.230.refs_2_), channel_id=1, source_target_pairs={{0,16},{4,20},{8,24},{12,28},{16,0},{20,4},{24,8},{28,12},{1,17},{... | collective-permute-start | bytes 786440 | tf_op jit(solution)/shard_map/ppermute | solution.py:912
  550.1 23.8 %collective-permute-start.46 = (f32[24,1024]{1,0:T(8,128)S(1)}, f32[24,1024]{1,0:T(8,128)S(1)}, u32[]{:S(2)}, u32[]{:S(2)}) collective-permute-start(f32[24,1024]{1,0:T(8,128)S(1)} %copy-done.27), channel_id=1, source_target_pairs={{0,16},{4,20},{8,24},{12,28},{16,0},{20,4},{24,8},{28,12},{1,17},{... | collective-permute-start | bytes 294920 | tf_op jit(solution)/shard_map/ppermute | solution.py:899
  560.2 22.5 %collective-permute-start.48 = (bf16[1,4,128,256]{3,2,1,0:T(8,128)(2,1)}, bf16[1,4,128,256]{3,2,1,0:T(8,128)(2,1)S(1)}, u32[]{:S(2)}, u32[]{:S(2)}) collective-permute-start(bf16[1,4,128,256]{3,2,1,0:T(8,128)(2,1)} %get-tuple-element.234.refs_0_), channel_id=1, source_target_pairs={{0,16},{4,20},{8,24},{12,28},{16,0},{20,4},{24,8},{28,12},{1,17},{... | collective-permute-start | bytes 786440 | tf_op jit(solution)/shard_map/ppermute | solution.py:912
  (34 other events, 68.9 us)

commit v3 on v2

--- a/solution.py
+++ b/solution.py
@@ -70,34 +70,34 @@
     return dots, out, rg
 
 
-def stage_grads(ST, UA, DA, me, up_order, dn_order):
-    bits = len(up_order)
+def stage_grads(ST, UA, DA, me, order, whole):
+    bits = len(order)
     blk = UA.shape[0] >> bits
 
     def body(c, _):
         r = pl.ds(pl.multiple_of(c * blk, blk), blk)
-        ST[slot_of(c ^ me, up_order), 0] = UA[r, :].astype(BF)
-        ST[slot_of(c ^ me, dn_order), 1] = DA[r, :].astype(BF)
+        slot = jnp.where(whole, c, slot_of(c ^ me, order))
+        ST[slot, 0] = UA[r, :].astype(BF)
+        ST[slot, 1] = DA[r, :].astype(BF)
         return 0
     lax.fori_loop(0, 1 << bits, body, 0)
 
 
-def column(v, n):
-    return jnp.broadcast_to(v, (v.shape[0], n))
+def dots_rows(dots):
+    return jnp.broadcast_to(dots, (dots.shape[0], 128)).T[0:PIECE, :]
 
 
 def dense_kernel(cfg, me_ref, *refs):
-    chunks, rows, tm, lanes, orders, first, deps = cfg
+    chunks, rows, tm, lanes, order, first, deps = cfg
     it = iter(refs[deps:])
     take = lambda k: [next(it) for _ in range(k)]
     x_hbm, dy_hbm = take(chunks), take(chunks)
     rm, up_hbm, dn_hbm = take(3)
     base_o, base_r, sums_in = ([], [], []) if first else (take(chunks), take(chunks), take(2))
     out_refs, rg_refs = take(chunks), take(chunks)
-    dots_ref, = take(1)
-    ends = take(2) if first else take(4)
-    X, DY, UP, DN, UA, DA, OB, RB, xsem, wsem, gsem, osem = take(12)
-    ST, BO, BR, bsem = (None,) * 4 if first else take(4)
+    ends = take(2)
+    X, DY, UP, DN, UA, DA, OB, RB, DT, OD, xsem, wsem, gsem, osem, dsem = take(15)
+    ST, BO, BR, BD, bsem = (None,) * 5 if first else take(5)
     per = rows // tm
     weights = [pltpu.make_async_copy(up_hbm, UP, wsem.at[0]), pltpu.make_async_copy(dn_hbm, DN, wsem.at[1])]
     loads, bases = [], []
@@ -105,10 +105,12 @@
         sl = pl.ds(q * rows, rows)
         loads.append([pltpu.make_async_copy(x_hbm[q], X.at[sl], xsem.at[q]), pltpu.make_async_copy(dy_hbm[q], DY.at[sl], xsem.at[chunks + q])])
         if not first:
-            bases.append([pltpu.make_async_copy(base_o[q], BO.at[sl], bsem.at[q]), pltpu.make_async_copy(base_r[q], BR.at[sl], bsem.at[chunks + q])])
+            bases.append([pltpu.make_async_copy(base_o[q], BO.at[sl], bsem.at[q]), pltpu.make_async_copy(base_r[q].at[pl.ds(0, rows)], BR.at[sl], bsem.at[chunks + q]),
+                          pltpu.make_async_copy(base_r[q].at[pl.ds(rows, PIECE)], BD.at[q], bsem.at[2 * chunks + q])])
     sums = [] if first else [pltpu.make_async_copy(sums_in[0], UA, gsem.at[0]), pltpu.make_async_copy(sums_in[1], DA, gsem.at[1])]
     for c in loads[0] + weights + sums + [c for q in loads[1:] for c in q] + [c for q in bases for c in q]:
         c.start()
+    DT[...] = jnp.zeros_like(DT)
     if first:
         UA[...] = jnp.zeros_like(UA)
         DA[...] = jnp.zeros_like(DA)
@@ -136,7 +138,13 @@
                     for c in sums:
                         c.wait()
         dots, out, rg = ffn_tile(lanes, rm, X[sl, :], DY[sl, :], lambda l, m: pick_lane(m, lanes), UP, DN, UA, DA, ready)
-        dots_ref[:, sl] = column(dots, 128).T[0:8, :]
+        lines = dots_rows(dots)
+        line = lax.broadcasted_iota(jnp.int32, lines.shape, 0)
+        for q in range(chunks):
+            for part in range(per):
+                @pl.when(i == q * per + part)
+                def _(q=q, part=part):
+                    DT[q, :, part * tm:(part + 1) * tm] = jnp.where(line == 0, lines, 0.0)
         if not first:
             for q in range(chunks):
                 @pl.when(i == q * per)
@@ -160,14 +168,17 @@
                         c.start()
         return 0
     lax.fori_loop(0, chunks * per, one, 0)
-    row = lax.broadcasted_iota(jnp.int32, dots_ref.shape, 0)
-    dots_ref[...] = jnp.where(row == 0, dots_ref[...], 0.0)
+    lines = []
+    for q in range(chunks):
+        total = DT[q] if first else DT[q] + BD[q].astype(F32)
+        OD[q] = total.astype(BF)
+        lines.append(pltpu.make_async_copy(OD.at[q], rg_refs[q].at[pl.ds(rows, PIECE)], dsem.at[q]))
     if first:
-        last = [pltpu.make_async_copy(UA, ends[0], gsem.at[0]), pltpu.make_async_copy(DA, ends[1], gsem.at[1])]
+        last = lines + [pltpu.make_async_copy(UA, ends[0], gsem.at[0]), pltpu.make_async_copy(DA, ends[1], gsem.at[1])]
     else:
-        stage_grads(ST, UA, DA, me_ref[0], *orders)
+        stage_grads(ST, UA, DA, me_ref[0], order, False)
         half = ST.shape[0] // 2
-        last = [pltpu.make_async_copy(ST.at[pl.ds(h * half, half), pl.ds(m, 1)], ends[2 * m + h], bsem.at[2 * m + h]) for m in range(2) for h in range(2)]
+        last = lines + [pltpu.make_async_copy(ST.at[pl.ds(h * half, half)], ends[h], gsem.at[h]) for h in range(2)]
     for c in last:
         c.start()
     for slot in range(min(2, chunks * per)):
@@ -177,41 +188,41 @@
         c.wait()
 
 
-def ffn_dense(me, xs, dys, rm, up, down, lanes, orders, base=None, sums=None, deps=()):
+def ffn_dense(me, xs, dys, rm, up, down, lanes, order, base=None, sums=None, deps=()):
     chunks = len(xs)
     rows, d = xs[0].shape
     f = up.shape[1]
     n = chunks * rows
     tm = min(TILE_DENSE, rows)
     first = base is None
-    bits = len(orders[0])
+    bits = len(order)
     half = 1 << (bits - 1)
     vm = pl.BlockSpec(memory_space=pltpu.VMEM)
-    part = jax.ShapeDtypeStruct((rows, d), BF)
+    part, lined = jax.ShapeDtypeStruct((rows, d), BF), jax.ShapeDtypeStruct((rows + PIECE, d), BF)
     total = jax.ShapeDtypeStruct((d, f), F32)
-    grad = jax.ShapeDtypeStruct((half, 1, d >> bits, f), BF)
-    ends = [total] * 2 if first else [grad] * 4
+    grad = jax.ShapeDtypeStruct((half, 2, d >> bits, f), BF)
+    ends = [total] * 2 if first else [grad] * 2
     more = [] if first else list(base[0]) + list(base[1]) + list(sums)
     scratch = [pltpu.VMEM((n, d), BF), pltpu.VMEM((n, d), BF), pltpu.VMEM((d, f), BF), pltpu.VMEM((f, d), BF), pltpu.VMEM((d, f), F32), pltpu.VMEM((d, f), F32),
-               pltpu.VMEM((2, tm, d), BF), pltpu.VMEM((2, tm, d), BF),
-               pltpu.SemaphoreType.DMA((2 * chunks,)), pltpu.SemaphoreType.DMA((2,)), pltpu.SemaphoreType.DMA((2,)), pltpu.SemaphoreType.DMA((2, 2))]
+               pltpu.VMEM((2, tm, d), BF), pltpu.VMEM((2, tm, d), BF), pltpu.VMEM((chunks, PIECE, d), F32), pltpu.VMEM((chunks, PIECE, d), BF),
+               pltpu.SemaphoreType.DMA((2 * chunks,)), pltpu.SemaphoreType.DMA((2,)), pltpu.SemaphoreType.DMA((2,)), pltpu.SemaphoreType.DMA((2, 2)), pltpu.SemaphoreType.DMA((chunks,))]
     if not first:
-        scratch += [pltpu.VMEM((2 * half, 2, d >> bits, f), BF), pltpu.VMEM((n, d), BF), pltpu.VMEM((n, d), BF), pltpu.SemaphoreType.DMA((max(4, 2 * chunks),))]
+        scratch += [pltpu.VMEM((2 * half, 2, d >> bits, f), BF), pltpu.VMEM((n, d), BF), pltpu.VMEM((n, d), BF), pltpu.VMEM((chunks, PIECE, d), BF), pltpu.SemaphoreType.DMA((3 * chunks,))]
     res = pl.pallas_call(
-        partial(dense_kernel, (chunks, rows, tm, lanes, orders, first, len(deps))),
+        partial(dense_kernel, (chunks, rows, tm, lanes, order, first, len(deps))),
         name="ffn_dense",
-        out_shape=[part] * (2 * chunks) + [jax.ShapeDtypeStruct((8, n), F32)] + ends,
+        out_shape=[part] * chunks + [lined] * chunks + ends,
         in_specs=[SMEM] + [ANY] * (len(deps) + 2 * chunks) + [vm] + [ANY] * (2 + len(more)),
-        out_specs=[ANY] * (2 * chunks) + [vm] + [ANY] * len(ends),
+        out_specs=[ANY] * (2 * chunks + len(ends)),
         scratch_shapes=scratch,
         cost_estimate=SMALL,
         compiler_params=pltpu.CompilerParams(vmem_limit_bytes=VMEM),
     )(me, *deps, *xs, *dys, rm, up, down, *more)
-    return res[:chunks], res[chunks:2 * chunks], res[2 * chunks], res[2 * chunks + 1:]
+    return res[:chunks], res[chunks:2 * chunks], res[2 * chunks:]
 
 
 def expert_kernel(cfg, me_ref, blk_ref, bnd_ref, *refs):
-    first, count, chunks, rows, d, tm, lanes, order, has, deps = cfg
+    first, count, whole, chunks, rows, d, tm, lanes, order, has, deps = cfg
     n = chunks * rows
     it = iter(refs[deps:])
     take = lambda k: [next(it) for _ in range(k)]
@@ -220,9 +231,8 @@
     based = [q for q in range(chunks) if has[q]]
     base_o, base_r = take(len(based)), take(len(based))
     out_refs, rg_refs = take(chunks), take(chunks)
-    dots_ref, = take(1)
-    keep_refs, send_refs = take(count), take(count)
-    X, DY, UP, DN, UA, DA, ST, XG, DG, VAL, OA, RA, DOT, TR, TL, TH, xsem, wsem, gsem, osem = it
+    whole_refs, keep_refs, send_refs = take(whole), take(count - whole), take(count - whole)
+    X, DY, UP, DN, UA, DA, ST, XG, DG, VAL, OA, RA, DOT, BD, TR, TL, TH, xsem, wsem, gsem, osem, dsem = it
     half = ST.shape[0] // 2
     pieces = tm // PIECE
     rows_of = [pl.ds(q * rows, rows) for q in range(chunks)]
@@ -233,13 +243,17 @@
     earlier = []
     for k, q in enumerate(based):
         earlier.append(pltpu.make_async_copy(base_o[k], X.at[rows_of[q]], xsem.at[q]))
-        earlier.append(pltpu.make_async_copy(base_r[k], DY.at[rows_of[q]], xsem.at[chunks + q]))
+        earlier.append(pltpu.make_async_copy(base_r[k].at[pl.ds(0, rows)], DY.at[rows_of[q]], xsem.at[chunks + q]))
+        earlier.append(pltpu.make_async_copy(base_r[k].at[pl.ds(rows, PIECE)], BD.at[q], dsem.at[q]))
 
     def weights(e, slot):
         return [pltpu.make_async_copy(up_hbm.at[first + e], UP.at[slot], wsem.at[slot, 0]),
                 pltpu.make_async_copy(dn_hbm.at[first + e], DN.at[slot], wsem.at[slot, 1])]
 
     def flush(g):
+        if g < whole:
+            return [pltpu.make_async_copy(ST, whole_refs[g], gsem.at[0])]
+        g = g - whole
         return [pltpu.make_async_copy(ST.at[pl.ds(0, half)], keep_refs[g], gsem.at[0]),
                 pltpu.make_async_copy(ST.at[pl.ds(half, half)], send_refs[g], gsem.at[1])]
 
@@ -302,7 +316,7 @@
             def coef_of(logits, mixing):
                 return pick_lane(mixing, lanes + 1) * pick_lane(lane_softmax(logits, 0, lanes), first + e) * valid
             dots, out, rg = ffn_tile(lanes, rm, XG[...], DG[...], coef_of, UP.at[slot], DN.at[slot], UA, DA, lambda: None)
-            dots = column(dots * valid, 128)
+            dots = jnp.broadcast_to(dots * valid, (tm, 128))
             for p in range(pieces):
                 r = pl.ds(pl.multiple_of(TR[base + p], PIECE), PIECE)
                 s = slice(p * PIECE, (p + 1) * PIECE)
@@ -317,11 +331,12 @@
             for c in earlier:
                 c.start()
 
-        @pl.when(e > 0)
-        def _():
-            for c in flush(0):
-                c.wait()
-        stage_grads(ST, UA, DA, me_ref[0], order, order)
+        for g in range(count - 1):
+            @pl.when(e == g + 1)
+            def _(g=g):
+                for c in flush(g):
+                    c.wait()
+        stage_grads(ST, UA, DA, me_ref[0], order, e < whole)
         for g in range(count):
             @pl.when(e == g)
             def _(g=g):
@@ -332,6 +347,8 @@
     for c in earlier:
         c.wait()
     last = []
+    step = min(256, rows)
+    line = lax.broadcasted_iota(jnp.int32, (PIECE, step), 0)
     for q in range(chunks):
         r = rows_of[q]
         o, g = OA[r, :], RA[r, :]
@@ -339,19 +356,21 @@
             o, g = o + X[r, :].astype(F32), g + DY[r, :].astype(F32)
         X[r, :] = o.astype(BF)
         DY[r, :] = g.astype(BF)
-        last += [pltpu.make_async_copy(X.at[r], out_refs[q], osem.at[0, q]), pltpu.make_async_copy(DY.at[r], rg_refs[q], osem.at[1, q])]
-        for c in last[-2:]:
+        if not has[q]:
+            BD[q] = jnp.zeros(BD.shape[1:], BF)
+        for i in range(rows // step):
+            sl = slice(i * step, (i + 1) * step)
+            dots = jnp.where(line == 1, DOT[pl.ds(q * rows + i * step, step), :].T[0:PIECE, :], 0.0)
+            BD[q, :, sl] = (BD[q, :, sl].astype(F32) + dots).astype(BF)
+        last += [pltpu.make_async_copy(X.at[r], out_refs[q], osem.at[0, q]), pltpu.make_async_copy(DY.at[r], rg_refs[q].at[pl.ds(0, rows)], osem.at[1, q]),
+                 pltpu.make_async_copy(BD.at[q], rg_refs[q].at[pl.ds(rows, PIECE)], dsem.at[q])]
+        for c in last[-3:]:
             c.start()
-    step = min(256, rows)
-    row = lax.broadcasted_iota(jnp.int32, (8, step), 0)
-    for i in range(n // step):
-        sl = pl.ds(i * step, step)
-        dots_ref[:, sl] = jnp.where(row == 1, DOT[sl, :].T[0:8, :], 0.0)
-    for c in last + flush(0):
+    for c in last + flush(count - 1):
         c.wait()
 
 
-def ffn_experts(me, blocks, bounds, xs, dys, rm, up, down, first, count, base, order, deps=()):
+def ffn_experts(me, blocks, bounds, xs, dys, rm, up, down, first, count, whole, base, order, deps=()):
     chunks = len(xs)
     rows, d = xs[0].shape
     lanes, _, f = up.shape
@@ -359,31 +378,31 @@
     tm = TILE_EXPERT
     bits = len(order)
     half = 1 << (bits - 1)
-    grad = jax.ShapeDtypeStruct((half, 2, d >> bits, f), BF)
-    part = jax.ShapeDtypeStruct((rows, d), BF)
+    grad, entire = [jax.ShapeDtypeStruct((k * half, 2, d >> bits, f), BF) for k in (1, 2)]
+    part, lined = jax.ShapeDtypeStruct((rows, d), BF), jax.ShapeDtypeStruct((rows + PIECE, d), BF)
     table = n // PIECE + chunks * lanes + 2 * tm // PIECE
     vm = pl.BlockSpec(memory_space=pltpu.VMEM)
     has = tuple(b is not None for b in base[0])
     more = [b for k in range(2) for b in base[k] if b is not None]
     res = pl.pallas_call(
-        partial(expert_kernel, (first, count, chunks, rows, d, tm, lanes, order, has, len(deps))),
+        partial(expert_kernel, (first, count, whole, chunks, rows, d, tm, lanes, order, has, len(deps))),
         name="ffn_experts",
-        out_shape=[part] * (2 * chunks) + [jax.ShapeDtypeStruct((8, n), F32)] + [grad] * (2 * count),
+        out_shape=[part] * chunks + [lined] * chunks + [entire] * whole + [grad] * (2 * (count - whole)),
         in_specs=[SMEM] * 3 + [ANY] * (len(deps) + 2 * chunks) + [vm] + [ANY] * (2 + len(more)),
-        out_specs=[ANY] * (2 * chunks) + [vm] + [ANY] * (2 * count),
+        out_specs=[ANY] * (2 * chunks + 2 * count - whole),
         scratch_shapes=[
             pltpu.VMEM((n, d), BF), pltpu.VMEM((n, d), BF), pltpu.VMEM((2, d, f), BF), pltpu.VMEM((2, f, d), BF),
             pltpu.VMEM((d, f), F32), pltpu.VMEM((d, f), F32), pltpu.VMEM((2 * half, 2, d >> bits, f), BF),
             pltpu.VMEM((tm, d), BF), pltpu.VMEM((tm, d), BF), pltpu.VMEM((tm, 128), F32),
-            pltpu.VMEM((n, d), F32), pltpu.VMEM((n, d), F32), pltpu.VMEM((n, 128), F32),
+            pltpu.VMEM((n, d), F32), pltpu.VMEM((n, d), F32), pltpu.VMEM((n, 128), F32), pltpu.VMEM((chunks, PIECE, d), BF),
             pltpu.SMEM((table,), jnp.int32), pltpu.SMEM((table,), jnp.int32), pltpu.SMEM((table,), jnp.int32),
-            pltpu.SemaphoreType.DMA((2 * chunks,)), pltpu.SemaphoreType.DMA((2, 2)), pltpu.SemaphoreType.DMA((2,)), pltpu.SemaphoreType.DMA((2, chunks)),
+            pltpu.SemaphoreType.DMA((2 * chunks,)), pltpu.SemaphoreType.DMA((2, 2)), pltpu.SemaphoreType.DMA((2,)), pltpu.SemaphoreType.DMA((2, chunks)), pltpu.SemaphoreType.DMA((chunks,)),
         ],
         cost_estimate=SMALL,
         compiler_params=pltpu.CompilerParams(vmem_limit_bytes=VMEM),
     )(me, blocks, bounds, *deps, *xs, *dys, rm, up, down, *more)
-    at = 2 * chunks + 1
-    return res[:chunks], res[chunks:2 * chunks], res[2 * chunks], res[at:at + count], res[at + count:]
+    at = 2 * chunks + whole
+    return res[:chunks], res[chunks:2 * chunks], res[2 * chunks:at], res[at:at + count - whole], res[at + count - whole:]
 
 
 def split_add_kernel(deps, *refs):
@@ -410,15 +429,17 @@
 
 
 def last_add_kernel(deps, turns, *refs):
-    kept, came = refs[deps:deps + 2]
+    terms = refs[deps:-len(turns)]
     outs = refs[-len(turns):]
     for k, turned in enumerate(turns):
-        total = kept[0, k].astype(F32) + came[0, k].astype(F32)
+        total = terms[0][0, k].astype(F32)
+        for v in terms[1:]:
+            total = total + v[0, k].astype(F32)
         outs[k][...] = (total.T if turned else total).reshape(outs[k].shape)
 
 
-def last_add(kept, came, turns, place=None, stacks=None, deps=()):
-    _, m, blk, f = kept.shape
+def last_add(terms, turns, place=None, stacks=None, deps=()):
+    _, m, blk, f = terms[0].shape
     shapes = [(f, blk) if turned else (blk, f) for turned in turns]
     aliases = {}
     if place is None:
@@ -436,13 +457,13 @@
         partial(last_add_kernel, len(deps), turns),
         name="last_add",
         grid=(1,),
-        in_specs=[ANY] * len(deps) + [full, full],
+        in_specs=[ANY] * len(deps) + [full] * len(terms),
         out_specs=out_specs,
         out_shape=out_shape,
         input_output_aliases=aliases,
         cost_estimate=SMALL,
         compiler_params=pltpu.CompilerParams(vmem_limit_bytes=VMEM),
-    )(*deps, kept, came)
+    )(*deps, *terms)
 
 
 def hold(v, deps):
@@ -755,13 +776,16 @@
 def middle_backward_kernel(single, bnd_ref, t_ref, *refs):
     it = iter(refs)
     parts = [next(it) for _ in range(single)]
-    dots, n2, rm, middle, dy, gain, pos, mg_ref, mc_ref, sums_ref = it
+    n2, rm, middle, dy, gain, pos, mg_ref, mc_ref, sums_ref = it
     t = t_ref[0]
-    total = parts[0][...].astype(F32)
-    for p in parts[1:]:
-        total = total + p[...].astype(F32)
     n2v, rmv = n2[...], rm[...]
     rows = n2v.shape[0]
+    total = parts[0][0:rows, :].astype(F32)
+    lines = parts[0][rows:rows + PIECE, 0:rows].astype(F32)
+    for p in parts[1:]:
+        total = total + p[0:rows, :].astype(F32)
+        lines = lines + p[rows:rows + PIECE, 0:rows].astype(F32)
+    dots = jnp.concatenate([lines, jnp.zeros((128 - PIECE, rows), F32)], axis=0).T
     experts = bnd_ref.shape[1] - 1
     logits = dot(n2v, rmv, 1, 0)
     route_prob = lane_softmax(logits, 0, experts)
@@ -793,7 +817,7 @@
     mc_ref[...] = mg.astype(BF)
 
 
-def middle_backward(bounds, t, parts, dots, n2, rm, middle, dy, gain, pos, deps=()):
+def middle_backward(bounds, t, parts, n2, rm, middle, dy, gain, pos, deps=()):
     rows, d = n2.shape
     fixed = lambda shape: pl.BlockSpec(shape, lambda p, *_: (0, 0))
     big = fixed((rows, d))
@@ -802,13 +826,13 @@
         name="middle_backward",
         grid_spec=pltpu.PrefetchScalarGridSpec(
             num_scalar_prefetch=2, grid=(1,),
-            in_specs=[ANY] * len(deps) + [big] * len(parts)
-            + [fixed((rows, 8)), big, fixed((d, 128)), big, big, fixed((1, d)), fixed((rows, 1))],
+            in_specs=[ANY] * len(deps) + [fixed((rows + PIECE, d))] * len(parts)
+            + [big, fixed((d, 128)), big, big, fixed((1, d)), fixed((rows, 1))],
             out_specs=[big, big, fixed((16, d))]),
         out_shape=[jax.ShapeDtypeStruct((rows, d), F32), jax.ShapeDtypeStruct((rows, d), BF), jax.ShapeDtypeStruct((16, d), F32)],
         cost_estimate=SMALL,
         compiler_params=pltpu.CompilerParams(vmem_limit_bytes=VMEM),
-    )(bounds, t, *deps, *parts, dots, n2, rm, middle, dy, gain, pos)
+    )(bounds, t, *deps, *parts, n2, rm, middle, dy, gain, pos)
 
 
 def layer_out_kernel(*refs):
@@ -845,11 +869,11 @@
 
 def add_parts(parts, deps=()):
     rows, d = parts[0].shape
-    tile = pl.BlockSpec((rows // 2, d), lambda p: (p, 0))
+    tile = pl.BlockSpec((rows, d), lambda p: (p, 0))
     return pl.pallas_call(
         skip(add_parts_kernel, 0, len(deps)),
         name="add_parts",
-        grid=(2,),
+        grid=(1,),
         in_specs=[ANY] * len(deps) + [tile] * len(parts),
         out_specs=tile,
         out_shape=jax.ShapeDtypeStruct((rows, d), BF),
@@ -1013,10 +1037,8 @@
 
     rm = jnp.concatenate([router_weight, mix_weight, jnp.zeros((d, LANES - experts - 2), BF)], axis=1)
     straight = tuple(range(bits))
-    turned = straight[1:] + straight[:1]
-    orders = (straight, turned)
     pick = lambda v, which: [v[q] for q in which]
-    out_a, rg_a, dots_a, sums = ffn_dense(me1, n2_near, dy_near, rm, up_weight, down_weight, experts, orders, deps=tuple(dy_mine[1:]))
+    out_a, rg_a, sums = ffn_dense(me1, n2_near, dy_near, rm, up_weight, down_weight, experts, straight, deps=tuple(dy_mine[1:]))
     n2_all, dy_all = [], []
     n2_far, dy_far = [[hold(v, (out_a[0],)) for v in mine[1:]] for mine in (n2_mine, dy_mine)]
     for k in range(members):
@@ -1025,31 +1047,20 @@
     base = [[None] * tensor, [None] * tensor]
     for k, q in enumerate(near):
         base[0][q], base[1][q] = out_a[k], rg_a[k]
-    cut = 1 if experts > 1 else experts
-    out_e, rg_e, dots_e, keep_e, send_e = ffn_experts(me1, blocks, bounds, n2_all, dy_all, rm, expert_up, expert_down, 0, cut, base, straight)
-    keep_e, send_e, dots = list(keep_e), list(send_e), dots_e
-    if cut < experts:
-        out_e, rg_e, dots_e, more_k, more_s = ffn_experts(me1, blocks, bounds, n2_all, dy_all, rm, expert_up, expert_down, cut, experts - cut, (out_e, rg_e), straight)
-        keep_e, send_e, dots = keep_e + list(more_k), send_e + list(more_s), dots + dots_e
+    apart = min(2, experts)
+    whole = []
+    for a, b in ((0, 1), (1, experts)):
+        if a < b:
+            out_e, rg_e, entire, keep_e, send_e = ffn_experts(me1, blocks, bounds, n2_all, dy_all, rm, expert_up, expert_down, a, b - a, 1, base, straight)
+            base = (out_e, rg_e)
+            whole += list(entire)
     out_e, rg_e = list(out_e), list(rg_e)
-    out_b, rg_b, dots_b, ends = ffn_dense(me1, pick(n2_all, far), pick(dy_all, far), rm, up_weight, down_weight, experts, orders,
-                                          (pick(out_e, far), pick(rg_e, far)), sums)
+    out_b, rg_b, ends = ffn_dense(me1, pick(n2_all, far), pick(dy_all, far), rm, up_weight, down_weight, experts, straight,
+                                  (pick(out_e, far), pick(rg_e, far)), sums)
     for k, q in enumerate(far):
         out_e[q], rg_e[q] = out_b[k], rg_b[k]
 
     index = {c: q for q, c in enumerate(chunk)}
-    cols = lambda v, k, n=1: v[:, k * rows:(k + n) * rows]
-    dot_part = []
-    for q, (dj, ds) in enumerate(chunk):
-        dense_part = cols(dots_a, near.index(q)) if ds == 0 else cols(dots_b, far.index(q))
-        dot_part.append(cols(dots, q) + dense_part)
-    held = jnp.concatenate(dot_part[:seqs], axis=1)
-    for k in range(1, members):
-        held = held + to_member(jnp.concatenate(dot_part[k * seqs:(k + 1) * seqs], axis=1), k)
-    own_dots = cols(held, 0)
-    for ds in range(1, seqs):
-        own_dots = own_dots + to_sequence(cols(held, ds), ds)
-
     def to_owner(parts):
         mine = [[parts[index[0, ds]]] + [to_member(parts[index[k, ds]], k) for k in range(1, members)] for ds in range(seqs)]
         return mine[0], mine[1:]
@@ -1078,52 +1089,57 @@
                 mark = self.add(mark)
             return mark
 
-    sums_e = [Halving(keep_e[e], send_e[e], straight) for e in range(experts)]
-    down_sum, up_sum = Halving(ends[2], ends[3], turned), Halving(ends[0], ends[1], straight)
+    scattered = []
+    for v in whole:
+        flat = v.reshape(-1, v.shape[-1])
+        flat = lax.psum_scatter(flat, "dp", scatter_dimension=0, tiled=True)
+        scattered.append(flat.reshape((1,) + v.shape[1:]))
+
+    sums_e = [Halving(keep_e[e], send_e[e], straight) for e in range(len(keep_e))]
+    dense_sum = Halving(ends[0], ends[1], straight)
     rg_near, rg_far = to_owner(rg_e)
-    for e in range(min(experts, 3)):
-        sums_e[e].launch()
-    down_sum.launch()
+    for v in sums_e + [dense_sum]:
+        v.launch()
     came_far, terms = onward(rg_far, ())
     mark = tuple(terms[:1])
-    for e in range(min(experts, 2)):
-        mark = sums_e[e].add(mark)
-    mg, mc, sums_two = middle_backward(bounds, t1, rg_near + came_far, own_dots.T, n2, rm, middle, cotangent, gain_two, pos_col, mark)
+    mg, mc, sums_two = middle_backward(bounds, t1, rg_near + came_far, n2, rm, middle, cotangent, gain_two, pos_col, mark)
     mcs = [mc] + [from_member(mc, k) for k in range(1, members)]
-    mark = down_sum.add((mc,))
+    mark = (mc,)
+    for v in sums_e[:1]:
+        mark = v.add(mark)
     ngs = None
     grads = [None] * seqs
     for ds in list(range(1, seqs)) + [0]:
         ngs, grads[ds] = attn_backward(prefix, me1, j1, mcs, n1, wo_all[ds], w_all[ds], saved[ds], ngs, bits, mark)
         mark = (grads[ds],)
         if ds == 1 or seqs == 1:
-            for e in range(3, experts):
-                sums_e[e].launch(mark)
-            mark = sums_e[0].add(mark)
-            if experts > 2:
-                mark = sums_e[2].add(mark)
+            for v in sums_e[1:]:
+                mark = v.add(mark)
+            for v in sums_e[:1]:
+                mark = v.add(mark)
     moved = [to_sequence(grads[ds], ds) for ds in range(1, seqs)]
     ng_parts = [ngs[0]] + [to_member(ngs[k], k) for k in range(1, members)]
-    up_sum.launch(mark)
-    if experts > 1:
-        mark = sums_e[1].add(mark)
+    mark = dense_sum.add(mark)
     input_grad, sums_one = input_backward(ng_parts, inputs, mg, gain_one, mark)
     mark = (sums_one,)
     sums = Everywhere(jnp.concatenate([sums_two, sums_one], axis=0))
     stacks = None
 
     def finish(e, mark):
-        mark = sums_e[e].rest(mark)
-        done = last_add(sums_e[e].keep, sums_e[e].came, (False, True), (experts, e), stacks, mark)
+        if e < apart:
+            terms = [scattered[e]]
+        else:
+            mark = sums_e[e - apart].rest(mark)
+            terms = [sums_e[e - apart].keep, sums_e[e - apart].came]
+        done = last_add(terms, (False, True), (experts, e), stacks, mark)
         return done, (done[1],)
 
+    for v in sums_e[1:]:
+        mark = v.add(mark)
     stacks, mark = finish(0, mark)
-    if experts > 2:
-        mark = sums_e[2].add(mark)
-    mark = down_sum.add(mark)
+    if experts > apart:
+        stacks, mark = finish(apart, mark)
     mark = sums.add(mark)
-    for e in range(3, experts):
-        mark = sums_e[e].add(mark)
     keep = grads[0]
     for v in moved[:-1]:
         keep = (keep.astype(F32) + v.astype(F32)).astype(BF)
@@ -1134,36 +1150,27 @@
         keep, send = keep[:dp // 2], keep[dp // 2:]
     attn_sum = Halving(keep, send, straight)
     attn_sum.launch()
+    mark = dense_sum.add(mark)
     out_near, out_far = to_owner([hold(v, mark) for v in out_e])
     out_came, terms = onward(out_far, mark)
     mark = tuple(terms[:1]) or mark
-    if experts > 1:
-        stacks, mark = finish(1, mark)
     mark = sums.add(mark)
-    mark = up_sum.add(mark)
-    mark = down_sum.rest(mark)
-    down_out, = last_add(down_sum.keep, down_sum.came, (True,), deps=mark)
-    mark = (down_out,)
-    for e in range(3, experts):
-        mark = sums_e[e].add(mark)
+    for e in range(apart + 1, experts):
+        stacks, mark = finish(e, mark)
     mark = sums.add(mark)
-    if experts > 2:
-        stacks, mark = finish(2, mark)
-    layer_output = layer_out(out_near + out_came, middle, pos_col, mark)
-    mark = (layer_output,)
     mark = attn_sum.add(mark)
     mark = sums.add(mark)
-    mark = up_sum.add(mark)
-    for e in range(3, experts):
+    mark = dense_sum.rest(mark)
+    up_out, down_out = last_add([dense_sum.keep, dense_sum.came], (False, True), deps=mark)
+    layer_output = layer_out(out_near + out_came, middle, pos_col, (up_out,))
+    mark = attn_sum.add((layer_output,))
+    for e in range(1, apart):
         stacks, mark = finish(e, mark)
     expert_up_out, expert_down_out = stacks
-    mark = attn_sum.add(mark)
     while sums.came is not None:
         mark = sums.add(mark)
-    mark = up_sum.rest(mark)
-    up_out, = last_add(up_sum.keep, up_sum.came, (False,), deps=mark)
-    mark = attn_sum.rest((up_out,))
-    *qkv_parts, out_out = last_add(attn_sum.keep, attn_sum.came, (False, False, False, True), deps=mark)
+    mark = attn_sum.rest(mark)
+    *qkv_parts, out_out = last_add([attn_sum.keep, attn_sum.came], (False, False, False, True), deps=mark)
     lanes = d // (dp * tensor)
     begin = (me * tensor + t) * lanes
     small = lax.dynamic_slice_in_dim(sums.v, begin, lanes, 1)

time: 596 us -> 590 us (0.990); the launches traced: 588 us -> 588 us
  Pallas kernels: 333 us -> 311 us
  between operations: 1.67 us -> 14.6 us
  blocking collectives: 8.71 us -> 21.1 us
  local copies, waits for them, and re-layouts: 30.8 us -> 37.6 us
  waiting for transfers between devices: 155 us -> 149 us
    pallas_call x15 -> x9, Pallas kernels: 53.8 us -> 38.2 us  [split_add(): pl.pallas_call(partial(split_add_kernel, len(deps)), name='split_add', gr...]
    all_to_all x1, blocking collectives: 8.71 us -> 21.1 us  [shards(): lax.all_to_all(sent, 'tensor', 0, 0, axis_index_groups=[[place(a, b) for...]
    ppermute x5, waiting for transfers between devices: 42 us -> 49.9 us  [launch(): lax.ppermute(self.v, axis, [(i, i ^ bit) for i in range(lax.axis_size(axi...]
    unnamed x102 -> x93, local copies, waits for them, and re-layouts: 20.4 us -> 27.6 us
    ppermute x23 -> x14, waiting for transfers between devices: 78.4 us -> 71.9 us  [over_dp(): lax.ppermute(v, 'dp', [(i, i ^ 1 << bit) for i in range(lax.axis_size('dp...]
    ppermute x9 -> x8, waiting for transfers between devices: 29.5 us -> 26.4 us  [from_sequence(): lax.ppermute(v, 'tensor', [(place(a, b), place(a - k, b)) for a, b in eve...]
    ppermute x23 -> x14, starting transfers between devices: 28.3 us -> 30.8 us  [over_dp(): lax.ppermute(v, 'dp', [(i, i ^ 1 << bit) for i in range(lax.axis_size('dp...]
    pallas_call x7 -> x6, Pallas kernels: 15.4 us -> 13.3 us  [last_add(): pl.pallas_call(partial(last_add_kernel, len(deps), turns), name='last_add...]
  transfers between devices with their start and end apart: 49 -> 40, of which waited for: 14 -> 12; matrix products, arithmetic and copies ran while one was open for 4% -> 4% of each run, Pallas kernels for 50% -> 49%
where the time goes in v3:
time: 590 us; the launch traced here: 588 us
  Pallas kernels  311 us (53%)
  waiting for transfers between devices  149 us (25%)
  starting transfers between devices  43 us (7%)
  local copies, waits for them, and re-layouts  37.6 us (6%)
  blocking collectives  21.1 us (4%)
  between operations  14.6 us (2%)
  other arithmetic  10.6 us (2%)
    pallas_call x2, Pallas kernels, ffn_experts(): pl.pallas_call(partial(expert_kernel, (first, count, whole, chunks, rows,...  75.3 us
    ppermute x14, waiting for transfers between devices, over_dp(): lax.ppermute(v, 'dp', [(i, i ^ 1 << bit) for i in range(lax.axis_size('dp...  71.9 us
    pallas_call x2, Pallas kernels, attn_backward(): pl.pallas_call(skip(partial(attn_backward_kernel, length, bits, members,...  55.2 us
    ppermute x5, waiting for transfers between devices, launch(): lax.ppermute(self.v, axis, [(i, i ^ bit) for i in range(lax.axis_size(axi...  49.9 us
    pallas_call x2, Pallas kernels, ffn_dense(): pl.pallas_call(partial(dense_kernel, (chunks, rows, tm, lanes, order, fir...  49.7 us
    pallas_call x9, Pallas kernels, split_add(): pl.pallas_call(partial(split_add_kernel, len(deps)), name='split_add', gr...  38.2 us
    pallas_call x3, Pallas kernels, attn_forward(): pl.pallas_call(skip(partial(attn_forward_kernel, length, tuple((w.shape[0...  31.6 us
    ppermute x14, starting transfers between devices, over_dp(): lax.ppermute(v, 'dp', [(i, i ^ 1 << bit) for i in range(lax.axis_size('dp...  30.8 us
  transfers between devices with their start and end apart: 40, of which 12 were waited for; matrix products, arithmetic and copies ran while one was open for 4% of the time, Pallas kernels for 49%

profile of v3, /device:TPU:0, one launch (start us, length us, event | category | flops | bytes accessed | tf_op | source)
XLA Modules:
  0.0 587.6 jit_solution(3748419872121194995)
XLA Ops:
  8.8 2.6 collective-permute-start
  15.0 5.1 first_norm.1
  20.2 4.0 collective-permute-done.refs_0_
  25.0 1.9 collective-permute-start.2
  29.5 14.2 %attn_forward.3 = (bf16[1024,256]{1,0:T(8,128)(2,1)}, bf16[1024,256]{1,0:T(8,128)(2,1)}, bf16[1024,256]{1,0:T(8,128)(2,1)}, bf16[1024,256]{1,0:T(8,128)(2,1)}, f32[2,8,1024]{2,1,0:T(8,128)}) custom-call(s32[1]{0:T(128)} %dynamic_slice.12.refs_0_, s32[2]{0:T(128)} %iota.11.refs_1_, bf16[2,1024,128]{2,1,0:T(8,128)(2,1)} %hold.8.refs_2_.refs_4_, ...), custom_call_target="tpu_custom_call" | custom-call | tf_op jit(solution)/shard_map/attn_forward/pallas_call | solution.py:542
  46.1 8.7 %attn_forward.4 = (bf16[1024,256]{1,0:T(8,128)(2,1)}, bf16[1024,256]{1,0:T(8,128)(2,1)}, bf16[1024,256]{1,0:T(8,128)(2,1)}, bf16[1024,256]{1,0:T(8,128)(2,1)}, f32[2,8,1024]{2,1,0:T(8,128)}) custom-call(s32[1]{0:T(128)} %dynamic_slice.12.refs_0_, s32[1]{0:T(128)} %bitcast.70, f32[2,8,1024]{2,1,0:T(8,128)} %get-tuple-element.112.refs_1_.refs_2_.refs_13_, ...), custom_call_target="tpu_custom_call" | custom-call | tf_op jit(solution)/shard_map/attn_forward/pallas_call | solution.py:542
  55.5 8.7 %attn_forward.5 = (bf16[1024,256]{1,0:T(8,128)(2,1)}, bf16[1024,256]{1,0:T(8,128)(2,1)}, bf16[1024,256]{1,0:T(8,128)(2,1)}, bf16[1024,256]{1,0:T(8,128)(2,1)}, f32[2,8,1024]{2,1,0:T(8,128)}) custom-call(s32[1]{0:T(128)} %dynamic_slice.12.refs_0_, s32[1]{0:T(128)} %bitcast.69, ...), custom_call_target="tpu_custom_call", output_to_operand_aliasing={{0}: (5, {}), {1}: (6, {}), {2}: (7, {}), {3}: (8, {}), {4}... | custom-call | tf_op jit(solution)/shard_map/attn_forward/pallas_call | solution.py:542
  65.0 3.8 project.1
  68.8 21.1 %all_to_all.5.came = bf16[2,512,1024]{2,1,0:T(8,128)(2,1)} all-to-all(bf16[2,512,1024]{2,1,0:T(8,128)(2,1)} %project.1), channel_id=1, replica_groups={{0,1},{2,3},{4,5},{6,7},{8,9},{10,11},{12,13},{14,15},{16,17},{18,19},{..., dimensions={0} | all-to-all | bytes 4194304 | tf_op jit(solution)/shard_map/all_to_all | solution.py:1033
  89.9 4.4 second_norm.1
  94.5 1.9 collective-permute-start.6
  97.5 1.8 maximum_maximum_fusion.refs_5_.refs_8_.refs_4_.refs_7_
  100.3 23.1 %ffn_dense.2 = (bf16[512,1024]{1,0:T(8,128)(2,1)}, bf16[512,1024]{1,0:T(8,128)(2,1)}, bf16[528,1024]{1,0:T(8,128)(2,1)}, bf16[528,1024]{1,0:T(8,128)(2,1)}, f32[1024,1024]{1,0:T(8,128)}, /*index=5*/f32[1024,1024]{1,0:T(8,128)}) custom-call(s32[1]{0:T(128)} %bitcast.me_ref.refs_1_, bf16[512,1024]{1,0:T(8,128)(2,1)} %copy-done, ...), custom_call_target="tpu_custom_call" | custom-call | tf_op jit(solution)/shard_map/ffn_dense/pallas_call | solution.py:211
  129.8 21.4 %ffn_experts.2 = (bf16[512,1024]{1,0:T(8,128)(2,1)}, bf16[512,1024]{1,0:T(8,128)(2,1)}, bf16[512,1024]{1,0:T(8,128)(2,1)}, bf16[512,1024]{1,0:T(8,128)(2,1)}, bf...) custom-call(s32[1]{0:T(128)} %bitcast.me_ref.refs_1_, ...), custom_call_target="tpu_custom_call" | custom-call | tf_op jit(solution)/shard_map/ffn_experts/pallas_call | solution.py:387
  151.6 53.9 %ffn_experts.3 = (bf16[512,1024]{1,0:T(8,128)(2,1)}, bf16[512,1024]{1,0:T(8,128)(2,1)}, bf16[512,1024]{1,0:T(8,128)(2,1)}, bf16[512,1024]{1,0:T(8,128)(2,1)}, bf...) custom-call(s32[1]{0:T(128)} %bitcast.me_ref.refs_1_, ...), custom_call_target="tpu_custom_call" | custom-call | tf_op jit(solution)/shard_map/ffn_experts/pallas_call | solution.py:387
  205.6 26.6 %ffn_dense.3 = (bf16[512,1024]{1,0:T(8,128)(2,1)}, bf16[512,1024]{1,0:T(8,128)(2,1)}, bf16[528,1024]{1,0:T(8,128)(2,1)}, bf16[528,1024]{1,0:T(8,128)(2,1)}, bf16...) custom-call(s32[1]{0:T(128)} %bitcast.me_ref.refs_1_, bf16[512,1024]{1,0:T(8,128)(2,1)} %hold.10.refs_1_.refs_0_, ...), custom_call_target="tpu_custom_call" | custom-call | tf_op jit(solution)/shard_map/ffn_dense/pallas_call | solution.py:211
  232.3 5.3 collective-permute-start.15
  238.6 2.8 add_parts.2.refs_2_
  242.0 2.7 collective-permute-start.17
  245.5 22.4 %collective-permute-done.14.refs_5_ = bf16[528,1024]{1,0:T(8,128)(2,1)S(1)} collective-permute-done((bf16[528,1024]{1,0:T(8,128)(2,1)}, bf16[528,1024]{1,0:T(8,128)(2,1)S(1)}, u32[]{:S(2)}, u32[]{:S(2)}) %collective-permute-start.14) | collective-permute-done | bytes 1081376 | tf_op jit(solution)/shard_map/ppermute | solution.py:961
  268.9 10.5 %middle_backward.1 = (f32[512,1024]{1,0:T(8,128)}, bf16[512,1024]{1,0:T(8,128)(2,1)}, f32[16,1024]{1,0:T(8,128)}) custom-call(s32[4,5]{1,0:T(4,128)} %stack.50.bnd_ref.refs_0_, s32[1]{0:T(128)} %bitcast.7.refs_1_, bf16[528,1024]{1,0:T(8,128)(2,1)} %add_parts.2.refs_2_, bf16[528,1024]{1,0:T(8,128)(2,1)} %get-tuple-element.141.refs_3_, ...), custom_call_target="tpu_custom_call" | custom-call | tf_op jit(solution)/shard_map/middle_backward/pallas_call | solution.py:824
  279.4 2.3 collective-permute-start.19
  282.8 13.4 %collective-permute-done.15.refs_3_.refs_4_ = bf16[4,2,128,1024]{3,2,1,0:T(8,128)(2,1)} collective-permute-done((bf16[4,2,128,1024]{3,2,1,0:T(8,128)(2,1)}, bf16[4,2,128,1024]{3,2,1,0:T(8,128)(2,1)}, u32[]{:S(2)}, u32[]{:S(2)}) %collective-permute-start.15) | collective-permute-done | bytes 2097184 | tf_op jit(solution)/shard_map/ppermute | solution.py:936
  296.3 4.3 split_add.9
  300.6 2.5 collective-permute-start.18
  303.0 3.0 maximum_select_fusion.refs_8_
  307.1 27.2 %attn_backward.2 = (bf16[512,1024]{1,0:T(8,128)(2,1)}, bf16[512,1024]{1,0:T(8,128)(2,1)}, bf16[8,4,128,256]{3,2,1,0:T(8,128)(2,1)}) custom-call(s32[1]{0:T(128)} %dynamic_slice.12.refs_0_, s32[1]{0:T(128)} %bitcast.me_ref.refs_1_, s32[1]{0:T(128)} %bitcast.1.j_ref.refs_2_, bf16[2,2,128,1024]{3,2,1,0:T(8,128)(2,1)} %get-tuple-element.147.refs_3_, ...), custom_call_target="tpu_custom_call" | custom-call | tf_op jit(solution)/shard_map/attn_backward/pallas_call | solution.py:648
  334.5 22.9 %collective-permute-done.17.refs_3_.refs_4_ = bf16[4,2,128,1024]{3,2,1,0:T(8,128)(2,1)} collective-permute-done((bf16[4,2,128,1024]{3,2,1,0:T(8,128)(2,1)}, bf16[4,2,128,1024]{3,2,1,0:T(8,128)(2,1)}, u32[]{:S(2)}, u32[]{:S(2)}) %collective-permute-start.17) | collective-permute-done | bytes 2097184 | tf_op jit(solution)/shard_map/ppermute | solution.py:936
  357.4 4.1 split_add.10
  361.5 2.4 split_add.11
  363.9 28.0 %attn_backward.3 = (bf16[512,1024]{1,0:T(8,128)(2,1)}, bf16[512,1024]{1,0:T(8,128)(2,1)}, bf16[8,4,128,256]{3,2,1,0:T(8,128)(2,1)}) custom-call(s32[1]{0:T(128)} %dynamic_slice.12.refs_0_, s32[1]{0:T(128)} %bitcast.me_ref.refs_1_, s32[1]{0:T(128)} %bitcast.1.j_ref.refs_2_, bf16[1,2,128,1024]{3,2,1,0:T(8,128)(2,1)} %get-tuple-element.157.refs_3_, ...), custom_call_target="tpu_custom_call" | custom-call | tf_op jit(solution)/shard_map/attn_backward/pallas_call | solution.py:648
  392.0 2.2 collective-permute-start.21
  394.2 7.7 %collective-permute-done.19.refs_3_.refs_4_ = bf16[4,2,128,1024]{3,2,1,0:T(8,128)(2,1)S(1)} collective-permute-done((bf16[4,2,128,1024]{3,2,1,0:T(8,128)(2,1)}, bf16[4,2,128,1024]{3,2,1,0:T(8,128)(2,1)S(1)}, u32[]{:S(2)}, u32[]{:S(2)}) %collective-permute-start.19) | collective-permute-done | bytes 2097184 | tf_op jit(solution)/shard_map/ppermute | solution.py:936
  403.2 4.2 split_add.12
  407.4 1.9 collective-permute-start.25
  409.3 2.6 collective-permute-start.22
  411.9 5.6 input_backward.1
  418.3 11.3 %collective-permute-done.21.refs_3_.refs_4_ = bf16[2,2,128,1024]{3,2,1,0:T(8,128)(2,1)S(1)} collective-permute-done((bf16[2,2,128,1024]{3,2,1,0:T(8,128)(2,1)}, bf16[2,2,128,1024]{3,2,1,0:T(8,128)(2,1)S(1)}, u32[]{:S(2)}, u32[]{:S(2)}) %collective-permute-start.21) | collective-permute-done | bytes 1048608 | tf_op jit(solution)/shard_map/ppermute | solution.py:936
  430.6 2.5 split_add.13
  433.1 2.2 last_add.6
  435.3 3.0 copy.85.refs_1_
  438.3 12.9 %collective-permute-done.22.refs_4_ = bf16[1,2,128,1024]{3,2,1,0:T(8,128)(2,1)S(1)} collective-permute-done((bf16[1,2,128,1024]{3,2,1,0:T(8,128)(2,1)}, bf16[1,2,128,1024]{3,2,1,0:T(8,128)(2,1)S(1)}, u32[]{:S(2)}, u32[]{:S(2)}) %collective-permute-start.22) | collective-permute-done | bytes 524320 | tf_op jit(solution)/shard_map/ppermute | solution.py:936
  452.0 2.4 last_add.7
  455.1 1.6 add_small.5.refs_0_.refs_1_
  456.6 9.7 %split_add.14 = (bf16[4,4,128,256]{3,2,1,0:T(8,128)(2,1)}, bf16[4,4,128,256]{3,2,1,0:T(8,128)(2,1)}) custom-call(f32[24,1024]{1,0:T(8,128)} %add_small.5.refs_0_.refs_1_, bf16[8,4,128,256]{3,2,1,0:T(8,128)(2,1)} %get-tuple-element.163.refs_0_.refs_1_.refs_2_, bf16[8,4,128,256]{3,2,1,0:T(8,128)(2,1)} %get-tuple-element.163.refs_0_.refs_1_.refs_2_, ...), custom_call_target="tpu_custom_call" | custom-call | tf_op jit(solution)/shard_map/split_add/pallas_call | solution.py:419
  467.4 2.4 split_add.15
  470.8 3.3 collective-permute-start.28
  474.1 2.8 add_parts.3.refs_0_
  478.9 25.8 %collective-permute-done.27.refs_2_ = f32[24,1024]{1,0:T(8,128)S(1)} collective-permute-done((f32[24,1024]{1,0:T(8,128)S(1)}, f32[24,1024]{1,0:T(8,128)S(1)}, u32[]{:S(2)}, u32[]{:S(2)}) %collective-permute-start.27) | collective-permute-done | bytes 98336 | tf_op jit(solution)/shard_map/ppermute | solution.py:923
  505.4 1.6 add_small.6.refs_2_.refs_1_
  508.8 2.4 last_add.8
  512.4 1.6 add_small.7.refs_0_.refs_1_
  515.0 5.4 split_add.16
  520.4 2.0 collective-permute-start.35
  522.5 23.5 %collective-permute-done.31.refs_2_ = f32[24,1024]{1,0:T(8,128)S(1)} collective-permute-done((f32[24,1024]{1,0:T(8,128)S(1)}, f32[24,1024]{1,0:T(8,128)S(1)}, u32[]{:S(2)}, u32[]{:S(2)}) %collective-permute-start.31) | collective-permute-done | bytes 98336 | tf_op jit(solution)/shard_map/ppermute | solution.py:923
  546.6 1.6 add_small.8.refs_0_.refs_1_
  549.2 2.4 last_add.9
  552.6 4.9 layer_out.1.refs_0_
  558.3 3.2 split_add.17
  561.6 2.7 collective-permute-start.37
  564.2 2.1 last_add.10
  572.6 3.7 collective-permute-done.37.refs_2_
  577.0 1.9 last_add.11
  578.8 1.8 pad_maximum_fusion
  (194 shorter events, 51.1 us)
Async XLA Ops:
  7.2 426.0 %reduce-scatter.3.cloned.1.call-start = ((), (), s32[]{:S(2)}) async-start(), calls=%async_computation.3 | async-start | bytes 4718592 | tf_op jit(solution)/shard_map/reduce_scatter | solution.py:1095
  7.2 6.8 %collective-permute-start.1 = (bf16[512,1024]{1,0:T(8,128)(2,1)}, bf16[512,1024]{1,0:T(8,128)(2,1)S(1)}, u32[]{:S(2)}, u32[]{:S(2)}) collective-permute-start(bf16[512,1024]{1,0:T(8,128)(2,1)} %refs_3_.1), channel_id=1, source_target_pairs={{0,1},{1,0},{2,3},{3,2},{4,5},{5,4},{6,7},{7,6},{8,9},{9,8},{10,11... | collective-permute-start | bytes 3145736 | tf_op jit(solution)/shard_map/ppermute | solution.py:958
  8.8 15.4 %collective-permute-start = (bf16[2,1024,128]{2,1,0:T(8,128)(2,1)S(1)}, bf16[2,1024,128]{2,1,0:T(8,128)(2,1)S(1)}, u32[]{:S(2)}, u32[]{:S(2)}) collective-permute-start(bf16[2,1024,128]{2,1,0:T(8,128)(2,1)S(1)} %dynamic-slice_bitcast_fusion), channel_id=1, source_target_pairs={{0,2},{1,3},{2,0},{3,1},{4,6},{5,7},{6,4},{7,5},{8,10},{9,11},{10,... | collective-permute-start | bytes 1572872 | tf_op jit(solution)/shard_map/ppermute | solution.py:961
  12.4 31.4 %collective-permute-start.3 = (bf16[1,1024,128]{2,1,0:T(8,128)(2,1)S(1)}, bf16[1,1024,128]{2,1,0:T(8,128)(2,1)S(1)}, u32[]{:S(2)}, u32[]{:S(2)}) collective-permute-start(bf16[1,1024,128]{2,1,0:T(8,128)(2,1)S(1)} %dynamic-slice_bitcast_fusion.1), channel_id=1, source_target_pairs={{0,2},{1,3},{2,0},{3,1},{4,6},{5,7},{6,4},{7,5},{8,10},{9,11},{10,... | collective-permute-start | bytes 786440 | tf_op jit(solution)/shard_map/ppermute | solution.py:961
  20.2 6.8 %copy-start.16 = (bf16[256,1024]{1,0:T(8,128)(2,1)S(1)}, bf16[256,1024]{1,0:T(8,128)(2,1)}, u32[]{:S(2)}) copy-start(bf16[256,1024]{1,0:T(8,128)(2,1)} %refs_7_.3) | copy-start | bytes 1572868
  20.2 8.3 %copy-start.43 = (s32[2]{0:T(128)S(1)}, s32[2]{0:T(128)}, u32[]{:S(2)}) copy-start(s32[2]{0:T(128)} %param.19) | copy-start | bytes 28
  25.0 29.8 %collective-permute-start.2 = (bf16[2,1024,128]{2,1,0:T(8,128)(2,1)}, bf16[2,1024,128]{2,1,0:T(8,128)(2,1)}, u32[]{:S(2)}, u32[]{:S(2)}) collective-permute-start(bf16[2,1024,128]{2,1,0:T(8,128)(2,1)} %hold.8.refs_2_.refs_4_), channel_id=1, source_target_pairs={{0,4},{4,0},{8,12},{12,8},{16,20},{20,16},{24,28},{28,24},{1,5},{5... | collective-permute-start | bytes 1572872 | tf_op jit(solution)/shard_map/ppermute | solution.py:936
  26.9 37.3 %collective-permute-start.5 = (bf16[256,1024]{1,0:T(8,128)(2,1)S(1)}, bf16[256,1024]{1,0:T(8,128)(2,1)S(1)}, u32[]{:S(2)}, u32[]{:S(2)}) collective-permute-start(bf16[256,1024]{1,0:T(8,128)(2,1)S(1)} %copy-done.16), channel_id=1, source_target_pairs={{0,2},{1,3},{2,0},{3,1},{4,6},{5,7},{6,4},{7,5},{8,10},{9,11},{10,... | collective-permute-start | bytes 1572872 | tf_op jit(solution)/shard_map/ppermute | solution.py:961
  29.5 16.5 %copy-start.3 = (bf16[512,1024]{1,0:T(8,128)(2,1)S(1)}, bf16[512,1024]{1,0:T(8,128)(2,1)}, u32[]{:S(2)}) copy-start(bf16[512,1024]{1,0:T(8,128)(2,1)} %get-tuple-element.120.refs_3_.refs_4_) | copy-start | bytes 3145732
  44.5 10.3 %collective-permute-start.4 = (bf16[1,1024,128]{2,1,0:T(8,128)(2,1)}, bf16[1,1024,128]{2,1,0:T(8,128)(2,1)S(1)}, u32[]{:S(2)}, u32[]{:S(2)}) collective-permute-start(bf16[1,1024,128]{2,1,0:T(8,128)(2,1)} %hold.9.refs_5_), channel_id=1, source_target_pairs={{0,4},{4,0},{8,12},{12,8},{16,20},{20,16},{24,28},{28,24},{1,5},{5... | collective-permute-start | bytes 786440 | tf_op jit(solution)/shard_map/ppermute | solution.py:936
  46.1 53.3 %collective-permute-start.9 = (bf16[512,1024]{1,0:T(8,128)(2,1)S(1)}, bf16[512,1024]{1,0:T(8,128)(2,1)}, u32[]{:S(2)}, u32[]{:S(2)}) collective-permute-start(bf16[512,1024]{1,0:T(8,128)(2,1)S(1)} %copy-done.3), channel_id=1, source_target_pairs={{0,1},{1,0},{2,3},{3,2},{4,5},{5,4},{6,7},{7,6},{8,9},{9,8},{10,11... | collective-permute-start | bytes 3145736 | tf_op jit(solution)/shard_map/ppermute | solution.py:958
  46.1 53.3 %collective-permute-start.7 = (bf16[512,1024]{1,0:T(8,128)(2,1)S(1)}, bf16[512,1024]{1,0:T(8,128)(2,1)S(1)}, u32[]{:S(2)}, u32[]{:S(2)}) collective-permute-start(bf16[512,1024]{1,0:T(8,128)(2,1)S(1)} %copy-done.3), channel_id=1, source_target_pairs={{0,2},{1,3},{2,0},{3,1},{4,6},{5,7},{6,4},{7,5},{8,10},{9,11},{10,... | collective-permute-start | bytes 3145736 | tf_op jit(solution)/shard_map/ppermute | solution.py:961
  89.9 6.4 %copy-start.40 = (bf16[1024,4]{0,1:T(4,128)(2,1)S(1)}, bf16[1024,4]{0,1:T(4,128)(2,1)}, u32[]{:S(2)}) copy-start(bf16[1024,4]{0,1:T(4,128)(2,1)} %param.30) | copy-start | bytes 24580
  89.9 6.6 %copy-start.41 = (bf16[1024,2]{0,1:T(2,128)(2,1)S(1)}, bf16[1024,2]{0,1:T(2,128)(2,1)}, u32[]{:S(2)}) copy-start(bf16[1024,2]{0,1:T(2,128)(2,1)} %param.31) | copy-start | bytes 12292
  94.3 5.0 collective-permute-start.8
  94.5 29.0 %collective-permute-start.6 = (bf16[512,1024]{1,0:T(8,128)(2,1)}, bf16[512,1024]{1,0:T(8,128)(2,1)S(1)}, u32[]{:S(2)}, u32[]{:S(2)}) collective-permute-start(bf16[512,1024]{1,0:T(8,128)(2,1)} %get-tuple-element.119.refs_1_.refs_0_.refs_6_), channel_id=1, source_target_pairs={{0,2},{1,3},{2,0},{3,1},{4,6},{5,7},{6,4},{7,5},{8,10},{9,11},{10,... | collective-permute-start | bytes 3145736 | tf_op jit(solution)/shard_map/ppermute | solution.py:961
  124.4 3.3 collective-permute-start.10
  124.4 4.4 collective-permute-start.11
  127.7 1.1 copy-start.4
  128.8 1.0 copy-start.5
  151.2 413.1 %reduce-scatter.5.cloned.1.call-start = ((), (), s32[]{:S(2)}) async-start(), calls=%async_computation.4 | async-start | bytes 4718592 | tf_op jit(solution)/shard_map/reduce_scatter | solution.py:1095
  205.6 32.0 %copy-start.42 = (bf16[528,1024]{1,0:T(8,128)(2,1)S(1)}, bf16[528,1024]{1,0:T(8,128)(2,1)}, u32[]{:S(2)}) copy-start(bf16[528,1024]{1,0:T(8,128)(2,1)} %get-tuple-element.142) | copy-start | bytes 3244036
  232.2 5.4 collective-permute-start.12
  232.3 64.0 %collective-permute-start.15 = (bf16[4,2,128,1024]{3,2,1,0:T(8,128)(2,1)}, bf16[4,2,128,1024]{3,2,1,0:T(8,128)(2,1)}, u32[]{:S(2)}, u32[]{:S(2)}) collective-permute-start(bf16[4,2,128,1024]{3,2,1,0:T(8,128)(2,1)} %get-tuple-element.146), channel_id=1, source_target_pairs={{0,4},{4,0},{8,12},{12,8},{16,20},{20,16},{24,28},{28,24},{1,5},{5... | collective-permute-start | bytes 6291464 | tf_op jit(solution)/shard_map/ppermute | solution.py:936
  237.6 7.9 %collective-permute-start.13 = (bf16[528,1024]{1,0:T(8,128)(2,1)S(1)}, bf16[528,1024]{1,0:T(8,128)(2,1)S(1)}, u32[]{:S(2)}, u32[]{:S(2)}) collective-permute-start(bf16[528,1024]{1,0:T(8,128)(2,1)S(1)} %copy-done.42), channel_id=1, source_target_pairs={{0,1},{1,0},{2,3},{3,2},{4,5},{5,4},{6,7},{7,6},{8,9},{9,8},{10,11... | collective-permute-start | bytes 3244040 | tf_op jit(solution)/shard_map/ppermute | solution.py:958
  241.4 26.4 %collective-permute-start.14 = (bf16[528,1024]{1,0:T(8,128)(2,1)}, bf16[528,1024]{1,0:T(8,128)(2,1)S(1)}, u32[]{:S(2)}, u32[]{:S(2)}) collective-permute-start(bf16[528,1024]{1,0:T(8,128)(2,1)} %add_parts.2.refs_2_), channel_id=1, source_target_pairs={{0,2},{1,3},{2,0},{3,1},{4,6},{5,7},{6,4},{7,5},{8,10},{9,11},{10,... | collective-permute-start | bytes 3244040 | tf_op jit(solution)/shard_map/ppermute | solution.py:961
  242.0 115.4 %collective-permute-start.17 = (bf16[4,2,128,1024]{3,2,1,0:T(8,128)(2,1)}, bf16[4,2,128,1024]{3,2,1,0:T(8,128)(2,1)}, u32[]{:S(2)}, u32[]{:S(2)}) collective-permute-start(bf16[4,2,128,1024]{3,2,1,0:T(8,128)(2,1)} %get-tuple-element.154), channel_id=1, source_target_pairs={{0,4},{4,0},{8,12},{12,8},{16,20},{20,16},{24,28},{28,24},{1,5},{5... | collective-permute-start | bytes 6291464 | tf_op jit(solution)/shard_map/ppermute | solution.py:936
  245.5 22.4 %copy-start.19 = (bf16[528,1024]{1,0:T(8,128)(2,1)}, bf16[528,1024]{1,0:T(8,128)(2,1)S(1)}, u32[]{:S(2)}) copy-start(bf16[528,1024]{1,0:T(8,128)(2,1)S(1)} %collective-permute-done.13.refs_4_) | copy-start | bytes 3244036
  268.9 13.9 %copy-start.25 = (bf16[1,1024,128]{2,1,0:T(8,128)(2,1)S(1)}, bf16[1,1024,128]{2,1,0:T(8,128)(2,1)}, u32[]{:S(2)}) copy-start(bf16[1,1024,128]{2,1,0:T(8,128)(2,1)} %copy-done.24) | copy-start | bytes 786436
  279.4 26.7 %collective-permute-start.16 = (bf16[512,1024]{1,0:T(8,128)(2,1)}, bf16[512,1024]{1,0:T(8,128)(2,1)S(1)}, u32[]{:S(2)}, u32[]{:S(2)}) collective-permute-start(bf16[512,1024]{1,0:T(8,128)(2,1)} %get-tuple-element.144.refs_0_.refs_4_), channel_id=1, source_target_pairs={{0,1},{1,0},{2,3},{3,2},{4,5},{5,4},{6,7},{7,6},{8,9},{9,8},{10,11... | collective-permute-start | bytes 3145736 | tf_op jit(solution)/shard_map/ppermute | solution.py:958
  279.4 122.5 %collective-permute-start.19 = (bf16[4,2,128,1024]{3,2,1,0:T(8,128)(2,1)}, bf16[4,2,128,1024]{3,2,1,0:T(8,128)(2,1)S(1)}, u32[]{:S(2)}, u32[]{:S(2)}) collective-permute-start(bf16[4,2,128,1024]{3,2,1,0:T(8,128)(2,1)} %get-tuple-element.165), channel_id=1, source_target_pairs={{0,4},{4,0},{8,12},{12,8},{16,20},{20,16},{24,28},{28,24},{1,5},{5... | collective-permute-start | bytes 6291464 | tf_op jit(solution)/shard_map/ppermute | solution.py:936
  282.8 13.4 %copy-start.15 = (bf16[3,1024,128]{2,1,0:T(8,128)(2,1)}, bf16[3,1024,128]{2,1,0:T(8,128)(2,1)S(1)}, u32[]{:S(2)}) copy-start(bf16[3,1024,128]{2,1,0:T(8,128)(2,1)S(1)} %constant_dynamic-update-slice_fusion) | copy-start | bytes 2359300
  296.3 6.8 %copy-start.8 = (bf16[2,1024,128]{2,1,0:T(8,128)(2,1)S(1)}, bf16[2,1024,128]{2,1,0:T(8,128)(2,1)}, u32[]{:S(2)}) copy-start(bf16[2,1024,128]{2,1,0:T(8,128)(2,1)} %hold.8.refs_2_.refs_4_) | copy-start | bytes 1572868
  296.3 6.8 %copy-start.14 = (bf16[1,1024,128]{2,1,0:T(8,128)(2,1)S(1)}, bf16[1,1024,128]{2,1,0:T(8,128)(2,1)}, u32[]{:S(2)}) copy-start(bf16[1,1024,128]{2,1,0:T(8,128)(2,1)} %hold.9.refs_5_) | copy-start | bytes 786436
  300.6 60.9 %collective-permute-start.18 = (bf16[2,2,128,1024]{3,2,1,0:T(8,128)(2,1)}, bf16[2,2,128,1024]{3,2,1,0:T(8,128)(2,1)}, u32[]{:S(2)}, u32[]{:S(2)}) collective-permute-start(bf16[2,2,128,1024]{3,2,1,0:T(8,128)(2,1)} %get-tuple-element.147.refs_3_), channel_id=1, source_target_pairs={{0,8},{4,12},{8,0},{12,4},{16,24},{20,28},{24,16},{28,20},{1,9},{5... | collective-permute-start | bytes 3145736 | tf_op jit(solution)/shard_map/ppermute | solution.py:936
  306.1 1.0 copy-start.9
  334.3 122.3 %collective-permute-start.24 = (bf16[8,4,128,256]{3,2,1,0:T(8,128)(2,1)}, bf16[8,4,128,256]{3,2,1,0:T(8,128)(2,1)}, u32[]{:S(2)}, u32[]{:S(2)}) collective-permute-start(bf16[8,4,128,256]{3,2,1,0:T(8,128)(2,1)} %get-tuple-element.152.refs_0_), channel_id=1, source_target_pairs={{0,2},{1,3},{2,0},{3,1},{4,6},{5,7},{6,4},{7,5},{8,10},{9,11},{10,... | collective-permute-start | bytes 6291464 | tf_op jit(solution)/shard_map/ppermute | solution.py:961
  391.9 20.0 %collective-permute-start.20 = (bf16[512,1024]{1,0:T(8,128)(2,1)}, bf16[512,1024]{1,0:T(8,128)(2,1)}, u32[]{:S(2)}, u32[]{:S(2)}) collective-permute-start(bf16[512,1024]{1,0:T(8,128)(2,1)} %get-tuple-element.168), channel_id=1, source_target_pairs={{0,1},{1,0},{2,3},{3,2},{4,5},{5,4},{6,7},{7,6},{8,9},{9,8},{10,11... | collective-permute-start | bytes 3145736 | tf_op jit(solution)/shard_map/ppermute | solution.py:958
  392.0 37.6 %collective-permute-start.21 = (bf16[2,2,128,1024]{3,2,1,0:T(8,128)(2,1)}, bf16[2,2,128,1024]{3,2,1,0:T(8,128)(2,1)S(1)}, u32[]{:S(2)}, u32[]{:S(2)}) collective-permute-start(bf16[2,2,128,1024]{3,2,1,0:T(8,128)(2,1)} %get-tuple-element.155.refs_0_), channel_id=1, source_target_pairs={{0,8},{4,12},{8,0},{12,4},{16,24},{20,28},{24,16},{28,20},{1,9},{5... | collective-permute-start | bytes 3145736 | tf_op jit(solution)/shard_map/ppermute | solution.py:936
  401.9 1.3 copy-start.6
  403.2 8.7 %copy-start.38 = (f32[16,1024]{1,0:T(8,128)S(1)}, f32[16,1024]{1,0:T(8,128)}, u32[]{:S(2)}) copy-start(f32[16,1024]{1,0:T(8,128)} %get-tuple-element.179) | copy-start | bytes 196612
  407.4 58.9 %collective-permute-start.25 = (bf16[2,2,128,1024]{3,2,1,0:T(8,128)(2,1)}, bf16[2,2,128,1024]{3,2,1,0:T(8,128)(2,1)S(1)}, u32[]{:S(2)}, u32[]{:S(2)}) collective-permute-start(bf16[2,2,128,1024]{3,2,1,0:T(8,128)(2,1)} %get-tuple-element.166.refs_0_), channel_id=1, source_target_pairs={{0,8},{4,12},{8,0},{12,4},{16,24},{20,28},{24,16},{28,20},{1,9},{5... | collective-permute-start | bytes 3145736 | tf_op jit(solution)/shard_map/ppermute | solution.py:936
  409.3 41.9 %collective-permute-start.22 = (bf16[1,2,128,1024]{3,2,1,0:T(8,128)(2,1)}, bf16[1,2,128,1024]{3,2,1,0:T(8,128)(2,1)S(1)}, u32[]{:S(2)}, u32[]{:S(2)}) collective-permute-start(bf16[1,2,128,1024]{3,2,1,0:T(8,128)(2,1)} %get-tuple-element.157.refs_3_), channel_id=1, source_target_pairs={{0,16},{4,20},{8,24},{12,28},{16,0},{20,4},{24,8},{28,12},{1,17},{... | collective-permute-start | bytes 1572872 | tf_op jit(solution)/shard_map/ppermute | solution.py:936
  418.3 36.1 %copy-start.31 = (f32[24,1024]{1,0:T(8,128)}, f32[24,1024]{1,0:T(8,128)S(1)}, u32[]{:S(2)}) copy-start(f32[24,1024]{1,0:T(8,128)S(1)} %constant_dynamic-update-slice_fusion.2.refs_1_) | copy-start | bytes 294916
  418.3 36.1 %collective-permute-start.23 = (f32[24,1024]{1,0:T(8,128)S(1)}, f32[24,1024]{1,0:T(8,128)S(1)}, u32[]{:S(2)}, u32[]{:S(2)}) collective-permute-start(f32[24,1024]{1,0:T(8,128)S(1)} %constant_dynamic-update-slice_fusion.2.refs_1_), channel_id=1, source_target_pairs={{0,1},{1,0},{2,3},{3,2},{4,5},{5,4},{6,7},{7,6},{8,9},{9,8},{10,11... | collective-permute-start | bytes 294920 | tf_op jit(solution)/shard_map/ppermute | solution.py:923
  466.4 1.0 copy-start.10
  469.7 1.0 copy-start.29
  469.7 4.3 collective-permute-start.26
  469.8 44.2 %collective-permute-start.30 = (bf16[4,4,128,256]{3,2,1,0:T(8,128)(2,1)}, bf16[4,4,128,256]{3,2,1,0:T(8,128)(2,1)S(1)}, u32[]{:S(2)}, u32[]{:S(2)}) collective-permute-start(bf16[4,4,128,256]{3,2,1,0:T(8,128)(2,1)} %get-tuple-element.180.refs_0_), channel_id=1, source_target_pairs={{0,4},{4,0},{8,12},{12,8},{16,20},{20,16},{24,28},{28,24},{1,5},{5... | collective-permute-start | bytes 3145736 | tf_op jit(solution)/shard_map/ppermute | solution.py:936
  470.8 37.3 %collective-permute-start.28 = (bf16[1,2,128,1024]{3,2,1,0:T(8,128)(2,1)S(1)}, bf16[1,2,128,1024]{3,2,1,0:T(8,128)(2,1)}, u32[]{:S(2)}, u32[]{:S(2)}) collective-permute-start(bf16[1,2,128,1024]{3,2,1,0:T(8,128)(2,1)S(1)} %copy-done.29), channel_id=1, source_target_pairs={{0,16},{4,20},{8,24},{12,28},{16,0},{20,4},{24,8},{28,12},{1,17},{... | collective-permute-start | bytes 1572872 | tf_op jit(solution)/shard_map/ppermute | solution.py:936
  474.0 3.4 copy-start.26
  474.0 34.1 %copy-start.2 = (bf16[1,2,128,1024]{3,2,1,0:T(8,128)(2,1)S(1)}, bf16[1,2,128,1024]{3,2,1,0:T(8,128)(2,1)}, u32[]{:S(2)}) copy-start(bf16[1,2,128,1024]{3,2,1,0:T(8,128)(2,1)} %get-tuple-element.182.refs_1_.refs_0_) | copy-start | bytes 1572868
  474.0 77.6 %collective-permute-start.33 = (bf16[512,1024]{1,0:T(8,128)(2,1)}, bf16[512,1024]{1,0:T(8,128)(2,1)S(1)}, u32[]{:S(2)}, u32[]{:S(2)}) collective-permute-start(bf16[512,1024]{1,0:T(8,128)(2,1)} %hold.15), channel_id=1, source_target_pairs={{0,1},{1,0},{2,3},{3,2},{4,5},{5,4},{6,7},{7,6},{8,9},{9,8},{10,11... | collective-permute-start | bytes 3145736 | tf_op jit(solution)/shard_map/ppermute | solution.py:958
  476.9 74.7 %collective-permute-start.34 = (bf16[512,1024]{1,0:T(8,128)(2,1)}, bf16[512,1024]{1,0:T(8,128)(2,1)}, u32[]{:S(2)}, u32[]{:S(2)}) collective-permute-start(bf16[512,1024]{1,0:T(8,128)(2,1)} %add_parts.3.refs_0_), channel_id=1, source_target_pairs={{0,2},{1,3},{2,0},{3,1},{4,6},{5,7},{6,4},{7,5},{8,10},{9,11},{10,... | collective-permute-start | bytes 3145736 | tf_op jit(solution)/shard_map/ppermute | solution.py:961
  477.4 27.3 %collective-permute-start.27 = (f32[24,1024]{1,0:T(8,128)S(1)}, f32[24,1024]{1,0:T(8,128)S(1)}, u32[]{:S(2)}, u32[]{:S(2)}) collective-permute-start(f32[24,1024]{1,0:T(8,128)S(1)} %copy-done.26), channel_id=1, source_target_pairs={{0,2},{1,3},{2,0},{3,1},{4,6},{5,7},{6,4},{7,5},{8,10},{9,11},{10,... | collective-permute-start | bytes 294920 | tf_op jit(solution)/shard_map/ppermute | solution.py:923
  507.0 4.8 collective-permute-start.29
  508.1 40.4 %collective-permute-start.32 = (bf16[1,2,128,1024]{3,2,1,0:T(8,128)(2,1)S(1)}, bf16[1,2,128,1024]{3,2,1,0:T(8,128)(2,1)S(1)}, u32[]{:S(2)}, u32[]{:S(2)}) collective-permute-start(bf16[1,2,128,1024]{3,2,1,0:T(8,128)(2,1)S(1)} %copy-done.2), channel_id=1, source_target_pairs={{0,16},{4,20},{8,24},{12,28},{16,0},{20,4},{24,8},{28,12},{1,17},{... | collective-permute-start | bytes 1572872 | tf_op jit(solution)/shard_map/ppermute | solution.py:936
  514.0 1.0 copy-start.11
  515.0 7.4 %copy-start.27 = (f32[24,1024]{1,0:T(8,128)S(1)}, f32[24,1024]{1,0:T(8,128)}, u32[]{:S(2)}) copy-start(f32[24,1024]{1,0:T(8,128)} %add_small.7.refs_0_.refs_1_) | copy-start | bytes 294916
  520.4 37.1 %collective-permute-start.35 = (bf16[2,4,128,256]{3,2,1,0:T(8,128)(2,1)}, bf16[2,4,128,256]{3,2,1,0:T(8,128)(2,1)S(1)}, u32[]{:S(2)}, u32[]{:S(2)}) collective-permute-start(bf16[2,4,128,256]{3,2,1,0:T(8,128)(2,1)} %get-tuple-element.188.refs_0_), channel_id=1, source_target_pairs={{0,8},{4,12},{8,0},{12,4},{16,24},{20,28},{24,16},{28,20},{1,9},{5... | collective-permute-start | bytes 1572872 | tf_op jit(solution)/shard_map/ppermute | solution.py:936
  522.4 23.6 %collective-permute-start.31 = (f32[24,1024]{1,0:T(8,128)S(1)}, f32[24,1024]{1,0:T(8,128)S(1)}, u32[]{:S(2)}, u32[]{:S(2)}) collective-permute-start(f32[24,1024]{1,0:T(8,128)S(1)} %copy-done.27), channel_id=1, source_target_pairs={{0,8},{4,12},{8,0},{12,4},{16,24},{20,28},{24,16},{28,20},{1,9},{5... | collective-permute-start | bytes 294920 | tf_op jit(solution)/shard_map/ppermute | solution.py:923
  548.2 18.2 %collective-permute-start.36 = (f32[24,1024]{1,0:T(8,128)}, f32[24,1024]{1,0:T(8,128)S(1)}, u32[]{:S(2)}, u32[]{:S(2)}) collective-permute-start(f32[24,1024]{1,0:T(8,128)} %add_small.8.refs_0_.refs_1_), channel_id=1, source_target_pairs={{0,16},{4,20},{8,24},{12,28},{16,0},{20,4},{24,8},{28,12},{1,17},{... | collective-permute-start | bytes 294920 | tf_op jit(solution)/shard_map/ppermute | solution.py:923
  551.6 1.0 copy-start.22
  561.6 14.7 %collective-permute-start.37 = (bf16[1,4,128,256]{3,2,1,0:T(8,128)(2,1)}, bf16[1,4,128,256]{3,2,1,0:T(8,128)(2,1)S(1)}, u32[]{:S(2)}, u32[]{:S(2)}) collective-permute-start(bf16[1,4,128,256]{3,2,1,0:T(8,128)(2,1)} %get-tuple-element.196.refs_2_), channel_id=1, source_target_pairs={{0,16},{4,20},{8,24},{12,28},{16,0},{20,4},{24,8},{28,12},{1,17},{... | collective-permute-start | bytes 786440 | tf_op jit(solution)/shard_map/ppermute | solution.py:936
  (20 other events, 15.8 us)
Sparse Core Ops, SparseCore 0:
  151.3 92.0 reduce-scatter.2
  247.5 110.5 reduce-scatter.4

commit v4 on v3

--- a/solution.py
+++ b/solution.py
@@ -8,11 +8,11 @@
 BF = jnp.bfloat16
 F32 = jnp.float32
 TILE_DENSE = 512
-TILE_EXPERT = 256
+TILE_EXPERT = 304
 PIECE = 16
 SMALL = pl.CostEstimate(flops=0, bytes_accessed=0, transcendentals=0)
 VMEM = 60 * 1024 * 1024
-ANY = pl.BlockSpec(memory_space=pl.ANY)
+ANY = pl.BlockSpec(memory_space=pltpu.HBM)
 SMEM = pl.BlockSpec(memory_space=pltpu.SMEM)
 
 
@@ -413,13 +413,13 @@
 
 def split_add(kept, came, deps=()):
     h, m, blk, f = kept.shape
-    near = pl.BlockSpec((1, 1, blk, f), lambda i, k: (i, k, 0, 0))
-    far = pl.BlockSpec((1, 1, blk, f), lambda i, k: (i + h // 2, k, 0, 0))
+    near = pl.BlockSpec((1, m, blk, f), lambda i: (i, 0, 0, 0))
+    far = pl.BlockSpec((1, m, blk, f), lambda i: (i + h // 2, 0, 0, 0))
     out = jax.ShapeDtypeStruct((h // 2, m, blk, f), BF)
     return pl.pallas_call(
         partial(split_add_kernel, len(deps)),
         name="split_add",
-        grid=(h // 2, m),
+        grid=(h // 2,),
         in_specs=[ANY] * len(deps) + [near, far, near, far],
         out_specs=[near, near],
         out_shape=[out, out],
@@ -991,6 +991,7 @@
     wo_all = [out_weight] + [from_sequence(out_weight, ds) for ds in range(1, seqs)]
     gain_one, shift_one, gain_two, shift_two = [v.reshape(1, d) for v in (gain_one, shift_one, gain_two, shift_two)]
     prefix = lax.dynamic_slice_in_dim(prefixes, s, 1)
+    rm = jnp.concatenate([router_weight, mix_weight, jnp.zeros((d, LANES - experts - 2), BF)], axis=1)
     n1, dys = first_norm(j1, xs, gain_one, shift_one, cotangent, pos_row)
     columns = jnp.arange(pairs, dtype=jnp.int32)
     pieces = [[] for _ in fetched]
@@ -1000,7 +1001,7 @@
             held = hold(got[0], (n1,))
             pieces[k] = [[held], [over_dp(held, 0)]]
             fence += (held,)
-    saved = [attn_forward(prefix, columns, n1, [w_own], heads, deps=fence[1:])]
+    saved = [attn_forward(prefix, columns, n1, [w_own], heads, deps=fence[1:] + (rm,))]
     if relay:
         for k, got in enumerate(fetched):
             held = hold(got[1], (saved[0][4],))
@@ -1035,7 +1036,6 @@
     n2_mine = [n2] + [from_sequence(n2, ds) for ds in range(1, seqs)]
     n2_near = [n2] + [from_member(n2, k) for k in range(1, members)]
 
-    rm = jnp.concatenate([router_weight, mix_weight, jnp.zeros((d, LANES - experts - 2), BF)], axis=1)
     straight = tuple(range(bits))
     pick = lambda v, which: [v[q] for q in which]
     out_a, rg_a, sums = ffn_dense(me1, n2_near, dy_near, rm, up_weight, down_weight, experts, straight, deps=tuple(dy_mine[1:]))
@@ -1102,24 +1102,24 @@
         v.launch()
     came_far, terms = onward(rg_far, ())
     mark = tuple(terms[:1])
+    for v in sums_e[:1]:
+        mark = v.add(mark)
     mg, mc, sums_two = middle_backward(bounds, t1, rg_near + came_far, n2, rm, middle, cotangent, gain_two, pos_col, mark)
     mcs = [mc] + [from_member(mc, k) for k in range(1, members)]
     mark = (mc,)
-    for v in sums_e[:1]:
-        mark = v.add(mark)
+    out_near, out_far = to_owner([hold(v, mark) for v in out_e])
     ngs = None
     grads = [None] * seqs
     for ds in list(range(1, seqs)) + [0]:
         ngs, grads[ds] = attn_backward(prefix, me1, j1, mcs, n1, wo_all[ds], w_all[ds], saved[ds], ngs, bits, mark)
         mark = (grads[ds],)
         if ds == 1 or seqs == 1:
-            for v in sums_e[1:]:
-                mark = v.add(mark)
-            for v in sums_e[:1]:
-                mark = v.add(mark)
+            out_came, terms = onward(out_far, mark)
+            mark = tuple(terms[:1]) or mark
     moved = [to_sequence(grads[ds], ds) for ds in range(1, seqs)]
     ng_parts = [ngs[0]] + [to_member(ngs[k], k) for k in range(1, members)]
-    mark = dense_sum.add(mark)
+    for v in sums_e[1:2]:
+        mark = v.add(mark)
     input_grad, sums_one = input_backward(ng_parts, inputs, mg, gain_one, mark)
     mark = (sums_one,)
     sums = Everywhere(jnp.concatenate([sums_two, sums_one], axis=0))
@@ -1134,11 +1134,8 @@
         done = last_add(terms, (False, True), (experts, e), stacks, mark)
         return done, (done[1],)
 
-    for v in sums_e[1:]:
+    for v in sums_e[:1]:
         mark = v.add(mark)
-    stacks, mark = finish(0, mark)
-    if experts > apart:
-        stacks, mark = finish(apart, mark)
     mark = sums.add(mark)
     keep = grads[0]
     for v in moved[:-1]:
@@ -1150,25 +1147,31 @@
         keep, send = keep[:dp // 2], keep[dp // 2:]
     attn_sum = Halving(keep, send, straight)
     attn_sum.launch()
+    mark = sums.add(mark)
     mark = dense_sum.add(mark)
-    out_near, out_far = to_owner([hold(v, mark) for v in out_e])
-    out_came, terms = onward(out_far, mark)
-    mark = tuple(terms[:1]) or mark
+    stacks, mark = finish(0, mark)
+    for v in sums_e[2:]:
+        mark = v.add(mark)
+    for v in sums_e[1:]:
+        mark = v.add(mark)
+    mark = sums.add(mark)
+    layer_output = layer_out(out_near + out_came, middle, pos_col, mark)
+    mark = (layer_output,)
+    if experts > apart:
+        stacks, mark = finish(apart, mark)
+    mark = dense_sum.add(mark)
+    mark = attn_sum.add(mark)
     mark = sums.add(mark)
     for e in range(apart + 1, experts):
         stacks, mark = finish(e, mark)
-    mark = sums.add(mark)
-    mark = attn_sum.add(mark)
-    mark = sums.add(mark)
     mark = dense_sum.rest(mark)
     up_out, down_out = last_add([dense_sum.keep, dense_sum.came], (False, True), deps=mark)
-    layer_output = layer_out(out_near + out_came, middle, pos_col, (up_out,))
-    mark = attn_sum.add((layer_output,))
+    mark = attn_sum.add((up_out,))
+    while sums.came is not None:
+        mark = sums.add(mark)
     for e in range(1, apart):
         stacks, mark = finish(e, mark)
     expert_up_out, expert_down_out = stacks
-    while sums.came is not None:
-        mark = sums.add(mark)
     mark = attn_sum.rest(mark)
     *qkv_parts, out_out = last_add([attn_sum.keep, attn_sum.came], (False, False, False, True), deps=mark)
     lanes = d // (dp * tensor)

time: 590 us -> 566 us (0.959)
  Pallas kernels: 311 us -> 300 us
  local copies, waits for them, and re-layouts: 37.6 us -> 30.7 us
  starting transfers between devices: 43 us -> 36.9 us
    ppermute x8, waiting for transfers between devices: 26.4 us -> 4.03 us  [from_sequence(): lax.ppermute(v, 'tensor', [(place(a, b), place(a - k, b)) for a, b in eve...]
    ppermute x14, waiting for transfers between devices: 71.9 us -> 89.9 us  [over_dp(): lax.ppermute(v, 'dp', [(i, i ^ 1 << bit) for i in range(lax.axis_size('dp...]
    pallas_call x9, Pallas kernels: 38.2 us -> 26.7 us  [split_add(): pl.pallas_call(partial(split_add_kernel, len(deps)), name='split_add', gr...]
    ppermute x14, starting transfers between devices: 30.8 us -> 20.5 us  [over_dp(): lax.ppermute(v, 'dp', [(i, i ^ 1 << bit) for i in range(lax.axis_size('dp...]
    unnamed x93 -> x80, local copies, waits for them, and re-layouts: 27.6 us -> 19.9 us
  transfers between devices with their start and end apart: 40 -> 40, of which waited for: 12 -> 11; matrix products, arithmetic and copies ran while one was open for 4% -> 4% of each run, Pallas kernels for 49% -> 49%
where the time goes in v4:
time: 566 us; the launch traced here: 560 us
  Pallas kernels  300 us (53%)
  waiting for transfers between devices  146 us (26%)
  starting transfers between devices  36.9 us (7%)
  local copies, waits for them, and re-layouts  30.7 us (5%)
  blocking collectives  21.5 us (4%)
  between operations  14.6 us (3%)
  other arithmetic  9.78 us (2%)
    ppermute x14, waiting for transfers between devices, over_dp(): lax.ppermute(v, 'dp', [(i, i ^ 1 << bit) for i in range(lax.axis_size('dp...  89.9 us
    pallas_call x2, Pallas kernels, ffn_experts(): pl.pallas_call(partial(expert_kernel, (first, count, whole, chunks, rows,...  76.1 us
    pallas_call x2, Pallas kernels, attn_backward(): pl.pallas_call(skip(partial(attn_backward_kernel, length, bits, members,...  55.2 us
    pallas_call x2, Pallas kernels, ffn_dense(): pl.pallas_call(partial(dense_kernel, (chunks, rows, tm, lanes, order, fir...  49.6 us
    ppermute x5, waiting for transfers between devices, launch(): lax.ppermute(self.v, axis, [(i, i ^ bit) for i in range(lax.axis_size(axi...  49 us
    pallas_call x3, Pallas kernels, attn_forward(): pl.pallas_call(skip(partial(attn_forward_kernel, length, tuple((w.shape[0...  31.6 us
    pallas_call x9, Pallas kernels, split_add(): pl.pallas_call(partial(split_add_kernel, len(deps)), name='split_add', gr...  26.7 us
    all_to_all x1, blocking collectives, shards(): lax.all_to_all(sent, 'tensor', 0, 0, axis_index_groups=[[place(a, b) for...  21.5 us
  transfers between devices with their start and end apart: 40, of which 11 were waited for; matrix products, arithmetic and copies ran while one was open for 4% of the time, Pallas kernels for 49%

profile of v4, /device:TPU:0, one launch (start us, length us, event | category | flops | bytes accessed | tf_op | source)
XLA Modules:
  0.0 559.6 jit_solution(868708881292994235)
XLA Ops:
  8.8 2.6 collective-permute-start
  15.0 5.1 first_norm.1
  20.2 4.0 collective-permute-done.refs_0_
  25.0 1.9 collective-permute-start.2
  26.9 1.5 collective-permute-start.5
  30.9 14.2 %attn_forward.3 = (bf16[1024,256]{1,0:T(8,128)(2,1)}, bf16[1024,256]{1,0:T(8,128)(2,1)}, bf16[1024,256]{1,0:T(8,128)(2,1)}, bf16[1024,256]{1,0:T(8,128)(2,1)}, f32[2,8,1024]{2,1,0:T(8,128)}) custom-call(s32[1]{0:T(128)} %dynamic_slice.12.refs_0_, s32[2]{0:T(128)} %iota.11.refs_1_, bf16[2,1024,128]{2,1,0:T(8,128)(2,1)} %hold.8.refs_2_.refs_4_, ...), custom_call_target="tpu_custom_call" | custom-call | tf_op jit(solution)/shard_map/attn_forward/pallas_call | solution.py:542
  47.5 8.7 %attn_forward.4 = (bf16[1024,256]{1,0:T(8,128)(2,1)}, bf16[1024,256]{1,0:T(8,128)(2,1)}, bf16[1024,256]{1,0:T(8,128)(2,1)}, bf16[1024,256]{1,0:T(8,128)(2,1)}, f32[2,8,1024]{2,1,0:T(8,128)}) custom-call(s32[1]{0:T(128)} %dynamic_slice.12.refs_0_, s32[1]{0:T(128)} %bitcast.70, f32[2,8,1024]{2,1,0:T(8,128)} %get-tuple-element.112.refs_1_.refs_2_.refs_13_, ...), custom_call_target="tpu_custom_call" | custom-call | tf_op jit(solution)/shard_map/attn_forward/pallas_call | solution.py:542
  56.9 8.7 %attn_forward.5 = (bf16[1024,256]{1,0:T(8,128)(2,1)}, bf16[1024,256]{1,0:T(8,128)(2,1)}, bf16[1024,256]{1,0:T(8,128)(2,1)}, bf16[1024,256]{1,0:T(8,128)(2,1)}, f32[2,8,1024]{2,1,0:T(8,128)}) custom-call(s32[1]{0:T(128)} %dynamic_slice.12.refs_0_, s32[1]{0:T(128)} %bitcast.69, ...), custom_call_target="tpu_custom_call", output_to_operand_aliasing={{0}: (5, {}), {1}: (6, {}), {2}: (7, {}), {3}: (8, {}), {4}... | custom-call | tf_op jit(solution)/shard_map/attn_forward/pallas_call | solution.py:542
  66.4 3.8 project.1
  70.1 21.5 %all_to_all.5.came = bf16[2,512,1024]{2,1,0:T(8,128)(2,1)} all-to-all(bf16[2,512,1024]{2,1,0:T(8,128)(2,1)} %project.1), channel_id=1, replica_groups={{0,1},{2,3},{4,5},{6,7},{8,9},{10,11},{12,13},{14,15},{16,17},{18,19},{..., dimensions={0} | all-to-all | bytes 4194304 | tf_op jit(solution)/shard_map/all_to_all | solution.py:1034
  91.6 4.4 second_norm.1
  96.1 1.9 collective-permute-start.6
  99.0 23.1 %ffn_dense.2 = (bf16[512,1024]{1,0:T(8,128)(2,1)}, bf16[512,1024]{1,0:T(8,128)(2,1)}, bf16[528,1024]{1,0:T(8,128)(2,1)}, bf16[528,1024]{1,0:T(8,128)(2,1)}, f32[1024,1024]{1,0:T(8,128)}, /*index=5*/f32[1024,1024]{1,0:T(8,128)}) custom-call(s32[1]{0:T(128)} %bitcast.me_ref.refs_1_, bf16[512,1024]{1,0:T(8,128)(2,1)} %copy-done, ...), custom_call_target="tpu_custom_call" | custom-call | tf_op jit(solution)/shard_map/ffn_dense/pallas_call | solution.py:211
  128.5 24.5 %ffn_experts.2 = (bf16[512,1024]{1,0:T(8,128)(2,1)}, bf16[512,1024]{1,0:T(8,128)(2,1)}, bf16[512,1024]{1,0:T(8,128)(2,1)}, bf16[512,1024]{1,0:T(8,128)(2,1)}, bf...) custom-call(s32[1]{0:T(128)} %bitcast.me_ref.refs_1_, ...), custom_call_target="tpu_custom_call" | custom-call | tf_op jit(solution)/shard_map/ffn_experts/pallas_call | solution.py:387
  153.6 51.6 %ffn_experts.3 = (bf16[512,1024]{1,0:T(8,128)(2,1)}, bf16[512,1024]{1,0:T(8,128)(2,1)}, bf16[512,1024]{1,0:T(8,128)(2,1)}, bf16[512,1024]{1,0:T(8,128)(2,1)}, bf...) custom-call(s32[1]{0:T(128)} %bitcast.me_ref.refs_1_, ...), custom_call_target="tpu_custom_call" | custom-call | tf_op jit(solution)/shard_map/ffn_experts/pallas_call | solution.py:387
  205.2 26.5 %ffn_dense.3 = (bf16[512,1024]{1,0:T(8,128)(2,1)}, bf16[512,1024]{1,0:T(8,128)(2,1)}, bf16[528,1024]{1,0:T(8,128)(2,1)}, bf16[528,1024]{1,0:T(8,128)(2,1)}, bf16...) custom-call(s32[1]{0:T(128)} %bitcast.me_ref.refs_1_, bf16[512,1024]{1,0:T(8,128)(2,1)} %hold.10.refs_1_.refs_0_, ...), custom_call_target="tpu_custom_call" | custom-call | tf_op jit(solution)/shard_map/ffn_dense/pallas_call | solution.py:211
  231.8 1.8 collective-permute-start.13
  234.8 2.8 add_parts.2.refs_0_
  237.6 1.7 collective-permute-start.15
  240.1 51.1 %collective-permute-done.13.refs_3_.refs_4_ = bf16[4,2,128,1024]{3,2,1,0:T(8,128)(2,1)S(1)} collective-permute-done((bf16[4,2,128,1024]{3,2,1,0:T(8,128)(2,1)}, bf16[4,2,128,1024]{3,2,1,0:T(8,128)(2,1)S(1)}, u32[]{:S(2)}, u32[]{:S(2)}) %collective-permute-start.13) | collective-permute-done | bytes 2097184 | tf_op jit(solution)/shard_map/ppermute | solution.py:936
  292.5 3.3 split_add.9
  296.9 10.3 %middle_backward.1 = (f32[512,1024]{1,0:T(8,128)}, bf16[512,1024]{1,0:T(8,128)(2,1)}, f32[16,1024]{1,0:T(8,128)}) custom-call(s32[4,5]{1,0:T(4,128)} %stack.50.bnd_ref.refs_0_, s32[1]{0:T(128)} %bitcast.7.refs_1_, bf16[2,2,128,1024]{3,2,1,0:T(8,128)(2,1)} %get-tuple-element.143.refs_2_, bf16[528,1024]{1,0:T(8,128)(2,1)} %get-tuple-element.144.refs_3_, ...), custom_call_target="tpu_custom_call" | custom-call | tf_op jit(solution)/shard_map/middle_backward/pallas_call | solution.py:824
  307.3 1.5 collective-permute-start.18
  308.8 1.9 constant_dynamic-update-slice_fusion.1
  311.8 3.1 maximum_select_fusion.refs_8_
  315.0 27.2 %attn_backward.2 = (bf16[512,1024]{1,0:T(8,128)(2,1)}, bf16[512,1024]{1,0:T(8,128)(2,1)}, bf16[8,4,128,256]{3,2,1,0:T(8,128)(2,1)}) custom-call(s32[1]{0:T(128)} %dynamic_slice.12.refs_0_, s32[1]{0:T(128)} %bitcast.me_ref.refs_1_, s32[1]{0:T(128)} %bitcast.1.j_ref.refs_2_, bf16[512,1024]{1,0:T(8,128)(2,1)} %get-tuple-element.147.refs_3_.refs_4_.refs_1_, ...), custom_call_target="tpu_custom_call" | custom-call | tf_op jit(solution)/shard_map/attn_backward/pallas_call | solution.py:648
  342.2 1.8 collective-permute-start.22
  344.3 2.8 add_parts.3.refs_3_
  347.1 27.9 %attn_backward.3 = (bf16[512,1024]{1,0:T(8,128)(2,1)}, bf16[512,1024]{1,0:T(8,128)(2,1)}, bf16[8,4,128,256]{3,2,1,0:T(8,128)(2,1)}) custom-call(s32[1]{0:T(128)} %dynamic_slice.12.refs_0_, s32[1]{0:T(128)} %bitcast.me_ref.refs_1_, s32[1]{0:T(128)} %bitcast.1.j_ref.refs_2_, bf16[512,1024]{1,0:T(8,128)(2,1)} %add_parts.3.refs_3_, ...), custom_call_target="tpu_custom_call" | custom-call | tf_op jit(solution)/shard_map/attn_backward/pallas_call | solution.py:648
  375.1 1.6 collective-permute-start.20
  378.0 3.5 split_add.10
  382.1 5.6 %input_backward.1 = (f32[512,1024]{1,0:T(8,128)}, f32[8,1024]{1,0:T(8,128)}) custom-call(bf16[2,2,128,1024]{3,2,1,0:T(8,128)(2,1)} %get-tuple-element.163.refs_0_, bf16[512,1024]{1,0:T(8,128)(2,1)} %get-tuple-element.164.refs_1_, bf16[512,1024]{1,0:T(8,128)(2,1)} %collective-permute-done.19.refs_2_, bf16[512,1024]{1,0:T(8,128)(2,1)} %refs_3_.1, ...), custom_call_target="tpu_custom_call" | custom-call | tf_op jit(solution)/shard_map/input_backward/pallas_call | solution.py:902
  388.5 12.9 %collective-permute-done.20.refs_3_.refs_4_ = bf16[2,2,128,1024]{3,2,1,0:T(8,128)(2,1)S(1)} collective-permute-done((bf16[2,2,128,1024]{3,2,1,0:T(8,128)(2,1)}, bf16[2,2,128,1024]{3,2,1,0:T(8,128)(2,1)S(1)}, u32[]{:S(2)}, u32[]{:S(2)}) %collective-permute-start.20) | collective-permute-done | bytes 1048608 | tf_op jit(solution)/shard_map/ppermute | solution.py:936
  402.3 2.6 split_add.11
  405.6 1.6 add_small.5.refs_0_.refs_1_
  407.6 1.7 collective-permute-start.28
  409.3 4.2 split_add.12
  414.1 1.6 add_small.6.refs_0_.refs_1_
  415.7 3.5 split_add.13
  419.1 1.5 collective-permute-start.30
  420.6 1.7 collective-permute-start.31
  423.8 1.8 collective-permute-start.26
  425.6 22.3 %collective-permute-done.26.refs_2_ = f32[24,1024]{1,0:T(8,128)S(1)} collective-permute-done((f32[24,1024]{1,0:T(8,128)S(1)}, f32[24,1024]{1,0:T(8,128)S(1)}, u32[]{:S(2)}, u32[]{:S(2)}) %collective-permute-start.26) | collective-permute-done | bytes 98336 | tf_op jit(solution)/shard_map/ppermute | solution.py:923
  447.9 2.5 collective-permute-start.29
  450.4 2.1 last_add.6
  452.5 2.7 split_add.14
  455.2 1.6 add_small.7.refs_0_.refs_1_
  457.2 4.9 layer_out.1.refs_2_
  462.1 22.5 %collective-permute-done.29.refs_4_ = bf16[1,2,128,1024]{3,2,1,0:T(8,128)(2,1)} collective-permute-done((bf16[1,2,128,1024]{3,2,1,0:T(8,128)(2,1)}, bf16[1,2,128,1024]{3,2,1,0:T(8,128)(2,1)}, u32[]{:S(2)}, u32[]{:S(2)}) %collective-permute-start.29) | collective-permute-done | bytes 524320 | tf_op jit(solution)/shard_map/ppermute | solution.py:936
  484.6 2.4 last_add.7
  487.0 2.6 split_add.15
  490.6 2.4 split_add.16
  493.0 3.9 collective-permute-start.35
  497.0 26.7 %collective-permute-done.32.refs_2_ = f32[24,1024]{1,0:T(8,128)S(1)} collective-permute-done((f32[24,1024]{1,0:T(8,128)S(1)}, f32[24,1024]{1,0:T(8,128)S(1)}, u32[]{:S(2)}, u32[]{:S(2)}) %collective-permute-start.32) | collective-permute-done | bytes 98336 | tf_op jit(solution)/shard_map/ppermute | solution.py:923
  524.4 1.6 add_small.8.refs_2_.refs_1_
  527.4 2.4 last_add.8
  530.6 2.4 last_add.9
  533.8 2.0 split_add.17
  535.8 2.3 collective-permute-start.37
  538.7 1.6 add_small.9.refs_2_
  541.6 2.1 last_add.10
  546.4 1.9 collective-permute-done.37.refs_2_
  549.0 1.9 last_add.11
  550.8 1.8 pad_maximum_fusion
  (181 shorter events, 43.7 us)
Async XLA Ops:
  7.2 443.2 %reduce-scatter.3.cloned.1.call-start = ((), (), s32[]{:S(2)}) async-start(), calls=%async_computation.3 | async-start | bytes 4718592 | tf_op jit(solution)/shard_map/reduce_scatter | solution.py:1095
  7.2 6.8 %collective-permute-start.1 = (bf16[512,1024]{1,0:T(8,128)(2,1)}, bf16[512,1024]{1,0:T(8,128)(2,1)S(1)}, u32[]{:S(2)}, u32[]{:S(2)}) collective-permute-start(bf16[512,1024]{1,0:T(8,128)(2,1)} %refs_3_.1), channel_id=1, source_target_pairs={{0,1},{1,0},{2,3},{3,2},{4,5},{5,4},{6,7},{7,6},{8,9},{9,8},{10,11... | collective-permute-start | bytes 3145736 | tf_op jit(solution)/shard_map/ppermute | solution.py:958
  8.8 15.4 %collective-permute-start = (bf16[2,1024,128]{2,1,0:T(8,128)(2,1)S(1)}, bf16[2,1024,128]{2,1,0:T(8,128)(2,1)S(1)}, u32[]{:S(2)}, u32[]{:S(2)}) collective-permute-start(bf16[2,1024,128]{2,1,0:T(8,128)(2,1)S(1)} %dynamic-slice_bitcast_fusion), channel_id=1, source_target_pairs={{0,2},{1,3},{2,0},{3,1},{4,6},{5,7},{6,4},{7,5},{8,10},{9,11},{10,... | collective-permute-start | bytes 1572872 | tf_op jit(solution)/shard_map/ppermute | solution.py:961
  12.4 32.8 %collective-permute-start.3 = (bf16[1,1024,128]{2,1,0:T(8,128)(2,1)S(1)}, bf16[1,1024,128]{2,1,0:T(8,128)(2,1)S(1)}, u32[]{:S(2)}, u32[]{:S(2)}) collective-permute-start(bf16[1,1024,128]{2,1,0:T(8,128)(2,1)S(1)} %dynamic-slice_bitcast_fusion.1), channel_id=1, source_target_pairs={{0,2},{1,3},{2,0},{3,1},{4,6},{5,7},{6,4},{7,5},{8,10},{9,11},{10,... | collective-permute-start | bytes 786440 | tf_op jit(solution)/shard_map/ppermute | solution.py:961
  14.0 1.0 copy-start.19
  20.2 6.8 %copy-start.16 = (bf16[256,1024]{1,0:T(8,128)(2,1)S(1)}, bf16[256,1024]{1,0:T(8,128)(2,1)}, u32[]{:S(2)}) copy-start(bf16[256,1024]{1,0:T(8,128)(2,1)} %refs_7_.3) | copy-start | bytes 1572868
  20.2 8.3 %copy-start.35 = (bf16[1024,4]{0,1:T(4,128)(2,1)S(1)}, bf16[1024,4]{0,1:T(4,128)(2,1)}, u32[]{:S(2)}) copy-start(bf16[1024,4]{0,1:T(4,128)(2,1)} %param.30) | copy-start | bytes 24580
  20.2 8.5 %copy-start.36 = (bf16[1024,2]{0,1:T(2,128)(2,1)S(1)}, bf16[1024,2]{0,1:T(2,128)(2,1)}, u32[]{:S(2)}) copy-start(bf16[1024,2]{0,1:T(2,128)(2,1)} %param.31) | copy-start | bytes 12292
  20.2 8.7 %copy-start.37 = (s32[2]{0:T(128)S(1)}, s32[2]{0:T(128)}, u32[]{:S(2)}) copy-start(s32[2]{0:T(128)} %param.19) | copy-start | bytes 28
  25.0 31.2 %collective-permute-start.2 = (bf16[2,1024,128]{2,1,0:T(8,128)(2,1)}, bf16[2,1024,128]{2,1,0:T(8,128)(2,1)}, u32[]{:S(2)}, u32[]{:S(2)}) collective-permute-start(bf16[2,1024,128]{2,1,0:T(8,128)(2,1)} %hold.8.refs_2_.refs_4_), channel_id=1, source_target_pairs={{0,4},{4,0},{8,12},{12,8},{16,20},{20,16},{24,28},{28,24},{1,5},{5... | collective-permute-start | bytes 1572872 | tf_op jit(solution)/shard_map/ppermute | solution.py:936
  26.9 38.6 %collective-permute-start.5 = (bf16[256,1024]{1,0:T(8,128)(2,1)S(1)}, bf16[256,1024]{1,0:T(8,128)(2,1)S(1)}, u32[]{:S(2)}, u32[]{:S(2)}) collective-permute-start(bf16[256,1024]{1,0:T(8,128)(2,1)S(1)} %copy-done.16), channel_id=1, source_target_pairs={{0,2},{1,3},{2,0},{3,1},{4,6},{5,7},{6,4},{7,5},{8,10},{9,11},{10,... | collective-permute-start | bytes 1572872 | tf_op jit(solution)/shard_map/ppermute | solution.py:961
  30.9 16.5 %copy-start.2 = (bf16[512,1024]{1,0:T(8,128)(2,1)S(1)}, bf16[512,1024]{1,0:T(8,128)(2,1)}, u32[]{:S(2)}) copy-start(bf16[512,1024]{1,0:T(8,128)(2,1)} %get-tuple-element.120.refs_3_.refs_4_) | copy-start | bytes 3145732
  45.8 10.3 %collective-permute-start.4 = (bf16[1,1024,128]{2,1,0:T(8,128)(2,1)}, bf16[1,1024,128]{2,1,0:T(8,128)(2,1)S(1)}, u32[]{:S(2)}, u32[]{:S(2)}) collective-permute-start(bf16[1,1024,128]{2,1,0:T(8,128)(2,1)} %hold.9.refs_5_), channel_id=1, source_target_pairs={{0,4},{4,0},{8,12},{12,8},{16,20},{20,16},{24,28},{28,24},{1,5},{5... | collective-permute-start | bytes 786440 | tf_op jit(solution)/shard_map/ppermute | solution.py:936
  47.4 50.6 %collective-permute-start.9 = (bf16[512,1024]{1,0:T(8,128)(2,1)S(1)}, bf16[512,1024]{1,0:T(8,128)(2,1)}, u32[]{:S(2)}, u32[]{:S(2)}) collective-permute-start(bf16[512,1024]{1,0:T(8,128)(2,1)S(1)} %copy-done.2), channel_id=1, source_target_pairs={{0,1},{1,0},{2,3},{3,2},{4,5},{5,4},{6,7},{7,6},{8,9},{9,8},{10,11... | collective-permute-start | bytes 3145736 | tf_op jit(solution)/shard_map/ppermute | solution.py:958
  47.4 50.6 %collective-permute-start.7 = (bf16[512,1024]{1,0:T(8,128)(2,1)S(1)}, bf16[512,1024]{1,0:T(8,128)(2,1)S(1)}, u32[]{:S(2)}, u32[]{:S(2)}) collective-permute-start(bf16[512,1024]{1,0:T(8,128)(2,1)S(1)} %copy-done.2), channel_id=1, source_target_pairs={{0,2},{1,3},{2,0},{3,1},{4,6},{5,7},{6,4},{7,5},{8,10},{9,11},{10,... | collective-permute-start | bytes 3145736 | tf_op jit(solution)/shard_map/ppermute | solution.py:961
  96.0 3.0 collective-permute-start.8
  96.1 26.0 %collective-permute-start.6 = (bf16[512,1024]{1,0:T(8,128)(2,1)}, bf16[512,1024]{1,0:T(8,128)(2,1)S(1)}, u32[]{:S(2)}, u32[]{:S(2)}) collective-permute-start(bf16[512,1024]{1,0:T(8,128)(2,1)} %get-tuple-element.119.refs_1_.refs_0_.refs_6_), channel_id=1, source_target_pairs={{0,2},{1,3},{2,0},{3,1},{4,6},{5,7},{6,4},{7,5},{8,10},{9,11},{10,... | collective-permute-start | bytes 3145736 | tf_op jit(solution)/shard_map/ppermute | solution.py:961
  98.0 1.0 copy-start
  122.1 1.0 copy-start.1
  123.1 3.3 collective-permute-start.10
  123.2 4.3 collective-permute-start.11
  126.4 1.1 copy-start.3
  127.5 1.1 copy-start.4
  153.1 388.5 %reduce-scatter.5.cloned.1.call-start = ((), (), s32[]{:S(2)}) async-start(), calls=%async_computation.4 | async-start | bytes 4718592 | tf_op jit(solution)/shard_map/reduce_scatter | solution.py:1095
  231.7 3.1 collective-permute-start.12
  231.8 59.5 %collective-permute-start.13 = (bf16[4,2,128,1024]{3,2,1,0:T(8,128)(2,1)}, bf16[4,2,128,1024]{3,2,1,0:T(8,128)(2,1)S(1)}, u32[]{:S(2)}, u32[]{:S(2)}) collective-permute-start(bf16[4,2,128,1024]{3,2,1,0:T(8,128)(2,1)} %get-tuple-element.142), channel_id=1, source_target_pairs={{0,4},{4,0},{8,12},{12,8},{16,20},{20,16},{24,28},{28,24},{1,5},{5... | collective-permute-start | bytes 6291464 | tf_op jit(solution)/shard_map/ppermute | solution.py:936
  233.5 62.4 %collective-permute-start.14 = (bf16[528,1024]{1,0:T(8,128)(2,1)}, bf16[528,1024]{1,0:T(8,128)(2,1)S(1)}, u32[]{:S(2)}, u32[]{:S(2)}) collective-permute-start(bf16[528,1024]{1,0:T(8,128)(2,1)} %get-tuple-element.145), channel_id=1, source_target_pairs={{0,1},{1,0},{2,3},{3,2},{4,5},{5,4},{6,7},{7,6},{8,9},{9,8},{10,11... | collective-permute-start | bytes 3244040 | tf_op jit(solution)/shard_map/ppermute | solution.py:958
  237.6 58.3 %collective-permute-start.15 = (bf16[528,1024]{1,0:T(8,128)(2,1)}, bf16[528,1024]{1,0:T(8,128)(2,1)}, u32[]{:S(2)}, u32[]{:S(2)}) collective-permute-start(bf16[528,1024]{1,0:T(8,128)(2,1)} %add_parts.2.refs_0_), channel_id=1, source_target_pairs={{0,2},{1,3},{2,0},{3,1},{4,6},{5,7},{6,4},{7,5},{8,10},{9,11},{10,... | collective-permute-start | bytes 3244040 | tf_op jit(solution)/shard_map/ppermute | solution.py:961
  291.3 1.3 copy-start.8
  295.9 1.1 copy-start.18
  307.3 7.7 %collective-permute-start.16 = (bf16[512,1024]{1,0:T(8,128)(2,1)}, bf16[512,1024]{1,0:T(8,128)(2,1)}, u32[]{:S(2)}, u32[]{:S(2)}) collective-permute-start(bf16[512,1024]{1,0:T(8,128)(2,1)} %get-tuple-element.147.refs_3_.refs_4_.refs_1_), channel_id=1, source_target_pairs={{0,1},{1,0},{2,3},{3,2},{4,5},{5,4},{6,7},{7,6},{8,9},{9,8},{10,11... | collective-permute-start | bytes 3145736 | tf_op jit(solution)/shard_map/ppermute | solution.py:958
  307.3 69.4 %collective-permute-start.18 = (bf16[4,2,128,1024]{3,2,1,0:T(8,128)(2,1)}, bf16[4,2,128,1024]{3,2,1,0:T(8,128)(2,1)S(1)}, u32[]{:S(2)}, u32[]{:S(2)}) collective-permute-start(bf16[4,2,128,1024]{3,2,1,0:T(8,128)(2,1)} %get-tuple-element.162), channel_id=1, source_target_pairs={{0,4},{4,0},{8,12},{12,8},{16,20},{20,16},{24,28},{28,24},{1,5},{5... | collective-permute-start | bytes 6291464 | tf_op jit(solution)/shard_map/ppermute | solution.py:936
  308.8 2.2 copy-start.21
  310.7 1.0 copy-start.7
  310.7 1.1 copy-start.14
  310.7 33.6 %collective-permute-start.17 = (bf16[512,1024]{1,0:T(8,128)(2,1)}, bf16[512,1024]{1,0:T(8,128)(2,1)}, u32[]{:S(2)}, u32[]{:S(2)}) collective-permute-start(bf16[512,1024]{1,0:T(8,128)(2,1)} %hold.13), channel_id=1, source_target_pairs={{0,1},{1,0},{2,3},{3,2},{4,5},{5,4},{6,7},{7,6},{8,9},{9,8},{10,11... | collective-permute-start | bytes 3145736 | tf_op jit(solution)/shard_map/ppermute | solution.py:958
  342.2 65.4 %collective-permute-start.22 = (bf16[8,4,128,256]{3,2,1,0:T(8,128)(2,1)}, bf16[8,4,128,256]{3,2,1,0:T(8,128)(2,1)}, u32[]{:S(2)}, u32[]{:S(2)}) collective-permute-start(bf16[8,4,128,256]{3,2,1,0:T(8,128)(2,1)} %get-tuple-element.152.refs_0_), channel_id=1, source_target_pairs={{0,2},{1,3},{2,0},{3,1},{4,6},{5,7},{6,4},{7,5},{8,10},{9,11},{10,... | collective-permute-start | bytes 6291464 | tf_op jit(solution)/shard_map/ppermute | solution.py:961
  344.0 71.7 %collective-permute-start.24 = (bf16[4,2,128,1024]{3,2,1,0:T(8,128)(2,1)}, bf16[4,2,128,1024]{3,2,1,0:T(8,128)(2,1)}, u32[]{:S(2)}, u32[]{:S(2)}) collective-permute-start(bf16[4,2,128,1024]{3,2,1,0:T(8,128)(2,1)} %get-tuple-element.173), channel_id=1, source_target_pairs={{0,4},{4,0},{8,12},{12,8},{16,20},{20,16},{24,28},{28,24},{1,5},{5... | collective-permute-start | bytes 6291464 | tf_op jit(solution)/shard_map/ppermute | solution.py:936
  375.0 7.1 %collective-permute-start.19 = (bf16[512,1024]{1,0:T(8,128)(2,1)}, bf16[512,1024]{1,0:T(8,128)(2,1)}, u32[]{:S(2)}, u32[]{:S(2)}) collective-permute-start(bf16[512,1024]{1,0:T(8,128)(2,1)} %get-tuple-element.165), channel_id=1, source_target_pairs={{0,1},{1,0},{2,3},{3,2},{4,5},{5,4},{6,7},{7,6},{8,9},{9,8},{10,11... | collective-permute-start | bytes 3145736 | tf_op jit(solution)/shard_map/ppermute | solution.py:958
  375.1 26.2 %collective-permute-start.20 = (bf16[2,2,128,1024]{3,2,1,0:T(8,128)(2,1)}, bf16[2,2,128,1024]{3,2,1,0:T(8,128)(2,1)S(1)}, u32[]{:S(2)}, u32[]{:S(2)}) collective-permute-start(bf16[2,2,128,1024]{3,2,1,0:T(8,128)(2,1)} %get-tuple-element.143.refs_2_), channel_id=1, source_target_pairs={{0,8},{4,12},{8,0},{12,4},{16,24},{20,28},{24,16},{28,20},{1,9},{5... | collective-permute-start | bytes 3145736 | tf_op jit(solution)/shard_map/ppermute | solution.py:936
  376.7 1.3 copy-start.5
  378.0 4.1 copy-start.33
  381.5 42.3 %collective-permute-start.25 = (bf16[2,2,128,1024]{3,2,1,0:T(8,128)(2,1)}, bf16[2,2,128,1024]{3,2,1,0:T(8,128)(2,1)S(1)}, u32[]{:S(2)}, u32[]{:S(2)}) collective-permute-start(bf16[2,2,128,1024]{3,2,1,0:T(8,128)(2,1)} %get-tuple-element.163.refs_0_), channel_id=1, source_target_pairs={{0,8},{4,12},{8,0},{12,4},{16,24},{20,28},{24,16},{28,20},{1,9},{5... | collective-permute-start | bytes 3145736 | tf_op jit(solution)/shard_map/ppermute | solution.py:936
  388.5 16.5 %copy-start.26 = (f32[24,1024]{1,0:T(8,128)}, f32[24,1024]{1,0:T(8,128)S(1)}, u32[]{:S(2)}) copy-start(f32[24,1024]{1,0:T(8,128)S(1)} %constant_dynamic-update-slice_fusion.2.refs_1_) | copy-start | bytes 294916
  388.5 16.4 %collective-permute-start.21 = (f32[24,1024]{1,0:T(8,128)S(1)}, f32[24,1024]{1,0:T(8,128)S(1)}, u32[]{:S(2)}, u32[]{:S(2)}) collective-permute-start(f32[24,1024]{1,0:T(8,128)S(1)} %constant_dynamic-update-slice_fusion.2.refs_1_), channel_id=1, source_target_pairs={{0,1},{1,0},{2,3},{3,2},{4,5},{5,4},{6,7},{7,6},{8,9},{9,8},{10,11... | collective-permute-start | bytes 294920 | tf_op jit(solution)/shard_map/ppermute | solution.py:923
  404.9 2.7 copy-start.9
  407.2 6.3 %collective-permute-start.23 = (f32[24,1024]{1,0:T(8,128)}, f32[24,1024]{1,0:T(8,128)S(1)}, u32[]{:S(2)}, u32[]{:S(2)}) collective-permute-start(f32[24,1024]{1,0:T(8,128)} %add_small.5.refs_0_.refs_1_), channel_id=1, source_target_pairs={{0,2},{1,3},{2,0},{3,1},{4,6},{5,7},{6,4},{7,5},{8,10},{9,11},{10,... | collective-permute-start | bytes 294920 | tf_op jit(solution)/shard_map/ppermute | solution.py:923
  407.6 49.2 %collective-permute-start.27 = (bf16[512,1024]{1,0:T(8,128)(2,1)}, bf16[512,1024]{1,0:T(8,128)(2,1)}, u32[]{:S(2)}, u32[]{:S(2)}) collective-permute-start(bf16[512,1024]{1,0:T(8,128)(2,1)} %hold.15), channel_id=1, source_target_pairs={{0,1},{1,0},{2,3},{3,2},{4,5},{5,4},{6,7},{7,6},{8,9},{9,8},{10,11... | collective-permute-start | bytes 3145736 | tf_op jit(solution)/shard_map/ppermute | solution.py:958
  407.6 49.6 %collective-permute-start.28 = (bf16[512,1024]{1,0:T(8,128)(2,1)S(1)}, bf16[512,1024]{1,0:T(8,128)(2,1)}, u32[]{:S(2)}, u32[]{:S(2)}) collective-permute-start(bf16[512,1024]{1,0:T(8,128)(2,1)S(1)} %copy-done.9), channel_id=1, source_target_pairs={{0,2},{1,3},{2,0},{3,1},{4,6},{5,7},{6,4},{7,5},{8,10},{9,11},{10,... | collective-permute-start | bytes 3145736 | tf_op jit(solution)/shard_map/ppermute | solution.py:961
  415.7 8.1 %copy-start.22 = (f32[24,1024]{1,0:T(8,128)S(1)}, f32[24,1024]{1,0:T(8,128)}, u32[]{:S(2)}) copy-start(f32[24,1024]{1,0:T(8,128)} %add_small.6.refs_0_.refs_1_) | copy-start | bytes 294916
  419.1 67.9 %collective-permute-start.30 = (bf16[2,2,128,1024]{3,2,1,0:T(8,128)(2,1)}, bf16[2,2,128,1024]{3,2,1,0:T(8,128)(2,1)}, u32[]{:S(2)}, u32[]{:S(2)}) collective-permute-start(bf16[2,2,128,1024]{3,2,1,0:T(8,128)(2,1)} %get-tuple-element.174.refs_0_), channel_id=1, source_target_pairs={{0,8},{4,12},{8,0},{12,4},{16,24},{20,28},{24,16},{28,20},{1,9},{5... | collective-permute-start | bytes 3145736 | tf_op jit(solution)/shard_map/ppermute | solution.py:936
  420.6 69.0 %collective-permute-start.31 = (bf16[4,4,128,256]{3,2,1,0:T(8,128)(2,1)}, bf16[4,4,128,256]{3,2,1,0:T(8,128)(2,1)S(1)}, u32[]{:S(2)}, u32[]{:S(2)}) collective-permute-start(bf16[4,4,128,256]{3,2,1,0:T(8,128)(2,1)} %get-tuple-element.171.refs_0_), channel_id=1, source_target_pairs={{0,4},{4,0},{8,12},{12,8},{16,20},{20,16},{24,28},{28,24},{1,5},{5... | collective-permute-start | bytes 3145736 | tf_op jit(solution)/shard_map/ppermute | solution.py:936
  423.8 28.7 %copy-start.10 = (bf16[2,2,128,1024]{3,2,1,0:T(8,128)(2,1)}, bf16[2,2,128,1024]{3,2,1,0:T(8,128)(2,1)S(1)}, u32[]{:S(2)}) copy-start(bf16[2,2,128,1024]{3,2,1,0:T(8,128)(2,1)S(1)} %collective-permute-done.25.refs_3_.refs_4_) | copy-start | bytes 3145732
  423.8 24.1 %collective-permute-start.26 = (f32[24,1024]{1,0:T(8,128)S(1)}, f32[24,1024]{1,0:T(8,128)S(1)}, u32[]{:S(2)}, u32[]{:S(2)}) collective-permute-start(f32[24,1024]{1,0:T(8,128)S(1)} %copy-done.22), channel_id=1, source_target_pairs={{0,4},{4,0},{8,12},{12,8},{16,20},{20,16},{24,28},{28,24},{1,5},{5... | collective-permute-start | bytes 294920 | tf_op jit(solution)/shard_map/ppermute | solution.py:923
  447.9 4.6 copy-start.28
  447.9 36.7 %collective-permute-start.29 = (bf16[1,2,128,1024]{3,2,1,0:T(8,128)(2,1)}, bf16[1,2,128,1024]{3,2,1,0:T(8,128)(2,1)}, u32[]{:S(2)}, u32[]{:S(2)}) collective-permute-start(bf16[1,2,128,1024]{3,2,1,0:T(8,128)(2,1)} %get-tuple-element.169.refs_0_), channel_id=1, source_target_pairs={{0,16},{4,20},{8,24},{12,28},{16,0},{20,4},{24,8},{28,12},{1,17},{... | collective-permute-start | bytes 1572872 | tf_op jit(solution)/shard_map/ppermute | solution.py:936
  456.8 69.8 %collective-permute-start.33 = (bf16[1,2,128,1024]{3,2,1,0:T(8,128)(2,1)}, bf16[1,2,128,1024]{3,2,1,0:T(8,128)(2,1)S(1)}, u32[]{:S(2)}, u32[]{:S(2)}) collective-permute-start(bf16[1,2,128,1024]{3,2,1,0:T(8,128)(2,1)} %get-tuple-element.178.refs_0_), channel_id=1, source_target_pairs={{0,16},{4,20},{8,24},{12,28},{16,0},{20,4},{24,8},{28,12},{1,17},{... | collective-permute-start | bytes 1572872 | tf_op jit(solution)/shard_map/ppermute | solution.py:936
  489.6 40.2 %collective-permute-start.34 = (bf16[1,2,128,1024]{3,2,1,0:T(8,128)(2,1)}, bf16[1,2,128,1024]{3,2,1,0:T(8,128)(2,1)S(1)}, u32[]{:S(2)}, u32[]{:S(2)}) collective-permute-start(bf16[1,2,128,1024]{3,2,1,0:T(8,128)(2,1)} %get-tuple-element.187.refs_0_), channel_id=1, source_target_pairs={{0,16},{4,20},{8,24},{12,28},{16,0},{20,4},{24,8},{28,12},{1,17},{... | collective-permute-start | bytes 1572872 | tf_op jit(solution)/shard_map/ppermute | solution.py:936
  489.6 1.0 copy-start.11
  490.6 6.3 %copy-start.23 = (f32[24,1024]{1,0:T(8,128)S(1)}, f32[24,1024]{1,0:T(8,128)}, u32[]{:S(2)}) copy-start(f32[24,1024]{1,0:T(8,128)} %add_small.7.refs_0_.refs_1_) | copy-start | bytes 294916
  493.0 40.0 %collective-permute-start.35 = (bf16[2,4,128,256]{3,2,1,0:T(8,128)(2,1)}, bf16[2,4,128,256]{3,2,1,0:T(8,128)(2,1)S(1)}, u32[]{:S(2)}, u32[]{:S(2)}) collective-permute-start(bf16[2,4,128,256]{3,2,1,0:T(8,128)(2,1)} %get-tuple-element.189.refs_0_), channel_id=1, source_target_pairs={{0,8},{4,12},{8,0},{12,4},{16,24},{20,28},{24,16},{28,20},{1,9},{5... | collective-permute-start | bytes 1572872 | tf_op jit(solution)/shard_map/ppermute | solution.py:936
  496.9 26.8 %collective-permute-start.32 = (f32[24,1024]{1,0:T(8,128)S(1)}, f32[24,1024]{1,0:T(8,128)S(1)}, u32[]{:S(2)}, u32[]{:S(2)}) collective-permute-start(f32[24,1024]{1,0:T(8,128)S(1)} %copy-done.23), channel_id=1, source_target_pairs={{0,8},{4,12},{8,0},{12,4},{16,24},{20,28},{24,16},{28,20},{1,9},{5... | collective-permute-start | bytes 294920 | tf_op jit(solution)/shard_map/ppermute | solution.py:923
  525.9 12.1 %collective-permute-start.36 = (f32[24,1024]{1,0:T(8,128)}, f32[24,1024]{1,0:T(8,128)S(1)}, u32[]{:S(2)}, u32[]{:S(2)}) collective-permute-start(f32[24,1024]{1,0:T(8,128)} %add_small.8.refs_2_.refs_1_), channel_id=1, source_target_pairs={{0,16},{4,20},{8,24},{12,28},{16,0},{20,4},{24,8},{28,12},{1,17},{... | collective-permute-start | bytes 294920 | tf_op jit(solution)/shard_map/ppermute | solution.py:923
  535.8 12.5 %collective-permute-start.37 = (bf16[1,4,128,256]{3,2,1,0:T(8,128)(2,1)}, bf16[1,4,128,256]{3,2,1,0:T(8,128)(2,1)S(1)}, u32[]{:S(2)}, u32[]{:S(2)}) collective-permute-start(bf16[1,4,128,256]{3,2,1,0:T(8,128)(2,1)} %get-tuple-element.195.refs_0_), channel_id=1, source_target_pairs={{0,16},{4,20},{8,24},{12,28},{16,0},{20,4},{24,8},{28,12},{1,17},{... | collective-permute-start | bytes 786440 | tf_op jit(solution)/shard_map/ppermute | solution.py:936
  (14 other events, 10.3 us)
Sparse Core Ops, SparseCore 0:
  153.2 89.4 reduce-scatter.2
  246.8 97.2 reduce-scatter.4

commit v5 on v4

--- a/solution.py
+++ b/solution.py
@@ -231,7 +231,9 @@
     based = [q for q in range(chunks) if has[q]]
     base_o, base_r = take(len(based)), take(len(based))
     out_refs, rg_refs = take(chunks), take(chunks)
-    whole_refs, keep_refs, send_refs = take(whole), take(count - whole), take(count - whole)
+    entire = [g for g in range(count) if whole[g]]
+    halved = [g for g in range(count) if not whole[g]]
+    whole_refs, keep_refs, send_refs = take(len(entire)), take(len(halved)), take(len(halved))
     X, DY, UP, DN, UA, DA, ST, XG, DG, VAL, OA, RA, DOT, BD, TR, TL, TH, xsem, wsem, gsem, osem, dsem = it
     half = ST.shape[0] // 2
     pieces = tm // PIECE
@@ -251,9 +253,9 @@
                 pltpu.make_async_copy(dn_hbm.at[first + e], DN.at[slot], wsem.at[slot, 1])]
 
     def flush(g):
-        if g < whole:
-            return [pltpu.make_async_copy(ST, whole_refs[g], gsem.at[0])]
-        g = g - whole
+        if whole[g]:
+            return [pltpu.make_async_copy(ST, whole_refs[entire.index(g)], gsem.at[0])]
+        g = halved.index(g)
         return [pltpu.make_async_copy(ST.at[pl.ds(0, half)], keep_refs[g], gsem.at[0]),
                 pltpu.make_async_copy(ST.at[pl.ds(half, half)], send_refs[g], gsem.at[1])]
 
@@ -336,7 +338,10 @@
             def _(g=g):
                 for c in flush(g):
                     c.wait()
-        stage_grads(ST, UA, DA, me_ref[0], order, e < whole)
+        kind = False
+        for g in entire:
+            kind = kind | (e == g)
+        stage_grads(ST, UA, DA, me_ref[0], order, kind)
         for g in range(count):
             @pl.when(e == g)
             def _(g=g):
@@ -387,9 +392,9 @@
     res = pl.pallas_call(
         partial(expert_kernel, (first, count, whole, chunks, rows, d, tm, lanes, order, has, len(deps))),
         name="ffn_experts",
-        out_shape=[part] * chunks + [lined] * chunks + [entire] * whole + [grad] * (2 * (count - whole)),
+        out_shape=[part] * chunks + [lined] * chunks + [entire] * sum(whole) + [grad] * (2 * (count - sum(whole))),
         in_specs=[SMEM] * 3 + [ANY] * (len(deps) + 2 * chunks) + [vm] + [ANY] * (2 + len(more)),
-        out_specs=[ANY] * (2 * chunks + 2 * count - whole),
+        out_specs=[ANY] * (2 * chunks + 2 * count - sum(whole)),
         scratch_shapes=[
             pltpu.VMEM((n, d), BF), pltpu.VMEM((n, d), BF), pltpu.VMEM((2, d, f), BF), pltpu.VMEM((2, f, d), BF),
             pltpu.VMEM((d, f), F32), pltpu.VMEM((d, f), F32), pltpu.VMEM((2 * half, 2, d >> bits, f), BF),
@@ -401,8 +406,10 @@
         cost_estimate=SMALL,
         compiler_params=pltpu.CompilerParams(vmem_limit_bytes=VMEM),
     )(me, blocks, bounds, *deps, *xs, *dys, rm, up, down, *more)
-    at = 2 * chunks + whole
-    return res[:chunks], res[chunks:2 * chunks], res[2 * chunks:at], res[at:at + count - whole], res[at + count - whole:]
+    at = 2 * chunks + sum(whole)
+    rest = iter(res[at:])
+    keep = [next(rest) for g in range(count) if not whole[g]]
+    return res[:chunks], res[chunks:2 * chunks], res[2 * chunks:at], keep, list(rest)
 
 
 def split_add_kernel(deps, *refs):
@@ -914,7 +921,8 @@
 class Everywhere:
     def __init__(self, v):
         self.v = v
-        self.hops = [(axis, 1 << b) for axis in ("tensor", "dp") for b in range(lax.axis_size(axis).bit_length() - 1)]
+        bits = {axis: lax.axis_size(axis).bit_length() - 1 for axis in ("tensor", "dp")}
+        self.hops = [("tensor", 1 << b) for b in range(bits["tensor"])] + [("dp", 1 << b) for b in range(1, bits["dp"])] + [("dp", 1)]
         self.launch()
 
     def launch(self):
@@ -1047,18 +1055,16 @@
     base = [[None] * tensor, [None] * tensor]
     for k, q in enumerate(near):
         base[0][q], base[1][q] = out_a[k], rg_a[k]
-    apart = min(2, experts)
-    whole = []
-    for a, b in ((0, 1), (1, experts)):
-        if a < b:
-            out_e, rg_e, entire, keep_e, send_e = ffn_experts(me1, blocks, bounds, n2_all, dy_all, rm, expert_up, expert_down, a, b - a, 1, base, straight)
-            base = (out_e, rg_e)
-            whole += list(entire)
-    out_e, rg_e = list(out_e), list(rg_e)
+    by_scatter = [e == 0 for e in range(experts)]
+    out_e, rg_e, whole, keep_e, send_e = ffn_experts(me1, blocks, bounds, n2_all, dy_all, rm, expert_up, expert_down, 0, 1, (True,), base, straight)
+    out_e, rg_e, whole = list(out_e), list(rg_e), list(whole)
     out_b, rg_b, ends = ffn_dense(me1, pick(n2_all, far), pick(dy_all, far), rm, up_weight, down_weight, experts, straight,
                                   (pick(out_e, far), pick(rg_e, far)), sums)
     for k, q in enumerate(far):
         out_e[q], rg_e[q] = out_b[k], rg_b[k]
+    if experts > 1:
+        out_e, rg_e, entire, keep_e, send_e = ffn_experts(me1, blocks, bounds, n2_all, dy_all, rm, expert_up, expert_down, 1, experts - 1, tuple(by_scatter[1:]), (out_e, rg_e), straight)
+        whole += list(entire)
 
     index = {c: q for q, c in enumerate(chunk)}
     def to_owner(parts):
@@ -1091,19 +1097,18 @@
 
     scattered = []
     for v in whole:
-        flat = v.reshape(-1, v.shape[-1])
-        flat = lax.psum_scatter(flat, "dp", scatter_dimension=0, tiled=True)
+        flat = lax.psum_scatter(v.reshape(-1, v.shape[-1]), "dp", scatter_dimension=0, tiled=True)
         scattered.append(flat.reshape((1,) + v.shape[1:]))
 
-    sums_e = [Halving(keep_e[e], send_e[e], straight) for e in range(len(keep_e))]
+    halvings = [Halving(keep, send, straight) for keep, send in zip(keep_e, send_e)]
     dense_sum = Halving(ends[0], ends[1], straight)
+    sum_of = dict(enumerate(scattered + halvings))
     rg_near, rg_far = to_owner(rg_e)
-    for v in sums_e + [dense_sum]:
+    for v in [dense_sum] + halvings[:2]:
         v.launch()
-    came_far, terms = onward(rg_far, ())
-    mark = tuple(terms[:1])
-    for v in sums_e[:1]:
-        mark = v.add(mark)
+    mark = dense_sum.add((out_e[0],))
+    came_far, terms = onward(rg_far, mark)
+    mark = tuple(terms[:1]) + tuple(w_all[1:])
     mg, mc, sums_two = middle_backward(bounds, t1, rg_near + came_far, n2, rm, middle, cotangent, gain_two, pos_col, mark)
     mcs = [mc] + [from_member(mc, k) for k in range(1, members)]
     mark = (mc,)
@@ -1116,9 +1121,14 @@
         if ds == 1 or seqs == 1:
             out_came, terms = onward(out_far, mark)
             mark = tuple(terms[:1]) or mark
+            mark = dense_sum.add(mark)
+            for v in halvings[:1]:
+                mark = v.add(mark)
+            for v in halvings[2:]:
+                v.launch(mark)
     moved = [to_sequence(grads[ds], ds) for ds in range(1, seqs)]
     ng_parts = [ngs[0]] + [to_member(ngs[k], k) for k in range(1, members)]
-    for v in sums_e[1:2]:
+    for v in halvings[:1]:
         mark = v.add(mark)
     input_grad, sums_one = input_backward(ng_parts, inputs, mg, gain_one, mark)
     mark = (sums_one,)
@@ -1126,15 +1136,15 @@
     stacks = None
 
     def finish(e, mark):
-        if e < apart:
-            terms = [scattered[e]]
+        if by_scatter[e]:
+            terms = [sum_of[e]]
         else:
-            mark = sums_e[e - apart].rest(mark)
-            terms = [sums_e[e - apart].keep, sums_e[e - apart].came]
+            mark = sum_of[e].rest(mark)
+            terms = [sum_of[e].keep, sum_of[e].came]
         done = last_add(terms, (False, True), (experts, e), stacks, mark)
         return done, (done[1],)
 
-    for v in sums_e[:1]:
+    for v in halvings[1:2]:
         mark = v.add(mark)
     mark = sums.add(mark)
     keep = grads[0]
@@ -1147,29 +1157,30 @@
         keep, send = keep[:dp // 2], keep[dp // 2:]
     attn_sum = Halving(keep, send, straight)
     attn_sum.launch()
+    mark = dense_sum.rest(mark)
+    up_out, down_out = last_add([dense_sum.keep, dense_sum.came], (False, True), deps=mark)
+    mark = (up_out,)
+    stacks, mark = finish(0, mark)
+    if experts > 1:
+        stacks, mark = finish(1, mark)
     mark = sums.add(mark)
-    mark = dense_sum.add(mark)
-    stacks, mark = finish(0, mark)
-    for v in sums_e[2:]:
+    for v in halvings[1:2]:
         mark = v.add(mark)
-    for v in sums_e[1:]:
+    layer_output = layer_out(out_near + out_came, middle, pos_col, mark)
+    mark = (layer_output,)
+    for v in halvings[2:]:
         mark = v.add(mark)
     mark = sums.add(mark)
-    layer_output = layer_out(out_near + out_came, middle, pos_col, mark)
-    mark = (layer_output,)
-    if experts > apart:
-        stacks, mark = finish(apart, mark)
-    mark = dense_sum.add(mark)
+    mark = sums.add(mark)
+    if experts > 2:
+        stacks, mark = finish(2, mark)
     mark = attn_sum.add(mark)
-    mark = sums.add(mark)
-    for e in range(apart + 1, experts):
-        stacks, mark = finish(e, mark)
-    mark = dense_sum.rest(mark)
-    up_out, down_out = last_add([dense_sum.keep, dense_sum.came], (False, True), deps=mark)
-    mark = attn_sum.add((up_out,))
+    for v in halvings[2:]:
+        mark = v.add(mark)
+    mark = attn_sum.add(mark)
     while sums.came is not None:
         mark = sums.add(mark)
-    for e in range(1, apart):
+    for e in range(3, experts):
         stacks, mark = finish(e, mark)
     expert_up_out, expert_down_out = stacks
     mark = attn_sum.rest(mark)

time: 566 us -> 544 us (0.961)
  waiting for transfers between devices: 146 us -> 130 us
  blocking collectives: 21.5 us -> 8.75 us
  Pallas kernels: 300 us -> 306 us
    ppermute x14 -> x17, waiting for transfers between devices: 89.9 us -> 64.9 us  [over_dp(): lax.ppermute(v, 'dp', [(i, i ^ 1 << bit) for i in range(lax.axis_size('dp...]
    ppermute x8, waiting for transfers between devices: 4.03 us -> 24.2 us  [from_sequence(): lax.ppermute(v, 'tensor', [(place(a, b), place(a - k, b)) for a, b in eve...]
    all_to_all x1, blocking collectives: 21.5 us -> 8.75 us  [shards(): lax.all_to_all(sent, 'tensor', 0, 0, axis_index_groups=[[place(a, b) for...]
    ppermute x5, waiting for transfers between devices: 49 us -> 36.7 us  [launch(): lax.ppermute(self.v, axis, [(i, i ^ bit) for i in range(lax.axis_size(axi...]
    pallas_call x9 -> x11, Pallas kernels: 26.7 us -> 32.7 us  [split_add(): pl.pallas_call(partial(split_add_kernel, len(deps)), name='split_add', gr...]
    unnamed x80 -> x85, local copies, waits for them, and re-layouts: 19.9 us -> 24.1 us
    ppermute x14 -> x17, starting transfers between devices: 20.5 us -> 16.7 us  [over_dp(): lax.ppermute(v, 'dp', [(i, i ^ 1 << bit) for i in range(lax.axis_size('dp...]
  transfers between devices with their start and end apart: 40 -> 42, of which waited for: 11 -> 12; matrix products, arithmetic and copies ran while one was open for 4% -> 4% of each run, Pallas kernels for 49% -> 52%
where the time goes in v5:
time: 544 us; the launch traced here: 537 us
  Pallas kernels  306 us (56%)
  waiting for transfers between devices  130 us (24%)
  starting transfers between devices  34.7 us (6%)
  local copies, waits for them, and re-layouts  34.1 us (6%)
  between operations  14.6 us (3%)
  blocking collectives  8.75 us (2%)
  other arithmetic  8.29 us (2%)
    pallas_call x2, Pallas kernels, ffn_experts(): pl.pallas_call(partial(expert_kernel, (first, count, whole, chunks, rows,...  76.4 us
    ppermute x17, waiting for transfers between devices, over_dp(): lax.ppermute(v, 'dp', [(i, i ^ 1 << bit) for i in range(lax.axis_size('dp...  64.9 us
    pallas_call x2, Pallas kernels, attn_backward(): pl.pallas_call(skip(partial(attn_backward_kernel, length, bits, members,...  55.1 us
    pallas_call x2, Pallas kernels, ffn_dense(): pl.pallas_call(partial(dense_kernel, (chunks, rows, tm, lanes, order, fir...  49.2 us
    ppermute x5, waiting for transfers between devices, launch(): lax.ppermute(self.v, axis, [(i, i ^ bit) for i in range(lax.axis_size(axi...  36.7 us
    pallas_call x11, Pallas kernels, split_add(): pl.pallas_call(partial(split_add_kernel, len(deps)), name='split_add', gr...  32.7 us
    pallas_call x3, Pallas kernels, attn_forward(): pl.pallas_call(skip(partial(attn_forward_kernel, length, tuple((w.shape[0...  31.7 us
    ppermute x8, waiting for transfers between devices, from_sequence(): lax.ppermute(v, 'tensor', [(place(a, b), place(a - k, b)) for a, b in eve...  24.2 us
  transfers between devices with their start and end apart: 42, of which 12 were waited for; matrix products, arithmetic and copies ran while one was open for 4% of the time, Pallas kernels for 52%

profile of v5, /device:TPU:0, one launch (start us, length us, event | category | flops | bytes accessed | tf_op | source)
XLA Modules:
  0.0 537.3 jit_solution(17412627008838127820)
XLA Ops:
  8.8 2.6 collective-permute-start
  15.0 5.1 first_norm.1
  20.2 4.0 collective-permute-done.refs_0_
  25.0 1.9 collective-permute-start.2
  26.9 1.5 collective-permute-start.5
  30.9 14.3 %attn_forward.3 = (bf16[1024,256]{1,0:T(8,128)(2,1)}, bf16[1024,256]{1,0:T(8,128)(2,1)}, bf16[1024,256]{1,0:T(8,128)(2,1)}, bf16[1024,256]{1,0:T(8,128)(2,1)}, f32[2,8,1024]{2,1,0:T(8,128)}) custom-call(s32[1]{0:T(128)} %dynamic_slice.12.refs_0_, s32[2]{0:T(128)} %iota.11.refs_1_, bf16[2,1024,128]{2,1,0:T(8,128)(2,1)} %hold.9.refs_2_.refs_4_, ...), custom_call_target="tpu_custom_call" | custom-call | tf_op jit(solution)/shard_map/attn_forward/pallas_call | solution.py:549
  47.6 8.7 %attn_forward.4 = (bf16[1024,256]{1,0:T(8,128)(2,1)}, bf16[1024,256]{1,0:T(8,128)(2,1)}, bf16[1024,256]{1,0:T(8,128)(2,1)}, bf16[1024,256]{1,0:T(8,128)(2,1)}, f32[2,8,1024]{2,1,0:T(8,128)}) custom-call(s32[1]{0:T(128)} %dynamic_slice.12.refs_0_, s32[1]{0:T(128)} %bitcast.66, f32[2,8,1024]{2,1,0:T(8,128)} %get-tuple-element.117.refs_1_.refs_2_.refs_13_, ...), custom_call_target="tpu_custom_call" | custom-call | tf_op jit(solution)/shard_map/attn_forward/pallas_call | solution.py:549
  57.1 8.7 %attn_forward.5 = (bf16[1024,256]{1,0:T(8,128)(2,1)}, bf16[1024,256]{1,0:T(8,128)(2,1)}, bf16[1024,256]{1,0:T(8,128)(2,1)}, bf16[1024,256]{1,0:T(8,128)(2,1)}, f32[2,8,1024]{2,1,0:T(8,128)}) custom-call(s32[1]{0:T(128)} %dynamic_slice.12.refs_0_, s32[1]{0:T(128)} %bitcast.65, ...), custom_call_target="tpu_custom_call", output_to_operand_aliasing={{0}: (5, {}), {1}: (6, {}), {2}: (7, {}), {3}: (8, {}), {4}... | custom-call | tf_op jit(solution)/shard_map/attn_forward/pallas_call | solution.py:549
  66.6 3.8 project.1
  70.3 8.7 %all_to_all.5.came = bf16[2,512,1024]{2,1,0:T(8,128)(2,1)} all-to-all(bf16[2,512,1024]{2,1,0:T(8,128)(2,1)} %project.1), channel_id=1, replica_groups={{0,1},{2,3},{4,5},{6,7},{8,9},{10,11},{12,13},{14,15},{16,17},{18,19},{..., dimensions={0} | all-to-all | bytes 4194304 | tf_op jit(solution)/shard_map/all_to_all | solution.py:1042
  79.1 4.4 second_norm.1
  83.6 2.0 collective-permute-start.6
  86.5 23.1 %ffn_dense.2 = (bf16[512,1024]{1,0:T(8,128)(2,1)}, bf16[512,1024]{1,0:T(8,128)(2,1)}, bf16[528,1024]{1,0:T(8,128)(2,1)}, bf16[528,1024]{1,0:T(8,128)(2,1)}, f32[1024,1024]{1,0:T(8,128)}, /*index=5*/f32[1024,1024]{1,0:T(8,128)}) custom-call(s32[1]{0:T(128)} %bitcast.me_ref.refs_1_, bf16[512,1024]{1,0:T(8,128)(2,1)} %copy-done, ...), custom_call_target="tpu_custom_call" | custom-call | tf_op jit(solution)/shard_map/ffn_dense/pallas_call | solution.py:211
  116.0 24.8 %ffn_experts.2 = (bf16[512,1024]{1,0:T(8,128)(2,1)}, bf16[512,1024]{1,0:T(8,128)(2,1)}, bf16[512,1024]{1,0:T(8,128)(2,1)}, bf16[512,1024]{1,0:T(8,128)(2,1)}, bf...) custom-call(s32[1]{0:T(128)} %bitcast.me_ref.refs_1_, ...), custom_call_target="tpu_custom_call" | custom-call | tf_op jit(solution)/shard_map/ffn_experts/pallas_call | solution.py:392
  140.8 26.2 %ffn_dense.3 = (bf16[512,1024]{1,0:T(8,128)(2,1)}, bf16[512,1024]{1,0:T(8,128)(2,1)}, bf16[528,1024]{1,0:T(8,128)(2,1)}, bf16[528,1024]{1,0:T(8,128)(2,1)}, bf16...) custom-call(s32[1]{0:T(128)} %bitcast.me_ref.refs_1_, bf16[512,1024]{1,0:T(8,128)(2,1)} %hold.11.refs_1_.refs_0_, ...), custom_call_target="tpu_custom_call" | custom-call | tf_op jit(solution)/shard_map/ffn_dense/pallas_call | solution.py:211
  167.0 1.9 collective-permute-start.12
  168.9 51.6 %ffn_experts.3 = (bf16[512,1024]{1,0:T(8,128)(2,1)}, bf16[512,1024]{1,0:T(8,128)(2,1)}, bf16[512,1024]{1,0:T(8,128)(2,1)}, bf16[512,1024]{1,0:T(8,128)(2,1)}, bf...) custom-call(s32[1]{0:T(128)} %bitcast.me_ref.refs_1_, ...), custom_call_target="tpu_custom_call" | custom-call | tf_op jit(solution)/shard_map/ffn_experts/pallas_call | solution.py:392
  221.1 14.5 %collective-permute-done.12.refs_3_.refs_4_ = bf16[4,2,128,1024]{3,2,1,0:T(8,128)(2,1)S(1)} collective-permute-done((bf16[4,2,128,1024]{3,2,1,0:T(8,128)(2,1)}, bf16[4,2,128,1024]{3,2,1,0:T(8,128)(2,1)S(1)}, u32[]{:S(2)}, u32[]{:S(2)}) %collective-permute-start.12) | collective-permute-done | bytes 2097184 | tf_op jit(solution)/shard_map/ppermute | solution.py:944
  236.9 3.4 split_add.11
  241.3 2.9 add_parts.2.refs_2_
  244.2 1.5 collective-permute-start.15
  248.2 1.7 maximum_select_fusion.refs_3_.refs_8_
  249.9 20.2 %collective-permute-done.15.refs_6_ = bf16[528,1024]{1,0:T(8,128)(2,1)} collective-permute-done((bf16[528,1024]{1,0:T(8,128)(2,1)}, bf16[528,1024]{1,0:T(8,128)(2,1)}, u32[]{:S(2)}, u32[]{:S(2)}) %collective-permute-start.15) | collective-permute-done | bytes 1081376 | tf_op jit(solution)/shard_map/ppermute | solution.py:969
  270.1 10.3 %middle_backward.1 = (f32[512,1024]{1,0:T(8,128)}, bf16[512,1024]{1,0:T(8,128)(2,1)}, f32[16,1024]{1,0:T(8,128)}) custom-call(s32[4,5]{1,0:T(4,128)} %stack.50.bnd_ref.refs_0_, s32[1]{0:T(128)} %bitcast.7.refs_1_, bf16[528,1024]{1,0:T(8,128)(2,1)} %add_parts.2.refs_2_, bf16[3,1024,256]{2,1,0:T(8,128)(2,1)} %maximum_select_fusion.refs_3_.refs_8_, ...), custom_call_target="tpu_custom_call" | custom-call | tf_op jit(solution)/shard_map/middle_backward/pallas_call | solution.py:831
  282.1 2.6 collective-permute-done.16.refs_5_
  285.6 27.3 %attn_backward.2 = (bf16[512,1024]{1,0:T(8,128)(2,1)}, bf16[512,1024]{1,0:T(8,128)(2,1)}, bf16[8,4,128,256]{3,2,1,0:T(8,128)(2,1)}) custom-call(s32[1]{0:T(128)} %dynamic_slice.12.refs_0_, s32[1]{0:T(128)} %bitcast.me_ref.refs_1_, s32[1]{0:T(128)} %bitcast.1.j_ref.refs_2_, bf16[512,1024]{1,0:T(8,128)(2,1)} %get-tuple-element.153.refs_3_.refs_4_.refs_1_, ...), custom_call_target="tpu_custom_call" | custom-call | tf_op jit(solution)/shard_map/attn_backward/pallas_call | solution.py:655
  313.0 1.7 collective-permute-start.24
  314.6 2.8 add_parts.3.refs_0_
  317.4 2.6 split_add.12
  321.4 3.3 split_add.13
  324.9 27.8 %attn_backward.3 = (bf16[512,1024]{1,0:T(8,128)(2,1)}, bf16[512,1024]{1,0:T(8,128)(2,1)}, bf16[8,4,128,256]{3,2,1,0:T(8,128)(2,1)}) custom-call(s32[1]{0:T(128)} %dynamic_slice.12.refs_0_, s32[1]{0:T(128)} %bitcast.me_ref.refs_1_, s32[1]{0:T(128)} %bitcast.1.j_ref.refs_2_, bf16[2,2,128,1024]{3,2,1,0:T(8,128)(2,1)} %get-tuple-element.165.refs_3_.refs_1_, ...), custom_call_target="tpu_custom_call" | custom-call | tf_op jit(solution)/shard_map/attn_backward/pallas_call | solution.py:655
  354.7 2.6 split_add.14
  357.3 5.6 %input_backward.1 = (f32[512,1024]{1,0:T(8,128)}, f32[8,1024]{1,0:T(8,128)}) custom-call(bf16[1,2,128,1024]{3,2,1,0:T(8,128)(2,1)} %get-tuple-element.173.refs_0_, bf16[512,1024]{1,0:T(8,128)(2,1)} %get-tuple-element.174.refs_1_, bf16[512,1024]{1,0:T(8,128)(2,1)} %collective-permute-done.21.refs_2_, bf16[512,1024]{1,0:T(8,128)(2,1)} %refs_3_.1, ...), custom_call_target="tpu_custom_call" | custom-call | tf_op jit(solution)/shard_map/input_backward/pallas_call | solution.py:909
  363.8 3.5 split_add.15
  368.0 1.7 add_small.5.refs_0_.refs_1_
  371.7 8.5 %collective-permute-done.25.refs_2_ = bf16[1,2,128,1024]{3,2,1,0:T(8,128)(2,1)} collective-permute-done((bf16[1,2,128,1024]{3,2,1,0:T(8,128)(2,1)}, bf16[1,2,128,1024]{3,2,1,0:T(8,128)(2,1)}, u32[]{:S(2)}, u32[]{:S(2)}) %collective-permute-start.25) | collective-permute-done | bytes 524320 | tf_op jit(solution)/shard_map/ppermute | solution.py:944
  381.0 4.2 split_add.16
  385.2 20.8 %collective-permute-done.26.refs_4_ = bf16[1,2,128,1024]{3,2,1,0:T(8,128)(2,1)} collective-permute-done((bf16[1,2,128,1024]{3,2,1,0:T(8,128)(2,1)}, bf16[1,2,128,1024]{3,2,1,0:T(8,128)(2,1)}, u32[]{:S(2)}, u32[]{:S(2)}) %collective-permute-start.26) | collective-permute-done | bytes 524320 | tf_op jit(solution)/shard_map/ppermute | solution.py:944
  407.5 2.4 last_add.6
  409.8 2.2 last_add.7
  412.0 3.0 copy.89.refs_1_
  415.0 2.4 last_add.8
  417.4 1.6 add_small.6.refs_0_.refs_1_
  419.0 2.6 split_add.17
  421.6 4.9 layer_out.1.refs_0_
  427.9 3.4 split_add.18
  431.2 2.8 collective-permute-start.36
  434.7 2.0 collective-permute-start.32
  436.6 33.3 %collective-permute-done.32.refs_2_ = f32[24,1024]{1,0:T(8,128)S(1)} collective-permute-done((f32[24,1024]{1,0:T(8,128)S(1)}, f32[24,1024]{1,0:T(8,128)S(1)}, u32[]{:S(2)}, u32[]{:S(2)}) %collective-permute-start.32) | collective-permute-done | bytes 98336 | tf_op jit(solution)/shard_map/ppermute | solution.py:931
  470.6 1.6 add_small.7.refs_0_.refs_1_
  472.2 2.4 collective-permute-start.33
  474.6 3.4 collective-permute-done.33.refs_2_
  478.6 1.6 add_small.8.refs_2_.refs_1_
  481.0 2.4 last_add.9
  483.4 2.4 split_add.19
  485.8 1.7 collective-permute-start.37
  488.5 2.6 split_add.20
  492.6 12.7 %collective-permute-done.37.refs_3_.refs_4_ = bf16[2,4,128,256]{3,2,1,0:T(8,128)(2,1)S(1)} collective-permute-done((bf16[2,4,128,256]{3,2,1,0:T(8,128)(2,1)}, bf16[2,4,128,256]{3,2,1,0:T(8,128)(2,1)S(1)}, u32[]{:S(2)}, u32[]{:S(2)}) %collective-permute-start.37) | collective-permute-done | bytes 524320 | tf_op jit(solution)/shard_map/ppermute | solution.py:944
  506.1 2.1 split_add.21
  508.8 1.6 add_small.9.refs_2_
  514.4 8.3 %collective-permute-done.39.refs_4_ = bf16[1,2,128,1024]{3,2,1,0:T(8,128)(2,1)S(1)} collective-permute-done((bf16[1,2,128,1024]{3,2,1,0:T(8,128)(2,1)}, bf16[1,2,128,1024]{3,2,1,0:T(8,128)(2,1)S(1)}, u32[]{:S(2)}, u32[]{:S(2)}) %collective-permute-start.39) | collective-permute-done | bytes 524320 | tf_op jit(solution)/shard_map/ppermute | solution.py:944
  523.5 2.4 last_add.10
  526.6 1.9 last_add.11
  528.5 1.8 pad_maximum_fusion
  (192 shorter events, 50.8 us)
Async XLA Ops:
  7.2 402.7 %reduce-scatter.2.cloned.1.call-start = ((), (), s32[]{:S(2)}) async-start(), calls=%async_computation.2 | async-start | bytes 4718592 | tf_op jit(solution)/shard_map/reduce_scatter | solution.py:1100
  7.2 6.8 %collective-permute-start.1 = (bf16[512,1024]{1,0:T(8,128)(2,1)}, bf16[512,1024]{1,0:T(8,128)(2,1)S(1)}, u32[]{:S(2)}, u32[]{:S(2)}) collective-permute-start(bf16[512,1024]{1,0:T(8,128)(2,1)} %refs_3_.1), channel_id=1, source_target_pairs={{0,1},{1,0},{2,3},{3,2},{4,5},{5,4},{6,7},{7,6},{8,9},{9,8},{10,11... | collective-permute-start | bytes 3145736 | tf_op jit(solution)/shard_map/ppermute | solution.py:966
  8.8 15.4 %collective-permute-start = (bf16[2,1024,128]{2,1,0:T(8,128)(2,1)S(1)}, bf16[2,1024,128]{2,1,0:T(8,128)(2,1)S(1)}, u32[]{:S(2)}, u32[]{:S(2)}) collective-permute-start(bf16[2,1024,128]{2,1,0:T(8,128)(2,1)S(1)} %dynamic-slice_bitcast_fusion), channel_id=1, source_target_pairs={{0,2},{1,3},{2,0},{3,1},{4,6},{5,7},{6,4},{7,5},{8,10},{9,11},{10,... | collective-permute-start | bytes 1572872 | tf_op jit(solution)/shard_map/ppermute | solution.py:969
  12.4 32.9 %collective-permute-start.3 = (bf16[1,1024,128]{2,1,0:T(8,128)(2,1)S(1)}, bf16[1,1024,128]{2,1,0:T(8,128)(2,1)S(1)}, u32[]{:S(2)}, u32[]{:S(2)}) collective-permute-start(bf16[1,1024,128]{2,1,0:T(8,128)(2,1)S(1)} %dynamic-slice_bitcast_fusion.1), channel_id=1, source_target_pairs={{0,2},{1,3},{2,0},{3,1},{4,6},{5,7},{6,4},{7,5},{8,10},{9,11},{10,... | collective-permute-start | bytes 786440 | tf_op jit(solution)/shard_map/ppermute | solution.py:969
  20.2 6.8 %copy-start.17 = (bf16[256,1024]{1,0:T(8,128)(2,1)S(1)}, bf16[256,1024]{1,0:T(8,128)(2,1)}, u32[]{:S(2)}) copy-start(bf16[256,1024]{1,0:T(8,128)(2,1)} %refs_7_.3) | copy-start | bytes 1572868
  20.2 8.3 %copy-start.37 = (bf16[1024,4]{0,1:T(4,128)(2,1)S(1)}, bf16[1024,4]{0,1:T(4,128)(2,1)}, u32[]{:S(2)}) copy-start(bf16[1024,4]{0,1:T(4,128)(2,1)} %param.30) | copy-start | bytes 24580
  20.2 8.5 %copy-start.38 = (bf16[1024,2]{0,1:T(2,128)(2,1)S(1)}, bf16[1024,2]{0,1:T(2,128)(2,1)}, u32[]{:S(2)}) copy-start(bf16[1024,2]{0,1:T(2,128)(2,1)} %param.31) | copy-start | bytes 12292
  20.2 8.7 %copy-start.39 = (s32[2]{0:T(128)S(1)}, s32[2]{0:T(128)}, u32[]{:S(2)}) copy-start(s32[2]{0:T(128)} %param.19) | copy-start | bytes 28
  25.0 31.4 %collective-permute-start.2 = (bf16[2,1024,128]{2,1,0:T(8,128)(2,1)}, bf16[2,1024,128]{2,1,0:T(8,128)(2,1)}, u32[]{:S(2)}, u32[]{:S(2)}) collective-permute-start(bf16[2,1024,128]{2,1,0:T(8,128)(2,1)} %hold.9.refs_2_.refs_4_), channel_id=1, source_target_pairs={{0,4},{4,0},{8,12},{12,8},{16,20},{20,16},{24,28},{28,24},{1,5},{5... | collective-permute-start | bytes 1572872 | tf_op jit(solution)/shard_map/ppermute | solution.py:944
  26.9 38.8 %collective-permute-start.5 = (bf16[256,1024]{1,0:T(8,128)(2,1)S(1)}, bf16[256,1024]{1,0:T(8,128)(2,1)S(1)}, u32[]{:S(2)}, u32[]{:S(2)}) collective-permute-start(bf16[256,1024]{1,0:T(8,128)(2,1)S(1)} %copy-done.17), channel_id=1, source_target_pairs={{0,2},{1,3},{2,0},{3,1},{4,6},{5,7},{6,4},{7,5},{8,10},{9,11},{10,... | collective-permute-start | bytes 1572872 | tf_op jit(solution)/shard_map/ppermute | solution.py:969
  30.9 16.6 %copy-start.2 = (bf16[512,1024]{1,0:T(8,128)(2,1)S(1)}, bf16[512,1024]{1,0:T(8,128)(2,1)}, u32[]{:S(2)}) copy-start(bf16[512,1024]{1,0:T(8,128)(2,1)} %get-tuple-element.125.refs_3_.refs_4_) | copy-start | bytes 3145732
  46.0 10.3 %collective-permute-start.4 = (bf16[1,1024,128]{2,1,0:T(8,128)(2,1)}, bf16[1,1024,128]{2,1,0:T(8,128)(2,1)S(1)}, u32[]{:S(2)}, u32[]{:S(2)}) collective-permute-start(bf16[1,1024,128]{2,1,0:T(8,128)(2,1)} %hold.10.refs_5_), channel_id=1, source_target_pairs={{0,4},{4,0},{8,12},{12,8},{16,20},{20,16},{24,28},{28,24},{1,5},{5... | collective-permute-start | bytes 786440 | tf_op jit(solution)/shard_map/ppermute | solution.py:944
  47.6 38.0 %collective-permute-start.9 = (bf16[512,1024]{1,0:T(8,128)(2,1)S(1)}, bf16[512,1024]{1,0:T(8,128)(2,1)}, u32[]{:S(2)}, u32[]{:S(2)}) collective-permute-start(bf16[512,1024]{1,0:T(8,128)(2,1)S(1)} %copy-done.2), channel_id=1, source_target_pairs={{0,1},{1,0},{2,3},{3,2},{4,5},{5,4},{6,7},{7,6},{8,9},{9,8},{10,11... | collective-permute-start | bytes 3145736 | tf_op jit(solution)/shard_map/ppermute | solution.py:966
  47.6 38.0 %collective-permute-start.7 = (bf16[512,1024]{1,0:T(8,128)(2,1)S(1)}, bf16[512,1024]{1,0:T(8,128)(2,1)S(1)}, u32[]{:S(2)}, u32[]{:S(2)}) collective-permute-start(bf16[512,1024]{1,0:T(8,128)(2,1)S(1)} %copy-done.2), channel_id=1, source_target_pairs={{0,2},{1,3},{2,0},{3,1},{4,6},{5,7},{6,4},{7,5},{8,10},{9,11},{10,... | collective-permute-start | bytes 3145736 | tf_op jit(solution)/shard_map/ppermute | solution.py:969
  83.5 3.0 collective-permute-start.8
  83.6 26.0 %collective-permute-start.6 = (bf16[512,1024]{1,0:T(8,128)(2,1)}, bf16[512,1024]{1,0:T(8,128)(2,1)S(1)}, u32[]{:S(2)}, u32[]{:S(2)}) collective-permute-start(bf16[512,1024]{1,0:T(8,128)(2,1)} %get-tuple-element.124.refs_1_.refs_0_.refs_7_), channel_id=1, source_target_pairs={{0,2},{1,3},{2,0},{3,1},{4,6},{5,7},{6,4},{7,5},{8,10},{9,11},{10,... | collective-permute-start | bytes 3145736 | tf_op jit(solution)/shard_map/ppermute | solution.py:969
  109.6 1.0 copy-start.1
  110.6 3.3 collective-permute-start.10
  110.7 4.3 collective-permute-start.11
  113.9 1.1 copy-start.3
  115.0 1.0 copy-start.4
  167.0 68.6 %collective-permute-start.12 = (bf16[4,2,128,1024]{3,2,1,0:T(8,128)(2,1)}, bf16[4,2,128,1024]{3,2,1,0:T(8,128)(2,1)S(1)}, u32[]{:S(2)}, u32[]{:S(2)}) collective-permute-start(bf16[4,2,128,1024]{3,2,1,0:T(8,128)(2,1)} %get-tuple-element.146), channel_id=1, source_target_pairs={{0,4},{4,0},{8,12},{12,8},{16,20},{20,16},{24,28},{28,24},{1,5},{5... | collective-permute-start | bytes 6291464 | tf_op jit(solution)/shard_map/ppermute | solution.py:944
  220.5 19.8 %collective-permute-start.13 = (bf16[528,1024]{1,0:T(8,128)(2,1)}, bf16[528,1024]{1,0:T(8,128)(2,1)S(1)}, u32[]{:S(2)}, u32[]{:S(2)}) collective-permute-start(bf16[528,1024]{1,0:T(8,128)(2,1)} %get-tuple-element.149), channel_id=1, source_target_pairs={{0,1},{1,0},{2,3},{3,2},{4,5},{5,4},{6,7},{7,6},{8,9},{9,8},{10,11... | collective-permute-start | bytes 3244040 | tf_op jit(solution)/shard_map/ppermute | solution.py:966
  220.6 29.3 %collective-permute-start.14 = (bf16[528,1024]{1,0:T(8,128)(2,1)}, bf16[528,1024]{1,0:T(8,128)(2,1)}, u32[]{:S(2)}, u32[]{:S(2)}) collective-permute-start(bf16[528,1024]{1,0:T(8,128)(2,1)} %get-tuple-element.151), channel_id=1, source_target_pairs={{0,1},{1,0},{2,3},{3,2},{4,5},{5,4},{6,7},{7,6},{8,9},{9,8},{10,11... | collective-permute-start | bytes 3244040 | tf_op jit(solution)/shard_map/ppermute | solution.py:966
  235.6 1.3 copy-start.9
  241.3 6.9 %copy-start.22 = (bf16[1,1024,128]{2,1,0:T(8,128)(2,1)S(1)}, bf16[1,1024,128]{2,1,0:T(8,128)(2,1)}, u32[]{:S(2)}) copy-start(bf16[1,1024,128]{2,1,0:T(8,128)(2,1)} %copy-done.21) | copy-start | bytes 786436
  241.3 6.9 %copy-start.7 = (bf16[2,1024,128]{2,1,0:T(8,128)(2,1)S(1)}, bf16[2,1024,128]{2,1,0:T(8,128)(2,1)}, u32[]{:S(2)}) copy-start(bf16[2,1024,128]{2,1,0:T(8,128)(2,1)} %hold.9.refs_2_.refs_4_) | copy-start | bytes 1572868
  241.3 7.0 %copy-start.15 = (bf16[1,1024,128]{2,1,0:T(8,128)(2,1)S(1)}, bf16[1,1024,128]{2,1,0:T(8,128)(2,1)}, u32[]{:S(2)}) copy-start(bf16[1,1024,128]{2,1,0:T(8,128)(2,1)} %hold.10.refs_5_) | copy-start | bytes 786436
  244.2 25.9 %collective-permute-start.15 = (bf16[528,1024]{1,0:T(8,128)(2,1)}, bf16[528,1024]{1,0:T(8,128)(2,1)}, u32[]{:S(2)}, u32[]{:S(2)}) collective-permute-start(bf16[528,1024]{1,0:T(8,128)(2,1)} %add_parts.2.refs_2_), channel_id=1, source_target_pairs={{0,2},{1,3},{2,0},{3,1},{4,6},{5,7},{6,4},{7,5},{8,10},{9,11},{10,... | collective-permute-start | bytes 3244040 | tf_op jit(solution)/shard_map/ppermute | solution.py:969
  245.7 74.4 %collective-permute-start.19 = (bf16[4,2,128,1024]{3,2,1,0:T(8,128)(2,1)}, bf16[4,2,128,1024]{3,2,1,0:T(8,128)(2,1)S(1)}, u32[]{:S(2)}, u32[]{:S(2)}) collective-permute-start(bf16[4,2,128,1024]{3,2,1,0:T(8,128)(2,1)} %get-tuple-element.164), channel_id=1, source_target_pairs={{0,4},{4,0},{8,12},{12,8},{16,20},{20,16},{24,28},{28,24},{1,5},{5... | collective-permute-start | bytes 6291464 | tf_op jit(solution)/shard_map/ppermute | solution.py:944
  280.3 4.3 collective-permute-start.16
  280.3 34.3 %collective-permute-start.17 = (bf16[512,1024]{1,0:T(8,128)(2,1)}, bf16[512,1024]{1,0:T(8,128)(2,1)}, u32[]{:S(2)}, u32[]{:S(2)}) collective-permute-start(bf16[512,1024]{1,0:T(8,128)(2,1)} %hold.14), channel_id=1, source_target_pairs={{0,1},{1,0},{2,3},{3,2},{4,5},{5,4},{6,7},{7,6},{8,9},{9,8},{10,11... | collective-permute-start | bytes 3145736 | tf_op jit(solution)/shard_map/ppermute | solution.py:966
  280.9 36.6 %collective-permute-start.18 = (bf16[2,2,128,1024]{3,2,1,0:T(8,128)(2,1)}, bf16[2,2,128,1024]{3,2,1,0:T(8,128)(2,1)}, u32[]{:S(2)}, u32[]{:S(2)}) collective-permute-start(bf16[2,2,128,1024]{3,2,1,0:T(8,128)(2,1)} %get-tuple-element.147.refs_0_), channel_id=1, source_target_pairs={{0,8},{4,12},{8,0},{12,4},{16,24},{20,28},{24,16},{28,20},{1,9},{5... | collective-permute-start | bytes 3145736 | tf_op jit(solution)/shard_map/ppermute | solution.py:944
  281.3 82.5 %collective-permute-start.22 = (bf16[4,2,128,1024]{3,2,1,0:T(8,128)(2,1)}, bf16[4,2,128,1024]{3,2,1,0:T(8,128)(2,1)}, u32[]{:S(2)}, u32[]{:S(2)}) collective-permute-start(bf16[4,2,128,1024]{3,2,1,0:T(8,128)(2,1)} %get-tuple-element.179), channel_id=1, source_target_pairs={{0,4},{4,0},{8,12},{12,8},{16,20},{20,16},{24,28},{28,24},{1,5},{5... | collective-permute-start | bytes 6291464 | tf_op jit(solution)/shard_map/ppermute | solution.py:944
  313.0 68.0 %collective-permute-start.24 = (bf16[8,4,128,256]{3,2,1,0:T(8,128)(2,1)}, bf16[8,4,128,256]{3,2,1,0:T(8,128)(2,1)}, u32[]{:S(2)}, u32[]{:S(2)}) collective-permute-start(bf16[8,4,128,256]{3,2,1,0:T(8,128)(2,1)} %get-tuple-element.158.refs_0_), channel_id=1, source_target_pairs={{0,2},{1,3},{2,0},{3,1},{4,6},{5,7},{6,4},{7,5},{8,10},{9,11},{10,... | collective-permute-start | bytes 6291464 | tf_op jit(solution)/shard_map/ppermute | solution.py:969
  320.0 1.3 copy-start.5
  324.6 29.0 %collective-permute-start.20 = (bf16[2,2,128,1024]{3,2,1,0:T(8,128)(2,1)}, bf16[2,2,128,1024]{3,2,1,0:T(8,128)(2,1)S(1)}, u32[]{:S(2)}, u32[]{:S(2)}) collective-permute-start(bf16[2,2,128,1024]{3,2,1,0:T(8,128)(2,1)} %get-tuple-element.165.refs_3_.refs_1_), channel_id=1, source_target_pairs={{0,8},{4,12},{8,0},{12,4},{16,24},{20,28},{24,16},{28,20},{1,9},{5... | collective-permute-start | bytes 3145736 | tf_op jit(solution)/shard_map/ppermute | solution.py:944
  352.7 4.5 collective-permute-start.21
  352.8 1.3 copy-start.35
  352.8 73.7 %collective-permute-start.31 = (bf16[4,2,128,1024]{3,2,1,0:T(8,128)(2,1)}, bf16[4,2,128,1024]{3,2,1,0:T(8,128)(2,1)S(1)}, u32[]{:S(2)}, u32[]{:S(2)}) collective-permute-start(bf16[4,2,128,1024]{3,2,1,0:T(8,128)(2,1)} %hold.17), channel_id=1, source_target_pairs={{0,4},{4,0},{8,12},{12,8},{16,20},{20,16},{24,28},{28,24},{1,5},{5... | collective-permute-start | bytes 6291464 | tf_op jit(solution)/shard_map/ppermute | solution.py:944
  353.7 26.5 %collective-permute-start.25 = (bf16[1,2,128,1024]{3,2,1,0:T(8,128)(2,1)}, bf16[1,2,128,1024]{3,2,1,0:T(8,128)(2,1)}, u32[]{:S(2)}, u32[]{:S(2)}) collective-permute-start(bf16[1,2,128,1024]{3,2,1,0:T(8,128)(2,1)} %get-tuple-element.162.refs_0_), channel_id=1, source_target_pairs={{0,16},{4,20},{8,24},{12,28},{16,0},{20,4},{24,8},{28,12},{1,17},{... | collective-permute-start | bytes 1572872 | tf_op jit(solution)/shard_map/ppermute | solution.py:944
  363.6 3.7 copy-start.28
  363.6 3.7 collective-permute-start.23
  368.0 12.2 %copy-start.10 = (bf16[512,1024]{1,0:T(8,128)(2,1)S(1)}, bf16[512,1024]{1,0:T(8,128)(2,1)}, u32[]{:S(2)}) copy-start(bf16[512,1024]{1,0:T(8,128)(2,1)} %add_parts.3.refs_0_) | copy-start | bytes 3145732
  369.7 10.6 %collective-permute-start.27 = (f32[24,1024]{1,0:T(8,128)}, f32[24,1024]{1,0:T(8,128)S(1)}, u32[]{:S(2)}, u32[]{:S(2)}) collective-permute-start(f32[24,1024]{1,0:T(8,128)} %add_small.5.refs_0_.refs_1_), channel_id=1, source_target_pairs={{0,2},{1,3},{2,0},{3,1},{4,6},{5,7},{6,4},{7,5},{8,10},{9,11},{10,... | collective-permute-start | bytes 294920 | tf_op jit(solution)/shard_map/ppermute | solution.py:931
  370.3 48.7 %collective-permute-start.28 = (bf16[2,2,128,1024]{3,2,1,0:T(8,128)(2,1)}, bf16[2,2,128,1024]{3,2,1,0:T(8,128)(2,1)}, u32[]{:S(2)}, u32[]{:S(2)}) collective-permute-start(bf16[2,2,128,1024]{3,2,1,0:T(8,128)(2,1)} %get-tuple-element.180.refs_0_), channel_id=1, source_target_pairs={{0,8},{4,12},{8,0},{12,4},{16,24},{20,28},{24,16},{28,20},{1,9},{5... | collective-permute-start | bytes 3145736 | tf_op jit(solution)/shard_map/ppermute | solution.py:944
  380.2 41.4 %collective-permute-start.29 = (bf16[512,1024]{1,0:T(8,128)(2,1)}, bf16[512,1024]{1,0:T(8,128)(2,1)}, u32[]{:S(2)}, u32[]{:S(2)}) collective-permute-start(bf16[512,1024]{1,0:T(8,128)(2,1)} %hold.16), channel_id=1, source_target_pairs={{0,1},{1,0},{2,3},{3,2},{4,5},{5,4},{6,7},{7,6},{8,9},{9,8},{10,11... | collective-permute-start | bytes 3145736 | tf_op jit(solution)/shard_map/ppermute | solution.py:966
  380.2 4.9 copy-start.30
  380.3 41.4 %collective-permute-start.30 = (bf16[512,1024]{1,0:T(8,128)(2,1)S(1)}, bf16[512,1024]{1,0:T(8,128)(2,1)}, u32[]{:S(2)}, u32[]{:S(2)}) collective-permute-start(bf16[512,1024]{1,0:T(8,128)(2,1)S(1)} %copy-done.10), channel_id=1, source_target_pairs={{0,2},{1,3},{2,0},{3,1},{4,6},{5,7},{6,4},{7,5},{8,10},{9,11},{10,... | collective-permute-start | bytes 3145736 | tf_op jit(solution)/shard_map/ppermute | solution.py:969
  381.0 25.0 %collective-permute-start.26 = (bf16[1,2,128,1024]{3,2,1,0:T(8,128)(2,1)}, bf16[1,2,128,1024]{3,2,1,0:T(8,128)(2,1)}, u32[]{:S(2)}, u32[]{:S(2)}) collective-permute-start(bf16[1,2,128,1024]{3,2,1,0:T(8,128)(2,1)} %get-tuple-element.173.refs_0_), channel_id=1, source_target_pairs={{0,16},{4,20},{8,24},{12,28},{16,0},{20,4},{24,8},{28,12},{1,17},{... | collective-permute-start | bytes 1572872 | tf_op jit(solution)/shard_map/ppermute | solution.py:944
  406.0 77.4 %collective-permute-start.35 = (bf16[4,4,128,256]{3,2,1,0:T(8,128)(2,1)}, bf16[4,4,128,256]{3,2,1,0:T(8,128)(2,1)}, u32[]{:S(2)}, u32[]{:S(2)}) collective-permute-start(bf16[4,4,128,256]{3,2,1,0:T(8,128)(2,1)} %get-tuple-element.182.refs_0_), channel_id=1, source_target_pairs={{0,4},{4,0},{8,12},{12,8},{16,20},{20,16},{24,28},{28,24},{1,5},{5... | collective-permute-start | bytes 3145736 | tf_op jit(solution)/shard_map/ppermute | solution.py:944
  426.5 1.3 copy-start.8
  427.9 6.1 %copy-start.25 = (bf16[1,2,128,1024]{3,2,1,0:T(8,128)(2,1)S(1)}, bf16[1,2,128,1024]{3,2,1,0:T(8,128)(2,1)}, u32[]{:S(2)}) copy-start(bf16[1,2,128,1024]{3,2,1,0:T(8,128)(2,1)} %get-tuple-element.191.refs_0_) | copy-start | bytes 1572868
  427.9 6.8 %copy-start.23 = (f32[24,1024]{1,0:T(8,128)S(1)}, f32[24,1024]{1,0:T(8,128)}, u32[]{:S(2)}) copy-start(f32[24,1024]{1,0:T(8,128)} %add_small.6.refs_0_.refs_1_) | copy-start | bytes 294916
  431.2 56.3 %collective-permute-start.36 = (bf16[2,2,128,1024]{3,2,1,0:T(8,128)(2,1)}, bf16[2,2,128,1024]{3,2,1,0:T(8,128)(2,1)S(1)}, u32[]{:S(2)}, u32[]{:S(2)}) collective-permute-start(bf16[2,2,128,1024]{3,2,1,0:T(8,128)(2,1)} %get-tuple-element.197.refs_0_), channel_id=1, source_target_pairs={{0,8},{4,12},{8,0},{12,4},{16,24},{20,28},{24,16},{28,20},{1,9},{5... | collective-permute-start | bytes 3145736 | tf_op jit(solution)/shard_map/ppermute | solution.py:944
  434.0 46.2 %collective-permute-start.34 = (bf16[1,2,128,1024]{3,2,1,0:T(8,128)(2,1)S(1)}, bf16[1,2,128,1024]{3,2,1,0:T(8,128)(2,1)S(1)}, u32[]{:S(2)}, u32[]{:S(2)}) collective-permute-start(bf16[1,2,128,1024]{3,2,1,0:T(8,128)(2,1)S(1)} %copy-done.25), channel_id=1, source_target_pairs={{0,16},{4,20},{8,24},{12,28},{16,0},{20,4},{24,8},{28,12},{1,17},{... | collective-permute-start | bytes 1572872 | tf_op jit(solution)/shard_map/ppermute | solution.py:944
  434.7 35.3 %collective-permute-start.32 = (f32[24,1024]{1,0:T(8,128)S(1)}, f32[24,1024]{1,0:T(8,128)S(1)}, u32[]{:S(2)}, u32[]{:S(2)}) collective-permute-start(f32[24,1024]{1,0:T(8,128)S(1)} %copy-done.23), channel_id=1, source_target_pairs={{0,8},{4,12},{8,0},{12,4},{16,24},{20,28},{24,16},{28,20},{1,9},{5... | collective-permute-start | bytes 294920 | tf_op jit(solution)/shard_map/ppermute | solution.py:931
  472.2 5.7 %collective-permute-start.33 = (f32[24,1024]{1,0:T(8,128)}, f32[24,1024]{1,0:T(8,128)S(1)}, u32[]{:S(2)}, u32[]{:S(2)}) collective-permute-start(f32[24,1024]{1,0:T(8,128)} %add_small.7.refs_0_.refs_1_), channel_id=1, source_target_pairs={{0,16},{4,20},{8,24},{12,28},{16,0},{20,4},{24,8},{28,12},{1,17},{... | collective-permute-start | bytes 294920 | tf_op jit(solution)/shard_map/ppermute | solution.py:931
  485.8 19.5 %collective-permute-start.37 = (bf16[2,4,128,256]{3,2,1,0:T(8,128)(2,1)}, bf16[2,4,128,256]{3,2,1,0:T(8,128)(2,1)S(1)}, u32[]{:S(2)}, u32[]{:S(2)}) collective-permute-start(bf16[2,4,128,256]{3,2,1,0:T(8,128)(2,1)} %get-tuple-element.201.refs_0_), channel_id=1, source_target_pairs={{0,8},{4,12},{8,0},{12,4},{16,24},{20,28},{24,16},{28,20},{1,9},{5... | collective-permute-start | bytes 1572872 | tf_op jit(solution)/shard_map/ppermute | solution.py:944
  487.5 1.0 copy-start.12
  488.5 3.6 copy-start.24
  491.2 31.5 %collective-permute-start.39 = (bf16[1,2,128,1024]{3,2,1,0:T(8,128)(2,1)}, bf16[1,2,128,1024]{3,2,1,0:T(8,128)(2,1)S(1)}, u32[]{:S(2)}, u32[]{:S(2)}) collective-permute-start(bf16[1,2,128,1024]{3,2,1,0:T(8,128)(2,1)} %get-tuple-element.203.refs_0_), channel_id=1, source_target_pairs={{0,16},{4,20},{8,24},{12,28},{16,0},{20,4},{24,8},{28,12},{1,17},{... | collective-permute-start | bytes 1572872 | tf_op jit(solution)/shard_map/ppermute | solution.py:944
  492.1 16.1 %collective-permute-start.38 = (f32[24,1024]{1,0:T(8,128)S(1)}, f32[24,1024]{1,0:T(8,128)S(1)}, u32[]{:S(2)}, u32[]{:S(2)}) collective-permute-start(f32[24,1024]{1,0:T(8,128)S(1)} %copy-done.24), channel_id=1, source_target_pairs={{0,4},{4,0},{8,12},{12,8},{16,20},{20,16},{24,28},{28,24},{1,5},{5... | collective-permute-start | bytes 294920 | tf_op jit(solution)/shard_map/ppermute | solution.py:931
  508.2 17.7 %collective-permute-start.40 = (bf16[1,4,128,256]{3,2,1,0:T(8,128)(2,1)}, bf16[1,4,128,256]{3,2,1,0:T(8,128)(2,1)S(1)}, u32[]{:S(2)}, u32[]{:S(2)}) collective-permute-start(bf16[1,4,128,256]{3,2,1,0:T(8,128)(2,1)} %get-tuple-element.205.refs_0_), channel_id=1, source_target_pairs={{0,16},{4,20},{8,24},{12,28},{16,0},{20,4},{24,8},{28,12},{1,17},{... | collective-permute-start | bytes 786440 | tf_op jit(solution)/shard_map/ppermute | solution.py:944
  (18 other events, 14.4 us)
Sparse Core Ops, SparseCore 0:
  140.9 105.7 reduce-scatter.1

commit v6 on v5

--- a/solution.py
+++ b/solution.py
@@ -922,7 +922,7 @@
     def __init__(self, v):
         self.v = v
         bits = {axis: lax.axis_size(axis).bit_length() - 1 for axis in ("tensor", "dp")}
-        self.hops = [("tensor", 1 << b) for b in range(bits["tensor"])] + [("dp", 1 << b) for b in range(1, bits["dp"])] + [("dp", 1)]
+        self.hops = [("tensor", 1 << b) for b in range(bits["tensor"])] + [("dp", 1 << b) for b in range(bits["dp"])]
         self.launch()
 
     def launch(self):
@@ -1112,23 +1112,23 @@
     mg, mc, sums_two = middle_backward(bounds, t1, rg_near + came_far, n2, rm, middle, cotangent, gain_two, pos_col, mark)
     mcs = [mc] + [from_member(mc, k) for k in range(1, members)]
     mark = (mc,)
-    out_near, out_far = to_owner([hold(v, mark) for v in out_e])
     ngs = None
     grads = [None] * seqs
     for ds in list(range(1, seqs)) + [0]:
         ngs, grads[ds] = attn_backward(prefix, me1, j1, mcs, n1, wo_all[ds], w_all[ds], saved[ds], ngs, bits, mark)
         mark = (grads[ds],)
         if ds == 1 or seqs == 1:
-            out_came, terms = onward(out_far, mark)
-            mark = tuple(terms[:1]) or mark
+            for v in halvings[2:]:
+                v.launch(mark)
             mark = dense_sum.add(mark)
             for v in halvings[:1]:
                 mark = v.add(mark)
-            for v in halvings[2:]:
-                v.launch(mark)
     moved = [to_sequence(grads[ds], ds) for ds in range(1, seqs)]
     ng_parts = [ngs[0]] + [to_member(ngs[k], k) for k in range(1, members)]
-    for v in halvings[:1]:
+    mark = dense_sum.rest(mark)
+    up_out, down_out = last_add([dense_sum.keep, dense_sum.came], (False, True), deps=mark)
+    mark = (up_out,)
+    for v in halvings[1:2]:
         mark = v.add(mark)
     input_grad, sums_one = input_backward(ng_parts, inputs, mg, gain_one, mark)
     mark = (sums_one,)
@@ -1144,9 +1144,6 @@
         done = last_add(terms, (False, True), (experts, e), stacks, mark)
         return done, (done[1],)
 
-    for v in halvings[1:2]:
-        mark = v.add(mark)
-    mark = sums.add(mark)
     keep = grads[0]
     for v in moved[:-1]:
         keep = (keep.astype(F32) + v.astype(F32)).astype(BF)
@@ -1157,32 +1154,34 @@
         keep, send = keep[:dp // 2], keep[dp // 2:]
     attn_sum = Halving(keep, send, straight)
     attn_sum.launch()
-    mark = dense_sum.rest(mark)
-    up_out, down_out = last_add([dense_sum.keep, dense_sum.came], (False, True), deps=mark)
-    mark = (up_out,)
+    for v in halvings[:1]:
+        mark = v.add(mark)
+    mark = sums.add(mark)
     stacks, mark = finish(0, mark)
+    for v in halvings[1:2]:
+        mark = v.add(mark)
+    out_near, out_far = to_owner([hold(v, mark) for v in out_e])
+    out_came, terms = onward(out_far, mark)
+    mark = tuple(terms[:1]) or mark
     if experts > 1:
         stacks, mark = finish(1, mark)
-    mark = sums.add(mark)
-    for v in halvings[1:2]:
+    for v in halvings[2:]:
         mark = v.add(mark)
     layer_output = layer_out(out_near + out_came, middle, pos_col, mark)
-    mark = (layer_output,)
-    for v in halvings[2:]:
-        mark = v.add(mark)
-    mark = sums.add(mark)
-    mark = sums.add(mark)
+    mark = sums.add((layer_output,))
+    mark = attn_sum.add(mark)
     if experts > 2:
         stacks, mark = finish(2, mark)
-    mark = attn_sum.add(mark)
     for v in halvings[2:]:
         mark = v.add(mark)
     mark = attn_sum.add(mark)
-    while sums.came is not None:
-        mark = sums.add(mark)
+    mark = sums.add(mark)
+    mark = sums.add(mark)
     for e in range(3, experts):
         stacks, mark = finish(e, mark)
     expert_up_out, expert_down_out = stacks
+    while sums.came is not None:
+        mark = sums.add(mark)
     mark = attn_sum.rest(mark)
     *qkv_parts, out_out = last_add([attn_sum.keep, attn_sum.came], (False, False, False, True), deps=mark)
     lanes = d // (dp * tensor)

time: 544 us -> 543 us (level)
  blocking collectives: 8.75 us -> 19.9 us
  waiting for transfers between devices: 130 us -> 123 us
    ppermute x5, waiting for transfers between devices: 36.7 us -> 13.3 us  [launch(): lax.ppermute(self.v, axis, [(i, i ^ bit) for i in range(lax.axis_size(axi...]
    ppermute x17, waiting for transfers between devices: 64.9 us -> 81.3 us  [over_dp(): lax.ppermute(v, 'dp', [(i, i ^ 1 << bit) for i in range(lax.axis_size('dp...]
    all_to_all x1, blocking collectives: 8.75 us -> 19.9 us  [shards(): lax.all_to_all(sent, 'tensor', 0, 0, axis_index_groups=[[place(a, b) for...]
    unnamed x85 -> x88, local copies, waits for them, and re-layouts: 24.1 us -> 25.2 us
  transfers between devices with their start and end apart: 42 -> 42, of which waited for: 12 -> 15; matrix products, arithmetic and copies ran while one was open for 4% -> 3% of each run, Pallas kernels for 52% -> 52%
where the time goes in v6:
time: 543 us; the launch traced here: 541 us
  Pallas kernels  306 us (56%)
  waiting for transfers between devices  123 us (23%)
  local copies, waits for them, and re-layouts  35.3 us (7%)
  starting transfers between devices  33.4 us (6%)
  blocking collectives  19.9 us (4%)
  between operations  14.6 us (3%)
  other arithmetic  8.26 us (2%)
    ppermute x17, waiting for transfers between devices, over_dp(): lax.ppermute(v, 'dp', [(i, i ^ 1 << bit) for i in range(lax.axis_size('dp...  81.3 us
    pallas_call x2, Pallas kernels, ffn_experts(): pl.pallas_call(partial(expert_kernel, (first, count, whole, chunks, rows,...  76.5 us
    pallas_call x2, Pallas kernels, attn_backward(): pl.pallas_call(skip(partial(attn_backward_kernel, length, bits, members,...  55.2 us
    pallas_call x2, Pallas kernels, ffn_dense(): pl.pallas_call(partial(dense_kernel, (chunks, rows, tm, lanes, order, fir...  49.2 us
    pallas_call x11, Pallas kernels, split_add(): pl.pallas_call(partial(split_add_kernel, len(deps)), name='split_add', gr...  32.7 us
    pallas_call x3, Pallas kernels, attn_forward(): pl.pallas_call(skip(partial(attn_forward_kernel, length, tuple((w.shape[0...  31.6 us
    unnamed x88, local copies, waits for them, and re-layouts  25.2 us
    ppermute x8, waiting for transfers between devices, from_sequence(): lax.ppermute(v, 'tensor', [(place(a, b), place(a - k, b)) for a, b in eve...  24.2 us
  transfers between devices with their start and end apart: 42, of which 15 were waited for; matrix products, arithmetic and copies ran while one was open for 3% of the time, Pallas kernels for 52%

profile of v6, /device:TPU:0, one launch (start us, length us, event | category | flops | bytes accessed | tf_op | source)
XLA Modules:
  0.0 541.3 jit_solution(12160123800882642939)
XLA Ops:
  8.8 2.6 collective-permute-start
  15.0 5.1 first_norm.1
  20.2 4.0 collective-permute-done.refs_0_
  25.0 1.9 collective-permute-start.2
  26.9 1.5 collective-permute-start.5
  30.9 14.2 %attn_forward.3 = (bf16[1024,256]{1,0:T(8,128)(2,1)}, bf16[1024,256]{1,0:T(8,128)(2,1)}, bf16[1024,256]{1,0:T(8,128)(2,1)}, bf16[1024,256]{1,0:T(8,128)(2,1)}, f32[2,8,1024]{2,1,0:T(8,128)}) custom-call(s32[1]{0:T(128)} %dynamic_slice.12.refs_0_, s32[2]{0:T(128)} %iota.11.refs_1_, bf16[2,1024,128]{2,1,0:T(8,128)(2,1)} %hold.9.refs_2_.refs_4_, ...), custom_call_target="tpu_custom_call" | custom-call | tf_op jit(solution)/shard_map/attn_forward/pallas_call | solution.py:549
  47.5 8.7 %attn_forward.4 = (bf16[1024,256]{1,0:T(8,128)(2,1)}, bf16[1024,256]{1,0:T(8,128)(2,1)}, bf16[1024,256]{1,0:T(8,128)(2,1)}, bf16[1024,256]{1,0:T(8,128)(2,1)}, f32[2,8,1024]{2,1,0:T(8,128)}) custom-call(s32[1]{0:T(128)} %dynamic_slice.12.refs_0_, s32[1]{0:T(128)} %bitcast.66, f32[2,8,1024]{2,1,0:T(8,128)} %get-tuple-element.117.refs_1_.refs_2_.refs_13_, ...), custom_call_target="tpu_custom_call" | custom-call | tf_op jit(solution)/shard_map/attn_forward/pallas_call | solution.py:549
  56.9 8.7 %attn_forward.5 = (bf16[1024,256]{1,0:T(8,128)(2,1)}, bf16[1024,256]{1,0:T(8,128)(2,1)}, bf16[1024,256]{1,0:T(8,128)(2,1)}, bf16[1024,256]{1,0:T(8,128)(2,1)}, f32[2,8,1024]{2,1,0:T(8,128)}) custom-call(s32[1]{0:T(128)} %dynamic_slice.12.refs_0_, s32[1]{0:T(128)} %bitcast.65, ...), custom_call_target="tpu_custom_call", output_to_operand_aliasing={{0}: (5, {}), {1}: (6, {}), {2}: (7, {}), {3}: (8, {}), {4}... | custom-call | tf_op jit(solution)/shard_map/attn_forward/pallas_call | solution.py:549
  66.4 3.8 project.1
  70.2 19.9 %all_to_all.5.came = bf16[2,512,1024]{2,1,0:T(8,128)(2,1)} all-to-all(bf16[2,512,1024]{2,1,0:T(8,128)(2,1)} %project.1), channel_id=1, replica_groups={{0,1},{2,3},{4,5},{6,7},{8,9},{10,11},{12,13},{14,15},{16,17},{18,19},{..., dimensions={0} | all-to-all | bytes 4194304 | tf_op jit(solution)/shard_map/all_to_all | solution.py:1042
  90.1 4.4 second_norm.1
  94.6 1.9 collective-permute-start.6
  97.5 23.1 %ffn_dense.2 = (bf16[512,1024]{1,0:T(8,128)(2,1)}, bf16[512,1024]{1,0:T(8,128)(2,1)}, bf16[528,1024]{1,0:T(8,128)(2,1)}, bf16[528,1024]{1,0:T(8,128)(2,1)}, f32[1024,1024]{1,0:T(8,128)}, /*index=5*/f32[1024,1024]{1,0:T(8,128)}) custom-call(s32[1]{0:T(128)} %bitcast.me_ref.refs_1_, bf16[512,1024]{1,0:T(8,128)(2,1)} %copy-done, ...), custom_call_target="tpu_custom_call" | custom-call | tf_op jit(solution)/shard_map/ffn_dense/pallas_call | solution.py:211
  127.0 24.8 %ffn_experts.2 = (bf16[512,1024]{1,0:T(8,128)(2,1)}, bf16[512,1024]{1,0:T(8,128)(2,1)}, bf16[512,1024]{1,0:T(8,128)(2,1)}, bf16[512,1024]{1,0:T(8,128)(2,1)}, bf...) custom-call(s32[1]{0:T(128)} %bitcast.me_ref.refs_1_, ...), custom_call_target="tpu_custom_call" | custom-call | tf_op jit(solution)/shard_map/ffn_experts/pallas_call | solution.py:392
  151.9 26.2 %ffn_dense.3 = (bf16[512,1024]{1,0:T(8,128)(2,1)}, bf16[512,1024]{1,0:T(8,128)(2,1)}, bf16[528,1024]{1,0:T(8,128)(2,1)}, bf16[528,1024]{1,0:T(8,128)(2,1)}, bf16...) custom-call(s32[1]{0:T(128)} %bitcast.me_ref.refs_1_, bf16[512,1024]{1,0:T(8,128)(2,1)} %hold.11.refs_1_.refs_0_, ...), custom_call_target="tpu_custom_call" | custom-call | tf_op jit(solution)/shard_map/ffn_dense/pallas_call | solution.py:211
  178.1 1.7 collective-permute-start.12
  179.8 51.6 %ffn_experts.3 = (bf16[512,1024]{1,0:T(8,128)(2,1)}, bf16[512,1024]{1,0:T(8,128)(2,1)}, bf16[512,1024]{1,0:T(8,128)(2,1)}, bf16[512,1024]{1,0:T(8,128)(2,1)}, bf...) custom-call(s32[1]{0:T(128)} %bitcast.me_ref.refs_1_, ...), custom_call_target="tpu_custom_call" | custom-call | tf_op jit(solution)/shard_map/ffn_experts/pallas_call | solution.py:392
  232.0 14.5 %collective-permute-done.12.refs_3_.refs_4_ = bf16[4,2,128,1024]{3,2,1,0:T(8,128)(2,1)S(1)} collective-permute-done((bf16[4,2,128,1024]{3,2,1,0:T(8,128)(2,1)}, bf16[4,2,128,1024]{3,2,1,0:T(8,128)(2,1)S(1)}, u32[]{:S(2)}, u32[]{:S(2)}) %collective-permute-start.12) | collective-permute-done | bytes 2097184 | tf_op jit(solution)/shard_map/ppermute | solution.py:944
  247.8 3.4 split_add.11
  252.2 2.9 add_parts.2.refs_2_
  259.2 1.7 maximum_select_fusion.refs_3_.refs_8_
  260.9 20.2 %collective-permute-done.15.refs_6_ = bf16[528,1024]{1,0:T(8,128)(2,1)S(1)} collective-permute-done((bf16[528,1024]{1,0:T(8,128)(2,1)}, bf16[528,1024]{1,0:T(8,128)(2,1)S(1)}, u32[]{:S(2)}, u32[]{:S(2)}) %collective-permute-start.15) | collective-permute-done | bytes 1081376 | tf_op jit(solution)/shard_map/ppermute | solution.py:969
  282.1 10.3 %middle_backward.1 = (f32[512,1024]{1,0:T(8,128)}, bf16[512,1024]{1,0:T(8,128)(2,1)}, f32[16,1024]{1,0:T(8,128)}) custom-call(s32[4,5]{1,0:T(4,128)} %stack.50.bnd_ref.refs_0_, s32[1]{0:T(128)} %bitcast.7.refs_1_, bf16[528,1024]{1,0:T(8,128)(2,1)} %add_parts.2.refs_2_, bf16[3,1024,256]{2,1,0:T(8,128)(2,1)} %maximum_select_fusion.refs_3_.refs_8_, ...), custom_call_target="tpu_custom_call" | custom-call | tf_op jit(solution)/shard_map/middle_backward/pallas_call | solution.py:831
  293.4 1.8 collective-permute-done.16.refs_5_
  296.2 27.1 %attn_backward.2 = (bf16[512,1024]{1,0:T(8,128)(2,1)}, bf16[512,1024]{1,0:T(8,128)(2,1)}, bf16[8,4,128,256]{3,2,1,0:T(8,128)(2,1)}) custom-call(s32[1]{0:T(128)} %dynamic_slice.12.refs_0_, s32[1]{0:T(128)} %bitcast.me_ref.refs_1_, s32[1]{0:T(128)} %bitcast.1.j_ref.refs_2_, bf16[512,1024]{1,0:T(8,128)(2,1)} %get-tuple-element.153.refs_3_.refs_4_, ...), custom_call_target="tpu_custom_call" | custom-call | tf_op jit(solution)/shard_map/attn_backward/pallas_call | solution.py:655
  324.7 2.6 split_add.12
  328.4 3.3 split_add.13
  331.8 28.1 %attn_backward.3 = (bf16[512,1024]{1,0:T(8,128)(2,1)}, bf16[512,1024]{1,0:T(8,128)(2,1)}, bf16[8,4,128,256]{3,2,1,0:T(8,128)(2,1)}) custom-call(s32[1]{0:T(128)} %dynamic_slice.12.refs_0_, s32[1]{0:T(128)} %bitcast.me_ref.refs_1_, s32[1]{0:T(128)} %bitcast.1.j_ref.refs_2_, bf16[2,2,128,1024]{3,2,1,0:T(8,128)(2,1)} %get-tuple-element.163.refs_3_, ...), custom_call_target="tpu_custom_call" | custom-call | tf_op jit(solution)/shard_map/attn_backward/pallas_call | solution.py:655
  360.9 2.4 last_add.6
  364.6 3.4 split_add.14
  368.0 2.0 collective-permute-start.25
  370.9 5.6 %input_backward.1 = (f32[512,1024]{1,0:T(8,128)}, f32[8,1024]{1,0:T(8,128)}) custom-call(bf16[2,2,128,1024]{3,2,1,0:T(8,128)(2,1)} %get-tuple-element.174.refs_0_, bf16[512,1024]{1,0:T(8,128)(2,1)} %get-tuple-element.175.refs_1_, bf16[512,1024]{1,0:T(8,128)(2,1)} %collective-permute-done.21.refs_2_, bf16[512,1024]{1,0:T(8,128)(2,1)} %refs_3_.1, ...), custom_call_target="tpu_custom_call" | custom-call | tf_op jit(solution)/shard_map/input_backward/pallas_call | solution.py:909
  377.3 4.2 split_add.15
  381.5 4.7 collective-permute-done.23.refs_3_.refs_4_
  387.1 2.7 split_add.16
  390.5 1.6 add_small.5.refs_0_.refs_1_
  392.1 2.1 last_add.7
  394.2 14.1 %collective-permute-done.25.refs_3_.refs_4_ = bf16[2,2,128,1024]{3,2,1,0:T(8,128)(2,1)} collective-permute-done((bf16[2,2,128,1024]{3,2,1,0:T(8,128)(2,1)}, bf16[2,2,128,1024]{3,2,1,0:T(8,128)(2,1)}, u32[]{:S(2)}, u32[]{:S(2)}) %collective-permute-start.25) | collective-permute-done | bytes 1048608 | tf_op jit(solution)/shard_map/ppermute | solution.py:944
  408.3 2.6 split_add.17
  410.9 1.8 collective-permute-start.27
  414.8 2.8 add_parts.3.refs_2_
  418.4 19.0 %collective-permute-done.27.refs_4_ = bf16[1,2,128,1024]{3,2,1,0:T(8,128)(2,1)} collective-permute-done((bf16[1,2,128,1024]{3,2,1,0:T(8,128)(2,1)}, bf16[1,2,128,1024]{3,2,1,0:T(8,128)(2,1)}, u32[]{:S(2)}, u32[]{:S(2)}) %collective-permute-start.27) | collective-permute-done | bytes 524320 | tf_op jit(solution)/shard_map/ppermute | solution.py:944
  437.4 2.4 last_add.8
  441.1 3.3 split_add.18
  444.4 2.6 collective-permute-start.33
  447.5 4.9 layer_out.1.refs_0_
  453.1 1.6 add_small.6.refs_0_.refs_1_
  454.7 2.4 split_add.19
  457.2 22.2 %collective-permute-done.33.refs_4_ = bf16[1,2,128,1024]{3,2,1,0:T(8,128)(2,1)S(1)} collective-permute-done((bf16[1,2,128,1024]{3,2,1,0:T(8,128)(2,1)S(1)}, bf16[1,2,128,1024]{3,2,1,0:T(8,128)(2,1)S(1)}, u32[]{:S(2)}, u32[]{:S(2)}) %collective-permute-start.33) | collective-permute-done | bytes 524320 | tf_op jit(solution)/shard_map/ppermute | solution.py:944
  480.2 2.4 last_add.9
  483.6 2.7 split_add.20
  486.2 3.4 collective-permute-start.38
  490.2 4.6 collective-permute-done.35.refs_3_.refs_4_
  495.6 2.0 split_add.21
  498.3 1.6 add_small.7.refs_0_.refs_1_
  499.9 11.5 %collective-permute-done.37.refs_2_ = f32[24,1024]{1,0:T(8,128)S(1)} collective-permute-done((f32[24,1024]{1,0:T(8,128)}, f32[24,1024]{1,0:T(8,128)S(1)}, u32[]{:S(2)}, u32[]{:S(2)}) %collective-permute-start.37) | collective-permute-done | bytes 98336 | tf_op jit(solution)/shard_map/ppermute | solution.py:931
  512.0 1.6 add_small.8.refs_2_.refs_1_
  513.6 2.9 collective-permute-start.40
  516.6 2.2 collective-permute-done.38.refs_4_
  519.6 2.4 last_add.10
  522.0 1.7 collective-permute-done.39.refs_2_
  524.3 1.6 add_small.9.refs_0_
  530.6 1.9 last_add.11
  532.5 1.8 pad_maximum_fusion
  (195 shorter events, 54.0 us)
Async XLA Ops:
  7.2 384.9 %reduce-scatter.2.cloned.1.call-start = ((), (), s32[]{:S(2)}) async-start(), calls=%async_computation.2 | async-start | bytes 4718592 | tf_op jit(solution)/shard_map/reduce_scatter | solution.py:1100
  7.2 6.8 %collective-permute-start.1 = (bf16[512,1024]{1,0:T(8,128)(2,1)}, bf16[512,1024]{1,0:T(8,128)(2,1)S(1)}, u32[]{:S(2)}, u32[]{:S(2)}) collective-permute-start(bf16[512,1024]{1,0:T(8,128)(2,1)} %refs_3_.1), channel_id=1, source_target_pairs={{0,1},{1,0},{2,3},{3,2},{4,5},{5,4},{6,7},{7,6},{8,9},{9,8},{10,11... | collective-permute-start | bytes 3145736 | tf_op jit(solution)/shard_map/ppermute | solution.py:966
  8.8 15.4 %collective-permute-start = (bf16[2,1024,128]{2,1,0:T(8,128)(2,1)S(1)}, bf16[2,1024,128]{2,1,0:T(8,128)(2,1)S(1)}, u32[]{:S(2)}, u32[]{:S(2)}) collective-permute-start(bf16[2,1024,128]{2,1,0:T(8,128)(2,1)S(1)} %dynamic-slice_bitcast_fusion), channel_id=1, source_target_pairs={{0,2},{1,3},{2,0},{3,1},{4,6},{5,7},{6,4},{7,5},{8,10},{9,11},{10,... | collective-permute-start | bytes 1572872 | tf_op jit(solution)/shard_map/ppermute | solution.py:969
  12.4 32.7 %collective-permute-start.3 = (bf16[1,1024,128]{2,1,0:T(8,128)(2,1)S(1)}, bf16[1,1024,128]{2,1,0:T(8,128)(2,1)S(1)}, u32[]{:S(2)}, u32[]{:S(2)}) collective-permute-start(bf16[1,1024,128]{2,1,0:T(8,128)(2,1)S(1)} %dynamic-slice_bitcast_fusion.1), channel_id=1, source_target_pairs={{0,2},{1,3},{2,0},{3,1},{4,6},{5,7},{6,4},{7,5},{8,10},{9,11},{10,... | collective-permute-start | bytes 786440 | tf_op jit(solution)/shard_map/ppermute | solution.py:969
  14.0 1.0 copy-start.21
  20.2 6.8 %copy-start.17 = (bf16[256,1024]{1,0:T(8,128)(2,1)S(1)}, bf16[256,1024]{1,0:T(8,128)(2,1)}, u32[]{:S(2)}) copy-start(bf16[256,1024]{1,0:T(8,128)(2,1)} %refs_7_.3) | copy-start | bytes 1572868
  20.2 8.3 %copy-start.39 = (bf16[1024,4]{0,1:T(4,128)(2,1)S(1)}, bf16[1024,4]{0,1:T(4,128)(2,1)}, u32[]{:S(2)}) copy-start(bf16[1024,4]{0,1:T(4,128)(2,1)} %param.30) | copy-start | bytes 24580
  20.2 8.5 %copy-start.40 = (bf16[1024,2]{0,1:T(2,128)(2,1)S(1)}, bf16[1024,2]{0,1:T(2,128)(2,1)}, u32[]{:S(2)}) copy-start(bf16[1024,2]{0,1:T(2,128)(2,1)} %param.31) | copy-start | bytes 12292
  20.2 8.7 %copy-start.41 = (s32[2]{0:T(128)S(1)}, s32[2]{0:T(128)}, u32[]{:S(2)}) copy-start(s32[2]{0:T(128)} %param.19) | copy-start | bytes 28
  25.0 31.2 %collective-permute-start.2 = (bf16[2,1024,128]{2,1,0:T(8,128)(2,1)}, bf16[2,1024,128]{2,1,0:T(8,128)(2,1)}, u32[]{:S(2)}, u32[]{:S(2)}) collective-permute-start(bf16[2,1024,128]{2,1,0:T(8,128)(2,1)} %hold.9.refs_2_.refs_4_), channel_id=1, source_target_pairs={{0,4},{4,0},{8,12},{12,8},{16,20},{20,16},{24,28},{28,24},{1,5},{5... | collective-permute-start | bytes 1572872 | tf_op jit(solution)/shard_map/ppermute | solution.py:944
  26.9 38.7 %collective-permute-start.5 = (bf16[256,1024]{1,0:T(8,128)(2,1)S(1)}, bf16[256,1024]{1,0:T(8,128)(2,1)S(1)}, u32[]{:S(2)}, u32[]{:S(2)}) collective-permute-start(bf16[256,1024]{1,0:T(8,128)(2,1)S(1)} %copy-done.17), channel_id=1, source_target_pairs={{0,2},{1,3},{2,0},{3,1},{4,6},{5,7},{6,4},{7,5},{8,10},{9,11},{10,... | collective-permute-start | bytes 1572872 | tf_op jit(solution)/shard_map/ppermute | solution.py:969
  30.9 16.5 %copy-start.3 = (bf16[512,1024]{1,0:T(8,128)(2,1)S(1)}, bf16[512,1024]{1,0:T(8,128)(2,1)}, u32[]{:S(2)}) copy-start(bf16[512,1024]{1,0:T(8,128)(2,1)} %get-tuple-element.125.refs_3_.refs_4_) | copy-start | bytes 3145732
  45.9 10.3 %collective-permute-start.4 = (bf16[1,1024,128]{2,1,0:T(8,128)(2,1)}, bf16[1,1024,128]{2,1,0:T(8,128)(2,1)S(1)}, u32[]{:S(2)}, u32[]{:S(2)}) collective-permute-start(bf16[1,1024,128]{2,1,0:T(8,128)(2,1)} %hold.10.refs_5_), channel_id=1, source_target_pairs={{0,4},{4,0},{8,12},{12,8},{16,20},{20,16},{24,28},{28,24},{1,5},{5... | collective-permute-start | bytes 786440 | tf_op jit(solution)/shard_map/ppermute | solution.py:944
  47.4 49.1 %collective-permute-start.9 = (bf16[512,1024]{1,0:T(8,128)(2,1)S(1)}, bf16[512,1024]{1,0:T(8,128)(2,1)}, u32[]{:S(2)}, u32[]{:S(2)}) collective-permute-start(bf16[512,1024]{1,0:T(8,128)(2,1)S(1)} %copy-done.3), channel_id=1, source_target_pairs={{0,1},{1,0},{2,3},{3,2},{4,5},{5,4},{6,7},{7,6},{8,9},{9,8},{10,11... | collective-permute-start | bytes 3145736 | tf_op jit(solution)/shard_map/ppermute | solution.py:966
  47.4 49.1 %collective-permute-start.7 = (bf16[512,1024]{1,0:T(8,128)(2,1)S(1)}, bf16[512,1024]{1,0:T(8,128)(2,1)S(1)}, u32[]{:S(2)}, u32[]{:S(2)}) collective-permute-start(bf16[512,1024]{1,0:T(8,128)(2,1)S(1)} %copy-done.3), channel_id=1, source_target_pairs={{0,2},{1,3},{2,0},{3,1},{4,6},{5,7},{6,4},{7,5},{8,10},{9,11},{10,... | collective-permute-start | bytes 3145736 | tf_op jit(solution)/shard_map/ppermute | solution.py:969
  94.5 3.0 collective-permute-start.8
  94.6 26.0 %collective-permute-start.6 = (bf16[512,1024]{1,0:T(8,128)(2,1)}, bf16[512,1024]{1,0:T(8,128)(2,1)S(1)}, u32[]{:S(2)}, u32[]{:S(2)}) collective-permute-start(bf16[512,1024]{1,0:T(8,128)(2,1)} %get-tuple-element.124.refs_1_.refs_0_.refs_7_), channel_id=1, source_target_pairs={{0,2},{1,3},{2,0},{3,1},{4,6},{5,7},{6,4},{7,5},{8,10},{9,11},{10,... | collective-permute-start | bytes 3145736 | tf_op jit(solution)/shard_map/ppermute | solution.py:969
  96.5 1.0 copy-start
  120.6 1.0 copy-start.1
  121.6 3.3 collective-permute-start.10
  121.7 4.3 collective-permute-start.11
  124.9 1.1 copy-start.4
  126.0 1.0 copy-start.5
  178.1 68.4 %collective-permute-start.12 = (bf16[4,2,128,1024]{3,2,1,0:T(8,128)(2,1)}, bf16[4,2,128,1024]{3,2,1,0:T(8,128)(2,1)S(1)}, u32[]{:S(2)}, u32[]{:S(2)}) collective-permute-start(bf16[4,2,128,1024]{3,2,1,0:T(8,128)(2,1)} %get-tuple-element.146), channel_id=1, source_target_pairs={{0,4},{4,0},{8,12},{12,8},{16,20},{20,16},{24,28},{28,24},{1,5},{5... | collective-permute-start | bytes 6291464 | tf_op jit(solution)/shard_map/ppermute | solution.py:944
  231.4 19.8 %collective-permute-start.13 = (bf16[528,1024]{1,0:T(8,128)(2,1)}, bf16[528,1024]{1,0:T(8,128)(2,1)S(1)}, u32[]{:S(2)}, u32[]{:S(2)}) collective-permute-start(bf16[528,1024]{1,0:T(8,128)(2,1)} %get-tuple-element.149), channel_id=1, source_target_pairs={{0,1},{1,0},{2,3},{3,2},{4,5},{5,4},{6,7},{7,6},{8,9},{9,8},{10,11... | collective-permute-start | bytes 3244040 | tf_op jit(solution)/shard_map/ppermute | solution.py:966
  231.5 29.3 %collective-permute-start.14 = (bf16[528,1024]{1,0:T(8,128)(2,1)}, bf16[528,1024]{1,0:T(8,128)(2,1)}, u32[]{:S(2)}, u32[]{:S(2)}) collective-permute-start(bf16[528,1024]{1,0:T(8,128)(2,1)} %get-tuple-element.151), channel_id=1, source_target_pairs={{0,1},{1,0},{2,3},{3,2},{4,5},{5,4},{6,7},{7,6},{8,9},{9,8},{10,11... | collective-permute-start | bytes 3244040 | tf_op jit(solution)/shard_map/ppermute | solution.py:966
  246.5 1.3 copy-start.10
  251.2 1.0 copy-start.19
  252.2 6.3 %copy-start.24 = (bf16[1,1024,128]{2,1,0:T(8,128)(2,1)S(1)}, bf16[1,1024,128]{2,1,0:T(8,128)(2,1)}, u32[]{:S(2)}) copy-start(bf16[1,1024,128]{2,1,0:T(8,128)(2,1)} %copy-done.23) | copy-start | bytes 786436
  252.2 7.0 %copy-start.9 = (bf16[2,1024,128]{2,1,0:T(8,128)(2,1)S(1)}, bf16[2,1024,128]{2,1,0:T(8,128)(2,1)}, u32[]{:S(2)}) copy-start(bf16[2,1024,128]{2,1,0:T(8,128)(2,1)} %hold.9.refs_2_.refs_4_) | copy-start | bytes 1572868
  252.2 7.0 %copy-start.15 = (bf16[1,1024,128]{2,1,0:T(8,128)(2,1)S(1)}, bf16[1,1024,128]{2,1,0:T(8,128)(2,1)}, u32[]{:S(2)}) copy-start(bf16[1,1024,128]{2,1,0:T(8,128)(2,1)} %hold.10.refs_5_) | copy-start | bytes 786436
  255.1 26.0 %collective-permute-start.15 = (bf16[528,1024]{1,0:T(8,128)(2,1)}, bf16[528,1024]{1,0:T(8,128)(2,1)S(1)}, u32[]{:S(2)}, u32[]{:S(2)}) collective-permute-start(bf16[528,1024]{1,0:T(8,128)(2,1)} %add_parts.2.refs_2_), channel_id=1, source_target_pairs={{0,2},{1,3},{2,0},{3,1},{4,6},{5,7},{6,4},{7,5},{8,10},{9,11},{10,... | collective-permute-start | bytes 3244040 | tf_op jit(solution)/shard_map/ppermute | solution.py:969
  258.6 69.9 %collective-permute-start.18 = (bf16[4,2,128,1024]{3,2,1,0:T(8,128)(2,1)}, bf16[4,2,128,1024]{3,2,1,0:T(8,128)(2,1)}, u32[]{:S(2)}, u32[]{:S(2)}) collective-permute-start(bf16[4,2,128,1024]{3,2,1,0:T(8,128)(2,1)} %get-tuple-element.162), channel_id=1, source_target_pairs={{0,4},{4,0},{8,12},{12,8},{16,20},{20,16},{24,28},{28,24},{1,5},{5... | collective-permute-start | bytes 6291464 | tf_op jit(solution)/shard_map/ppermute | solution.py:944
  281.1 1.0 copy-start.20
  292.4 2.9 collective-permute-start.16
  292.4 70.9 %collective-permute-start.20 = (bf16[4,2,128,1024]{3,2,1,0:T(8,128)(2,1)}, bf16[4,2,128,1024]{3,2,1,0:T(8,128)(2,1)S(1)}, u32[]{:S(2)}, u32[]{:S(2)}) collective-permute-start(bf16[4,2,128,1024]{3,2,1,0:T(8,128)(2,1)} %get-tuple-element.173), channel_id=1, source_target_pairs={{0,4},{4,0},{8,12},{12,8},{16,20},{20,16},{24,28},{28,24},{1,5},{5... | collective-permute-start | bytes 6291464 | tf_op jit(solution)/shard_map/ppermute | solution.py:944
  292.8 31.9 %collective-permute-start.17 = (bf16[2,2,128,1024]{3,2,1,0:T(8,128)(2,1)}, bf16[2,2,128,1024]{3,2,1,0:T(8,128)(2,1)}, u32[]{:S(2)}, u32[]{:S(2)}) collective-permute-start(bf16[2,2,128,1024]{3,2,1,0:T(8,128)(2,1)} %get-tuple-element.147.refs_0_), channel_id=1, source_target_pairs={{0,8},{4,12},{8,0},{12,4},{16,24},{20,28},{24,16},{28,20},{1,9},{5... | collective-permute-start | bytes 3145736 | tf_op jit(solution)/shard_map/ppermute | solution.py:944
  323.3 53.9 %collective-permute-start.22 = (bf16[8,4,128,256]{3,2,1,0:T(8,128)(2,1)}, bf16[8,4,128,256]{3,2,1,0:T(8,128)(2,1)}, u32[]{:S(2)}, u32[]{:S(2)}) collective-permute-start(bf16[8,4,128,256]{3,2,1,0:T(8,128)(2,1)} %get-tuple-element.158.refs_0_.refs_1_), channel_id=1, source_target_pairs={{0,2},{1,3},{2,0},{3,1},{4,6},{5,7},{6,4},{7,5},{8,10},{9,11},{10,... | collective-permute-start | bytes 6291464 | tf_op jit(solution)/shard_map/ppermute | solution.py:969
  327.4 32.7 %collective-permute-start.19 = (bf16[1,2,128,1024]{3,2,1,0:T(8,128)(2,1)}, bf16[1,2,128,1024]{3,2,1,0:T(8,128)(2,1)S(1)}, u32[]{:S(2)}, u32[]{:S(2)}) collective-permute-start(bf16[1,2,128,1024]{3,2,1,0:T(8,128)(2,1)} %get-tuple-element.160.refs_0_), channel_id=1, source_target_pairs={{0,16},{4,20},{8,24},{12,28},{16,0},{20,4},{24,8},{28,12},{1,17},{... | collective-permute-start | bytes 1572872 | tf_op jit(solution)/shard_map/ppermute | solution.py:944
  359.9 11.0 %collective-permute-start.21 = (bf16[512,1024]{1,0:T(8,128)(2,1)}, bf16[512,1024]{1,0:T(8,128)(2,1)}, u32[]{:S(2)}, u32[]{:S(2)}) collective-permute-start(bf16[512,1024]{1,0:T(8,128)(2,1)} %get-tuple-element.176), channel_id=1, source_target_pairs={{0,1},{1,0},{2,3},{3,2},{4,5},{5,4},{6,7},{7,6},{8,9},{9,8},{10,11... | collective-permute-start | bytes 3145736 | tf_op jit(solution)/shard_map/ppermute | solution.py:966
  359.9 26.2 %collective-permute-start.23 = (bf16[2,2,128,1024]{3,2,1,0:T(8,128)(2,1)}, bf16[2,2,128,1024]{3,2,1,0:T(8,128)(2,1)S(1)}, u32[]{:S(2)}, u32[]{:S(2)}) collective-permute-start(bf16[2,2,128,1024]{3,2,1,0:T(8,128)(2,1)} %get-tuple-element.163.refs_3_), channel_id=1, source_target_pairs={{0,8},{4,12},{8,0},{12,4},{16,24},{20,28},{24,16},{28,20},{1,9},{5... | collective-permute-start | bytes 3145736 | tf_op jit(solution)/shard_map/ppermute | solution.py:944
  363.3 1.3 copy-start.7
  368.0 40.3 %collective-permute-start.25 = (bf16[2,2,128,1024]{3,2,1,0:T(8,128)(2,1)}, bf16[2,2,128,1024]{3,2,1,0:T(8,128)(2,1)}, u32[]{:S(2)}, u32[]{:S(2)}) collective-permute-start(bf16[2,2,128,1024]{3,2,1,0:T(8,128)(2,1)} %get-tuple-element.174.refs_0_), channel_id=1, source_target_pairs={{0,8},{4,12},{8,0},{12,4},{16,24},{20,28},{24,16},{28,20},{1,9},{5... | collective-permute-start | bytes 3145736 | tf_op jit(solution)/shard_map/ppermute | solution.py:944
  370.0 69.8 %collective-permute-start.28 = (bf16[4,2,128,1024]{3,2,1,0:T(8,128)(2,1)}, bf16[4,2,128,1024]{3,2,1,0:T(8,128)(2,1)S(1)}, u32[]{:S(2)}, u32[]{:S(2)}) collective-permute-start(bf16[4,2,128,1024]{3,2,1,0:T(8,128)(2,1)} %hold.15), channel_id=1, source_target_pairs={{0,4},{4,0},{8,12},{12,8},{16,20},{20,16},{24,28},{28,24},{1,5},{5... | collective-permute-start | bytes 6291464 | tf_op jit(solution)/shard_map/ppermute | solution.py:944
  377.3 4.2 copy-start.30
  377.3 12.6 %collective-permute-start.24 = (f32[24,1024]{1,0:T(8,128)S(1)}, f32[24,1024]{1,0:T(8,128)S(1)}, u32[]{:S(2)}, u32[]{:S(2)}) collective-permute-start(f32[24,1024]{1,0:T(8,128)S(1)} %constant_dynamic-update-slice_fusion.2.refs_1_), channel_id=1, source_target_pairs={{0,1},{1,0},{2,3},{3,2},{4,5},{5,4},{6,7},{7,6},{8,9},{9,8},{10,11... | collective-permute-start | bytes 294920 | tf_op jit(solution)/shard_map/ppermute | solution.py:931
  410.9 2.9 collective-permute-start.26
  410.9 26.5 %collective-permute-start.27 = (bf16[1,2,128,1024]{3,2,1,0:T(8,128)(2,1)}, bf16[1,2,128,1024]{3,2,1,0:T(8,128)(2,1)}, u32[]{:S(2)}, u32[]{:S(2)}) collective-permute-start(bf16[1,2,128,1024]{3,2,1,0:T(8,128)(2,1)} %get-tuple-element.181.refs_0_), channel_id=1, source_target_pairs={{0,16},{4,20},{8,24},{12,28},{16,0},{20,4},{24,8},{28,12},{1,17},{... | collective-permute-start | bytes 1572872 | tf_op jit(solution)/shard_map/ppermute | solution.py:944
  412.8 34.3 %collective-permute-start.29 = (bf16[512,1024]{1,0:T(8,128)(2,1)}, bf16[512,1024]{1,0:T(8,128)(2,1)}, u32[]{:S(2)}, u32[]{:S(2)}) collective-permute-start(bf16[512,1024]{1,0:T(8,128)(2,1)} %hold.17), channel_id=1, source_target_pairs={{0,1},{1,0},{2,3},{3,2},{4,5},{5,4},{6,7},{7,6},{8,9},{9,8},{10,11... | collective-permute-start | bytes 3145736 | tf_op jit(solution)/shard_map/ppermute | solution.py:966
  417.5 30.0 %collective-permute-start.30 = (bf16[512,1024]{1,0:T(8,128)(2,1)}, bf16[512,1024]{1,0:T(8,128)(2,1)}, u32[]{:S(2)}, u32[]{:S(2)}) collective-permute-start(bf16[512,1024]{1,0:T(8,128)(2,1)} %add_parts.3.refs_2_), channel_id=1, source_target_pairs={{0,2},{1,3},{2,0},{3,1},{4,6},{5,7},{6,4},{7,5},{8,10},{9,11},{10,... | collective-permute-start | bytes 3145736 | tf_op jit(solution)/shard_map/ppermute | solution.py:969
  418.1 36.6 %collective-permute-start.32 = (bf16[4,4,128,256]{3,2,1,0:T(8,128)(2,1)}, bf16[4,4,128,256]{3,2,1,0:T(8,128)(2,1)}, u32[]{:S(2)}, u32[]{:S(2)}) collective-permute-start(bf16[4,4,128,256]{3,2,1,0:T(8,128)(2,1)} %get-tuple-element.179.refs_0_), channel_id=1, source_target_pairs={{0,4},{4,0},{8,12},{12,8},{16,20},{20,16},{24,28},{28,24},{1,5},{5... | collective-permute-start | bytes 3145736 | tf_op jit(solution)/shard_map/ppermute | solution.py:944
  439.8 1.3 copy-start.6
  441.1 3.4 copy-start.2
  441.1 5.9 %copy-start.25 = (f32[24,1024]{1,0:T(8,128)S(1)}, f32[24,1024]{1,0:T(8,128)}, u32[]{:S(2)}) copy-start(f32[24,1024]{1,0:T(8,128)} %add_small.5.refs_0_.refs_1_) | copy-start | bytes 294916
  444.4 38.1 %collective-permute-start.34 = (bf16[2,2,128,1024]{3,2,1,0:T(8,128)(2,1)}, bf16[2,2,128,1024]{3,2,1,0:T(8,128)(2,1)S(1)}, u32[]{:S(2)}, u32[]{:S(2)}) collective-permute-start(bf16[2,2,128,1024]{3,2,1,0:T(8,128)(2,1)} %get-tuple-element.194.refs_0_), channel_id=1, source_target_pairs={{0,8},{4,12},{8,0},{12,4},{16,24},{20,28},{24,16},{28,20},{1,9},{5... | collective-permute-start | bytes 3145736 | tf_op jit(solution)/shard_map/ppermute | solution.py:944
  444.4 34.9 %collective-permute-start.33 = (bf16[1,2,128,1024]{3,2,1,0:T(8,128)(2,1)S(1)}, bf16[1,2,128,1024]{3,2,1,0:T(8,128)(2,1)S(1)}, u32[]{:S(2)}, u32[]{:S(2)}) collective-permute-start(bf16[1,2,128,1024]{3,2,1,0:T(8,128)(2,1)S(1)} %copy-done.2), channel_id=1, source_target_pairs={{0,16},{4,20},{8,24},{12,28},{16,0},{20,4},{24,8},{28,12},{1,17},{... | collective-permute-start | bytes 1572872 | tf_op jit(solution)/shard_map/ppermute | solution.py:944
  447.0 5.4 %collective-permute-start.31 = (f32[24,1024]{1,0:T(8,128)S(1)}, f32[24,1024]{1,0:T(8,128)S(1)}, u32[]{:S(2)}, u32[]{:S(2)}) collective-permute-start(f32[24,1024]{1,0:T(8,128)S(1)} %copy-done.25), channel_id=1, source_target_pairs={{0,2},{1,3},{2,0},{3,1},{4,6},{5,7},{6,4},{7,5},{8,10},{9,11},{10,... | collective-permute-start | bytes 294920 | tf_op jit(solution)/shard_map/ppermute | solution.py:931
  457.1 37.7 %collective-permute-start.35 = (bf16[2,4,128,256]{3,2,1,0:T(8,128)(2,1)}, bf16[2,4,128,256]{3,2,1,0:T(8,128)(2,1)S(1)}, u32[]{:S(2)}, u32[]{:S(2)}) collective-permute-start(bf16[2,4,128,256]{3,2,1,0:T(8,128)(2,1)} %get-tuple-element.199.refs_2_), channel_id=1, source_target_pairs={{0,8},{4,12},{8,0},{12,4},{16,24},{20,28},{24,16},{28,20},{1,9},{5... | collective-permute-start | bytes 1572872 | tf_op jit(solution)/shard_map/ppermute | solution.py:944
  483.5 6.1 %copy-start.26 = (f32[24,1024]{1,0:T(8,128)S(1)}, f32[24,1024]{1,0:T(8,128)}, u32[]{:S(2)}) copy-start(f32[24,1024]{1,0:T(8,128)} %add_small.6.refs_0_.refs_1_) | copy-start | bytes 294916
  486.2 32.6 %collective-permute-start.38 = (bf16[1,2,128,1024]{3,2,1,0:T(8,128)(2,1)}, bf16[1,2,128,1024]{3,2,1,0:T(8,128)(2,1)S(1)}, u32[]{:S(2)}, u32[]{:S(2)}) collective-permute-start(bf16[1,2,128,1024]{3,2,1,0:T(8,128)(2,1)} %get-tuple-element.204.refs_0_), channel_id=1, source_target_pairs={{0,16},{4,20},{8,24},{12,28},{16,0},{20,4},{24,8},{28,12},{1,17},{... | collective-permute-start | bytes 1572872 | tf_op jit(solution)/shard_map/ppermute | solution.py:944
  489.6 8.1 %collective-permute-start.36 = (f32[24,1024]{1,0:T(8,128)S(1)}, f32[24,1024]{1,0:T(8,128)S(1)}, u32[]{:S(2)}, u32[]{:S(2)}) collective-permute-start(f32[24,1024]{1,0:T(8,128)S(1)} %copy-done.26), channel_id=1, source_target_pairs={{0,4},{4,0},{8,12},{12,8},{16,20},{20,16},{24,28},{28,24},{1,5},{5... | collective-permute-start | bytes 294920 | tf_op jit(solution)/shard_map/ppermute | solution.py:931
  499.9 11.5 %collective-permute-start.37 = (f32[24,1024]{1,0:T(8,128)}, f32[24,1024]{1,0:T(8,128)S(1)}, u32[]{:S(2)}, u32[]{:S(2)}) collective-permute-start(f32[24,1024]{1,0:T(8,128)} %add_small.7.refs_0_.refs_1_), channel_id=1, source_target_pairs={{0,8},{4,12},{8,0},{12,4},{16,24},{20,28},{24,16},{28,20},{1,9},{5... | collective-permute-start | bytes 294920 | tf_op jit(solution)/shard_map/ppermute | solution.py:931
  513.6 10.0 %collective-permute-start.39 = (f32[24,1024]{1,0:T(8,128)}, f32[24,1024]{1,0:T(8,128)S(1)}, u32[]{:S(2)}, u32[]{:S(2)}) collective-permute-start(f32[24,1024]{1,0:T(8,128)} %add_small.8.refs_2_.refs_1_), channel_id=1, source_target_pairs={{0,16},{4,20},{8,24},{12,28},{16,0},{20,4},{24,8},{28,12},{1,17},{... | collective-permute-start | bytes 294920 | tf_op jit(solution)/shard_map/ppermute | solution.py:931
  513.6 16.3 %collective-permute-start.40 = (bf16[1,4,128,256]{3,2,1,0:T(8,128)(2,1)}, bf16[1,4,128,256]{3,2,1,0:T(8,128)(2,1)S(1)}, u32[]{:S(2)}, u32[]{:S(2)}) collective-permute-start(bf16[1,4,128,256]{3,2,1,0:T(8,128)(2,1)} %get-tuple-element.206.refs_0_), channel_id=1, source_target_pairs={{0,16},{4,20},{8,24},{12,28},{16,0},{20,4},{24,8},{28,12},{1,17},{... | collective-permute-start | bytes 786440 | tf_op jit(solution)/shard_map/ppermute | solution.py:944
  (20 other events, 15.5 us)
Sparse Core Ops, SparseCore 0:
  152.0 105.5 reduce-scatter.1

commit v7 on v6

--- a/solution.py
+++ b/solution.py
@@ -561,29 +561,14 @@
     )(prefix, at, *deps, n1, *ws, *earlier)
 
 
-def attn_backward_kernel(length, bits, members, based, prefix_ref, me_ref, j_ref, *refs):
-    it = iter(refs)
-    take = lambda k: [next(it) for _ in range(k)]
-    mcs = take(members)
-    n1_ref, wo_ref, w_ref, q_ref, k_ref, v_ref, ctx_ref, lse_ref = take(8)
-    bases = take(members) if based else []
-    ng_refs = take(members)
-    grad_ref, NG, MC, DC, DK, DV, DQ, sem = it
-    rows_each = length // members
-    where = [pl.ds(pl.multiple_of(lax.rem(j_ref[0] + k, members) * rows_each, rows_each), rows_each) for k in range(members)]
+def attn_backward_kernel(length, bits, based, prefix_ref, me_ref, mc_ref, n1_ref, wo_ref, w_ref, q_ref, k_ref, v_ref, ctx_ref, lse_ref, *refs):
+    base_ref = refs[0] if based else None
+    ng_ref, grad_ref, NG, DC, DK, DV, DQ = refs[based:]
     mid = length // 2
     prefix = prefix_ref[0]
     me = me_ref[0]
     pair = pl.program_id(0)
-    copies = [pltpu.make_async_copy(mcs[k], MC.at[where[k]], sem.at[k]) for k in range(members)]
-
-    @pl.when(pair == 0)
-    def _():
-        for c in copies:
-            c.start()
-        for c in copies:
-            c.wait()
-    mc = MC[...]
+    mc = mc_ref[...]
     DC[...] = dot(mc, wo_ref[...], 1, 1).astype(BF)
     k2, v2 = k_ref[...], v_ref[...]
     kt = k2.T
@@ -634,40 +619,35 @@
 
     @pl.when(pair == pl.num_programs(0) - 1)
     def _():
-        for k in range(members):
-            done = NG[where[k], :]
-            if based:
-                done = done + bases[k][...].astype(F32)
-            ng_refs[k][...] = done.astype(BF)
-
-
-def attn_backward(prefix, me, j, mcs, n1, wo, w, saved, base, bits, deps=()):
+        done = NG[...]
+        if based:
+            done = done + base_ref[...].astype(F32)
+        ng_ref[...] = done.astype(BF)
+
+
+def attn_backward(prefix, me, mc, n1, wo, w, saved, base, bits, deps=()):
     q, k, v, ctx, lse = saved
     length, d = n1.shape
     heads = w.shape[2]
     pairs = heads // LANES
     blk = d >> bits
-    members = len(mcs)
     col = pl.BlockSpec((length, LANES), lambda p, *_: (0, p))
     full = pl.BlockSpec((length, d), lambda p, *_: (0, 0))
-    part = pl.BlockSpec((length // members, d), lambda p, *_: (0, 0))
-    extra = [] if base is None else list(base)
-    res = pl.pallas_call(
-        skip(partial(attn_backward_kernel, length, bits, members, base is not None), 3, len(deps)),
+    extra = [] if base is None else [base]
+    return pl.pallas_call(
+        skip(partial(attn_backward_kernel, length, bits, len(extra)), 2, len(deps)),
         name="attn_backward",
         grid_spec=pltpu.PrefetchScalarGridSpec(
-            num_scalar_prefetch=3, grid=(pairs,),
-            in_specs=[ANY] * (len(deps) + members) + [full, pl.BlockSpec((LANES, d), lambda p, *_: (p, 0)), pl.BlockSpec((3, d, LANES), lambda p, *_: (0, 0, p)),
-                      col, col, col, col, pl.BlockSpec((1, 8, length), lambda p, *_: (p, 0, 0))] + [part] * len(extra),
-            out_specs=[part] * members + [pl.BlockSpec((1 << bits, 4, blk, LANES), lambda p, *_: (0, 0, 0, p))],
-            scratch_shapes=[pltpu.VMEM((length, d), F32), pltpu.VMEM((length, d), BF), pltpu.VMEM((length, LANES), BF),
-                            pltpu.VMEM((length, LANES), F32), pltpu.VMEM((length, LANES), F32), pltpu.VMEM((length, LANES), BF),
-                            pltpu.SemaphoreType.DMA((members,))]),
-        out_shape=[jax.ShapeDtypeStruct((length // members, d), BF)] * members + [jax.ShapeDtypeStruct((1 << bits, 4, blk, heads), BF)],
-        cost_estimate=SMALL,
-        compiler_params=pltpu.CompilerParams(vmem_limit_bytes=VMEM),
-    )(prefix, me, j, *deps, *mcs, n1, wo, w, q, k, v, ctx, lse, *extra)
-    return res[:members], res[members]
+            num_scalar_prefetch=2, grid=(pairs,),
+            in_specs=[ANY] * len(deps) + [full, full, pl.BlockSpec((LANES, d), lambda p, *_: (p, 0)), pl.BlockSpec((3, d, LANES), lambda p, *_: (0, 0, p)),
+                      col, col, col, col, pl.BlockSpec((1, 8, length), lambda p, *_: (p, 0, 0))] + [full] * len(extra),
+            out_specs=[full, pl.BlockSpec((1 << bits, 4, blk, LANES), lambda p, *_: (0, 0, 0, p))],
+            scratch_shapes=[pltpu.VMEM((length, d), F32), pltpu.VMEM((length, LANES), BF),
+                            pltpu.VMEM((length, LANES), F32), pltpu.VMEM((length, LANES), F32), pltpu.VMEM((length, LANES), BF)]),
+        out_shape=[jax.ShapeDtypeStruct((length, d), BF), jax.ShapeDtypeStruct((1 << bits, 4, blk, heads), BF)],
+        cost_estimate=SMALL,
+        compiler_params=pltpu.CompilerParams(vmem_limit_bytes=VMEM),
+    )(prefix, me, *deps, mc, n1, wo, w, q, k, v, ctx, lse, *extra)
 
 
 EPS = 1e-5
@@ -821,10 +801,11 @@
     sums_ref[9:10, :] = jnp.sum(g, axis=0, keepdims=True)
     mg = dy[...].astype(F32) + norm_backward(xhat, r, g, gain[...])
     mg_ref[...] = mg
-    mc_ref[...] = mg.astype(BF)
-
-
-def middle_backward(bounds, t, parts, n2, rm, middle, dy, gain, pos, deps=()):
+    for k in range(mc_ref.shape[0]):
+        mc_ref[k] = mg.astype(BF)
+
+
+def middle_backward(bounds, t, parts, n2, rm, middle, dy, gain, pos, members, deps=()):
     rows, d = n2.shape
     fixed = lambda shape: pl.BlockSpec(shape, lambda p, *_: (0, 0))
     big = fixed((rows, d))
@@ -835,8 +816,8 @@
             num_scalar_prefetch=2, grid=(1,),
             in_specs=[ANY] * len(deps) + [fixed((rows + PIECE, d))] * len(parts)
             + [big, fixed((d, 128)), big, big, fixed((1, d)), fixed((rows, 1))],
-            out_specs=[big, big, fixed((16, d))]),
-        out_shape=[jax.ShapeDtypeStruct((rows, d), F32), jax.ShapeDtypeStruct((rows, d), BF), jax.ShapeDtypeStruct((16, d), F32)],
+            out_specs=[big, pl.BlockSpec((members, rows, d), lambda p, *_: (0, 0, 0)), fixed((16, d))]),
+        out_shape=[jax.ShapeDtypeStruct((rows, d), F32), jax.ShapeDtypeStruct((members, rows, d), BF), jax.ShapeDtypeStruct((16, d), F32)],
         cost_estimate=SMALL,
         compiler_params=pltpu.CompilerParams(vmem_limit_bytes=VMEM),
     )(bounds, t, *deps, *parts, n2, rm, middle, dy, gain, pos)
@@ -889,12 +870,10 @@
     )(*deps, *parts)
 
 
-def input_backward_kernel(count, *refs):
-    parts = refs[:count]
-    x, mg, gain, out, sums = refs[count:]
-    g = parts[0][...].astype(F32)
-    for p in parts[1:]:
-        g = g + p[...].astype(F32)
+def input_backward_kernel(parts, x, mg, gain, out, sums):
+    g = parts[0].astype(F32)
+    for k in range(1, parts.shape[0]):
+        g = g + parts[k].astype(F32)
     xhat, r = normalise(x[...].astype(F32))
     sums[...] = jnp.zeros_like(sums)
     sums[0:1, :] = jnp.sum(g * xhat, axis=0, keepdims=True)
@@ -907,15 +886,15 @@
     fixed = lambda shape: pl.BlockSpec(shape, lambda p: (0, 0))
     big = fixed((rows, d))
     return pl.pallas_call(
-        skip(partial(input_backward_kernel, len(parts)), 0, len(deps)),
+        skip(input_backward_kernel, 0, len(deps)),
         name="input_backward",
         grid=(1,),
-        in_specs=[ANY] * len(deps) + [big] * (len(parts) + 2) + [fixed((1, d))],
+        in_specs=[ANY] * len(deps) + [pl.BlockSpec(parts.shape, lambda p: (0, 0, 0))] + [big] * 2 + [fixed((1, d))],
         out_specs=[big, fixed((8, d))],
         out_shape=[jax.ShapeDtypeStruct((rows, d), F32), jax.ShapeDtypeStruct((8, d), F32)],
         cost_estimate=SMALL,
         compiler_params=pltpu.CompilerParams(vmem_limit_bytes=VMEM),
-    )(*deps, *parts, x, mg, gain)
+    )(*deps, parts, x, mg, gain)
 
 
 class Everywhere:
@@ -1039,7 +1018,11 @@
     dy_mine = [dys] + [from_sequence(dys, ds) for ds in range(1, seqs)]
     dy_near = [dys] + [from_member(dys, k) for k in range(1, members)]
     sent = project(contexts, wo_all, members)
-    came = lax.all_to_all(sent, "tensor", 0, 0, axis_index_groups=[[place(a, b) for b in range(members)] for a in range(seqs)], tiled=True)
+
+    def exchange(v):
+        return lax.all_to_all(v, "tensor", 0, 0, axis_index_groups=[[place(a, b) for b in range(members)] for a in range(seqs)], tiled=True)
+
+    came = exchange(sent)
     middle, n2 = second_norm(came, inputs, gain_two, shift_two, pos_row)
     n2_mine = [n2] + [from_sequence(n2, ds) for ds in range(1, seqs)]
     n2_near = [n2] + [from_member(n2, k) for k in range(1, members)]
@@ -1109,23 +1092,22 @@
     mark = dense_sum.add((out_e[0],))
     came_far, terms = onward(rg_far, mark)
     mark = tuple(terms[:1]) + tuple(w_all[1:])
-    mg, mc, sums_two = middle_backward(bounds, t1, rg_near + came_far, n2, rm, middle, cotangent, gain_two, pos_col, mark)
-    mcs = [mc] + [from_member(mc, k) for k in range(1, members)]
-    mark = (mc,)
+    mg, mc, sums_two = middle_backward(bounds, t1, rg_near + came_far, n2, rm, middle, cotangent, gain_two, pos_col, members, mark)
+    mcs = exchange(mc).reshape(members * rows, d)
+    mark = dense_sum.add((mc,))
     ngs = None
     grads = [None] * seqs
     for ds in list(range(1, seqs)) + [0]:
-        ngs, grads[ds] = attn_backward(prefix, me1, j1, mcs, n1, wo_all[ds], w_all[ds], saved[ds], ngs, bits, mark)
+        ngs, grads[ds] = attn_backward(prefix, me1, mcs, n1, wo_all[ds], w_all[ds], saved[ds], ngs, bits, mark)
         mark = (grads[ds],)
         if ds == 1 or seqs == 1:
             for v in halvings[2:]:
-                v.launch(mark)
-            mark = dense_sum.add(mark)
+                v.launch()
+            mark = dense_sum.rest(mark)
             for v in halvings[:1]:
                 mark = v.add(mark)
     moved = [to_sequence(grads[ds], ds) for ds in range(1, seqs)]
-    ng_parts = [ngs[0]] + [to_member(ngs[k], k) for k in range(1, members)]
-    mark = dense_sum.rest(mark)
+    ng_parts = exchange(ngs.reshape(members, rows, d))
     up_out, down_out = last_add([dense_sum.keep, dense_sum.came], (False, True), deps=mark)
     mark = (up_out,)
     for v in halvings[1:2]:

time: 543 us -> 534 us (0.983)
  waiting for transfers between devices: 123 us -> 104 us
  starting transfers between devices: 33.4 us -> 46.5 us
    ppermute x17, waiting for transfers between devices: 81.3 us -> 57.3 us  [over_dp(): lax.ppermute(v, 'dp', [(i, i ^ 1 << bit) for i in range(lax.axis_size('dp...]
    all_to_all x0 -> x2, starting transfers between devices: none -> 8.87 us  [exchange(): lax.all_to_all(v, 'tensor', 0, 0, axis_index_groups=[[place(a, b) for b i...]
    ppermute x5, waiting for transfers between devices: 13.3 us -> 19.2 us  [launch(): lax.ppermute(self.v, axis, [(i, i ^ bit) for i in range(lax.axis_size(axi...]
  transfers between devices with their start and end apart: 42 -> 42, of which waited for: 15 -> 12; matrix products, arithmetic and copies ran while one was open for 3% -> 3% of each run, Pallas kernels for 52% -> 52%
where the time goes in v7:
time: 534 us; the launch traced here: 532 us
  Pallas kernels  305 us (57%)
  waiting for transfers between devices  104 us (19%)
  starting transfers between devices  46.5 us (9%)
  local copies, waits for them, and re-layouts  33.7 us (6%)
  blocking collectives  19.9 us (4%)
  between operations  14.6 us (3%)
  other arithmetic  8.26 us (2%)
    pallas_call x2, Pallas kernels, ffn_experts(): pl.pallas_call(partial(expert_kernel, (first, count, whole, chunks, rows,...  76.4 us
    ppermute x17, waiting for transfers between devices, over_dp(): lax.ppermute(v, 'dp', [(i, i ^ 1 << bit) for i in range(lax.axis_size('dp...  57.3 us
    pallas_call x2, Pallas kernels, attn_backward(): pl.pallas_call(skip(partial(attn_backward_kernel, length, bits, len(extra...  53.3 us
    pallas_call x2, Pallas kernels, ffn_dense(): pl.pallas_call(partial(dense_kernel, (chunks, rows, tm, lanes, order, fir...  49.3 us
    pallas_call x11, Pallas kernels, split_add(): pl.pallas_call(partial(split_add_kernel, len(deps)), name='split_add', gr...  32.7 us
    pallas_call x3, Pallas kernels, attn_forward(): pl.pallas_call(skip(partial(attn_forward_kernel, length, tuple((w.shape[0...  31.6 us
    ppermute x17, starting transfers between devices, over_dp(): lax.ppermute(v, 'dp', [(i, i ^ 1 << bit) for i in range(lax.axis_size('dp...  23.7 us
    unnamed x88, local copies, waits for them, and re-layouts  23.6 us
  transfers between devices with their start and end apart: 42, of which 12 were waited for; matrix products, arithmetic and copies ran while one was open for 3% of the time, Pallas kernels for 52%

profile of v7, /device:TPU:0, one launch (start us, length us, event | category | flops | bytes accessed | tf_op | source)
XLA Modules:
  0.0 532.2 jit_solution(3598115051796626073)
XLA Ops:
  8.8 2.6 collective-permute-start
  15.0 5.1 first_norm.1
  20.2 4.0 collective-permute-done.refs_0_
  25.0 1.9 collective-permute-start.2
  30.9 14.2 %attn_forward.3 = (bf16[1024,256]{1,0:T(8,128)(2,1)}, bf16[1024,256]{1,0:T(8,128)(2,1)}, bf16[1024,256]{1,0:T(8,128)(2,1)}, bf16[1024,256]{1,0:T(8,128)(2,1)}, f32[2,8,1024]{2,1,0:T(8,128)}) custom-call(s32[1]{0:T(128)} %dynamic_slice.12.refs_0_, s32[2]{0:T(128)} %iota.11.refs_1_, bf16[2,1024,128]{2,1,0:T(8,128)(2,1)} %hold.8.refs_2_.refs_4_, ...), custom_call_target="tpu_custom_call" | custom-call | tf_op jit(solution)/shard_map/attn_forward/pallas_call | solution.py:549
  47.5 8.7 %attn_forward.4 = (bf16[1024,256]{1,0:T(8,128)(2,1)}, bf16[1024,256]{1,0:T(8,128)(2,1)}, bf16[1024,256]{1,0:T(8,128)(2,1)}, bf16[1024,256]{1,0:T(8,128)(2,1)}, f32[2,8,1024]{2,1,0:T(8,128)}) custom-call(s32[1]{0:T(128)} %dynamic_slice.12.refs_0_, s32[1]{0:T(128)} %bitcast.71, f32[2,8,1024]{2,1,0:T(8,128)} %get-tuple-element.115.refs_1_.refs_2_.refs_11_, ...), custom_call_target="tpu_custom_call" | custom-call | tf_op jit(solution)/shard_map/attn_forward/pallas_call | solution.py:549
  56.9 8.7 %attn_forward.5 = (bf16[1024,256]{1,0:T(8,128)(2,1)}, bf16[1024,256]{1,0:T(8,128)(2,1)}, bf16[1024,256]{1,0:T(8,128)(2,1)}, bf16[1024,256]{1,0:T(8,128)(2,1)}, f32[2,8,1024]{2,1,0:T(8,128)}) custom-call(s32[1]{0:T(128)} %dynamic_slice.12.refs_0_, s32[1]{0:T(128)} %bitcast.70, ...), custom_call_target="tpu_custom_call", output_to_operand_aliasing={{0}: (5, {}), {1}: (6, {}), {2}: (7, {}), {3}: (8, {}), {4}... | custom-call | tf_op jit(solution)/shard_map/attn_forward/pallas_call | solution.py:549
  66.4 3.8 project.1
  70.2 19.9 %all_to_all.15.came = bf16[2,512,1024]{2,1,0:T(8,128)(2,1)} all-to-all(bf16[2,512,1024]{2,1,0:T(8,128)(2,1)} %project.1), channel_id=1, replica_groups={{0,1},{2,3},{4,5},{6,7},{8,9},{10,11},{12,13},{14,15},{16,17},{18,19},{..., dimensions={0} | all-to-all | bytes 4194304 | tf_op jit(solution)/shard_map/all_to_all | solution.py:1023
  90.1 4.4 second_norm.1
  94.6 1.9 collective-permute-start.6
  97.5 23.1 %ffn_dense.2 = (bf16[512,1024]{1,0:T(8,128)(2,1)}, bf16[512,1024]{1,0:T(8,128)(2,1)}, bf16[528,1024]{1,0:T(8,128)(2,1)}, bf16[528,1024]{1,0:T(8,128)(2,1)}, f32[1024,1024]{1,0:T(8,128)}, /*index=5*/f32[1024,1024]{1,0:T(8,128)}) custom-call(s32[1]{0:T(128)} %bitcast.me_ref.refs_1_, bf16[512,1024]{1,0:T(8,128)(2,1)} %copy-done, ...), custom_call_target="tpu_custom_call" | custom-call | tf_op jit(solution)/shard_map/ffn_dense/pallas_call | solution.py:211
  126.9 24.8 %ffn_experts.2 = (bf16[512,1024]{1,0:T(8,128)(2,1)}, bf16[512,1024]{1,0:T(8,128)(2,1)}, bf16[512,1024]{1,0:T(8,128)(2,1)}, bf16[512,1024]{1,0:T(8,128)(2,1)}, bf...) custom-call(s32[1]{0:T(128)} %bitcast.me_ref.refs_1_, ...), custom_call_target="tpu_custom_call" | custom-call | tf_op jit(solution)/shard_map/ffn_experts/pallas_call | solution.py:392
  151.7 26.2 %ffn_dense.3 = (bf16[512,1024]{1,0:T(8,128)(2,1)}, bf16[512,1024]{1,0:T(8,128)(2,1)}, bf16[528,1024]{1,0:T(8,128)(2,1)}, bf16[528,1024]{1,0:T(8,128)(2,1)}, bf16...) custom-call(s32[1]{0:T(128)} %bitcast.me_ref.refs_1_, bf16[512,1024]{1,0:T(8,128)(2,1)} %hold.10.refs_1_.refs_0_, ...), custom_call_target="tpu_custom_call" | custom-call | tf_op jit(solution)/shard_map/ffn_dense/pallas_call | solution.py:211
  178.0 1.8 collective-permute-start.12
  179.7 51.6 %ffn_experts.3 = (bf16[512,1024]{1,0:T(8,128)(2,1)}, bf16[512,1024]{1,0:T(8,128)(2,1)}, bf16[512,1024]{1,0:T(8,128)(2,1)}, bf16[512,1024]{1,0:T(8,128)(2,1)}, bf...) custom-call(s32[1]{0:T(128)} %bitcast.me_ref.refs_1_, ...), custom_call_target="tpu_custom_call" | custom-call | tf_op jit(solution)/shard_map/ffn_experts/pallas_call | solution.py:392
  231.9 14.4 %collective-permute-done.12.refs_3_.refs_4_ = bf16[4,2,128,1024]{3,2,1,0:T(8,128)(2,1)S(1)} collective-permute-done((bf16[4,2,128,1024]{3,2,1,0:T(8,128)(2,1)}, bf16[4,2,128,1024]{3,2,1,0:T(8,128)(2,1)S(1)}, u32[]{:S(2)}, u32[]{:S(2)}) %collective-permute-start.12) | collective-permute-done | bytes 2097184 | tf_op jit(solution)/shard_map/ppermute | solution.py:923
  247.7 3.4 split_add.11
  252.1 2.9 add_parts.2.refs_2_
  261.2 1.6 maximum_select_fusion.refs_3_.refs_6_
  262.9 18.2 %collective-permute-done.15.refs_6_ = bf16[528,1024]{1,0:T(8,128)(2,1)} collective-permute-done((bf16[528,1024]{1,0:T(8,128)(2,1)}, bf16[528,1024]{1,0:T(8,128)(2,1)}, u32[]{:S(2)}, u32[]{:S(2)}) %collective-permute-start.15) | collective-permute-done | bytes 1081376 | tf_op jit(solution)/shard_map/ppermute | solution.py:948
  281.1 10.6 %middle_backward.1 = (f32[512,1024]{1,0:T(8,128)}, bf16[2,512,1024]{2,1,0:T(8,128)(2,1)}, f32[16,1024]{1,0:T(8,128)}) custom-call(s32[4,5]{1,0:T(4,128)} %stack.50.bnd_ref.refs_0_, s32[1]{0:T(128)} %bitcast.6.refs_1_, bf16[528,1024]{1,0:T(8,128)(2,1)} %add_parts.2.refs_2_, bf16[3,1024,256]{2,1,0:T(8,128)(2,1)} %maximum_select_fusion.refs_3_.refs_6_, ...), custom_call_target="tpu_custom_call" | custom-call | tf_op jit(solution)/shard_map/middle_backward/pallas_call | solution.py:812
  291.7 3.8 all-to-all-start.1
  296.5 2.6 split_add.12
  300.4 26.2 %attn_backward.2 = (bf16[1024,1024]{1,0:T(8,128)(2,1)}, bf16[8,4,128,256]{3,2,1,0:T(8,128)(2,1)}) custom-call(s32[1]{0:T(128)} %dynamic_slice.12.refs_0_, s32[1]{0:T(128)} %bitcast.me_ref.refs_1_, bf16[1,2,128,1024]{3,2,1,0:T(8,128)(2,1)} %get-tuple-element.153.refs_2_, bf16[1024,1024]{1,0:T(8,128)(2,1)} %bitcast.45, ...), custom_call_target="tpu_custom_call" | custom-call | tf_op jit(solution)/shard_map/attn_backward/pallas_call | solution.py:637
  328.9 3.3 split_add.13
  332.3 27.1 %attn_backward.3 = (bf16[1024,1024]{1,0:T(8,128)(2,1)}, bf16[8,4,128,256]{3,2,1,0:T(8,128)(2,1)}) custom-call(s32[1]{0:T(128)} %dynamic_slice.12.refs_0_, s32[1]{0:T(128)} %bitcast.me_ref.refs_1_, bf16[2,2,128,1024]{3,2,1,0:T(8,128)(2,1)} %get-tuple-element.161.refs_2_, bf16[1024,1024]{1,0:T(8,128)(2,1)} %bitcast.46, ...), custom_call_target="tpu_custom_call" | custom-call | tf_op jit(solution)/shard_map/attn_backward/pallas_call | solution.py:637
  360.2 2.4 last_add.6
  362.6 3.4 split_add.14
  366.0 2.0 collective-permute-start.23
  368.3 5.1 all-to-all-start.2
  373.4 2.9 all-to-all-done.2.refs_1_
  376.3 5.7 %input_backward.1 = (f32[512,1024]{1,0:T(8,128)}, f32[8,1024]{1,0:T(8,128)}) custom-call(bf16[2,2,128,1024]{3,2,1,0:T(8,128)(2,1)} %get-tuple-element.171.refs_0_, bf16[2,512,1024]{2,1,0:T(8,128)(2,1)} %all-to-all-done.2.refs_1_, bf16[512,1024]{1,0:T(8,128)(2,1)} %refs_2_.3, f32[512,1024]{1,0:T(8,128)} %get-tuple-element.173.refs_3_, f32[1,1024]{1,0:T(1,128)} %bitcast.61), custom_call_target="tpu_custom_call" | custom-call | tf_op jit(solution)/shard_map/input_backward/pallas_call | solution.py:888
  382.9 4.2 split_add.15
  388.1 2.6 split_add.16
  391.4 1.6 add_small.5.refs_0_.refs_1_
  393.0 2.1 last_add.7
  395.1 2.7 split_add.17
  398.1 2.0 collective-permute-start.25
  401.6 2.8 add_parts.3.refs_2_
  405.0 1.7 collective-permute-start.30
  406.7 17.5 %collective-permute-done.25.refs_4_ = bf16[1,2,128,1024]{3,2,1,0:T(8,128)(2,1)} collective-permute-done((bf16[1,2,128,1024]{3,2,1,0:T(8,128)(2,1)}, bf16[1,2,128,1024]{3,2,1,0:T(8,128)(2,1)}, u32[]{:S(2)}, u32[]{:S(2)}) %collective-permute-start.25) | collective-permute-done | bytes 524320 | tf_op jit(solution)/shard_map/ppermute | solution.py:923
  424.1 2.4 last_add.8
  427.8 3.4 split_add.18
  431.2 3.2 collective-permute-start.31
  435.0 4.9 layer_out.1.refs_0_
  440.5 1.6 add_small.6.refs_0_.refs_1_
  442.1 2.4 split_add.19
  444.6 21.6 %collective-permute-done.31.refs_4_ = bf16[1,2,128,1024]{3,2,1,0:T(8,128)(2,1)S(1)} collective-permute-done((bf16[1,2,128,1024]{3,2,1,0:T(8,128)(2,1)S(1)}, bf16[1,2,128,1024]{3,2,1,0:T(8,128)(2,1)S(1)}, u32[]{:S(2)}, u32[]{:S(2)}) %collective-permute-start.31) | collective-permute-done | bytes 524320 | tf_op jit(solution)/shard_map/ppermute | solution.py:923
  467.0 2.4 last_add.9
  470.3 2.7 split_add.20
  473.0 3.4 collective-permute-start.36
  476.4 1.7 collective-permute-start.34
  478.1 3.8 collective-permute-done.33.refs_3_.refs_4_
  482.7 2.0 split_add.21
  485.3 1.6 add_small.7.refs_0_.refs_1_
  486.9 16.7 %collective-permute-done.35.refs_2_ = f32[24,1024]{1,0:T(8,128)S(1)} collective-permute-done((f32[24,1024]{1,0:T(8,128)}, f32[24,1024]{1,0:T(8,128)S(1)}, u32[]{:S(2)}, u32[]{:S(2)}) %collective-permute-start.35) | collective-permute-done | bytes 98336 | tf_op jit(solution)/shard_map/ppermute | solution.py:910
  504.3 1.6 add_small.8.refs_2_.refs_1_
  505.9 2.9 collective-permute-start.38
  509.6 2.4 last_add.10
  512.0 2.5 collective-permute-done.37.refs_2_
  515.2 1.6 add_small.9.refs_0_
  521.5 1.9 last_add.11
  523.4 1.8 pad_maximum_fusion
  (194 shorter events, 53.8 us)
Async XLA Ops:
  7.2 385.8 %reduce-scatter.2.cloned.1.call-start = ((), (), s32[]{:S(2)}) async-start(), calls=%async_computation.4 | async-start | bytes 4718592 | tf_op jit(solution)/shard_map/reduce_scatter | solution.py:1083
  7.2 6.8 %collective-permute-start.1 = (bf16[512,1024]{1,0:T(8,128)(2,1)}, bf16[512,1024]{1,0:T(8,128)(2,1)S(1)}, u32[]{:S(2)}, u32[]{:S(2)}) collective-permute-start(bf16[512,1024]{1,0:T(8,128)(2,1)} %refs_2_.3), channel_id=1, source_target_pairs={{0,1},{1,0},{2,3},{3,2},{4,5},{5,4},{6,7},{7,6},{8,9},{9,8},{10,11... | collective-permute-start | bytes 3145736 | tf_op jit(solution)/shard_map/ppermute | solution.py:945
  8.8 15.4 %collective-permute-start = (bf16[2,1024,128]{2,1,0:T(8,128)(2,1)S(1)}, bf16[2,1024,128]{2,1,0:T(8,128)(2,1)S(1)}, u32[]{:S(2)}, u32[]{:S(2)}) collective-permute-start(bf16[2,1024,128]{2,1,0:T(8,128)(2,1)S(1)} %dynamic-slice_bitcast_fusion), channel_id=1, source_target_pairs={{0,2},{1,3},{2,0},{3,1},{4,6},{5,7},{6,4},{7,5},{8,10},{9,11},{10,... | collective-permute-start | bytes 1572872 | tf_op jit(solution)/shard_map/ppermute | solution.py:948
  12.4 32.8 %collective-permute-start.3 = (bf16[1,1024,128]{2,1,0:T(8,128)(2,1)S(1)}, bf16[1,1024,128]{2,1,0:T(8,128)(2,1)S(1)}, u32[]{:S(2)}, u32[]{:S(2)}) collective-permute-start(bf16[1,1024,128]{2,1,0:T(8,128)(2,1)S(1)} %dynamic-slice_bitcast_fusion.1), channel_id=1, source_target_pairs={{0,2},{1,3},{2,0},{3,1},{4,6},{5,7},{6,4},{7,5},{8,10},{9,11},{10,... | collective-permute-start | bytes 786440 | tf_op jit(solution)/shard_map/ppermute | solution.py:948
  20.2 6.8 %copy-start.17 = (bf16[256,1024]{1,0:T(8,128)(2,1)S(1)}, bf16[256,1024]{1,0:T(8,128)(2,1)}, u32[]{:S(2)}) copy-start(bf16[256,1024]{1,0:T(8,128)(2,1)} %refs_5_.3) | copy-start | bytes 1572868
  20.2 8.3 %copy-start.39 = (bf16[1024,4]{0,1:T(4,128)(2,1)S(1)}, bf16[1024,4]{0,1:T(4,128)(2,1)}, u32[]{:S(2)}) copy-start(bf16[1024,4]{0,1:T(4,128)(2,1)} %param.30) | copy-start | bytes 24580
  20.2 8.5 %copy-start.40 = (bf16[1024,2]{0,1:T(2,128)(2,1)S(1)}, bf16[1024,2]{0,1:T(2,128)(2,1)}, u32[]{:S(2)}) copy-start(bf16[1024,2]{0,1:T(2,128)(2,1)} %param.31) | copy-start | bytes 12292
  20.2 8.7 %copy-start.41 = (s32[2]{0:T(128)S(1)}, s32[2]{0:T(128)}, u32[]{:S(2)}) copy-start(s32[2]{0:T(128)} %param.19) | copy-start | bytes 28
  25.0 31.2 %collective-permute-start.2 = (bf16[2,1024,128]{2,1,0:T(8,128)(2,1)}, bf16[2,1024,128]{2,1,0:T(8,128)(2,1)}, u32[]{:S(2)}, u32[]{:S(2)}) collective-permute-start(bf16[2,1024,128]{2,1,0:T(8,128)(2,1)} %hold.8.refs_2_.refs_4_), channel_id=1, source_target_pairs={{0,4},{4,0},{8,12},{12,8},{16,20},{20,16},{24,28},{28,24},{1,5},{5... | collective-permute-start | bytes 1572872 | tf_op jit(solution)/shard_map/ppermute | solution.py:923
  26.9 38.7 %collective-permute-start.5 = (bf16[256,1024]{1,0:T(8,128)(2,1)S(1)}, bf16[256,1024]{1,0:T(8,128)(2,1)S(1)}, u32[]{:S(2)}, u32[]{:S(2)}) collective-permute-start(bf16[256,1024]{1,0:T(8,128)(2,1)S(1)} %copy-done.17), channel_id=1, source_target_pairs={{0,2},{1,3},{2,0},{3,1},{4,6},{5,7},{6,4},{7,5},{8,10},{9,11},{10,... | collective-permute-start | bytes 1572872 | tf_op jit(solution)/shard_map/ppermute | solution.py:948
  30.9 16.5 %copy-start.4 = (bf16[512,1024]{1,0:T(8,128)(2,1)S(1)}, bf16[512,1024]{1,0:T(8,128)(2,1)}, u32[]{:S(2)}) copy-start(bf16[512,1024]{1,0:T(8,128)(2,1)} %get-tuple-element.123.refs_3_.refs_4_) | copy-start | bytes 3145732
  45.9 10.3 %collective-permute-start.4 = (bf16[1,1024,128]{2,1,0:T(8,128)(2,1)}, bf16[1,1024,128]{2,1,0:T(8,128)(2,1)S(1)}, u32[]{:S(2)}, u32[]{:S(2)}) collective-permute-start(bf16[1,1024,128]{2,1,0:T(8,128)(2,1)} %hold.9.refs_5_), channel_id=1, source_target_pairs={{0,4},{4,0},{8,12},{12,8},{16,20},{20,16},{24,28},{28,24},{1,5},{5... | collective-permute-start | bytes 786440 | tf_op jit(solution)/shard_map/ppermute | solution.py:923
  47.4 49.1 %collective-permute-start.9 = (bf16[512,1024]{1,0:T(8,128)(2,1)S(1)}, bf16[512,1024]{1,0:T(8,128)(2,1)}, u32[]{:S(2)}, u32[]{:S(2)}) collective-permute-start(bf16[512,1024]{1,0:T(8,128)(2,1)S(1)} %copy-done.4), channel_id=1, source_target_pairs={{0,1},{1,0},{2,3},{3,2},{4,5},{5,4},{6,7},{7,6},{8,9},{9,8},{10,11... | collective-permute-start | bytes 3145736 | tf_op jit(solution)/shard_map/ppermute | solution.py:945
  47.4 49.1 %collective-permute-start.7 = (bf16[512,1024]{1,0:T(8,128)(2,1)S(1)}, bf16[512,1024]{1,0:T(8,128)(2,1)S(1)}, u32[]{:S(2)}, u32[]{:S(2)}) collective-permute-start(bf16[512,1024]{1,0:T(8,128)(2,1)S(1)} %copy-done.4), channel_id=1, source_target_pairs={{0,2},{1,3},{2,0},{3,1},{4,6},{5,7},{6,4},{7,5},{8,10},{9,11},{10,... | collective-permute-start | bytes 3145736 | tf_op jit(solution)/shard_map/ppermute | solution.py:948
  94.5 3.0 collective-permute-start.8
  94.6 25.9 %collective-permute-start.6 = (bf16[512,1024]{1,0:T(8,128)(2,1)}, bf16[512,1024]{1,0:T(8,128)(2,1)S(1)}, u32[]{:S(2)}, u32[]{:S(2)}) collective-permute-start(bf16[512,1024]{1,0:T(8,128)(2,1)} %get-tuple-element.122.refs_1_.refs_0_.refs_7_), channel_id=1, source_target_pairs={{0,2},{1,3},{2,0},{3,1},{4,6},{5,7},{6,4},{7,5},{8,10},{9,11},{10,... | collective-permute-start | bytes 3145736 | tf_op jit(solution)/shard_map/ppermute | solution.py:948
  96.5 1.0 copy-start
  121.5 3.3 collective-permute-start.10
  121.7 4.2 collective-permute-start.11
  124.8 1.1 copy-start.5
  125.9 1.0 copy-start.6
  178.0 68.4 %collective-permute-start.12 = (bf16[4,2,128,1024]{3,2,1,0:T(8,128)(2,1)}, bf16[4,2,128,1024]{3,2,1,0:T(8,128)(2,1)S(1)}, u32[]{:S(2)}, u32[]{:S(2)}) collective-permute-start(bf16[4,2,128,1024]{3,2,1,0:T(8,128)(2,1)} %get-tuple-element.144), channel_id=1, source_target_pairs={{0,4},{4,0},{8,12},{12,8},{16,20},{20,16},{24,28},{28,24},{1,5},{5... | collective-permute-start | bytes 6291464 | tf_op jit(solution)/shard_map/ppermute | solution.py:923
  231.4 19.7 %collective-permute-start.13 = (bf16[528,1024]{1,0:T(8,128)(2,1)}, bf16[528,1024]{1,0:T(8,128)(2,1)S(1)}, u32[]{:S(2)}, u32[]{:S(2)}) collective-permute-start(bf16[528,1024]{1,0:T(8,128)(2,1)} %get-tuple-element.147), channel_id=1, source_target_pairs={{0,1},{1,0},{2,3},{3,2},{4,5},{5,4},{6,7},{7,6},{8,9},{9,8},{10,11... | collective-permute-start | bytes 3244040 | tf_op jit(solution)/shard_map/ppermute | solution.py:945
  231.4 31.4 %collective-permute-start.14 = (bf16[528,1024]{1,0:T(8,128)(2,1)}, bf16[528,1024]{1,0:T(8,128)(2,1)}, u32[]{:S(2)}, u32[]{:S(2)}) collective-permute-start(bf16[528,1024]{1,0:T(8,128)(2,1)} %get-tuple-element.149), channel_id=1, source_target_pairs={{0,1},{1,0},{2,3},{3,2},{4,5},{5,4},{6,7},{7,6},{8,9},{9,8},{10,11... | collective-permute-start | bytes 3244040 | tf_op jit(solution)/shard_map/ppermute | solution.py:945
  246.4 1.3 copy-start.10
  251.1 1.0 copy-start.19
  252.1 9.1 %copy-start.23 = (bf16[1,1024,128]{2,1,0:T(8,128)(2,1)S(1)}, bf16[1,1024,128]{2,1,0:T(8,128)(2,1)}, u32[]{:S(2)}) copy-start(bf16[1,1024,128]{2,1,0:T(8,128)(2,1)} %copy-done.22) | copy-start | bytes 786436
  252.1 9.1 %copy-start.9 = (bf16[2,1024,128]{2,1,0:T(8,128)(2,1)S(1)}, bf16[2,1024,128]{2,1,0:T(8,128)(2,1)}, u32[]{:S(2)}) copy-start(bf16[2,1024,128]{2,1,0:T(8,128)(2,1)} %hold.8.refs_2_.refs_4_) | copy-start | bytes 1572868
  252.1 9.1 %copy-start.15 = (bf16[1,1024,128]{2,1,0:T(8,128)(2,1)S(1)}, bf16[1,1024,128]{2,1,0:T(8,128)(2,1)}, u32[]{:S(2)}) copy-start(bf16[1,1024,128]{2,1,0:T(8,128)(2,1)} %hold.9.refs_5_) | copy-start | bytes 786436
  255.0 26.1 %collective-permute-start.15 = (bf16[528,1024]{1,0:T(8,128)(2,1)}, bf16[528,1024]{1,0:T(8,128)(2,1)}, u32[]{:S(2)}, u32[]{:S(2)}) collective-permute-start(bf16[528,1024]{1,0:T(8,128)(2,1)} %add_parts.2.refs_2_), channel_id=1, source_target_pairs={{0,2},{1,3},{2,0},{3,1},{4,6},{5,7},{6,4},{7,5},{8,10},{9,11},{10,... | collective-permute-start | bytes 3244040 | tf_op jit(solution)/shard_map/ppermute | solution.py:948
  256.4 39.0 %collective-permute-start.16 = (bf16[2,2,128,1024]{3,2,1,0:T(8,128)(2,1)}, bf16[2,2,128,1024]{3,2,1,0:T(8,128)(2,1)S(1)}, u32[]{:S(2)}, u32[]{:S(2)}) collective-permute-start(bf16[2,2,128,1024]{3,2,1,0:T(8,128)(2,1)} %get-tuple-element.145.refs_0_), channel_id=1, source_target_pairs={{0,8},{4,12},{8,0},{12,4},{16,24},{20,28},{24,16},{28,20},{1,9},{5... | collective-permute-start | bytes 3145736 | tf_op jit(solution)/shard_map/ppermute | solution.py:923
  257.2 71.7 %collective-permute-start.17 = (bf16[4,2,128,1024]{3,2,1,0:T(8,128)(2,1)}, bf16[4,2,128,1024]{3,2,1,0:T(8,128)(2,1)}, u32[]{:S(2)}, u32[]{:S(2)}) collective-permute-start(bf16[4,2,128,1024]{3,2,1,0:T(8,128)(2,1)} %get-tuple-element.160), channel_id=1, source_target_pairs={{0,4},{4,0},{8,12},{12,8},{16,20},{20,16},{24,28},{28,24},{1,5},{5... | collective-permute-start | bytes 6291464 | tf_op jit(solution)/shard_map/ppermute | solution.py:923
  257.7 104.9 %collective-permute-start.19 = (bf16[4,2,128,1024]{3,2,1,0:T(8,128)(2,1)}, bf16[4,2,128,1024]{3,2,1,0:T(8,128)(2,1)}, u32[]{:S(2)}, u32[]{:S(2)}) collective-permute-start(bf16[4,2,128,1024]{3,2,1,0:T(8,128)(2,1)} %get-tuple-element.170), channel_id=1, source_target_pairs={{0,4},{4,0},{8,12},{12,8},{16,20},{20,16},{24,28},{28,24},{1,5},{5... | collective-permute-start | bytes 6291464 | tf_op jit(solution)/shard_map/ppermute | solution.py:923
  291.7 7.4 %all-to-all-start.1 = ((bf16[2,512,1024]{2,1,0:T(8,128)(2,1)}), bf16[2,512,1024]{2,1,0:T(8,128)(2,1)S(1)}, u32[]{:S(2)}, u32[]{:S(2)}) async-start(bf16[2,512,1024]{2,1,0:T(8,128)(2,1)} %get-tuple-element.151.refs_0_), calls=%async_computation.1 | async-start | bytes 4194304 | tf_op jit(solution)/shard_map/all_to_all | solution.py:1023
  299.1 1.3 copy-start.1
  300.4 27.4 %copy-start.26 = (bf16[1,2,128,1024]{3,2,1,0:T(8,128)(2,1)S(1)}, bf16[1,2,128,1024]{3,2,1,0:T(8,128)(2,1)}, u32[]{:S(2)}) copy-start(bf16[1,2,128,1024]{3,2,1,0:T(8,128)(2,1)} %get-tuple-element.153.refs_2_) | copy-start | bytes 1572868
  326.6 56.3 %collective-permute-start.20 = (bf16[8,4,128,256]{3,2,1,0:T(8,128)(2,1)}, bf16[8,4,128,256]{3,2,1,0:T(8,128)(2,1)}, u32[]{:S(2)}, u32[]{:S(2)}) collective-permute-start(bf16[8,4,128,256]{3,2,1,0:T(8,128)(2,1)} %get-tuple-element.158.refs_0_), channel_id=1, source_target_pairs={{0,2},{1,3},{2,0},{3,1},{4,6},{5,7},{6,4},{7,5},{8,10},{9,11},{10,... | collective-permute-start | bytes 6291464 | tf_op jit(solution)/shard_map/ppermute | solution.py:948
  327.8 31.6 %collective-permute-start.18 = (bf16[1,2,128,1024]{3,2,1,0:T(8,128)(2,1)S(1)}, bf16[1,2,128,1024]{3,2,1,0:T(8,128)(2,1)S(1)}, u32[]{:S(2)}, u32[]{:S(2)}) collective-permute-start(bf16[1,2,128,1024]{3,2,1,0:T(8,128)(2,1)S(1)} %copy-done.26), channel_id=1, source_target_pairs={{0,16},{4,20},{8,24},{12,28},{16,0},{20,4},{24,8},{28,12},{1,17},{... | collective-permute-start | bytes 1572872 | tf_op jit(solution)/shard_map/ppermute | solution.py:923
  332.2 54.9 %collective-permute-start.21 = (bf16[2,2,128,1024]{3,2,1,0:T(8,128)(2,1)}, bf16[2,2,128,1024]{3,2,1,0:T(8,128)(2,1)S(1)}, u32[]{:S(2)}, u32[]{:S(2)}) collective-permute-start(bf16[2,2,128,1024]{3,2,1,0:T(8,128)(2,1)} %get-tuple-element.161.refs_2_), channel_id=1, source_target_pairs={{0,8},{4,12},{8,0},{12,4},{16,24},{20,28},{24,16},{28,20},{1,9},{5... | collective-permute-start | bytes 3145736 | tf_op jit(solution)/shard_map/ppermute | solution.py:923
  366.0 29.1 %collective-permute-start.23 = (bf16[2,2,128,1024]{3,2,1,0:T(8,128)(2,1)}, bf16[2,2,128,1024]{3,2,1,0:T(8,128)(2,1)}, u32[]{:S(2)}, u32[]{:S(2)}) collective-permute-start(bf16[2,2,128,1024]{3,2,1,0:T(8,128)(2,1)} %get-tuple-element.171.refs_0_), channel_id=1, source_target_pairs={{0,8},{4,12},{8,0},{12,4},{16,24},{20,28},{24,16},{28,20},{1,9},{5... | collective-permute-start | bytes 3145736 | tf_op jit(solution)/shard_map/ppermute | solution.py:923
  368.0 58.5 %collective-permute-start.26 = (bf16[4,2,128,1024]{3,2,1,0:T(8,128)(2,1)}, bf16[4,2,128,1024]{3,2,1,0:T(8,128)(2,1)S(1)}, u32[]{:S(2)}, u32[]{:S(2)}) collective-permute-start(bf16[4,2,128,1024]{3,2,1,0:T(8,128)(2,1)} %get-tuple-element.189), channel_id=1, source_target_pairs={{0,4},{4,0},{8,12},{12,8},{16,20},{20,16},{24,28},{28,24},{1,5},{5... | collective-permute-start | bytes 6291464 | tf_op jit(solution)/shard_map/ppermute | solution.py:923
  368.3 5.1 copy-start.37
  368.3 8.1 %all-to-all-start.2 = ((bf16[2,512,1024]{2,1,0:T(8,128)(2,1)}), bf16[2,512,1024]{2,1,0:T(8,128)(2,1)}, u32[]{:S(2)}, u32[]{:S(2)}) async-start(bf16[2,512,1024]{2,1,0:T(8,128)(2,1)} %bitcast.50), calls=%async_computation.2 | async-start | bytes 4194304 | tf_op jit(solution)/shard_map/all_to_all | solution.py:1023
  382.8 4.4 copy-start.30
  382.8 8.0 %collective-permute-start.22 = (f32[24,1024]{1,0:T(8,128)S(1)}, f32[24,1024]{1,0:T(8,128)S(1)}, u32[]{:S(2)}, u32[]{:S(2)}) collective-permute-start(f32[24,1024]{1,0:T(8,128)S(1)} %constant_dynamic-update-slice_fusion.2.refs_1_), channel_id=1, source_target_pairs={{0,1},{1,0},{2,3},{3,2},{4,5},{5,4},{6,7},{7,6},{8,9},{9,8},{10,11... | collective-permute-start | bytes 294920 | tf_op jit(solution)/shard_map/ppermute | solution.py:910
  397.8 2.9 collective-permute-start.24
  398.1 26.0 %collective-permute-start.25 = (bf16[1,2,128,1024]{3,2,1,0:T(8,128)(2,1)}, bf16[1,2,128,1024]{3,2,1,0:T(8,128)(2,1)}, u32[]{:S(2)}, u32[]{:S(2)}) collective-permute-start(bf16[1,2,128,1024]{3,2,1,0:T(8,128)(2,1)} %get-tuple-element.177.refs_0_), channel_id=1, source_target_pairs={{0,16},{4,20},{8,24},{12,28},{16,0},{20,4},{24,8},{28,12},{1,17},{... | collective-permute-start | bytes 1572872 | tf_op jit(solution)/shard_map/ppermute | solution.py:923
  400.1 34.3 %collective-permute-start.27 = (bf16[512,1024]{1,0:T(8,128)(2,1)}, bf16[512,1024]{1,0:T(8,128)(2,1)}, u32[]{:S(2)}, u32[]{:S(2)}) collective-permute-start(bf16[512,1024]{1,0:T(8,128)(2,1)} %hold.15), channel_id=1, source_target_pairs={{0,1},{1,0},{2,3},{3,2},{4,5},{5,4},{6,7},{7,6},{8,9},{9,8},{10,11... | collective-permute-start | bytes 3145736 | tf_op jit(solution)/shard_map/ppermute | solution.py:945
  404.4 30.6 %collective-permute-start.28 = (bf16[512,1024]{1,0:T(8,128)(2,1)}, bf16[512,1024]{1,0:T(8,128)(2,1)}, u32[]{:S(2)}, u32[]{:S(2)}) collective-permute-start(bf16[512,1024]{1,0:T(8,128)(2,1)} %add_parts.3.refs_2_), channel_id=1, source_target_pairs={{0,2},{1,3},{2,0},{3,1},{4,6},{5,7},{6,4},{7,5},{8,10},{9,11},{10,... | collective-permute-start | bytes 3145736 | tf_op jit(solution)/shard_map/ppermute | solution.py:948
  405.0 37.1 %collective-permute-start.30 = (bf16[4,4,128,256]{3,2,1,0:T(8,128)(2,1)}, bf16[4,4,128,256]{3,2,1,0:T(8,128)(2,1)}, u32[]{:S(2)}, u32[]{:S(2)}) collective-permute-start(bf16[4,4,128,256]{3,2,1,0:T(8,128)(2,1)} %get-tuple-element.175.refs_0_), channel_id=1, source_target_pairs={{0,4},{4,0},{8,12},{12,8},{16,20},{20,16},{24,28},{28,24},{1,5},{5... | collective-permute-start | bytes 3145736 | tf_op jit(solution)/shard_map/ppermute | solution.py:923
  426.5 1.3 copy-start.7
  427.8 3.4 copy-start.3
  427.8 6.6 %copy-start.24 = (f32[24,1024]{1,0:T(8,128)S(1)}, f32[24,1024]{1,0:T(8,128)}, u32[]{:S(2)}) copy-start(f32[24,1024]{1,0:T(8,128)} %add_small.5.refs_0_.refs_1_) | copy-start | bytes 294916
  431.2 38.1 %collective-permute-start.32 = (bf16[2,2,128,1024]{3,2,1,0:T(8,128)(2,1)}, bf16[2,2,128,1024]{3,2,1,0:T(8,128)(2,1)S(1)}, u32[]{:S(2)}, u32[]{:S(2)}) collective-permute-start(bf16[2,2,128,1024]{3,2,1,0:T(8,128)(2,1)} %get-tuple-element.190.refs_0_), channel_id=1, source_target_pairs={{0,8},{4,12},{8,0},{12,4},{16,24},{20,28},{24,16},{28,20},{1,9},{5... | collective-permute-start | bytes 3145736 | tf_op jit(solution)/shard_map/ppermute | solution.py:923
  431.2 34.9 %collective-permute-start.31 = (bf16[1,2,128,1024]{3,2,1,0:T(8,128)(2,1)S(1)}, bf16[1,2,128,1024]{3,2,1,0:T(8,128)(2,1)S(1)}, u32[]{:S(2)}, u32[]{:S(2)}) collective-permute-start(bf16[1,2,128,1024]{3,2,1,0:T(8,128)(2,1)S(1)} %copy-done.3), channel_id=1, source_target_pairs={{0,16},{4,20},{8,24},{12,28},{16,0},{20,4},{24,8},{28,12},{1,17},{... | collective-permute-start | bytes 1572872 | tf_op jit(solution)/shard_map/ppermute | solution.py:923
  434.4 5.4 %collective-permute-start.29 = (f32[24,1024]{1,0:T(8,128)S(1)}, f32[24,1024]{1,0:T(8,128)S(1)}, u32[]{:S(2)}, u32[]{:S(2)}) collective-permute-start(f32[24,1024]{1,0:T(8,128)S(1)} %copy-done.24), channel_id=1, source_target_pairs={{0,2},{1,3},{2,0},{3,1},{4,6},{5,7},{6,4},{7,5},{8,10},{9,11},{10,... | collective-permute-start | bytes 294920 | tf_op jit(solution)/shard_map/ppermute | solution.py:910
  444.5 37.4 %collective-permute-start.33 = (bf16[2,4,128,256]{3,2,1,0:T(8,128)(2,1)}, bf16[2,4,128,256]{3,2,1,0:T(8,128)(2,1)S(1)}, u32[]{:S(2)}, u32[]{:S(2)}) collective-permute-start(bf16[2,4,128,256]{3,2,1,0:T(8,128)(2,1)} %get-tuple-element.195.refs_2_), channel_id=1, source_target_pairs={{0,8},{4,12},{8,0},{12,4},{16,24},{20,28},{24,16},{28,20},{1,9},{5... | collective-permute-start | bytes 1572872 | tf_op jit(solution)/shard_map/ppermute | solution.py:923
  469.3 1.0 copy-start.12
  470.3 6.0 %copy-start.25 = (f32[24,1024]{1,0:T(8,128)S(1)}, f32[24,1024]{1,0:T(8,128)}, u32[]{:S(2)}) copy-start(f32[24,1024]{1,0:T(8,128)} %add_small.6.refs_0_.refs_1_) | copy-start | bytes 294916
  473.0 35.8 %collective-permute-start.36 = (bf16[1,2,128,1024]{3,2,1,0:T(8,128)(2,1)}, bf16[1,2,128,1024]{3,2,1,0:T(8,128)(2,1)S(1)}, u32[]{:S(2)}, u32[]{:S(2)}) collective-permute-start(bf16[1,2,128,1024]{3,2,1,0:T(8,128)(2,1)} %get-tuple-element.200.refs_0_), channel_id=1, source_target_pairs={{0,16},{4,20},{8,24},{12,28},{16,0},{20,4},{24,8},{28,12},{1,17},{... | collective-permute-start | bytes 1572872 | tf_op jit(solution)/shard_map/ppermute | solution.py:923
  476.4 8.3 %collective-permute-start.34 = (f32[24,1024]{1,0:T(8,128)S(1)}, f32[24,1024]{1,0:T(8,128)S(1)}, u32[]{:S(2)}, u32[]{:S(2)}) collective-permute-start(f32[24,1024]{1,0:T(8,128)S(1)} %copy-done.25), channel_id=1, source_target_pairs={{0,4},{4,0},{8,12},{12,8},{16,20},{20,16},{24,28},{28,24},{1,5},{5... | collective-permute-start | bytes 294920 | tf_op jit(solution)/shard_map/ppermute | solution.py:910
  486.9 16.7 %collective-permute-start.35 = (f32[24,1024]{1,0:T(8,128)}, f32[24,1024]{1,0:T(8,128)S(1)}, u32[]{:S(2)}, u32[]{:S(2)}) collective-permute-start(f32[24,1024]{1,0:T(8,128)} %add_small.7.refs_0_.refs_1_), channel_id=1, source_target_pairs={{0,8},{4,12},{8,0},{12,4},{16,24},{20,28},{24,16},{28,20},{1,9},{5... | collective-permute-start | bytes 294920 | tf_op jit(solution)/shard_map/ppermute | solution.py:910
  505.9 8.7 %collective-permute-start.37 = (f32[24,1024]{1,0:T(8,128)}, f32[24,1024]{1,0:T(8,128)S(1)}, u32[]{:S(2)}, u32[]{:S(2)}) collective-permute-start(f32[24,1024]{1,0:T(8,128)} %add_small.8.refs_2_.refs_1_), channel_id=1, source_target_pairs={{0,16},{4,20},{8,24},{12,28},{16,0},{20,4},{24,8},{28,12},{1,17},{... | collective-permute-start | bytes 294920 | tf_op jit(solution)/shard_map/ppermute | solution.py:910
  505.9 14.9 %collective-permute-start.38 = (bf16[1,4,128,256]{3,2,1,0:T(8,128)(2,1)}, bf16[1,4,128,256]{3,2,1,0:T(8,128)(2,1)S(1)}, u32[]{:S(2)}, u32[]{:S(2)}) collective-permute-start(bf16[1,4,128,256]{3,2,1,0:T(8,128)(2,1)} %get-tuple-element.202.refs_0_), channel_id=1, source_target_pairs={{0,16},{4,20},{8,24},{12,28},{16,0},{20,4},{24,8},{28,12},{1,17},{... | collective-permute-start | bytes 786440 | tf_op jit(solution)/shard_map/ppermute | solution.py:923
  (20 other events, 15.7 us)
Sparse Core Ops, SparseCore 0:
  151.9 105.6 reduce-scatter.1

commit v8 on v7

--- a/solution.py
+++ b/solution.py
@@ -1103,14 +1103,16 @@
         if ds == 1 or seqs == 1:
             for v in halvings[2:]:
                 v.launch()
-            mark = dense_sum.rest(mark)
             for v in halvings[:1]:
                 mark = v.add(mark)
     moved = [to_sequence(grads[ds], ds) for ds in range(1, seqs)]
     ng_parts = exchange(ngs.reshape(members, rows, d))
+    mark = dense_sum.rest(mark)
     up_out, down_out = last_add([dense_sum.keep, dense_sum.came], (False, True), deps=mark)
     mark = (up_out,)
     for v in halvings[1:2]:
+        mark = v.add(mark)
+    for v in halvings[:1]:
         mark = v.add(mark)
     input_grad, sums_one = input_backward(ng_parts, inputs, mg, gain_one, mark)
     mark = (sums_one,)
@@ -1136,32 +1138,30 @@
         keep, send = keep[:dp // 2], keep[dp // 2:]
     attn_sum = Halving(keep, send, straight)
     attn_sum.launch()
-    for v in halvings[:1]:
-        mark = v.add(mark)
     mark = sums.add(mark)
     stacks, mark = finish(0, mark)
+    mark = sums.add(mark)
     for v in halvings[1:2]:
+        mark = v.add(mark)
+    for v in halvings[2:]:
+        mark = v.add(mark)
+    for e in range(1, min(3, experts)):
+        stacks, mark = finish(e, mark)
+    mark = sums.add(mark)
+    mark = attn_sum.add(mark)
+    for v in halvings[2:]:
         mark = v.add(mark)
     out_near, out_far = to_owner([hold(v, mark) for v in out_e])
     out_came, terms = onward(out_far, mark)
     mark = tuple(terms[:1]) or mark
-    if experts > 1:
-        stacks, mark = finish(1, mark)
-    for v in halvings[2:]:
-        mark = v.add(mark)
-    layer_output = layer_out(out_near + out_came, middle, pos_col, mark)
-    mark = sums.add((layer_output,))
     mark = attn_sum.add(mark)
-    if experts > 2:
-        stacks, mark = finish(2, mark)
-    for v in halvings[2:]:
-        mark = v.add(mark)
-    mark = attn_sum.add(mark)
-    mark = sums.add(mark)
     mark = sums.add(mark)
     for e in range(3, experts):
         stacks, mark = finish(e, mark)
     expert_up_out, expert_down_out = stacks
+    mark = sums.add(mark)
+    layer_output = layer_out(out_near + out_came, middle, pos_col, mark)
+    mark = (layer_output,)
     while sums.came is not None:
         mark = sums.add(mark)
     mark = attn_sum.rest(mark)

time: 534 us -> 542 us (1.015)
    ppermute x17, waiting for transfers between devices: 57.3 us -> 69.5 us  [over_dp(): lax.ppermute(v, 'dp', [(i, i ^ 1 << bit) for i in range(lax.axis_size('dp...]
    ppermute x5, waiting for transfers between devices: 19.2 us -> 8.84 us  [launch(): lax.ppermute(self.v, axis, [(i, i ^ bit) for i in range(lax.axis_size(axi...]
    unnamed x88 -> x97, local copies, waits for them, and re-layouts: 23.6 us -> 28.8 us
  transfers between devices with their start and end apart: 42 -> 42, of which waited for: 12 -> 11; matrix products, arithmetic and copies ran while one was open for 3% -> 4% of each run, Pallas kernels for 52% -> 51%
where the time goes in v8:
time: 542 us; the launch traced here: 540 us
  Pallas kernels  305 us (56%)
  waiting for transfers between devices  106 us (20%)
  starting transfers between devices  47.2 us (9%)
  local copies, waits for them, and re-layouts  38.8 us (7%)
  blocking collectives  19.9 us (4%)
  between operations  14.6 us (3%)
  other arithmetic  8.24 us (2%)
    pallas_call x2, Pallas kernels, ffn_experts(): pl.pallas_call(partial(expert_kernel, (first, count, whole, chunks, rows,...  76.6 us
    ppermute x17, waiting for transfers between devices, over_dp(): lax.ppermute(v, 'dp', [(i, i ^ 1 << bit) for i in range(lax.axis_size('dp...  69.5 us
    pallas_call x2, Pallas kernels, attn_backward(): pl.pallas_call(skip(partial(attn_backward_kernel, length, bits, len(extra...  53.3 us
    pallas_call x2, Pallas kernels, ffn_dense(): pl.pallas_call(partial(dense_kernel, (chunks, rows, tm, lanes, order, fir...  49.2 us
    pallas_call x11, Pallas kernels, split_add(): pl.pallas_call(partial(split_add_kernel, len(deps)), name='split_add', gr...  32.3 us
    pallas_call x3, Pallas kernels, attn_forward(): pl.pallas_call(skip(partial(attn_forward_kernel, length, tuple((w.shape[0...  31.7 us
    unnamed x97, local copies, waits for them, and re-layouts  28.8 us
    ppermute x8, waiting for transfers between devices, from_sequence(): lax.ppermute(v, 'tensor', [(place(a, b), place(a - k, b)) for a, b in eve...  23.7 us
  transfers between devices with their start and end apart: 42, of which 11 were waited for; matrix products, arithmetic and copies ran while one was open for 4% of the time, Pallas kernels for 51%

profile of v8, /device:TPU:0, one launch (start us, length us, event | category | flops | bytes accessed | tf_op | source)
XLA Modules:
  0.0 540.1 jit_solution(6853601325758914230)
XLA Ops:
  8.8 2.6 collective-permute-start
  15.0 5.1 first_norm.1
  20.2 4.0 collective-permute-done.refs_0_
  25.0 1.9 collective-permute-start.2
  30.9 14.2 %attn_forward.3 = (bf16[1024,256]{1,0:T(8,128)(2,1)}, bf16[1024,256]{1,0:T(8,128)(2,1)}, bf16[1024,256]{1,0:T(8,128)(2,1)}, bf16[1024,256]{1,0:T(8,128)(2,1)}, f32[2,8,1024]{2,1,0:T(8,128)}) custom-call(s32[1]{0:T(128)} %dynamic_slice.12.refs_0_, s32[2]{0:T(128)} %iota.11.refs_1_, bf16[2,1024,128]{2,1,0:T(8,128)(2,1)} %hold.8.refs_2_.refs_4_, ...), custom_call_target="tpu_custom_call" | custom-call | tf_op jit(solution)/shard_map/attn_forward/pallas_call | solution.py:549
  47.5 8.7 %attn_forward.4 = (bf16[1024,256]{1,0:T(8,128)(2,1)}, bf16[1024,256]{1,0:T(8,128)(2,1)}, bf16[1024,256]{1,0:T(8,128)(2,1)}, bf16[1024,256]{1,0:T(8,128)(2,1)}, f32[2,8,1024]{2,1,0:T(8,128)}) custom-call(s32[1]{0:T(128)} %dynamic_slice.12.refs_0_, s32[1]{0:T(128)} %bitcast.71, f32[2,8,1024]{2,1,0:T(8,128)} %get-tuple-element.115.refs_1_.refs_2_.refs_11_, ...), custom_call_target="tpu_custom_call" | custom-call | tf_op jit(solution)/shard_map/attn_forward/pallas_call | solution.py:549
  56.9 8.7 %attn_forward.5 = (bf16[1024,256]{1,0:T(8,128)(2,1)}, bf16[1024,256]{1,0:T(8,128)(2,1)}, bf16[1024,256]{1,0:T(8,128)(2,1)}, bf16[1024,256]{1,0:T(8,128)(2,1)}, f32[2,8,1024]{2,1,0:T(8,128)}) custom-call(s32[1]{0:T(128)} %dynamic_slice.12.refs_0_, s32[1]{0:T(128)} %bitcast.70, ...), custom_call_target="tpu_custom_call", output_to_operand_aliasing={{0}: (5, {}), {1}: (6, {}), {2}: (7, {}), {3}: (8, {}), {4}... | custom-call | tf_op jit(solution)/shard_map/attn_forward/pallas_call | solution.py:549
  66.5 3.8 project.1
  70.2 19.9 %all_to_all.15.came = bf16[2,512,1024]{2,1,0:T(8,128)(2,1)} all-to-all(bf16[2,512,1024]{2,1,0:T(8,128)(2,1)} %project.1), channel_id=1, replica_groups={{0,1},{2,3},{4,5},{6,7},{8,9},{10,11},{12,13},{14,15},{16,17},{18,19},{..., dimensions={0} | all-to-all | bytes 4194304 | tf_op jit(solution)/shard_map/all_to_all | solution.py:1023
  90.1 4.4 second_norm.1
  94.6 1.9 collective-permute-start.6
  97.6 23.1 %ffn_dense.2 = (bf16[512,1024]{1,0:T(8,128)(2,1)}, bf16[512,1024]{1,0:T(8,128)(2,1)}, bf16[528,1024]{1,0:T(8,128)(2,1)}, bf16[528,1024]{1,0:T(8,128)(2,1)}, f32[1024,1024]{1,0:T(8,128)}, /*index=5*/f32[1024,1024]{1,0:T(8,128)}) custom-call(s32[1]{0:T(128)} %bitcast.me_ref.refs_1_, bf16[512,1024]{1,0:T(8,128)(2,1)} %copy-done, ...), custom_call_target="tpu_custom_call" | custom-call | tf_op jit(solution)/shard_map/ffn_dense/pallas_call | solution.py:211
  127.1 25.0 %ffn_experts.2 = (bf16[512,1024]{1,0:T(8,128)(2,1)}, bf16[512,1024]{1,0:T(8,128)(2,1)}, bf16[512,1024]{1,0:T(8,128)(2,1)}, bf16[512,1024]{1,0:T(8,128)(2,1)}, bf...) custom-call(s32[1]{0:T(128)} %bitcast.me_ref.refs_1_, ...), custom_call_target="tpu_custom_call" | custom-call | tf_op jit(solution)/shard_map/ffn_experts/pallas_call | solution.py:392
  152.1 26.2 %ffn_dense.3 = (bf16[512,1024]{1,0:T(8,128)(2,1)}, bf16[512,1024]{1,0:T(8,128)(2,1)}, bf16[528,1024]{1,0:T(8,128)(2,1)}, bf16[528,1024]{1,0:T(8,128)(2,1)}, bf16...) custom-call(s32[1]{0:T(128)} %bitcast.me_ref.refs_1_, bf16[512,1024]{1,0:T(8,128)(2,1)} %hold.10.refs_1_.refs_0_, ...), custom_call_target="tpu_custom_call" | custom-call | tf_op jit(solution)/shard_map/ffn_dense/pallas_call | solution.py:211
  178.2 1.8 collective-permute-start.12
  180.0 51.6 %ffn_experts.3 = (bf16[512,1024]{1,0:T(8,128)(2,1)}, bf16[512,1024]{1,0:T(8,128)(2,1)}, bf16[512,1024]{1,0:T(8,128)(2,1)}, bf16[512,1024]{1,0:T(8,128)(2,1)}, bf...) custom-call(s32[1]{0:T(128)} %bitcast.me_ref.refs_1_, ...), custom_call_target="tpu_custom_call" | custom-call | tf_op jit(solution)/shard_map/ffn_experts/pallas_call | solution.py:392
  232.2 14.5 %collective-permute-done.12.refs_3_.refs_4_ = bf16[4,2,128,1024]{3,2,1,0:T(8,128)(2,1)S(1)} collective-permute-done((bf16[4,2,128,1024]{3,2,1,0:T(8,128)(2,1)}, bf16[4,2,128,1024]{3,2,1,0:T(8,128)(2,1)S(1)}, u32[]{:S(2)}, u32[]{:S(2)}) %collective-permute-start.12) | collective-permute-done | bytes 2097184 | tf_op jit(solution)/shard_map/ppermute | solution.py:923
  248.1 3.3 split_add.11
  252.4 2.9 add_parts.2.refs_2_
  260.0 1.7 maximum_select_fusion.refs_3_.refs_6_
  261.7 19.7 %collective-permute-done.15.refs_6_ = bf16[528,1024]{1,0:T(8,128)(2,1)} collective-permute-done((bf16[528,1024]{1,0:T(8,128)(2,1)}, bf16[528,1024]{1,0:T(8,128)(2,1)}, u32[]{:S(2)}, u32[]{:S(2)}) %collective-permute-start.15) | collective-permute-done | bytes 1081376 | tf_op jit(solution)/shard_map/ppermute | solution.py:948
  281.4 10.6 %middle_backward.1 = (f32[512,1024]{1,0:T(8,128)}, bf16[2,512,1024]{2,1,0:T(8,128)(2,1)}, f32[16,1024]{1,0:T(8,128)}) custom-call(s32[4,5]{1,0:T(4,128)} %stack.50.bnd_ref.refs_0_, s32[1]{0:T(128)} %bitcast.6.refs_1_, bf16[528,1024]{1,0:T(8,128)(2,1)} %add_parts.2.refs_2_, bf16[3,1024,256]{2,1,0:T(8,128)(2,1)} %maximum_select_fusion.refs_3_.refs_6_, ...), custom_call_target="tpu_custom_call" | custom-call | tf_op jit(solution)/shard_map/middle_backward/pallas_call | solution.py:812
  292.0 3.8 all-to-all-start.1
  296.8 2.6 split_add.12
  300.7 26.2 %attn_backward.2 = (bf16[1024,1024]{1,0:T(8,128)(2,1)}, bf16[8,4,128,256]{3,2,1,0:T(8,128)(2,1)}) custom-call(s32[1]{0:T(128)} %dynamic_slice.12.refs_0_, s32[1]{0:T(128)} %bitcast.me_ref.refs_1_, bf16[1,2,128,1024]{3,2,1,0:T(8,128)(2,1)} %get-tuple-element.153.refs_2_, bf16[1024,1024]{1,0:T(8,128)(2,1)} %bitcast.45, ...), custom_call_target="tpu_custom_call" | custom-call | tf_op jit(solution)/shard_map/attn_backward/pallas_call | solution.py:637
  329.6 3.3 split_add.13
  333.0 27.1 %attn_backward.3 = (bf16[1024,1024]{1,0:T(8,128)(2,1)}, bf16[8,4,128,256]{3,2,1,0:T(8,128)(2,1)}) custom-call(s32[1]{0:T(128)} %dynamic_slice.12.refs_0_, s32[1]{0:T(128)} %bitcast.me_ref.refs_1_, bf16[2,2,128,1024]{3,2,1,0:T(8,128)(2,1)} %get-tuple-element.161.refs_2_, bf16[1024,1024]{1,0:T(8,128)(2,1)} %bitcast.46, ...), custom_call_target="tpu_custom_call" | custom-call | tf_op jit(solution)/shard_map/attn_backward/pallas_call | solution.py:637
  360.1 2.4 last_add.6
  362.5 3.3 split_add.14
  365.8 1.9 collective-permute-start.24
  367.7 5.2 all-to-all-start.2
  373.9 2.6 split_add.15
  376.5 5.7 %input_backward.1 = (f32[512,1024]{1,0:T(8,128)}, f32[8,1024]{1,0:T(8,128)}) custom-call(bf16[1,2,128,1024]{3,2,1,0:T(8,128)(2,1)} %get-tuple-element.173.refs_0_, bf16[2,512,1024]{2,1,0:T(8,128)(2,1)} %all-to-all-done.2.refs_1_, bf16[512,1024]{1,0:T(8,128)(2,1)} %refs_2_.3, f32[512,1024]{1,0:T(8,128)} %get-tuple-element.175.refs_3_, f32[1,1024]{1,0:T(1,128)} %bitcast.61), custom_call_target="tpu_custom_call" | custom-call | tf_op jit(solution)/shard_map/input_backward/pallas_call | solution.py:888
  383.4 4.2 split_add.16
  388.2 1.6 add_small.5.refs_0_.refs_1_
  390.4 1.6 collective-permute-start.29
  392.0 2.1 last_add.7
  395.4 1.6 add_small.6.refs_0_.refs_1_
  397.0 2.6 split_add.17
  401.0 3.4 split_add.18
  404.5 2.5 collective-permute-start.26
  407.4 1.6 collective-permute-start.28
  409.0 30.7 %collective-permute-done.26.refs_4_ = bf16[1,2,128,1024]{3,2,1,0:T(8,128)(2,1)S(1)} collective-permute-done((bf16[1,2,128,1024]{3,2,1,0:T(8,128)(2,1)}, bf16[1,2,128,1024]{3,2,1,0:T(8,128)(2,1)S(1)}, u32[]{:S(2)}, u32[]{:S(2)}) %collective-permute-start.26) | collective-permute-done | bytes 524320 | tf_op jit(solution)/shard_map/ppermute | solution.py:923
  440.5 2.4 last_add.8
  442.9 3.0 copy.88.refs_1_
  445.9 3.3 collective-permute-done.27.refs_4_
  450.0 2.4 last_add.9
  453.0 1.6 add_small.7.refs_0_.refs_1_
  455.6 2.4 split_add.19
  459.0 2.6 split_add.20
  462.1 2.3 collective-permute-done.31.refs_2_
  465.4 2.8 add_parts.3.refs_0_
  469.4 3.9 collective-permute-start.32
  473.3 2.7 collective-permute-start.34
  476.0 21.0 %collective-permute-done.32.refs_3_.refs_4_ = bf16[2,4,128,256]{3,2,1,0:T(8,128)(2,1)S(1)} collective-permute-done((bf16[2,4,128,256]{3,2,1,0:T(8,128)(2,1)S(1)}, bf16[2,4,128,256]{3,2,1,0:T(8,128)(2,1)S(1)}, u32[]{:S(2)}, u32[]{:S(2)}) %collective-permute-start.32) | collective-permute-done | bytes 524320 | tf_op jit(solution)/shard_map/ppermute | solution.py:923
  497.8 2.0 split_add.21
  500.5 1.6 add_small.8.refs_2_.refs_1_
  502.1 2.1 collective-permute-start.35
  505.0 2.4 last_add.10
  507.4 8.2 %collective-permute-done.35.refs_2_ = f32[24,1024]{1,0:T(8,128)S(1)} collective-permute-done((f32[24,1024]{1,0:T(8,128)}, f32[24,1024]{1,0:T(8,128)S(1)}, u32[]{:S(2)}, u32[]{:S(2)}) %collective-permute-start.35) | collective-permute-done | bytes 98336 | tf_op jit(solution)/shard_map/ppermute | solution.py:910
  516.2 1.6 add_small.9.refs_0_
  523.8 4.9 layer_out.1.refs_0_
  529.4 1.9 last_add.11
  531.2 1.8 pad_maximum_fusion
  (203 shorter events, 57.2 us)
Async XLA Ops:
  7.2 384.9 %reduce-scatter.2.cloned.1.call-start = ((), (), s32[]{:S(2)}) async-start(), calls=%async_computation.4 | async-start | bytes 4718592 | tf_op jit(solution)/shard_map/reduce_scatter | solution.py:1083
  7.2 6.8 %collective-permute-start.1 = (bf16[512,1024]{1,0:T(8,128)(2,1)}, bf16[512,1024]{1,0:T(8,128)(2,1)S(1)}, u32[]{:S(2)}, u32[]{:S(2)}) collective-permute-start(bf16[512,1024]{1,0:T(8,128)(2,1)} %refs_2_.3), channel_id=1, source_target_pairs={{0,1},{1,0},{2,3},{3,2},{4,5},{5,4},{6,7},{7,6},{8,9},{9,8},{10,11... | collective-permute-start | bytes 3145736 | tf_op jit(solution)/shard_map/ppermute | solution.py:945
  8.8 15.4 %collective-permute-start = (bf16[2,1024,128]{2,1,0:T(8,128)(2,1)S(1)}, bf16[2,1024,128]{2,1,0:T(8,128)(2,1)S(1)}, u32[]{:S(2)}, u32[]{:S(2)}) collective-permute-start(bf16[2,1024,128]{2,1,0:T(8,128)(2,1)S(1)} %dynamic-slice_bitcast_fusion), channel_id=1, source_target_pairs={{0,2},{1,3},{2,0},{3,1},{4,6},{5,7},{6,4},{7,5},{8,10},{9,11},{10,... | collective-permute-start | bytes 1572872 | tf_op jit(solution)/shard_map/ppermute | solution.py:948
  12.4 32.8 %collective-permute-start.3 = (bf16[1,1024,128]{2,1,0:T(8,128)(2,1)S(1)}, bf16[1,1024,128]{2,1,0:T(8,128)(2,1)S(1)}, u32[]{:S(2)}, u32[]{:S(2)}) collective-permute-start(bf16[1,1024,128]{2,1,0:T(8,128)(2,1)S(1)} %dynamic-slice_bitcast_fusion.1), channel_id=1, source_target_pairs={{0,2},{1,3},{2,0},{3,1},{4,6},{5,7},{6,4},{7,5},{8,10},{9,11},{10,... | collective-permute-start | bytes 786440 | tf_op jit(solution)/shard_map/ppermute | solution.py:948
  20.2 6.8 %copy-start.17 = (bf16[256,1024]{1,0:T(8,128)(2,1)S(1)}, bf16[256,1024]{1,0:T(8,128)(2,1)}, u32[]{:S(2)}) copy-start(bf16[256,1024]{1,0:T(8,128)(2,1)} %refs_5_.3) | copy-start | bytes 1572868
  20.2 8.3 %copy-start.43 = (bf16[1024,4]{0,1:T(4,128)(2,1)S(1)}, bf16[1024,4]{0,1:T(4,128)(2,1)}, u32[]{:S(2)}) copy-start(bf16[1024,4]{0,1:T(4,128)(2,1)} %param.30) | copy-start | bytes 24580
  20.2 8.5 %copy-start.44 = (bf16[1024,2]{0,1:T(2,128)(2,1)S(1)}, bf16[1024,2]{0,1:T(2,128)(2,1)}, u32[]{:S(2)}) copy-start(bf16[1024,2]{0,1:T(2,128)(2,1)} %param.31) | copy-start | bytes 12292
  20.2 8.7 %copy-start.45 = (s32[2]{0:T(128)S(1)}, s32[2]{0:T(128)}, u32[]{:S(2)}) copy-start(s32[2]{0:T(128)} %param.19) | copy-start | bytes 28
  25.0 31.2 %collective-permute-start.2 = (bf16[2,1024,128]{2,1,0:T(8,128)(2,1)}, bf16[2,1024,128]{2,1,0:T(8,128)(2,1)}, u32[]{:S(2)}, u32[]{:S(2)}) collective-permute-start(bf16[2,1024,128]{2,1,0:T(8,128)(2,1)} %hold.8.refs_2_.refs_4_), channel_id=1, source_target_pairs={{0,4},{4,0},{8,12},{12,8},{16,20},{20,16},{24,28},{28,24},{1,5},{5... | collective-permute-start | bytes 1572872 | tf_op jit(solution)/shard_map/ppermute | solution.py:923
  26.9 38.7 %collective-permute-start.5 = (bf16[256,1024]{1,0:T(8,128)(2,1)S(1)}, bf16[256,1024]{1,0:T(8,128)(2,1)S(1)}, u32[]{:S(2)}, u32[]{:S(2)}) collective-permute-start(bf16[256,1024]{1,0:T(8,128)(2,1)S(1)} %copy-done.17), channel_id=1, source_target_pairs={{0,2},{1,3},{2,0},{3,1},{4,6},{5,7},{6,4},{7,5},{8,10},{9,11},{10,... | collective-permute-start | bytes 1572872 | tf_op jit(solution)/shard_map/ppermute | solution.py:948
  30.9 16.5 %copy-start.4 = (bf16[512,1024]{1,0:T(8,128)(2,1)S(1)}, bf16[512,1024]{1,0:T(8,128)(2,1)}, u32[]{:S(2)}) copy-start(bf16[512,1024]{1,0:T(8,128)(2,1)} %get-tuple-element.123.refs_3_.refs_4_) | copy-start | bytes 3145732
  45.9 10.3 %collective-permute-start.4 = (bf16[1,1024,128]{2,1,0:T(8,128)(2,1)}, bf16[1,1024,128]{2,1,0:T(8,128)(2,1)S(1)}, u32[]{:S(2)}, u32[]{:S(2)}) collective-permute-start(bf16[1,1024,128]{2,1,0:T(8,128)(2,1)} %hold.9.refs_5_), channel_id=1, source_target_pairs={{0,4},{4,0},{8,12},{12,8},{16,20},{20,16},{24,28},{28,24},{1,5},{5... | collective-permute-start | bytes 786440 | tf_op jit(solution)/shard_map/ppermute | solution.py:923
  47.4 49.1 %collective-permute-start.9 = (bf16[512,1024]{1,0:T(8,128)(2,1)S(1)}, bf16[512,1024]{1,0:T(8,128)(2,1)}, u32[]{:S(2)}, u32[]{:S(2)}) collective-permute-start(bf16[512,1024]{1,0:T(8,128)(2,1)S(1)} %copy-done.4), channel_id=1, source_target_pairs={{0,1},{1,0},{2,3},{3,2},{4,5},{5,4},{6,7},{7,6},{8,9},{9,8},{10,11... | collective-permute-start | bytes 3145736 | tf_op jit(solution)/shard_map/ppermute | solution.py:945
  47.4 49.1 %collective-permute-start.7 = (bf16[512,1024]{1,0:T(8,128)(2,1)S(1)}, bf16[512,1024]{1,0:T(8,128)(2,1)S(1)}, u32[]{:S(2)}, u32[]{:S(2)}) collective-permute-start(bf16[512,1024]{1,0:T(8,128)(2,1)S(1)} %copy-done.4), channel_id=1, source_target_pairs={{0,2},{1,3},{2,0},{3,1},{4,6},{5,7},{6,4},{7,5},{8,10},{9,11},{10,... | collective-permute-start | bytes 3145736 | tf_op jit(solution)/shard_map/ppermute | solution.py:948
  94.5 3.0 collective-permute-start.8
  94.6 26.0 %collective-permute-start.6 = (bf16[512,1024]{1,0:T(8,128)(2,1)}, bf16[512,1024]{1,0:T(8,128)(2,1)S(1)}, u32[]{:S(2)}, u32[]{:S(2)}) collective-permute-start(bf16[512,1024]{1,0:T(8,128)(2,1)} %get-tuple-element.122.refs_1_.refs_0_.refs_7_), channel_id=1, source_target_pairs={{0,2},{1,3},{2,0},{3,1},{4,6},{5,7},{6,4},{7,5},{8,10},{9,11},{10,... | collective-permute-start | bytes 3145736 | tf_op jit(solution)/shard_map/ppermute | solution.py:948
  120.6 1.0 copy-start.2
  121.7 3.2 collective-permute-start.10
  121.8 4.3 collective-permute-start.11
  124.9 1.1 copy-start.5
  126.0 1.0 copy-start.6
  178.2 68.5 %collective-permute-start.12 = (bf16[4,2,128,1024]{3,2,1,0:T(8,128)(2,1)}, bf16[4,2,128,1024]{3,2,1,0:T(8,128)(2,1)S(1)}, u32[]{:S(2)}, u32[]{:S(2)}) collective-permute-start(bf16[4,2,128,1024]{3,2,1,0:T(8,128)(2,1)} %get-tuple-element.144), channel_id=1, source_target_pairs={{0,4},{4,0},{8,12},{12,8},{16,20},{20,16},{24,28},{28,24},{1,5},{5... | collective-permute-start | bytes 6291464 | tf_op jit(solution)/shard_map/ppermute | solution.py:923
  231.6 19.8 %collective-permute-start.13 = (bf16[528,1024]{1,0:T(8,128)(2,1)}, bf16[528,1024]{1,0:T(8,128)(2,1)S(1)}, u32[]{:S(2)}, u32[]{:S(2)}) collective-permute-start(bf16[528,1024]{1,0:T(8,128)(2,1)} %get-tuple-element.147), channel_id=1, source_target_pairs={{0,1},{1,0},{2,3},{3,2},{4,5},{5,4},{6,7},{7,6},{8,9},{9,8},{10,11... | collective-permute-start | bytes 3244040 | tf_op jit(solution)/shard_map/ppermute | solution.py:945
  231.7 97.9 %collective-permute-start.17 = (bf16[4,2,128,1024]{3,2,1,0:T(8,128)(2,1)}, bf16[4,2,128,1024]{3,2,1,0:T(8,128)(2,1)}, u32[]{:S(2)}, u32[]{:S(2)}) collective-permute-start(bf16[4,2,128,1024]{3,2,1,0:T(8,128)(2,1)} %get-tuple-element.160), channel_id=1, source_target_pairs={{0,4},{4,0},{8,12},{12,8},{16,20},{20,16},{24,28},{28,24},{1,5},{5... | collective-permute-start | bytes 6291464 | tf_op jit(solution)/shard_map/ppermute | solution.py:923
  232.1 29.6 %collective-permute-start.14 = (bf16[528,1024]{1,0:T(8,128)(2,1)}, bf16[528,1024]{1,0:T(8,128)(2,1)}, u32[]{:S(2)}, u32[]{:S(2)}) collective-permute-start(bf16[528,1024]{1,0:T(8,128)(2,1)} %get-tuple-element.149), channel_id=1, source_target_pairs={{0,1},{1,0},{2,3},{3,2},{4,5},{5,4},{6,7},{7,6},{8,9},{9,8},{10,11... | collective-permute-start | bytes 3244040 | tf_op jit(solution)/shard_map/ppermute | solution.py:945
  246.8 1.3 copy-start.10
  252.4 7.5 %copy-start.26 = (bf16[1,1024,128]{2,1,0:T(8,128)(2,1)S(1)}, bf16[1,1024,128]{2,1,0:T(8,128)(2,1)}, u32[]{:S(2)}) copy-start(bf16[1,1024,128]{2,1,0:T(8,128)(2,1)} %copy-done.25) | copy-start | bytes 786436
  252.4 7.6 %copy-start.9 = (bf16[2,1024,128]{2,1,0:T(8,128)(2,1)S(1)}, bf16[2,1024,128]{2,1,0:T(8,128)(2,1)}, u32[]{:S(2)}) copy-start(bf16[2,1024,128]{2,1,0:T(8,128)(2,1)} %hold.8.refs_2_.refs_4_) | copy-start | bytes 1572868
  252.4 7.6 %copy-start.16 = (bf16[1,1024,128]{2,1,0:T(8,128)(2,1)S(1)}, bf16[1,1024,128]{2,1,0:T(8,128)(2,1)}, u32[]{:S(2)}) copy-start(bf16[1,1024,128]{2,1,0:T(8,128)(2,1)} %hold.9.refs_5_) | copy-start | bytes 786436
  255.3 26.0 %collective-permute-start.15 = (bf16[528,1024]{1,0:T(8,128)(2,1)}, bf16[528,1024]{1,0:T(8,128)(2,1)}, u32[]{:S(2)}, u32[]{:S(2)}) collective-permute-start(bf16[528,1024]{1,0:T(8,128)(2,1)} %add_parts.2.refs_2_), channel_id=1, source_target_pairs={{0,2},{1,3},{2,0},{3,1},{4,6},{5,7},{6,4},{7,5},{8,10},{9,11},{10,... | collective-permute-start | bytes 3244040 | tf_op jit(solution)/shard_map/ppermute | solution.py:948
  256.9 38.8 %collective-permute-start.16 = (bf16[2,2,128,1024]{3,2,1,0:T(8,128)(2,1)}, bf16[2,2,128,1024]{3,2,1,0:T(8,128)(2,1)S(1)}, u32[]{:S(2)}, u32[]{:S(2)}) collective-permute-start(bf16[2,2,128,1024]{3,2,1,0:T(8,128)(2,1)} %get-tuple-element.145.refs_0_), channel_id=1, source_target_pairs={{0,8},{4,12},{8,0},{12,4},{16,24},{20,28},{24,16},{28,20},{1,9},{5... | collective-permute-start | bytes 3145736 | tf_op jit(solution)/shard_map/ppermute | solution.py:923
  257.7 104.9 %collective-permute-start.19 = (bf16[4,2,128,1024]{3,2,1,0:T(8,128)(2,1)}, bf16[4,2,128,1024]{3,2,1,0:T(8,128)(2,1)}, u32[]{:S(2)}, u32[]{:S(2)}) collective-permute-start(bf16[4,2,128,1024]{3,2,1,0:T(8,128)(2,1)} %get-tuple-element.170), channel_id=1, source_target_pairs={{0,4},{4,0},{8,12},{12,8},{16,20},{20,16},{24,28},{28,24},{1,5},{5... | collective-permute-start | bytes 6291464 | tf_op jit(solution)/shard_map/ppermute | solution.py:923
  292.0 7.4 %all-to-all-start.1 = ((bf16[2,512,1024]{2,1,0:T(8,128)(2,1)}), bf16[2,512,1024]{2,1,0:T(8,128)(2,1)S(1)}, u32[]{:S(2)}, u32[]{:S(2)}) async-start(bf16[2,512,1024]{2,1,0:T(8,128)(2,1)} %get-tuple-element.151.refs_0_), calls=%async_computation.1 | async-start | bytes 4194304 | tf_op jit(solution)/shard_map/all_to_all | solution.py:1023
  299.4 1.3 copy-start.1
  300.7 28.0 %copy-start.30 = (bf16[1,2,128,1024]{3,2,1,0:T(8,128)(2,1)S(1)}, bf16[1,2,128,1024]{3,2,1,0:T(8,128)(2,1)}, u32[]{:S(2)}) copy-start(bf16[1,2,128,1024]{3,2,1,0:T(8,128)(2,1)} %get-tuple-element.153.refs_2_) | copy-start | bytes 1572868
  326.9 56.5 %collective-permute-start.21 = (bf16[8,4,128,256]{3,2,1,0:T(8,128)(2,1)}, bf16[8,4,128,256]{3,2,1,0:T(8,128)(2,1)}, u32[]{:S(2)}, u32[]{:S(2)}) collective-permute-start(bf16[8,4,128,256]{3,2,1,0:T(8,128)(2,1)} %get-tuple-element.158.refs_0_), channel_id=1, source_target_pairs={{0,2},{1,3},{2,0},{3,1},{4,6},{5,7},{6,4},{7,5},{8,10},{9,11},{10,... | collective-permute-start | bytes 6291464 | tf_op jit(solution)/shard_map/ppermute | solution.py:948
  328.1 71.5 %collective-permute-start.25 = (bf16[4,2,128,1024]{3,2,1,0:T(8,128)(2,1)}, bf16[4,2,128,1024]{3,2,1,0:T(8,128)(2,1)S(1)}, u32[]{:S(2)}, u32[]{:S(2)}) collective-permute-start(bf16[4,2,128,1024]{3,2,1,0:T(8,128)(2,1)} %get-tuple-element.185), channel_id=1, source_target_pairs={{0,4},{4,0},{8,12},{12,8},{16,20},{20,16},{24,28},{28,24},{1,5},{5... | collective-permute-start | bytes 6291464 | tf_op jit(solution)/shard_map/ppermute | solution.py:923
  328.6 31.5 %collective-permute-start.18 = (bf16[1,2,128,1024]{3,2,1,0:T(8,128)(2,1)S(1)}, bf16[1,2,128,1024]{3,2,1,0:T(8,128)(2,1)}, u32[]{:S(2)}, u32[]{:S(2)}) collective-permute-start(bf16[1,2,128,1024]{3,2,1,0:T(8,128)(2,1)S(1)} %copy-done.30), channel_id=1, source_target_pairs={{0,16},{4,20},{8,24},{12,28},{16,0},{20,4},{24,8},{28,12},{1,17},{... | collective-permute-start | bytes 1572872 | tf_op jit(solution)/shard_map/ppermute | solution.py:923
  332.9 40.0 %collective-permute-start.20 = (bf16[2,2,128,1024]{3,2,1,0:T(8,128)(2,1)}, bf16[2,2,128,1024]{3,2,1,0:T(8,128)(2,1)S(1)}, u32[]{:S(2)}, u32[]{:S(2)}) collective-permute-start(bf16[2,2,128,1024]{3,2,1,0:T(8,128)(2,1)} %get-tuple-element.161.refs_2_), channel_id=1, source_target_pairs={{0,8},{4,12},{8,0},{12,4},{16,24},{20,28},{24,16},{28,20},{1,9},{5... | collective-permute-start | bytes 3145736 | tf_op jit(solution)/shard_map/ppermute | solution.py:923
  365.8 31.2 %collective-permute-start.24 = (bf16[2,2,128,1024]{3,2,1,0:T(8,128)(2,1)}, bf16[2,2,128,1024]{3,2,1,0:T(8,128)(2,1)}, u32[]{:S(2)}, u32[]{:S(2)}) collective-permute-start(bf16[2,2,128,1024]{3,2,1,0:T(8,128)(2,1)} %get-tuple-element.171.refs_0_), channel_id=1, source_target_pairs={{0,8},{4,12},{8,0},{12,4},{16,24},{20,28},{24,16},{28,20},{1,9},{5... | collective-permute-start | bytes 3145736 | tf_op jit(solution)/shard_map/ppermute | solution.py:923
  367.7 5.2 copy-start.41
  367.7 8.8 %all-to-all-start.2 = ((bf16[2,512,1024]{2,1,0:T(8,128)(2,1)}), bf16[2,512,1024]{2,1,0:T(8,128)(2,1)}, u32[]{:S(2)}, u32[]{:S(2)}) async-start(bf16[2,512,1024]{2,1,0:T(8,128)(2,1)} %bitcast.50), calls=%async_computation.2 | async-start | bytes 4194304 | tf_op jit(solution)/shard_map/all_to_all | solution.py:1023
  382.9 4.7 copy-start.33
  382.9 4.7 collective-permute-start.22
  389.8 4.9 collective-permute-start.23
  390.4 64.2 %collective-permute-start.29 = (bf16[4,4,128,256]{3,2,1,0:T(8,128)(2,1)}, bf16[4,4,128,256]{3,2,1,0:T(8,128)(2,1)S(1)}, u32[]{:S(2)}, u32[]{:S(2)}) collective-permute-start(bf16[4,4,128,256]{3,2,1,0:T(8,128)(2,1)} %get-tuple-element.177.refs_0_), channel_id=1, source_target_pairs={{0,4},{4,0},{8,12},{12,8},{16,20},{20,16},{24,28},{28,24},{1,5},{5... | collective-permute-start | bytes 3145736 | tf_op jit(solution)/shard_map/ppermute | solution.py:923
  399.6 1.3 copy-start.7
  401.0 6.5 %copy-start.27 = (f32[24,1024]{1,0:T(8,128)S(1)}, f32[24,1024]{1,0:T(8,128)}, u32[]{:S(2)}) copy-start(f32[24,1024]{1,0:T(8,128)} %add_small.6.refs_0_.refs_1_) | copy-start | bytes 294916
  404.3 53.7 %collective-permute-start.30 = (bf16[2,2,128,1024]{3,2,1,0:T(8,128)(2,1)}, bf16[2,2,128,1024]{3,2,1,0:T(8,128)(2,1)S(1)}, u32[]{:S(2)}, u32[]{:S(2)}) collective-permute-start(bf16[2,2,128,1024]{3,2,1,0:T(8,128)(2,1)} %get-tuple-element.186.refs_2_), channel_id=1, source_target_pairs={{0,8},{4,12},{8,0},{12,4},{16,24},{20,28},{24,16},{28,20},{1,9},{5... | collective-permute-start | bytes 3145736 | tf_op jit(solution)/shard_map/ppermute | solution.py:923
  404.5 35.2 %collective-permute-start.26 = (bf16[1,2,128,1024]{3,2,1,0:T(8,128)(2,1)}, bf16[1,2,128,1024]{3,2,1,0:T(8,128)(2,1)S(1)}, u32[]{:S(2)}, u32[]{:S(2)}) collective-permute-start(bf16[1,2,128,1024]{3,2,1,0:T(8,128)(2,1)} %get-tuple-element.173.refs_0_), channel_id=1, source_target_pairs={{0,16},{4,20},{8,24},{12,28},{16,0},{20,4},{24,8},{28,12},{1,17},{... | collective-permute-start | bytes 1572872 | tf_op jit(solution)/shard_map/ppermute | solution.py:923
  407.0 42.2 %collective-permute-start.27 = (bf16[1,2,128,1024]{3,2,1,0:T(8,128)(2,1)}, bf16[1,2,128,1024]{3,2,1,0:T(8,128)(2,1)S(1)}, u32[]{:S(2)}, u32[]{:S(2)}) collective-permute-start(bf16[1,2,128,1024]{3,2,1,0:T(8,128)(2,1)} %get-tuple-element.183.refs_0_), channel_id=1, source_target_pairs={{0,16},{4,20},{8,24},{12,28},{16,0},{20,4},{24,8},{28,12},{1,17},{... | collective-permute-start | bytes 1572872 | tf_op jit(solution)/shard_map/ppermute | solution.py:923
  407.4 45.0 %collective-permute-start.28 = (f32[24,1024]{1,0:T(8,128)S(1)}, f32[24,1024]{1,0:T(8,128)S(1)}, u32[]{:S(2)}, u32[]{:S(2)}) collective-permute-start(f32[24,1024]{1,0:T(8,128)S(1)} %copy-done.27), channel_id=1, source_target_pairs={{0,4},{4,0},{8,12},{12,8},{16,20},{20,16},{24,28},{28,24},{1,5},{5... | collective-permute-start | bytes 294920 | tf_op jit(solution)/shard_map/ppermute | solution.py:910
  461.6 2.9 collective-permute-start.31
  461.6 7.8 %copy-start.31 = (bf16[2,4,128,256]{3,2,1,0:T(8,128)(2,1)S(1)}, bf16[2,4,128,256]{3,2,1,0:T(8,128)(2,1)}, u32[]{:S(2)}) copy-start(bf16[2,4,128,256]{3,2,1,0:T(8,128)(2,1)} %get-tuple-element.194.refs_0_) | copy-start | bytes 1572868
  461.6 11.7 %copy-start.3 = (bf16[1,2,128,1024]{3,2,1,0:T(8,128)(2,1)S(1)}, bf16[1,2,128,1024]{3,2,1,0:T(8,128)(2,1)}, u32[]{:S(2)}) copy-start(bf16[1,2,128,1024]{3,2,1,0:T(8,128)(2,1)} %get-tuple-element.196.refs_1_.refs_0_) | copy-start | bytes 1572868
  461.6 14.4 %copy-start.28 = (f32[24,1024]{1,0:T(8,128)S(1)}, f32[24,1024]{1,0:T(8,128)}, u32[]{:S(2)}) copy-start(f32[24,1024]{1,0:T(8,128)} %add_small.7.refs_0_.refs_1_) | copy-start | bytes 294916
  461.6 60.2 %collective-permute-start.36 = (bf16[512,1024]{1,0:T(8,128)(2,1)}, bf16[512,1024]{1,0:T(8,128)(2,1)S(1)}, u32[]{:S(2)}, u32[]{:S(2)}) collective-permute-start(bf16[512,1024]{1,0:T(8,128)(2,1)} %hold.15), channel_id=1, source_target_pairs={{0,1},{1,0},{2,3},{3,2},{4,5},{5,4},{6,7},{7,6},{8,9},{9,8},{10,11... | collective-permute-start | bytes 3145736 | tf_op jit(solution)/shard_map/ppermute | solution.py:945
  468.2 53.6 %collective-permute-start.37 = (bf16[512,1024]{1,0:T(8,128)(2,1)}, bf16[512,1024]{1,0:T(8,128)(2,1)S(1)}, u32[]{:S(2)}, u32[]{:S(2)}) collective-permute-start(bf16[512,1024]{1,0:T(8,128)(2,1)} %add_parts.3.refs_0_), channel_id=1, source_target_pairs={{0,2},{1,3},{2,0},{3,1},{4,6},{5,7},{6,4},{7,5},{8,10},{9,11},{10,... | collective-permute-start | bytes 3145736 | tf_op jit(solution)/shard_map/ppermute | solution.py:948
  469.4 27.6 %collective-permute-start.32 = (bf16[2,4,128,256]{3,2,1,0:T(8,128)(2,1)S(1)}, bf16[2,4,128,256]{3,2,1,0:T(8,128)(2,1)S(1)}, u32[]{:S(2)}, u32[]{:S(2)}) collective-permute-start(bf16[2,4,128,256]{3,2,1,0:T(8,128)(2,1)S(1)} %copy-done.31), channel_id=1, source_target_pairs={{0,8},{4,12},{8,0},{12,4},{16,24},{20,28},{24,16},{28,20},{1,9},{5... | collective-permute-start | bytes 1572872 | tf_op jit(solution)/shard_map/ppermute | solution.py:923
  473.3 31.7 %collective-permute-start.34 = (bf16[1,2,128,1024]{3,2,1,0:T(8,128)(2,1)S(1)}, bf16[1,2,128,1024]{3,2,1,0:T(8,128)(2,1)}, u32[]{:S(2)}, u32[]{:S(2)}) collective-permute-start(bf16[1,2,128,1024]{3,2,1,0:T(8,128)(2,1)S(1)} %copy-done.3), channel_id=1, source_target_pairs={{0,16},{4,20},{8,24},{12,28},{16,0},{20,4},{24,8},{28,12},{1,17},{... | collective-permute-start | bytes 1572872 | tf_op jit(solution)/shard_map/ppermute | solution.py:923
  476.0 23.9 %collective-permute-start.33 = (f32[24,1024]{1,0:T(8,128)S(1)}, f32[24,1024]{1,0:T(8,128)S(1)}, u32[]{:S(2)}, u32[]{:S(2)}) collective-permute-start(f32[24,1024]{1,0:T(8,128)S(1)} %copy-done.28), channel_id=1, source_target_pairs={{0,8},{4,12},{8,0},{12,4},{16,24},{20,28},{24,16},{28,20},{1,9},{5... | collective-permute-start | bytes 294920 | tf_op jit(solution)/shard_map/ppermute | solution.py:910
  499.8 4.4 copy-start.34
  502.1 13.5 %collective-permute-start.35 = (f32[24,1024]{1,0:T(8,128)}, f32[24,1024]{1,0:T(8,128)S(1)}, u32[]{:S(2)}, u32[]{:S(2)}) collective-permute-start(f32[24,1024]{1,0:T(8,128)} %add_small.8.refs_2_.refs_1_), channel_id=1, source_target_pairs={{0,16},{4,20},{8,24},{12,28},{16,0},{20,4},{24,8},{28,12},{1,17},{... | collective-permute-start | bytes 294920 | tf_op jit(solution)/shard_map/ppermute | solution.py:910
  504.2 24.4 %collective-permute-start.38 = (bf16[1,4,128,256]{3,2,1,0:T(8,128)(2,1)S(1)}, bf16[1,4,128,256]{3,2,1,0:T(8,128)(2,1)S(1)}, u32[]{:S(2)}, u32[]{:S(2)}) collective-permute-start(bf16[1,4,128,256]{3,2,1,0:T(8,128)(2,1)S(1)} %copy-done.34), channel_id=1, source_target_pairs={{0,16},{4,20},{8,24},{12,28},{16,0},{20,4},{24,8},{28,12},{1,17},{... | collective-permute-start | bytes 786440 | tf_op jit(solution)/shard_map/ppermute | solution.py:923
  (24 other events, 19.7 us)
Sparse Core Ops, SparseCore 0:
  152.2 106.1 reduce-scatter.1

commit v9 on v8

--- a/solution.py
+++ b/solution.py
@@ -1103,13 +1103,15 @@
         if ds == 1 or seqs == 1:
             for v in halvings[2:]:
                 v.launch()
+            mark = dense_sum.rest(mark)
+            up_out, down_out = last_add([dense_sum.keep, dense_sum.came], (False, True), deps=mark)
+            mark = (up_out,)
+            if seqs > 1:
+                grads[1] = hold(grads[1], mark)
             for v in halvings[:1]:
                 mark = v.add(mark)
     moved = [to_sequence(grads[ds], ds) for ds in range(1, seqs)]
     ng_parts = exchange(ngs.reshape(members, rows, d))
-    mark = dense_sum.rest(mark)
-    up_out, down_out = last_add([dense_sum.keep, dense_sum.came], (False, True), deps=mark)
-    mark = (up_out,)
     for v in halvings[1:2]:
         mark = v.add(mark)
     for v in halvings[:1]:
@@ -1138,19 +1140,17 @@
         keep, send = keep[:dp // 2], keep[dp // 2:]
     attn_sum = Halving(keep, send, straight)
     attn_sum.launch()
-    mark = sums.add(mark)
-    stacks, mark = finish(0, mark)
-    mark = sums.add(mark)
     for v in halvings[1:2]:
         mark = v.add(mark)
     for v in halvings[2:]:
         mark = v.add(mark)
-    for e in range(1, min(3, experts)):
+    for e in range(min(3, experts)):
         stacks, mark = finish(e, mark)
+    mark = attn_sum.add(mark)
     mark = sums.add(mark)
-    mark = attn_sum.add(mark)
     for v in halvings[2:]:
         mark = v.add(mark)
+    mark = sums.add(mark)
     out_near, out_far = to_owner([hold(v, mark) for v in out_e])
     out_came, terms = onward(out_far, mark)
     mark = tuple(terms[:1]) or mark

time: 542 us -> 536 us (0.989)
  starting transfers between devices: 47.2 us -> 40.5 us
    unnamed x97 -> x92, local copies, waits for them, and re-layouts: 28.8 us -> 32.4 us
    all_to_all x1 -> x2, blocking collectives: 19.9 us -> 17.7 us  [exchange(): lax.all_to_all(v, 'tensor', 0, 0, axis_index_groups=[[place(a, b) for b i...]
  transfers between devices with their start and end apart: 42 -> 41, of which waited for: 11 -> 15; matrix products, arithmetic and copies ran while one was open for 4% -> 4% of each run, Pallas kernels for 51% -> 52%
where the time goes in v9:
time: 536 us; the launch traced here: 529 us
  Pallas kernels  305 us (57%)
  waiting for transfers between devices  102 us (19%)
  local copies, waits for them, and re-layouts  41.6 us (8%)
  starting transfers between devices  40.5 us (8%)
  blocking collectives  17.7 us (3%)
  between operations  14.7 us (3%)
  other arithmetic  8.27 us (2%)
    pallas_call x2, Pallas kernels, ffn_experts(): pl.pallas_call(partial(expert_kernel, (first, count, whole, chunks, rows,...  76.5 us
    ppermute x17, waiting for transfers between devices, over_dp(): lax.ppermute(v, 'dp', [(i, i ^ 1 << bit) for i in range(lax.axis_size('dp...  71.2 us
    pallas_call x2, Pallas kernels, attn_backward(): pl.pallas_call(skip(partial(attn_backward_kernel, length, bits, len(extra...  52.7 us
    pallas_call x2, Pallas kernels, ffn_dense(): pl.pallas_call(partial(dense_kernel, (chunks, rows, tm, lanes, order, fir...  49.2 us
    pallas_call x11, Pallas kernels, split_add(): pl.pallas_call(partial(split_add_kernel, len(deps)), name='split_add', gr...  32.7 us
    unnamed x92, local copies, waits for them, and re-layouts  32.4 us
    pallas_call x3, Pallas kernels, attn_forward(): pl.pallas_call(skip(partial(attn_forward_kernel, length, tuple((w.shape[0...  31.7 us
    ppermute x17, starting transfers between devices, over_dp(): lax.ppermute(v, 'dp', [(i, i ^ 1 << bit) for i in range(lax.axis_size('dp...  22.1 us
  transfers between devices with their start and end apart: 41, of which 15 were waited for; matrix products, arithmetic and copies ran while one was open for 4% of the time, Pallas kernels for 52%

profile of v9, /device:TPU:0, one launch (start us, length us, event | category | flops | bytes accessed | tf_op | source)
XLA Modules:
  0.0 528.9 jit_solution(6474117091208648624)
XLA Ops:
  8.8 2.6 collective-permute-start
  15.0 5.1 first_norm.1
  20.2 4.0 collective-permute-done.refs_0_
  25.0 1.9 collective-permute-start.2
  30.9 14.4 %attn_forward.3 = (bf16[1024,256]{1,0:T(8,128)(2,1)}, bf16[1024,256]{1,0:T(8,128)(2,1)}, bf16[1024,256]{1,0:T(8,128)(2,1)}, bf16[1024,256]{1,0:T(8,128)(2,1)}, f32[2,8,1024]{2,1,0:T(8,128)}) custom-call(s32[1]{0:T(128)} %dynamic_slice.12.refs_0_, s32[2]{0:T(128)} %iota.11.refs_1_, bf16[2,1024,128]{2,1,0:T(8,128)(2,1)} %hold.9.refs_2_.refs_4_, ...), custom_call_target="tpu_custom_call" | custom-call | tf_op jit(solution)/shard_map/attn_forward/pallas_call | solution.py:549
  47.7 8.7 %attn_forward.4 = (bf16[1024,256]{1,0:T(8,128)(2,1)}, bf16[1024,256]{1,0:T(8,128)(2,1)}, bf16[1024,256]{1,0:T(8,128)(2,1)}, bf16[1024,256]{1,0:T(8,128)(2,1)}, f32[2,8,1024]{2,1,0:T(8,128)}) custom-call(s32[1]{0:T(128)} %dynamic_slice.12.refs_0_, s32[1]{0:T(128)} %bitcast.71, f32[2,8,1024]{2,1,0:T(8,128)} %get-tuple-element.115.refs_1_.refs_2_.refs_11_, ...), custom_call_target="tpu_custom_call" | custom-call | tf_op jit(solution)/shard_map/attn_forward/pallas_call | solution.py:549
  57.0 8.7 %attn_forward.5 = (bf16[1024,256]{1,0:T(8,128)(2,1)}, bf16[1024,256]{1,0:T(8,128)(2,1)}, bf16[1024,256]{1,0:T(8,128)(2,1)}, bf16[1024,256]{1,0:T(8,128)(2,1)}, f32[2,8,1024]{2,1,0:T(8,128)}) custom-call(s32[1]{0:T(128)} %dynamic_slice.12.refs_0_, s32[1]{0:T(128)} %bitcast.70, ...), custom_call_target="tpu_custom_call", output_to_operand_aliasing={{0}: (5, {}), {1}: (6, {}), {2}: (7, {}), {3}: (8, {}), {4}... | custom-call | tf_op jit(solution)/shard_map/attn_forward/pallas_call | solution.py:549
  66.5 3.8 project.1
  70.3 8.7 %all_to_all.15.came = bf16[2,512,1024]{2,1,0:T(8,128)(2,1)} all-to-all(bf16[2,512,1024]{2,1,0:T(8,128)(2,1)} %project.1), channel_id=1, replica_groups={{0,1},{2,3},{4,5},{6,7},{8,9},{10,11},{12,13},{14,15},{16,17},{18,19},{..., dimensions={0} | all-to-all | bytes 4194304 | tf_op jit(solution)/shard_map/all_to_all | solution.py:1023
  79.0 4.4 second_norm.1
  83.5 2.0 collective-permute-start.6
  86.5 23.1 %ffn_dense.2 = (bf16[512,1024]{1,0:T(8,128)(2,1)}, bf16[512,1024]{1,0:T(8,128)(2,1)}, bf16[528,1024]{1,0:T(8,128)(2,1)}, bf16[528,1024]{1,0:T(8,128)(2,1)}, f32[1024,1024]{1,0:T(8,128)}, /*index=5*/f32[1024,1024]{1,0:T(8,128)}) custom-call(s32[1]{0:T(128)} %bitcast.me_ref.refs_1_, bf16[512,1024]{1,0:T(8,128)(2,1)} %copy-done, ...), custom_call_target="tpu_custom_call" | custom-call | tf_op jit(solution)/shard_map/ffn_dense/pallas_call | solution.py:211
  116.0 24.9 %ffn_experts.2 = (bf16[512,1024]{1,0:T(8,128)(2,1)}, bf16[512,1024]{1,0:T(8,128)(2,1)}, bf16[512,1024]{1,0:T(8,128)(2,1)}, bf16[512,1024]{1,0:T(8,128)(2,1)}, bf...) custom-call(s32[1]{0:T(128)} %bitcast.me_ref.refs_1_, ...), custom_call_target="tpu_custom_call" | custom-call | tf_op jit(solution)/shard_map/ffn_experts/pallas_call | solution.py:392
  140.9 26.2 %ffn_dense.3 = (bf16[512,1024]{1,0:T(8,128)(2,1)}, bf16[512,1024]{1,0:T(8,128)(2,1)}, bf16[528,1024]{1,0:T(8,128)(2,1)}, bf16[528,1024]{1,0:T(8,128)(2,1)}, bf16...) custom-call(s32[1]{0:T(128)} %bitcast.me_ref.refs_1_, bf16[512,1024]{1,0:T(8,128)(2,1)} %hold.11.refs_1_.refs_0_, ...), custom_call_target="tpu_custom_call" | custom-call | tf_op jit(solution)/shard_map/ffn_dense/pallas_call | solution.py:211
  167.1 1.9 collective-permute-start.12
  169.0 51.6 %ffn_experts.3 = (bf16[512,1024]{1,0:T(8,128)(2,1)}, bf16[512,1024]{1,0:T(8,128)(2,1)}, bf16[512,1024]{1,0:T(8,128)(2,1)}, bf16[512,1024]{1,0:T(8,128)(2,1)}, bf...) custom-call(s32[1]{0:T(128)} %bitcast.me_ref.refs_1_, ...), custom_call_target="tpu_custom_call" | custom-call | tf_op jit(solution)/shard_map/ffn_experts/pallas_call | solution.py:392
  221.2 14.5 %collective-permute-done.12.refs_3_.refs_4_ = bf16[4,2,128,1024]{3,2,1,0:T(8,128)(2,1)S(1)} collective-permute-done((bf16[4,2,128,1024]{3,2,1,0:T(8,128)(2,1)}, bf16[4,2,128,1024]{3,2,1,0:T(8,128)(2,1)S(1)}, u32[]{:S(2)}, u32[]{:S(2)}) %collective-permute-start.12) | collective-permute-done | bytes 2097184 | tf_op jit(solution)/shard_map/ppermute | solution.py:923
  237.0 3.4 split_add.11
  241.3 2.9 add_parts.2.refs_2_
  250.6 1.7 maximum_select_fusion.refs_3_.refs_6_
  252.3 17.7 %collective-permute-done.15.refs_6_ = bf16[528,1024]{1,0:T(8,128)(2,1)} collective-permute-done((bf16[528,1024]{1,0:T(8,128)(2,1)}, bf16[528,1024]{1,0:T(8,128)(2,1)}, u32[]{:S(2)}, u32[]{:S(2)}) %collective-permute-start.15) | collective-permute-done | bytes 1081376 | tf_op jit(solution)/shard_map/ppermute | solution.py:948
  270.0 10.6 %middle_backward.1 = (f32[512,1024]{1,0:T(8,128)}, bf16[2,512,1024]{2,1,0:T(8,128)(2,1)}, f32[16,1024]{1,0:T(8,128)}) custom-call(s32[4,5]{1,0:T(4,128)} %stack.50.bnd_ref.refs_0_, s32[1]{0:T(128)} %bitcast.6.refs_1_, bf16[528,1024]{1,0:T(8,128)(2,1)} %add_parts.2.refs_2_, bf16[3,1024,256]{2,1,0:T(8,128)(2,1)} %maximum_select_fusion.refs_3_.refs_6_, ...), custom_call_target="tpu_custom_call" | custom-call | tf_op jit(solution)/shard_map/middle_backward/pallas_call | solution.py:812
  280.7 2.6 split_add.12
  284.4 9.0 %all_to_all.16 = bf16[2,512,1024]{2,1,0:T(8,128)(2,1)} all-to-all(bf16[2,512,1024]{2,1,0:T(8,128)(2,1)} %get-tuple-element.151.refs_0_), channel_id=1, replica_groups={{0,1},{2,3},{4,5},{6,7},{8,9},{10,11},{12,13},{14,15},{16,17},{18,19},{..., dimensions={0} | all-to-all | bytes 4194304 | tf_op jit(solution)/shard_map/all_to_all | solution.py:1023
  293.4 26.0 %attn_backward.2 = (bf16[1024,1024]{1,0:T(8,128)(2,1)}, bf16[8,4,128,256]{3,2,1,0:T(8,128)(2,1)}) custom-call(s32[1]{0:T(128)} %dynamic_slice.12.refs_0_, s32[1]{0:T(128)} %bitcast.me_ref.refs_1_, bf16[1,2,128,1024]{3,2,1,0:T(8,128)(2,1)} %get-tuple-element.153.refs_2_, bf16[1024,1024]{1,0:T(8,128)(2,1)} %bitcast.45, ...), custom_call_target="tpu_custom_call" | custom-call | tf_op jit(solution)/shard_map/attn_backward/pallas_call | solution.py:637
  320.2 2.4 last_add.6
  324.5 3.3 split_add.13
  327.9 26.7 %attn_backward.3 = (bf16[1024,1024]{1,0:T(8,128)(2,1)}, bf16[8,4,128,256]{3,2,1,0:T(8,128)(2,1)}) custom-call(s32[1]{0:T(128)} %dynamic_slice.12.refs_0_, s32[1]{0:T(128)} %bitcast.me_ref.refs_1_, bf16[2,2,128,1024]{3,2,1,0:T(8,128)(2,1)} %get-tuple-element.163.refs_2_, bf16[1024,1024]{1,0:T(8,128)(2,1)} %bitcast.46, ...), custom_call_target="tpu_custom_call" | custom-call | tf_op jit(solution)/shard_map/attn_backward/pallas_call | solution.py:637
  356.0 3.3 split_add.14
  359.3 1.9 collective-permute-start.22
  361.2 3.8 all-to-all-start.2
  365.0 2.7 split_add.15
  369.2 5.7 %input_backward.1 = (f32[512,1024]{1,0:T(8,128)}, f32[8,1024]{1,0:T(8,128)}) custom-call(bf16[1,2,128,1024]{3,2,1,0:T(8,128)(2,1)} %get-tuple-element.173.refs_0_, bf16[2,512,1024]{2,1,0:T(8,128)(2,1)} %copy-done.6, bf16[512,1024]{1,0:T(8,128)(2,1)} %refs_2_.3, f32[512,1024]{1,0:T(8,128)} %get-tuple-element.175.refs_3_, f32[1,1024]{1,0:T(1,128)} %bitcast.61), custom_call_target="tpu_custom_call" | custom-call | tf_op jit(solution)/shard_map/input_backward/pallas_call | solution.py:888
  374.8 4.4 split_add.16
  380.8 3.3 collective-permute-done.22.refs_3_.refs_4_
  385.0 2.7 split_add.17
  387.7 3.4 split_add.18
  391.0 1.7 collective-permute-start.28
  392.8 1.8 collective-permute-start.24
  395.9 2.1 last_add.7
  398.0 3.1 copy.87.refs_1_
  401.0 27.0 %collective-permute-done.24.refs_4_ = bf16[1,2,128,1024]{3,2,1,0:T(8,128)(2,1)S(1)} collective-permute-done((bf16[1,2,128,1024]{3,2,1,0:T(8,128)(2,1)}, bf16[1,2,128,1024]{3,2,1,0:T(8,128)(2,1)S(1)}, u32[]{:S(2)}, u32[]{:S(2)}) %collective-permute-start.24) | collective-permute-done | bytes 524320 | tf_op jit(solution)/shard_map/ppermute | solution.py:923
  428.8 2.4 last_add.8
  431.2 3.0 copy.89.refs_1_
  434.3 5.4 %collective-permute-done.25.refs_4_ = bf16[1,2,128,1024]{3,2,1,0:T(8,128)(2,1)S(1)} collective-permute-done((bf16[1,2,128,1024]{3,2,1,0:T(8,128)(2,1)}, bf16[1,2,128,1024]{3,2,1,0:T(8,128)(2,1)S(1)}, u32[]{:S(2)}, u32[]{:S(2)}) %collective-permute-start.25) | collective-permute-done | bytes 524320 | tf_op jit(solution)/shard_map/ppermute | solution.py:923
  440.5 2.4 last_add.9
  443.9 2.4 split_add.19
  446.9 1.6 add_small.5.refs_0_.refs_1_
  450.0 2.6 split_add.20
  453.9 1.6 add_small.6.refs_1_.refs_0_
  459.4 2.8 add_parts.3.refs_0_
  463.0 2.5 collective-permute-start.33
  466.7 20.7 %collective-permute-done.31.refs_3_.refs_4_ = bf16[2,4,128,256]{3,2,1,0:T(8,128)(2,1)S(1)} collective-permute-done((bf16[2,4,128,256]{3,2,1,0:T(8,128)(2,1)}, bf16[2,4,128,256]{3,2,1,0:T(8,128)(2,1)S(1)}, u32[]{:S(2)}, u32[]{:S(2)}) %collective-permute-start.31) | collective-permute-done | bytes 524320 | tf_op jit(solution)/shard_map/ppermute | solution.py:923
  488.2 2.1 split_add.21
  490.9 1.6 add_small.7.refs_2_.refs_1_
  492.5 2.4 last_add.10
  494.9 2.4 collective-permute-done.34.refs_2_
  498.0 1.6 add_small.8.refs_0_.refs_1_
  500.0 2.5 collective-permute-start.38
  504.5 4.9 layer_out.1.refs_0_
  509.4 2.2 collective-permute-done.37.refs_2_
  512.2 1.6 add_small.9.refs_0_
  516.8 1.9 last_add.11
  518.7 1.8 pad_maximum_fusion
  (198 shorter events, 62.6 us)
Async XLA Ops:
  7.2 388.7 %reduce-scatter.2.cloned.1.call-start = ((), (), s32[]{:S(2)}) async-start(), calls=%async_computation.4 | async-start | bytes 4718592 | tf_op jit(solution)/shard_map/reduce_scatter | solution.py:1083
  7.2 6.8 %collective-permute-start.1 = (bf16[512,1024]{1,0:T(8,128)(2,1)}, bf16[512,1024]{1,0:T(8,128)(2,1)S(1)}, u32[]{:S(2)}, u32[]{:S(2)}) collective-permute-start(bf16[512,1024]{1,0:T(8,128)(2,1)} %refs_2_.3), channel_id=1, source_target_pairs={{0,1},{1,0},{2,3},{3,2},{4,5},{5,4},{6,7},{7,6},{8,9},{9,8},{10,11... | collective-permute-start | bytes 3145736 | tf_op jit(solution)/shard_map/ppermute | solution.py:945
  8.8 15.4 %collective-permute-start = (bf16[2,1024,128]{2,1,0:T(8,128)(2,1)S(1)}, bf16[2,1024,128]{2,1,0:T(8,128)(2,1)S(1)}, u32[]{:S(2)}, u32[]{:S(2)}) collective-permute-start(bf16[2,1024,128]{2,1,0:T(8,128)(2,1)S(1)} %dynamic-slice_bitcast_fusion), channel_id=1, source_target_pairs={{0,2},{1,3},{2,0},{3,1},{4,6},{5,7},{6,4},{7,5},{8,10},{9,11},{10,... | collective-permute-start | bytes 1572872 | tf_op jit(solution)/shard_map/ppermute | solution.py:948
  12.4 32.9 %collective-permute-start.3 = (bf16[1,1024,128]{2,1,0:T(8,128)(2,1)S(1)}, bf16[1,1024,128]{2,1,0:T(8,128)(2,1)S(1)}, u32[]{:S(2)}, u32[]{:S(2)}) collective-permute-start(bf16[1,1024,128]{2,1,0:T(8,128)(2,1)S(1)} %dynamic-slice_bitcast_fusion.1), channel_id=1, source_target_pairs={{0,2},{1,3},{2,0},{3,1},{4,6},{5,7},{6,4},{7,5},{8,10},{9,11},{10,... | collective-permute-start | bytes 786440 | tf_op jit(solution)/shard_map/ppermute | solution.py:948
  20.2 6.8 %copy-start.16 = (bf16[256,1024]{1,0:T(8,128)(2,1)S(1)}, bf16[256,1024]{1,0:T(8,128)(2,1)}, u32[]{:S(2)}) copy-start(bf16[256,1024]{1,0:T(8,128)(2,1)} %refs_5_.3) | copy-start | bytes 1572868
  20.2 8.3 %copy-start.40 = (bf16[1024,4]{0,1:T(4,128)(2,1)S(1)}, bf16[1024,4]{0,1:T(4,128)(2,1)}, u32[]{:S(2)}) copy-start(bf16[1024,4]{0,1:T(4,128)(2,1)} %param.30) | copy-start | bytes 24580
  20.2 8.5 %copy-start.41 = (bf16[1024,2]{0,1:T(2,128)(2,1)S(1)}, bf16[1024,2]{0,1:T(2,128)(2,1)}, u32[]{:S(2)}) copy-start(bf16[1024,2]{0,1:T(2,128)(2,1)} %param.31) | copy-start | bytes 12292
  20.2 8.7 %copy-start.42 = (s32[2]{0:T(128)S(1)}, s32[2]{0:T(128)}, u32[]{:S(2)}) copy-start(s32[2]{0:T(128)} %param.19) | copy-start | bytes 28
  25.0 31.3 %collective-permute-start.2 = (bf16[2,1024,128]{2,1,0:T(8,128)(2,1)}, bf16[2,1024,128]{2,1,0:T(8,128)(2,1)}, u32[]{:S(2)}, u32[]{:S(2)}) collective-permute-start(bf16[2,1024,128]{2,1,0:T(8,128)(2,1)} %hold.9.refs_2_.refs_4_), channel_id=1, source_target_pairs={{0,4},{4,0},{8,12},{12,8},{16,20},{20,16},{24,28},{28,24},{1,5},{5... | collective-permute-start | bytes 1572872 | tf_op jit(solution)/shard_map/ppermute | solution.py:923
  26.9 38.8 %collective-permute-start.5 = (bf16[256,1024]{1,0:T(8,128)(2,1)S(1)}, bf16[256,1024]{1,0:T(8,128)(2,1)S(1)}, u32[]{:S(2)}, u32[]{:S(2)}) collective-permute-start(bf16[256,1024]{1,0:T(8,128)(2,1)S(1)} %copy-done.16), channel_id=1, source_target_pairs={{0,2},{1,3},{2,0},{3,1},{4,6},{5,7},{6,4},{7,5},{8,10},{9,11},{10,... | collective-permute-start | bytes 1572872 | tf_op jit(solution)/shard_map/ppermute | solution.py:948
  30.9 16.6 %copy-start.2 = (bf16[512,1024]{1,0:T(8,128)(2,1)S(1)}, bf16[512,1024]{1,0:T(8,128)(2,1)}, u32[]{:S(2)}) copy-start(bf16[512,1024]{1,0:T(8,128)(2,1)} %get-tuple-element.123.refs_3_.refs_4_) | copy-start | bytes 3145732
  46.0 10.3 %collective-permute-start.4 = (bf16[1,1024,128]{2,1,0:T(8,128)(2,1)}, bf16[1,1024,128]{2,1,0:T(8,128)(2,1)S(1)}, u32[]{:S(2)}, u32[]{:S(2)}) collective-permute-start(bf16[1,1024,128]{2,1,0:T(8,128)(2,1)} %hold.10.refs_5_), channel_id=1, source_target_pairs={{0,4},{4,0},{8,12},{12,8},{16,20},{20,16},{24,28},{28,24},{1,5},{5... | collective-permute-start | bytes 786440 | tf_op jit(solution)/shard_map/ppermute | solution.py:923
  47.6 37.9 %collective-permute-start.9 = (bf16[512,1024]{1,0:T(8,128)(2,1)S(1)}, bf16[512,1024]{1,0:T(8,128)(2,1)}, u32[]{:S(2)}, u32[]{:S(2)}) collective-permute-start(bf16[512,1024]{1,0:T(8,128)(2,1)S(1)} %copy-done.2), channel_id=1, source_target_pairs={{0,1},{1,0},{2,3},{3,2},{4,5},{5,4},{6,7},{7,6},{8,9},{9,8},{10,11... | collective-permute-start | bytes 3145736 | tf_op jit(solution)/shard_map/ppermute | solution.py:945
  47.6 37.9 %collective-permute-start.7 = (bf16[512,1024]{1,0:T(8,128)(2,1)S(1)}, bf16[512,1024]{1,0:T(8,128)(2,1)S(1)}, u32[]{:S(2)}, u32[]{:S(2)}) collective-permute-start(bf16[512,1024]{1,0:T(8,128)(2,1)S(1)} %copy-done.2), channel_id=1, source_target_pairs={{0,2},{1,3},{2,0},{3,1},{4,6},{5,7},{6,4},{7,5},{8,10},{9,11},{10,... | collective-permute-start | bytes 3145736 | tf_op jit(solution)/shard_map/ppermute | solution.py:948
  83.4 3.0 collective-permute-start.8
  83.5 26.0 %collective-permute-start.6 = (bf16[512,1024]{1,0:T(8,128)(2,1)}, bf16[512,1024]{1,0:T(8,128)(2,1)S(1)}, u32[]{:S(2)}, u32[]{:S(2)}) collective-permute-start(bf16[512,1024]{1,0:T(8,128)(2,1)} %get-tuple-element.122.refs_1_.refs_0_.refs_7_), channel_id=1, source_target_pairs={{0,2},{1,3},{2,0},{3,1},{4,6},{5,7},{6,4},{7,5},{8,10},{9,11},{10,... | collective-permute-start | bytes 3145736 | tf_op jit(solution)/shard_map/ppermute | solution.py:948
  85.5 1.0 copy-start
  109.6 1.0 copy-start.1
  110.6 3.3 collective-permute-start.10
  110.6 4.3 collective-permute-start.11
  113.8 1.1 copy-start.3
  114.9 1.0 copy-start.4
  167.1 68.6 %collective-permute-start.12 = (bf16[4,2,128,1024]{3,2,1,0:T(8,128)(2,1)}, bf16[4,2,128,1024]{3,2,1,0:T(8,128)(2,1)S(1)}, u32[]{:S(2)}, u32[]{:S(2)}) collective-permute-start(bf16[4,2,128,1024]{3,2,1,0:T(8,128)(2,1)} %get-tuple-element.144), channel_id=1, source_target_pairs={{0,4},{4,0},{8,12},{12,8},{16,20},{20,16},{24,28},{28,24},{1,5},{5... | collective-permute-start | bytes 6291464 | tf_op jit(solution)/shard_map/ppermute | solution.py:923
  220.6 19.8 %collective-permute-start.13 = (bf16[528,1024]{1,0:T(8,128)(2,1)}, bf16[528,1024]{1,0:T(8,128)(2,1)S(1)}, u32[]{:S(2)}, u32[]{:S(2)}) collective-permute-start(bf16[528,1024]{1,0:T(8,128)(2,1)} %get-tuple-element.147), channel_id=1, source_target_pairs={{0,1},{1,0},{2,3},{3,2},{4,5},{5,4},{6,7},{7,6},{8,9},{9,8},{10,11... | collective-permute-start | bytes 3244040 | tf_op jit(solution)/shard_map/ppermute | solution.py:945
  220.7 31.6 %collective-permute-start.14 = (bf16[528,1024]{1,0:T(8,128)(2,1)}, bf16[528,1024]{1,0:T(8,128)(2,1)}, u32[]{:S(2)}, u32[]{:S(2)}) collective-permute-start(bf16[528,1024]{1,0:T(8,128)(2,1)} %get-tuple-element.149), channel_id=1, source_target_pairs={{0,1},{1,0},{2,3},{3,2},{4,5},{5,4},{6,7},{7,6},{8,9},{9,8},{10,11... | collective-permute-start | bytes 3244040 | tf_op jit(solution)/shard_map/ppermute | solution.py:945
  235.7 1.3 copy-start.9
  241.3 9.2 %copy-start.25 = (bf16[1,1024,128]{2,1,0:T(8,128)(2,1)S(1)}, bf16[1,1024,128]{2,1,0:T(8,128)(2,1)}, u32[]{:S(2)}) copy-start(bf16[1,1024,128]{2,1,0:T(8,128)(2,1)} %copy-done.24) | copy-start | bytes 786436
  241.3 9.3 %copy-start.8 = (bf16[2,1024,128]{2,1,0:T(8,128)(2,1)S(1)}, bf16[2,1024,128]{2,1,0:T(8,128)(2,1)}, u32[]{:S(2)}) copy-start(bf16[2,1024,128]{2,1,0:T(8,128)(2,1)} %hold.9.refs_2_.refs_4_) | copy-start | bytes 1572868
  241.3 9.3 %copy-start.15 = (bf16[1,1024,128]{2,1,0:T(8,128)(2,1)S(1)}, bf16[1,1024,128]{2,1,0:T(8,128)(2,1)}, u32[]{:S(2)}) copy-start(bf16[1,1024,128]{2,1,0:T(8,128)(2,1)} %hold.10.refs_5_) | copy-start | bytes 786436
  244.2 25.8 %collective-permute-start.15 = (bf16[528,1024]{1,0:T(8,128)(2,1)}, bf16[528,1024]{1,0:T(8,128)(2,1)}, u32[]{:S(2)}, u32[]{:S(2)}) collective-permute-start(bf16[528,1024]{1,0:T(8,128)(2,1)} %add_parts.2.refs_2_), channel_id=1, source_target_pairs={{0,2},{1,3},{2,0},{3,1},{4,6},{5,7},{6,4},{7,5},{8,10},{9,11},{10,... | collective-permute-start | bytes 3244040 | tf_op jit(solution)/shard_map/ppermute | solution.py:948
  245.7 35.0 %collective-permute-start.16 = (bf16[2,2,128,1024]{3,2,1,0:T(8,128)(2,1)}, bf16[2,2,128,1024]{3,2,1,0:T(8,128)(2,1)}, u32[]{:S(2)}, u32[]{:S(2)}) collective-permute-start(bf16[2,2,128,1024]{3,2,1,0:T(8,128)(2,1)} %get-tuple-element.145.refs_0_), channel_id=1, source_target_pairs={{0,8},{4,12},{8,0},{12,4},{16,24},{20,28},{24,16},{28,20},{1,9},{5... | collective-permute-start | bytes 3145736 | tf_op jit(solution)/shard_map/ppermute | solution.py:923
  246.6 77.9 %collective-permute-start.18 = (bf16[4,2,128,1024]{3,2,1,0:T(8,128)(2,1)}, bf16[4,2,128,1024]{3,2,1,0:T(8,128)(2,1)}, u32[]{:S(2)}, u32[]{:S(2)}) collective-permute-start(bf16[4,2,128,1024]{3,2,1,0:T(8,128)(2,1)} %get-tuple-element.162), channel_id=1, source_target_pairs={{0,4},{4,0},{8,12},{12,8},{16,20},{20,16},{24,28},{28,24},{1,5},{5... | collective-permute-start | bytes 6291464 | tf_op jit(solution)/shard_map/ppermute | solution.py:923
  247.9 106.7 %collective-permute-start.19 = (bf16[4,2,128,1024]{3,2,1,0:T(8,128)(2,1)}, bf16[4,2,128,1024]{3,2,1,0:T(8,128)(2,1)S(1)}, u32[]{:S(2)}, u32[]{:S(2)}) collective-permute-start(bf16[4,2,128,1024]{3,2,1,0:T(8,128)(2,1)} %get-tuple-element.170), channel_id=1, source_target_pairs={{0,4},{4,0},{8,12},{12,8},{16,20},{20,16},{24,28},{28,24},{1,5},{5... | collective-permute-start | bytes 6291464 | tf_op jit(solution)/shard_map/ppermute | solution.py:923
  283.3 36.1 %collective-permute-start.17 = (bf16[1,2,128,1024]{3,2,1,0:T(8,128)(2,1)}, bf16[1,2,128,1024]{3,2,1,0:T(8,128)(2,1)S(1)}, u32[]{:S(2)}, u32[]{:S(2)}) collective-permute-start(bf16[1,2,128,1024]{3,2,1,0:T(8,128)(2,1)} %get-tuple-element.153.refs_2_), channel_id=1, source_target_pairs={{0,16},{4,20},{8,24},{12,28},{16,0},{20,4},{24,8},{28,12},{1,17},{... | collective-permute-start | bytes 1572872 | tf_op jit(solution)/shard_map/ppermute | solution.py:923
  322.6 52.2 %collective-permute-start.21 = (bf16[8,4,128,256]{3,2,1,0:T(8,128)(2,1)}, bf16[8,4,128,256]{3,2,1,0:T(8,128)(2,1)}, u32[]{:S(2)}, u32[]{:S(2)}) collective-permute-start(bf16[8,4,128,256]{3,2,1,0:T(8,128)(2,1)} %hold.13), channel_id=1, source_target_pairs={{0,2},{1,3},{2,0},{3,1},{4,6},{5,7},{6,4},{7,5},{8,10},{9,11},{10,... | collective-permute-start | bytes 6291464 | tf_op jit(solution)/shard_map/ppermute | solution.py:948
  324.0 63.6 %collective-permute-start.23 = (bf16[4,2,128,1024]{3,2,1,0:T(8,128)(2,1)}, bf16[4,2,128,1024]{3,2,1,0:T(8,128)(2,1)}, u32[]{:S(2)}, u32[]{:S(2)}) collective-permute-start(bf16[4,2,128,1024]{3,2,1,0:T(8,128)(2,1)} %get-tuple-element.181), channel_id=1, source_target_pairs={{0,4},{4,0},{8,12},{12,8},{16,20},{20,16},{24,28},{28,24},{1,5},{5... | collective-permute-start | bytes 6291464 | tf_op jit(solution)/shard_map/ppermute | solution.py:923
  327.8 37.2 %collective-permute-start.20 = (bf16[2,2,128,1024]{3,2,1,0:T(8,128)(2,1)}, bf16[2,2,128,1024]{3,2,1,0:T(8,128)(2,1)}, u32[]{:S(2)}, u32[]{:S(2)}) collective-permute-start(bf16[2,2,128,1024]{3,2,1,0:T(8,128)(2,1)} %get-tuple-element.163.refs_2_), channel_id=1, source_target_pairs={{0,8},{4,12},{8,0},{12,4},{16,24},{20,28},{24,16},{28,20},{1,9},{5... | collective-permute-start | bytes 3145736 | tf_op jit(solution)/shard_map/ppermute | solution.py:923
  354.6 1.3 copy-start.5
  359.3 24.7 %collective-permute-start.22 = (bf16[2,2,128,1024]{3,2,1,0:T(8,128)(2,1)}, bf16[2,2,128,1024]{3,2,1,0:T(8,128)(2,1)S(1)}, u32[]{:S(2)}, u32[]{:S(2)}) collective-permute-start(bf16[2,2,128,1024]{3,2,1,0:T(8,128)(2,1)} %get-tuple-element.171.refs_0_), channel_id=1, source_target_pairs={{0,8},{4,12},{8,0},{12,4},{16,24},{20,28},{24,16},{28,20},{1,9},{5... | collective-permute-start | bytes 3145736 | tf_op jit(solution)/shard_map/ppermute | solution.py:923
  361.2 6.6 %all-to-all-start.2 = ((bf16[2,512,1024]{2,1,0:T(8,128)(2,1)}), bf16[2,512,1024]{2,1,0:T(8,128)(2,1)S(1)}, u32[]{:S(2)}, u32[]{:S(2)}) async-start(bf16[2,512,1024]{2,1,0:T(8,128)(2,1)} %bitcast.50), calls=%async_computation.2 | async-start | bytes 4194304 | tf_op jit(solution)/shard_map/all_to_all | solution.py:1023
  367.8 1.3 copy-start.6
  379.2 63.7 %collective-permute-start.26 = (bf16[4,4,128,256]{3,2,1,0:T(8,128)(2,1)}, bf16[4,4,128,256]{3,2,1,0:T(8,128)(2,1)S(1)}, u32[]{:S(2)}, u32[]{:S(2)}) collective-permute-start(bf16[4,4,128,256]{3,2,1,0:T(8,128)(2,1)} %get-tuple-element.177.refs_0_), channel_id=1, source_target_pairs={{0,4},{4,0},{8,12},{12,8},{16,20},{20,16},{24,28},{28,24},{1,5},{5... | collective-permute-start | bytes 3145736 | tf_op jit(solution)/shard_map/ppermute | solution.py:923
  387.7 8.0 %copy-start.38 = (f32[16,1024]{1,0:T(8,128)S(1)}, f32[16,1024]{1,0:T(8,128)}, u32[]{:S(2)}) copy-start(f32[16,1024]{1,0:T(8,128)} %get-tuple-element.194) | copy-start | bytes 196612
  387.7 8.0 %copy-start.32 = (f32[8,1024]{1,0:T(8,128)S(1)}, f32[8,1024]{1,0:T(8,128)}, u32[]{:S(2)}) copy-start(f32[8,1024]{1,0:T(8,128)} %get-tuple-element.176.refs_0_) | copy-start | bytes 98308
  391.0 58.0 %collective-permute-start.28 = (bf16[2,2,128,1024]{3,2,1,0:T(8,128)(2,1)}, bf16[2,2,128,1024]{3,2,1,0:T(8,128)(2,1)S(1)}, u32[]{:S(2)}, u32[]{:S(2)}) collective-permute-start(bf16[2,2,128,1024]{3,2,1,0:T(8,128)(2,1)} %get-tuple-element.182.refs_0_), channel_id=1, source_target_pairs={{0,8},{4,12},{8,0},{12,4},{16,24},{20,28},{24,16},{28,20},{1,9},{5... | collective-permute-start | bytes 3145736 | tf_op jit(solution)/shard_map/ppermute | solution.py:923
  392.8 35.2 %collective-permute-start.24 = (bf16[1,2,128,1024]{3,2,1,0:T(8,128)(2,1)}, bf16[1,2,128,1024]{3,2,1,0:T(8,128)(2,1)S(1)}, u32[]{:S(2)}, u32[]{:S(2)}) collective-permute-start(bf16[1,2,128,1024]{3,2,1,0:T(8,128)(2,1)} %get-tuple-element.173.refs_0_), channel_id=1, source_target_pairs={{0,16},{4,20},{8,24},{12,28},{16,0},{20,4},{24,8},{28,12},{1,17},{... | collective-permute-start | bytes 1572872 | tf_op jit(solution)/shard_map/ppermute | solution.py:923
  394.6 45.1 %collective-permute-start.25 = (bf16[1,2,128,1024]{3,2,1,0:T(8,128)(2,1)}, bf16[1,2,128,1024]{3,2,1,0:T(8,128)(2,1)S(1)}, u32[]{:S(2)}, u32[]{:S(2)}) collective-permute-start(bf16[1,2,128,1024]{3,2,1,0:T(8,128)(2,1)} %get-tuple-element.179.refs_0_), channel_id=1, source_target_pairs={{0,16},{4,20},{8,24},{12,28},{16,0},{20,4},{24,8},{28,12},{1,17},{... | collective-permute-start | bytes 1572872 | tf_op jit(solution)/shard_map/ppermute | solution.py:923
  395.7 5.3 %copy-start.30 = (f32[24,1024]{1,0:T(8,128)}, f32[24,1024]{1,0:T(8,128)S(1)}, u32[]{:S(2)}) copy-start(f32[24,1024]{1,0:T(8,128)S(1)} %constant_dynamic-update-slice_fusion.2.refs_1_) | copy-start | bytes 294916
  395.7 50.5 %collective-permute-start.27 = (f32[24,1024]{1,0:T(8,128)S(1)}, f32[24,1024]{1,0:T(8,128)S(1)}, u32[]{:S(2)}, u32[]{:S(2)}) collective-permute-start(f32[24,1024]{1,0:T(8,128)S(1)} %constant_dynamic-update-slice_fusion.2.refs_1_), channel_id=1, source_target_pairs={{0,1},{1,0},{2,3},{3,2},{4,5},{5,4},{6,7},{7,6},{8,9},{9,8},{10,11... | collective-permute-start | bytes 294920 | tf_op jit(solution)/shard_map/ppermute | solution.py:910
  448.5 4.8 collective-permute-start.29
  455.5 2.9 collective-permute-start.30
  455.5 1.2 copy-start.26
  456.7 8.7 %copy-start.10 = (f32[24,1024]{1,0:T(8,128)S(1)}, f32[24,1024]{1,0:T(8,128)}, u32[]{:S(2)}) copy-start(f32[24,1024]{1,0:T(8,128)} %add_small.6.refs_1_.refs_0_) | copy-start | bytes 294916
  456.7 45.8 %collective-permute-start.35 = (bf16[512,1024]{1,0:T(8,128)(2,1)S(1)}, bf16[512,1024]{1,0:T(8,128)(2,1)S(1)}, u32[]{:S(2)}, u32[]{:S(2)}) collective-permute-start(bf16[512,1024]{1,0:T(8,128)(2,1)S(1)} %copy-done.26), channel_id=1, source_target_pairs={{0,1},{1,0},{2,3},{3,2},{4,5},{5,4},{6,7},{7,6},{8,9},{9,8},{10,11... | collective-permute-start | bytes 3145736 | tf_op jit(solution)/shard_map/ppermute | solution.py:945
  462.2 40.4 %collective-permute-start.36 = (bf16[512,1024]{1,0:T(8,128)(2,1)}, bf16[512,1024]{1,0:T(8,128)(2,1)S(1)}, u32[]{:S(2)}, u32[]{:S(2)}) collective-permute-start(bf16[512,1024]{1,0:T(8,128)(2,1)} %add_parts.3.refs_0_), channel_id=1, source_target_pairs={{0,2},{1,3},{2,0},{3,1},{4,6},{5,7},{6,4},{7,5},{8,10},{9,11},{10,... | collective-permute-start | bytes 3145736 | tf_op jit(solution)/shard_map/ppermute | solution.py:948
  463.0 24.5 %collective-permute-start.31 = (bf16[2,4,128,256]{3,2,1,0:T(8,128)(2,1)}, bf16[2,4,128,256]{3,2,1,0:T(8,128)(2,1)S(1)}, u32[]{:S(2)}, u32[]{:S(2)}) collective-permute-start(bf16[2,4,128,256]{3,2,1,0:T(8,128)(2,1)} %get-tuple-element.193.refs_0_), channel_id=1, source_target_pairs={{0,8},{4,12},{8,0},{12,4},{16,24},{20,28},{24,16},{28,20},{1,9},{5... | collective-permute-start | bytes 1572872 | tf_op jit(solution)/shard_map/ppermute | solution.py:923
  463.0 29.6 %collective-permute-start.33 = (bf16[1,2,128,1024]{3,2,1,0:T(8,128)(2,1)}, bf16[1,2,128,1024]{3,2,1,0:T(8,128)(2,1)}, u32[]{:S(2)}, u32[]{:S(2)}) collective-permute-start(bf16[1,2,128,1024]{3,2,1,0:T(8,128)(2,1)} %get-tuple-element.196.refs_0_), channel_id=1, source_target_pairs={{0,16},{4,20},{8,24},{12,28},{16,0},{20,4},{24,8},{28,12},{1,17},{... | collective-permute-start | bytes 1572872 | tf_op jit(solution)/shard_map/ppermute | solution.py:923
  465.5 24.8 %collective-permute-start.32 = (f32[24,1024]{1,0:T(8,128)S(1)}, f32[24,1024]{1,0:T(8,128)S(1)}, u32[]{:S(2)}, u32[]{:S(2)}) collective-permute-start(f32[24,1024]{1,0:T(8,128)S(1)} %copy-done.10), channel_id=1, source_target_pairs={{0,4},{4,0},{8,12},{12,8},{16,20},{20,16},{24,28},{28,24},{1,5},{5... | collective-permute-start | bytes 294920 | tf_op jit(solution)/shard_map/ppermute | solution.py:910
  492.5 4.8 collective-permute-start.34
  494.9 5.1 copy-start.31
  499.6 12.0 %collective-permute-start.37 = (f32[24,1024]{1,0:T(8,128)}, f32[24,1024]{1,0:T(8,128)S(1)}, u32[]{:S(2)}, u32[]{:S(2)}) collective-permute-start(f32[24,1024]{1,0:T(8,128)} %add_small.8.refs_0_.refs_1_), channel_id=1, source_target_pairs={{0,16},{4,20},{8,24},{12,28},{16,0},{20,4},{24,8},{28,12},{1,17},{... | collective-permute-start | bytes 294920 | tf_op jit(solution)/shard_map/ppermute | solution.py:910
  500.0 16.8 %collective-permute-start.38 = (bf16[1,4,128,256]{3,2,1,0:T(8,128)(2,1)S(1)}, bf16[1,4,128,256]{3,2,1,0:T(8,128)(2,1)}, u32[]{:S(2)}, u32[]{:S(2)}) collective-permute-start(bf16[1,4,128,256]{3,2,1,0:T(8,128)(2,1)S(1)} %copy-done.31), channel_id=1, source_target_pairs={{0,16},{4,20},{8,24},{12,28},{16,0},{20,4},{24,8},{28,12},{1,17},{... | collective-permute-start | bytes 786440 | tf_op jit(solution)/shard_map/ppermute | solution.py:923
  502.5 1.0 copy-start.20
  503.5 1.0 copy-start.21
  (20 other events, 16.0 us)
Sparse Core Ops, SparseCore 0:
  141.0 105.6 reduce-scatter.1
